TPU v7x, 32 devices: a whole 2x2x4 slice. The times are simulated.
32 devices in a mesh: dom: 8 (over z, y), pipe: 4 (over x, core).
Axes of the slice: x: 2, y: 2, z: 4, core: 2. Of those that a mesh axis runs over, the one named last changes fastest.
Arguments:
- inputs: bfloat16 [2, 2048, 512], P(None, 'dom'), may hold values from -6 to 6
- cotangent: bfloat16 [2, 2048, 512], P(None, 'dom'), may hold values from -6 to 6
- w_send: bfloat16 [4, 512, 512], P('pipe'), may hold values from -0.25 to 0.25
- w_recv: bfloat16 [4, 512, 512], P('pipe'), may hold values from -0.25 to 0.25
- w_message: bfloat16 [4, 512, 512], P('pipe'), may hold values from -0.25 to 0.25
- w_node: bfloat16 [4, 512, 512], P('pipe'), may hold values from -0.25 to 0.25
- w_aggregate: bfloat16 [4, 512, 512], P('pipe'), may hold values from -0.25 to 0.25
- gains: float32 [4, 512], P('pipe'), may hold values from 0.1 to 1.9
- edge_send: int32 [16, 128], P('dom'), may hold values from 0 to 511, as said below
- edge_recv: int32 [16, 128], P('dom'), may hold values from 0 to 255, as said below
- edge_count: int32 [16], P('dom'), may hold values from 1 to 128, as said below
- halo_send: int32 [8, 2, 1], P('dom'), may hold values from 0 to 1, as said below
Outputs:
- section_out: bfloat16 [4, 2, 2048, 512], P('pipe', None, 'dom')
- input_grad: bfloat16 [4, 2, 2048, 512], P('pipe', None, 'dom')
Inputs may be any that keep to these rules, and one draw needn't show every extreme that they name: `edge_send`: rows 0 to 255 are the partition's own rows, the next 128 the blocks received from the previous partition in list order, the last 128 those from the next partition. The largest and smallest values are reached. `edge_recv`: both ends are reached. `edge_count`: the live slots of a block are its first ones; one block is full and one has a single live slot. `halo_send`: each list names 1 distinct own blocks. Lists wrap around the partitions.
All inputs are finite; a program needn't handle non-finite values.
Results may differ from a plain program's by a relative error of at most 0.015.
Values may be sent and summed in bfloat16 or wider, within the bound.
No kernel may reach another device: no remote copies, remote signals or barrier semaphores. Data moves between devices by JAX's collectives and lax.ppermute only.
A program may use at most 64 MiB of HBM per device.

v0:
```python
import functools

import jax
import jax.numpy as jnp
from jax import lax
from jax.experimental import pallas as pl
from jax.experimental.pallas import tpu as pltpu
from jax.sharding import PartitionSpec as P

EPSILON = 1e-05
F32 = jnp.float32
BF16 = jnp.bfloat16
AXES = ("dom", "pipe")
PIPE, A_NEXT, A_PREV, B_NEXT, B_PREV = range(5)


def mul(a, b):
    return jnp.dot(a, b, preferred_element_type=F32)


def mul_t(a, b):
    return lax.dot_general(a, b, (((1,), (1,)), ((), ())), preferred_element_type=F32)


def slope(v):
    s = jax.nn.sigmoid(v)
    return s * (1.0 + v * (1.0 - s))


def normalize(z):
    centred = z - jnp.mean(z, axis=-1, keepdims=True)
    inverse = lax.rsqrt(jnp.mean(centred * centred, axis=-1, keepdims=True) + EPSILON)
    return centred * inverse, inverse


def block_at(scalars, place, base, rows):
    return pl.ds(pl.multiple_of(base + scalars[place] * rows, rows), rows)


def fold_kernel(a, b, out):
    out[...] = mul(a[...], b[...]).astype(BF16)


def forward_own_kernel(tick, scalars, h, gown, ginner, w_send, w_recv, w_node, a_out, u_out):
    @pl.when(scalars[PIPE] == tick)
    def _():
        rows = h.shape[0] // 2
        edges = ginner.shape[1]
        block = ginner.shape[2]
        for i in range(2):
            own = mul(gown[i], h[i * rows : (i + 1) * rows, :])
            if i == 0:
                inner = h[block_at(scalars, B_PREV, rows, block), :]
            else:
                inner = h[block_at(scalars, A_NEXT, 0, block), :]
            sent = (own[:edges] + mul(ginner[i], inner)).astype(BF16)
            received = own[edges:].astype(BF16)
            a_out[i * edges : (i + 1) * edges, :] = mul(sent, w_send[...]) + mul(received, w_recv[...])
        u_out[...] = mul(h[...], w_node[...])


def forward_kernel(
    tick, scalars, h, a_own, u_own, prev, after, gouter, gown_t, w_send, w_fold, gain, h_out, to_prev, to_next, a_out, u_out
):
    @pl.when(scalars[PIPE] == tick)
    def _():
        rows = h.shape[0] // 2
        edges = gouter.shape[1]
        block = gouter.shape[2]
        outer = jnp.concatenate([mul(gouter[0], prev[...]), mul(gouter[1], after[...])], axis=0).astype(BF16)
        a = a_own[...] + mul(outer, w_send[...])
        a_out[...] = a
        q = (a * jax.nn.sigmoid(a)).astype(BF16)
        summed = jnp.concatenate(
            [mul(gown_t[i, :, edges:], q[i * edges : (i + 1) * edges]) for i in range(2)], axis=0
        ).astype(BF16)
        u = u_own[...] + mul(summed, w_fold[...])
        u_out[...] = u
        t, _ = normalize(u * jax.nn.sigmoid(u))
        h_out[...] = (h[...].astype(F32) + t * gain[...]).astype(BF16)
        to_prev[...] = h_out[block_at(scalars, A_PREV, 0, block), :]
        to_next[...] = h_out[block_at(scalars, B_NEXT, rows, block), :]


def save_kernel(tick, scalars, a, u, h, *refs):
    t_out, r_out, s_out, h_out = refs[-4:]

    @pl.when(scalars[PIPE] == tick)
    def _():
        s_out[...] = slope(a[...])
        u_value = u[...]
        t, inverse = normalize(u_value * jax.nn.sigmoid(u_value))
        t_out[...] = t
        r_out[...] = inverse * slope(u_value)
        h_out[...] = h[...]


def backward_kernel(
    tick,
    scalars,
    upstream,
    from_prev,
    from_next,
    t_in,
    r_in,
    s_in,
    gain,
    gown,
    gouter_t,
    w_fold,
    w_send,
    c_out,
    cb_out,
    du_out,
    da_out,
    es_out,
    to_prev,
    to_next,
):
    @pl.when(scalars[PIPE] == tick)
    def _():
        rows = upstream.shape[0] // 2
        edges = gouter_t.shape[2]
        block = gouter_t.shape[1]
        c_out[...] = upstream[...].astype(F32)
        if from_prev is not None:
            at = block_at(scalars, A_PREV, 0, block)
            c_out[at, :] = c_out[at, :] + from_prev[...].astype(F32)
            at = block_at(scalars, B_NEXT, rows, block)
            c_out[at, :] = c_out[at, :] + from_next[...].astype(F32)
            cb_out[...] = c_out[...].astype(BF16)
        g = c_out[...] * gain[...]
        t = t_in[...]
        centre = jnp.mean(g, axis=-1, keepdims=True)
        along = jnp.mean(g * t, axis=-1, keepdims=True)
        du = ((g - centre - t * along) * r_in[...]).astype(BF16)
        du_out[...] = du
        spread = jnp.concatenate(
            [mul(gown[i, edges:, :], du[i * rows : (i + 1) * rows]) for i in range(2)], axis=0
        ).astype(BF16)
        da = (mul_t(spread, w_fold[...]) * s_in[...]).astype(BF16)
        da_out[...] = da
        es = mul_t(da, w_send[...]).astype(BF16)
        es_out[...] = es
        to_prev[...] = mul(gouter_t[0], es[:edges]).astype(BF16)
        to_next[...] = mul(gouter_t[1], es[edges:]).astype(BF16)


def backward_own_kernel(
    tick, scalars, c, du, da, es, gown_t, ginner_t, w_node, w_recv, out, total
):
    @pl.when(scalars[PIPE] == tick)
    def _():
        rows = c.shape[0] // 2
        edges = ginner_t.shape[2]
        block = ginner_t.shape[1]
        er = mul_t(da[...], w_recv[...]).astype(BF16)
        direct = mul_t(du[...], w_node[...])
        for i in range(2):
            here = slice(i * rows, (i + 1) * rows)
            there = slice(i * edges, (i + 1) * edges)
            both = jnp.concatenate([es[there, :], er[there]], axis=0)
            total[here, :] = c[here, :] + direct[here] + mul(gown_t[i], both)
        at = block_at(scalars, B_PREV, rows, block)
        total[at, :] = total[at, :] + mul(ginner_t[0], es[:edges, :])
        at = block_at(scalars, A_NEXT, 0, block)
        total[at, :] = total[at, :] + mul(ginner_t[1], es[edges:, :])
        out[...] = total[...].astype(BF16)


def run(kernel, operands, outs, scratch=(), aliases=None, flops=0):
    specs = [pl.BlockSpec(memory_space=pltpu.SMEM)] + [pl.BlockSpec(memory_space=pltpu.VMEM)] * (len(operands) - 1)
    return pl.pallas_call(
        kernel,
        out_shape=[jax.ShapeDtypeStruct(s, t) for s, t in outs],
        in_specs=specs,
        out_specs=[pl.BlockSpec(memory_space=pltpu.VMEM)] * len(outs),
        scratch_shapes=list(scratch),
        input_output_aliases=aliases or {},
        compiler_params=pltpu.CompilerParams(vmem_limit_bytes=24 * 2**20),
        cost_estimate=pl.CostEstimate(flops=flops, bytes_accessed=2**20, transcendentals=0),
    )(*operands)


def shards(
    inputs,
    cotangent,
    w_send,
    w_recv,
    w_message,
    w_node,
    w_aggregate,
    gains,
    edge_send,
    edge_recv,
    edge_count,
    halo_send,
):
    sections = lax.axis_size("pipe")
    last = sections - 1
    pairs_total = lax.axis_size("dom") // 2
    phase = lax.axis_index("pipe")
    y = lax.rem(lax.axis_index("dom"), 2)
    rows, latent = inputs.shape[1:]
    edge_blocks, block = edge_send.shape
    edges = edge_blocks * block
    w_send, w_recv, w_node = w_send[0], w_recv[0], w_node[0]

    def device(pair, which, pipe):
        return (2 * (pair % pairs_total) + which) * sections + pipe

    def table(rule):
        pairs = []
        for pair in range(pairs_total):
            for which in range(2):
                for pipe in range(sections):
                    target = rule(pair, which, pipe)
                    if target is not None and 0 <= target[2] < sections:
                        pairs.append((device(pair, which, pipe), device(*target)))
        return pairs

    def send(value, rule):
        return lax.ppermute(value, AXES, table(rule))

    numbers = jnp.concatenate([edge_count, halo_send[0, :, 0]])
    packed = jnp.concatenate(
        [edge_send, edge_recv, jnp.pad(numbers, (0, block - numbers.shape[0]))[None]], axis=0
    )
    packed_other = send(packed, lambda z, w, p: (z, 1 - w, p))

    source = jnp.where(phase == last, cotangent, inputs)
    here = lax.dynamic_index_in_dim(source, y, 0, keepdims=False)
    there = lax.dynamic_index_in_dim(source, 1 - y, 0, keepdims=False)
    out_block = jnp.where(y == 1, halo_send[0, 0, 0], halo_send[0, 1, 0])
    boundary = lax.dynamic_slice(inputs, (jnp.minimum(phase, 1), out_block * block, 0), (1, block, latent))[0]
    start_prev = send(boundary, lambda z, w, p: (z + 1, p, 0) if w == 1 and p <= 1 else None)
    start_next = send(boundary, lambda z, w, p: (z - 1, p, 0) if w == 0 and p <= 1 else None)
    arrived = send(there, lambda z, w, p: (z, 1 - w, p) if p in (0, last) else None)
    start = jnp.where(
        y == 0, jnp.concatenate([here, arrived], axis=0), jnp.concatenate([arrived, here], axis=0)
    )

    first = jnp.where(y == 0, packed, packed_other)
    second = jnp.where(y == 0, packed_other, packed)
    both = jnp.stack([first, second])
    senders = both[:, :edge_blocks].reshape(2, edges)
    receivers = both[:, edge_blocks : 2 * edge_blocks].reshape(2, edges)
    counts = both[:, 2 * edge_blocks, :edge_blocks]
    lists = both[:, 2 * edge_blocks, edge_blocks : edge_blocks + 2]
    live = (jnp.arange(block)[None, None, :] < counts[:, :, None]).reshape(2, edges)
    senders = jnp.where(live, senders, -1)
    receivers = jnp.where(live, receivers, -1)
    scalars = jnp.concatenate([phase[None], lists.reshape(-1)]).astype(jnp.int32)

    inner_base = jnp.array([rows + block, rows], jnp.int32)[:, None]
    outer_base = jnp.array([rows, rows + block], jnp.int32)[:, None]

    def one_hot(index, width):
        return (index[:, :, None] == jnp.arange(width, dtype=jnp.int32)).astype(BF16)

    def one_hot_t(index, width):
        return (index[:, None, :] == jnp.arange(width, dtype=jnp.int32)[None, :, None]).astype(BF16)

    gown = one_hot(jnp.concatenate([senders, receivers], axis=1), rows)
    gown_t = one_hot_t(jnp.concatenate([senders, receivers], axis=1), rows)
    ginner = one_hot(senders - inner_base, block)
    ginner_t = one_hot_t(senders - inner_base, block)
    gouter = one_hot(senders - outer_base, block)
    gouter_t = one_hot_t(senders - outer_base, block)

    wide = (2 * rows, latent)
    edge_wide = (2 * edges, latent)
    narrow = (block, latent)
    unit = 2 * 2 * rows * latent * latent

    w_fold = pl.pallas_call(
        fold_kernel,
        out_shape=jax.ShapeDtypeStruct(w_message.shape[1:], BF16),
        in_specs=[pl.BlockSpec(memory_space=pltpu.VMEM)] * 2,
        out_specs=pl.BlockSpec(memory_space=pltpu.VMEM),
        compiler_params=pltpu.CompilerParams(vmem_limit_bytes=24 * 2**20),
    )(w_message[0], w_aggregate[0])

    hidden, from_prev, from_next = start, start_prev, start_next
    state = ()
    for tick in range(sections):
        a_own, u_own = run(
            functools.partial(forward_own_kernel, tick),
            (scalars, hidden, gown, ginner, w_send, w_recv, w_node),
            [(edge_wide, F32), (wide, F32)],
            flops=4 * unit,
        )
        hidden, to_prev, to_next, a, u = run(
            functools.partial(forward_kernel, tick),
            (scalars, hidden, a_own, u_own, from_prev, from_next, gouter, gown_t, w_send, w_fold, gains),
            [(wide, BF16), (narrow, BF16), (narrow, BF16), (edge_wide, F32), (wide, F32)],
            flops=4 * unit,
        )
        produced = hidden
        if tick < last:
            from_next = send(to_prev, lambda z, w, p: (z - 1, w, p + 1) if p == tick else None)
            from_prev = send(to_next, lambda z, w, p: (z + 1, w, p + 1) if p == tick else None)
            hidden = send(hidden, lambda z, w, p: (z, w, p + 1) if p == tick else None)
        state = run(
            functools.partial(save_kernel, tick),
            (scalars, a, u, produced) + tuple(state),
            [(wide, F32), (wide, F32), (edge_wide, F32), (wide, BF16)],
            aliases={4 + k: k for k in range(4)} if state else None,
        )
    t_saved, r_saved, s_saved, h_saved = state

    upstream = start
    from_prev = from_next = None
    returned = jnp.zeros(wide, BF16)
    for tick in range(last, -1, -1):
        operands = (t_saved, r_saved, s_saved, gains, gown, gouter_t, w_fold, w_send)
        outs = [
            (wide, F32),
            (wide, BF16),
            (wide, BF16),
            (edge_wide, BF16),
            (edge_wide, BF16),
            (narrow, BF16),
            (narrow, BF16),
        ]
        if from_prev is None:

            def body(scalars, upstream, *refs, tick=tick):
                backward_kernel(tick, scalars, upstream, None, None, *refs)

            c, cb, du, da, es, to_prev, to_next = run(body, (scalars, upstream) + operands, outs, flops=4 * unit)
        else:
            c, cb, du, da, es, to_prev, to_next = run(
                functools.partial(backward_kernel, tick),
                (scalars, upstream, from_prev, from_next) + operands,
                outs,
                flops=4 * unit,
            )
            back = send(cb, lambda z, w, p: (z, w, p + 1) if p == tick else None)
            returned = jnp.where(phase == tick + 1, back, returned)
        [own] = run(
            functools.partial(backward_own_kernel, tick),
            (scalars, c, du, da, es, gown_t, ginner_t, w_node, w_recv),
            [(wide, BF16)],
            scratch=[pltpu.VMEM(wide, F32)],
            flops=4 * unit,
        )
        if tick > 0:
            from_next = send(to_prev, lambda z, w, p: (z - 1, w, p - 1) if p == tick else None)
            from_prev = send(to_next, lambda z, w, p: (z + 1, w, p - 1) if p == tick else None)
            upstream = send(own, lambda z, w, p: (z, w, p - 1) if p == tick else None)

    across = jnp.where(y == 0, to_prev, to_next)
    along = jnp.where(y == 0, to_next, to_prev)
    across = send(across, lambda z, w, p: None if p else (z - 1, 1, 0) if w == 0 else (z + 1, 0, 0))
    along = send(along, lambda z, w, p: None if p else (z + 1, 0, 0) if w == 0 else (z - 1, 1, 0))

    def mine(value):
        return lax.dynamic_slice(value, (y * rows, 0), (rows, latent))

    def others(value):
        return lax.dynamic_slice(value, ((1 - y) * rows, 0), (rows, latent))

    def swap(value):
        return send(others(value), lambda z, w, p: (z, 1 - w, p))

    h_other = swap(h_saved)
    final = jnp.where(phase == 0, own, returned)
    g_other = swap(final)
    g_mine = mine(final)
    at = jnp.where(y == 1, halo_send[0, 0, 0], halo_send[0, 1, 0])
    covered = ((jnp.arange(rows) // block == at) & (phase == 0))[:, None]

    def place(value, halo):
        tiled = jnp.concatenate([halo] * (rows // block), axis=0)
        return (value.astype(F32) + jnp.where(covered, tiled.astype(F32), 0.0)).astype(BF16)

    g_mine = place(g_mine, along)
    g_other = place(g_other, across)

    def by_micro(value, other):
        return jnp.where(y == 0, jnp.stack([value, other]), jnp.stack([other, value]))[None]

    return by_micro(mine(h_saved), h_other), by_micro(g_mine, g_other)


def solution(mesh):
    in_specs = (
        P(None, "dom", None),
        P(None, "dom", None),
        P("pipe", None, None),
        P("pipe", None, None),
        P("pipe", None, None),
        P("pipe", None, None),
        P("pipe", None, None),
        P("pipe", None),
        P("dom", None),
        P("dom", None),
        P("dom"),
        P("dom", None, None),
    )
    out_specs = (P("pipe", None, "dom", None), P("pipe", None, "dom", None))
    return jax.shard_map(shards, mesh=mesh, in_specs=in_specs, out_specs=out_specs, check_vma=False)
```

profile of v0, /device:TPU:0, one launch (start us, length us, event | category | flops | bytes accessed | tf_op | source)
XLA Modules:
  0.0 138.9 jit_solution(5160237432264223048)
XLA Ops:
  5.4 7.0 %collective-permute-start.3 = (bf16[128,512]{1,0:T(8,128)(2,1)S(1)}, bf16[128,512]{1,0:T(8,128)(2,1)S(1)}, u32[]{:S(2)}, u32[]{:S(2)}) collective-permute-start(bf16[128,512]{1,0:T(8,128)(2,1)S(1)} %dynamic-slice_bitcast_fusion.3), channel_id=1, source_target_pairs={{0,24},{1,28},{8,0},{9,4},{16,8},{17,12},{24,16},{25,20}} | collective-permute-start | bytes 393224 | tf_op jit(solution)/shard_map/ppermute | solution.py:223
  13.6 2.1 %collective-permute-start.1 = (bf16[256,512]{1,0:T(8,128)(2,1)S(1)}, bf16[256,512]{1,0:T(8,128)(2,1)}, u32[]{:S(2)}, u32[]{:S(2)}) collective-permute-start(bf16[256,512]{1,0:T(8,128)(2,1)S(1)} %get-tuple-element.145), channel_id=1, source_target_pairs={{0,4},{3,7},{4,0},{7,3},{8,12},{11,15},{12,8},{15,11},{16,20},{19,... | collective-permute-start | bytes 786440 | tf_op jit(solution)/shard_map/ppermute | solution.py:223
  16.4 2.0 %collective-permute-start = (s32[5,128]{1,0:T(8,128)S(1)}, s32[5,128]{1,0:T(8,128)S(1)}, u32[]{:S(2)}, u32[]{:S(2)}) collective-permute-start(s32[5,128]{1,0:T(8,128)S(1)} %pad_add_fusion), channel_id=1, source_target_pairs={{0,4},{1,5},{2,6},{3,7},{4,0},{5,1},{6,2},{7,3},{8,12},{9,13},{10,... | collective-permute-start | bytes 7688 | tf_op jit(solution)/shard_map/ppermute | solution.py:223
  18.9 3.2 %collective-permute-done = s32[5,128]{1,0:T(8,128)S(1)} collective-permute-done((s32[5,128]{1,0:T(8,128)S(1)}, s32[5,128]{1,0:T(8,128)S(1)}, u32[]{:S(2)}, u32[]{:S(2)}) %collective-permute-start) | collective-permute-done | bytes 2592 | tf_op jit(solution)/shard_map/ppermute | solution.py:223
  25.8 1.9 %shard_map.149 = (f32[512,512]{1,0:T(8,128)S(1)}, f32[512,512]{1,0:T(8,128)S(1)}) custom-call(s32[5]{0:T(128)S(1)} %pad_add_fusion.5.scalars, bf16[512,512]{1,0:T(8,128)(2,1)S(1)} %maximum_select_fusion.h.upstream, bf16[2,512,256]{2,1,0:T(8,128)(2,1)S(1)} %fusion.gown.refs_4_, bf16[2,256,128]{2,1,0:T(8,128)(2,1)S(1)} %fusion.4.ginner, ...), custom_call_target="tpu_custom_call" | custom-call | flops 1073741824 | bytes 1048576 | tf_op jit(solution)/shard_map/pallas_call | solution.py:173
  28.4 2.0 %shard_map.151 = (bf16[512,512]{1,0:T(8,128)(2,1)S(1)}, bf16[128,512]{1,0:T(8,128)(2,1)S(1)}, bf16[128,512]{1,0:T(8,128)(2,1)S(1)}, f32[512,512]{1,0:T(8,128)S(1)}, f32[512,512]{1,0:T(8,128)S(1)}) custom-call(s32[5]{0:T(128)S(1)} %pad_add_fusion.5.scalars, bf16[512,512]{1,0:T(8,128)(2,1)S(1)} %maximum_select_fusion.h.upstream, ...), custom_call_target="tpu_custom_call" | custom-call | flops 1073741824 | bytes 1048576 | tf_op jit(solution)/shard_map/pallas_call | solution.py:173
  30.4 1.3 collective-permute-start.4
  31.7 1.3 collective-permute-start.5
  33.0 1.3 collective-permute-start.6
  35.5 1.4 collective-permute-done.6.after
  42.8 1.6 %shard_map.158 = (f32[512,512]{1,0:T(8,128)S(1)}, f32[512,512]{1,0:T(8,128)S(1)}, f32[512,512]{1,0:T(8,128)S(1)}, bf16[512,512]{1,0:T(8,128)(2,1)S(1)}) custom-call(s32[5]{0:T(128)S(1)} %pad_add_fusion.5.scalars, f32[512,512]{1,0:T(8,128)S(1)} %get-tuple-element.95.a, f32[512,512]{1,0:T(8,128)S(1)} %get-tuple-element.96.u, ...), custom_call_target="tpu_custom_call" | custom-call | bytes 1048576 | tf_op jit(solution)/shard_map/pallas_call | solution.py:173
  48.1 1.4 shard_map.162
  52.1 1.4 shard_map.164
  56.1 1.4 shard_map.166
  61.9 1.5 %collective-permute-start.25 = (bf16[512,512]{1,0:T(8,128)(2,1)}, bf16[512,512]{1,0:T(8,128)(2,1)}, u32[]{:S(2)}, u32[]{:S(2)}) collective-permute-start(bf16[512,512]{1,0:T(8,128)(2,1)} %get-tuple-element.137), channel_id=1, source_target_pairs={{2,3},{6,7},{10,11},{14,15},{18,19},{22,23},{26,27},{30,31}} | collective-permute-start | bytes 1572872 | tf_op jit(solution)/shard_map/ppermute | solution.py:223
  63.3 1.5 %collective-permute-start.24 = (bf16[512,512]{1,0:T(8,128)(2,1)}, bf16[512,512]{1,0:T(8,128)(2,1)}, u32[]{:S(2)}, u32[]{:S(2)}) collective-permute-start(bf16[512,512]{1,0:T(8,128)(2,1)} %get-tuple-element.136), channel_id=1, source_target_pairs={{1,2},{5,6},{9,10},{13,14},{17,18},{21,22},{25,26},{29,30}} | collective-permute-start | bytes 1572872 | tf_op jit(solution)/shard_map/ppermute | solution.py:223
  64.8 43.9 %collective-permute-done.21.from_prev = bf16[128,512]{1,0:T(8,128)(2,1)S(1)} collective-permute-done((bf16[128,512]{1,0:T(8,128)(2,1)S(1)}, bf16[128,512]{1,0:T(8,128)(2,1)S(1)}, u32[]{:S(2)}, u32[]{:S(2)}) %collective-permute-start.21) | collective-permute-done | bytes 131104 | tf_op jit(solution)/shard_map/ppermute | solution.py:223
  109.8 3.1 %shard_map.168 = (f32[512,512]{1,0:T(8,128)S(1)}, bf16[512,512]{1,0:T(8,128)(2,1)}, bf16[512,512]{1,0:T(8,128)(2,1)S(1)}, bf16[512,512]{1,0:T(8,128)(2,1)S(1)}, ...) custom-call(s32[5]{0:T(128)S(1)} %pad_add_fusion.5.scalars, ...), custom_call_target="tpu_custom_call" | custom-call | flops 1073741824 | bytes 1048576 | tf_op jit(solution)/shard_map/pallas_call | solution.py:173
  116.3 2.2 %collective-permute-start.23 = (bf16[512,512]{1,0:T(8,128)(2,1)}, bf16[512,512]{1,0:T(8,128)(2,1)}, u32[]{:S(2)}, u32[]{:S(2)}) collective-permute-start(bf16[512,512]{1,0:T(8,128)(2,1)} %get-tuple-element.135), channel_id=1, source_target_pairs={{0,1},{4,5},{8,9},{12,13},{16,17},{20,21},{24,25},{28,29}} | collective-permute-start | bytes 1572872 | tf_op jit(solution)/shard_map/ppermute | solution.py:223
  118.5 1.6 %collective-permute-start.13 = (bf16[256,512]{1,0:T(8,128)(2,1)S(1)}, bf16[256,512]{1,0:T(8,128)(2,1)S(1)}, u32[]{:S(2)}, u32[]{:S(2)}) collective-permute-start(bf16[256,512]{1,0:T(8,128)(2,1)S(1)} %get-tuple-element.143), channel_id=1, source_target_pairs={{0,4},{1,5},{2,6},{3,7},{4,0},{5,1},{6,2},{7,3},{8,12},{9,13},{10,... | collective-permute-start | bytes 786440 | tf_op jit(solution)/shard_map/ppermute | solution.py:223
  123.3 1.7 %shard_map.169 = bf16[512,512]{1,0:T(8,128)(2,1)S(1)} custom-call(s32[5]{0:T(128)S(1)} %pad_add_fusion.5.scalars, f32[512,512]{1,0:T(8,128)S(1)} %copy-done.4, bf16[512,512]{1,0:T(8,128)(2,1)S(1)} %copy-done.8, bf16[512,512]{1,0:T(8,128)(2,1)S(1)} %copy-done.10, bf16[512,512]{1,0:T(8,128)(2,1)S(1)} %copy-done.12, bf16[2,256,512]{2,1,0:T(8,128)(2,1)S(1)} %fusion.1.gown_t, ...), custom_call_target="tpu_custom_call" | custom-call | flops 1073741824 | bytes 1048576 | tf_op jit(solution)/shard_map/pallas_call | solution.py:173
  125.7 2.5 %collective-permute-start.26 = (bf16[128,512]{1,0:T(8,128)(2,1)S(1)}, bf16[128,512]{1,0:T(8,128)(2,1)S(1)}, u32[]{:S(2)}, u32[]{:S(2)}) collective-permute-start(bf16[128,512]{1,0:T(8,128)(2,1)S(1)} %get-tuple-element.146), channel_id=1, source_target_pairs={{0,8},{4,28},{8,16},{12,4},{16,24},{20,12},{24,0},{28,20}} | collective-permute-start | bytes 393224 | tf_op jit(solution)/shard_map/ppermute | solution.py:223
  128.2 4.5 %collective-permute-start.28 = (bf16[128,512]{1,0:T(8,128)(2,1)S(1)}, bf16[128,512]{1,0:T(8,128)(2,1)S(1)}, u32[]{:S(2)}, u32[]{:S(2)}) collective-permute-start(bf16[128,512]{1,0:T(8,128)(2,1)S(1)} %get-tuple-element.147), channel_id=1, source_target_pairs={{0,28},{4,8},{8,4},{12,16},{16,12},{20,24},{24,20},{28,0}} | collective-permute-start | bytes 393224 | tf_op jit(solution)/shard_map/ppermute | solution.py:223
  134.4 3.4 %collective-permute-done.28 = bf16[128,512]{1,0:T(8,128)(2,1)S(1)} collective-permute-done((bf16[128,512]{1,0:T(8,128)(2,1)S(1)}, bf16[128,512]{1,0:T(8,128)(2,1)S(1)}, u32[]{:S(2)}, u32[]{:S(2)}) %collective-permute-start.28) | collective-permute-done | bytes 131104 | tf_op jit(solution)/shard_map/ppermute | solution.py:223
  (126 shorter events, 41.4 us)
Async XLA Ops:
  4.1 23.6 %collective-permute-start.2 = (bf16[128,512]{1,0:T(8,128)(2,1)S(1)}, bf16[128,512]{1,0:T(8,128)(2,1)S(1)}, u32[]{:S(2)}, u32[]{:S(2)}) collective-permute-start(bf16[128,512]{1,0:T(8,128)(2,1)S(1)} %dynamic-slice_bitcast_fusion.3), channel_id=1, source_target_pairs={{4,8},{5,12},{12,16},{13,20},{20,24},{21,28},{28,0},{29,4}} | collective-permute-start | bytes 393224 | tf_op jit(solution)/shard_map/ppermute | solution.py:223
  5.4 22.3 %collective-permute-start.3 = (bf16[128,512]{1,0:T(8,128)(2,1)S(1)}, bf16[128,512]{1,0:T(8,128)(2,1)S(1)}, u32[]{:S(2)}, u32[]{:S(2)}) collective-permute-start(bf16[128,512]{1,0:T(8,128)(2,1)S(1)} %dynamic-slice_bitcast_fusion.3), channel_id=1, source_target_pairs={{0,24},{1,28},{8,0},{9,4},{16,8},{17,12},{24,16},{25,20}} | collective-permute-start | bytes 393224 | tf_op jit(solution)/shard_map/ppermute | solution.py:223
  13.6 10.8 %collective-permute-start.1 = (bf16[256,512]{1,0:T(8,128)(2,1)S(1)}, bf16[256,512]{1,0:T(8,128)(2,1)}, u32[]{:S(2)}, u32[]{:S(2)}) collective-permute-start(bf16[256,512]{1,0:T(8,128)(2,1)S(1)} %get-tuple-element.145), channel_id=1, source_target_pairs={{0,4},{3,7},{4,0},{7,3},{8,12},{11,15},{12,8},{15,11},{16,20},{19,... | collective-permute-start | bytes 786440 | tf_op jit(solution)/shard_map/ppermute | solution.py:223
  16.4 5.7 %collective-permute-start = (s32[5,128]{1,0:T(8,128)S(1)}, s32[5,128]{1,0:T(8,128)S(1)}, u32[]{:S(2)}, u32[]{:S(2)}) collective-permute-start(s32[5,128]{1,0:T(8,128)S(1)} %pad_add_fusion), channel_id=1, source_target_pairs={{0,4},{1,5},{2,6},{3,7},{4,0},{5,1},{6,2},{7,3},{8,12},{9,13},{10,... | collective-permute-start | bytes 7688 | tf_op jit(solution)/shard_map/ppermute | solution.py:223
  30.4 3.9 %collective-permute-start.4 = (bf16[512,512]{1,0:T(8,128)(2,1)S(1)}, bf16[512,512]{1,0:T(8,128)(2,1)S(1)}, u32[]{:S(2)}, u32[]{:S(2)}) collective-permute-start(bf16[512,512]{1,0:T(8,128)(2,1)S(1)} %get-tuple-element.73.h), channel_id=1, source_target_pairs={{0,1},{4,5},{8,9},{12,13},{16,17},{20,21},{24,25},{28,29}} | collective-permute-start | bytes 1572872 | tf_op jit(solution)/shard_map/ppermute | solution.py:223
  31.7 3.8 %collective-permute-start.5 = (bf16[128,512]{1,0:T(8,128)(2,1)S(1)}, bf16[128,512]{1,0:T(8,128)(2,1)S(1)}, u32[]{:S(2)}, u32[]{:S(2)}) collective-permute-start(bf16[128,512]{1,0:T(8,128)(2,1)S(1)} %get-tuple-element.76), channel_id=1, source_target_pairs={{0,9},{4,13},{8,17},{12,21},{16,25},{20,29},{24,1},{28,5}} | collective-permute-start | bytes 393224 | tf_op jit(solution)/shard_map/ppermute | solution.py:223
  33.0 3.9 %collective-permute-start.6 = (bf16[128,512]{1,0:T(8,128)(2,1)S(1)}, bf16[128,512]{1,0:T(8,128)(2,1)S(1)}, u32[]{:S(2)}, u32[]{:S(2)}) collective-permute-start(bf16[128,512]{1,0:T(8,128)(2,1)S(1)} %get-tuple-element.77), channel_id=1, source_target_pairs={{0,25},{4,29},{8,1},{12,5},{16,9},{20,13},{24,17},{28,21}} | collective-permute-start | bytes 393224 | tf_op jit(solution)/shard_map/ppermute | solution.py:223
  37.4 2.1 %collective-permute-start.7 = (bf16[512,512]{1,0:T(8,128)(2,1)S(1)}, bf16[512,512]{1,0:T(8,128)(2,1)S(1)}, u32[]{:S(2)}, u32[]{:S(2)}) collective-permute-start(bf16[512,512]{1,0:T(8,128)(2,1)S(1)} %get-tuple-element.78.h), channel_id=1, source_target_pairs={{1,2},{5,6},{9,10},{13,14},{17,18},{21,22},{25,26},{29,30}} | collective-permute-start | bytes 1572872 | tf_op jit(solution)/shard_map/ppermute | solution.py:223
  38.1 1.9 %collective-permute-start.8 = (bf16[128,512]{1,0:T(8,128)(2,1)S(1)}, bf16[128,512]{1,0:T(8,128)(2,1)S(1)}, u32[]{:S(2)}, u32[]{:S(2)}) collective-permute-start(bf16[128,512]{1,0:T(8,128)(2,1)S(1)} %get-tuple-element.81), channel_id=1, source_target_pairs={{1,10},{5,14},{9,18},{13,22},{17,26},{21,30},{25,2},{29,6}} | collective-permute-start | bytes 393224 | tf_op jit(solution)/shard_map/ppermute | solution.py:223
  40.7 5.0 %collective-permute-start.10 = (bf16[512,512]{1,0:T(8,128)(2,1)S(1)}, bf16[512,512]{1,0:T(8,128)(2,1)S(1)}, u32[]{:S(2)}, u32[]{:S(2)}) collective-permute-start(bf16[512,512]{1,0:T(8,128)(2,1)S(1)} %get-tuple-element.83.h), channel_id=1, source_target_pairs={{2,3},{6,7},{10,11},{14,15},{18,19},{22,23},{26,27},{30,31}} | collective-permute-start | bytes 1572872 | tf_op jit(solution)/shard_map/ppermute | solution.py:223
  41.4 4.8 %collective-permute-start.11 = (bf16[128,512]{1,0:T(8,128)(2,1)S(1)}, bf16[128,512]{1,0:T(8,128)(2,1)S(1)}, u32[]{:S(2)}, u32[]{:S(2)}) collective-permute-start(bf16[128,512]{1,0:T(8,128)(2,1)S(1)} %get-tuple-element.86), channel_id=1, source_target_pairs={{2,11},{6,15},{10,19},{14,23},{18,27},{22,31},{26,3},{30,7}} | collective-permute-start | bytes 393224 | tf_op jit(solution)/shard_map/ppermute | solution.py:223
  42.1 4.2 %collective-permute-start.12 = (bf16[128,512]{1,0:T(8,128)(2,1)S(1)}, bf16[128,512]{1,0:T(8,128)(2,1)S(1)}, u32[]{:S(2)}, u32[]{:S(2)}) collective-permute-start(bf16[128,512]{1,0:T(8,128)(2,1)S(1)} %get-tuple-element.87), channel_id=1, source_target_pairs={{2,27},{6,31},{10,3},{14,7},{18,11},{22,15},{26,19},{30,23}} | collective-permute-start | bytes 393224 | tf_op jit(solution)/shard_map/ppermute | solution.py:223
  50.0 2.1 %collective-permute-start.14 = (bf16[512,512]{1,0:T(8,128)(2,1)S(1)}, bf16[512,512]{1,0:T(8,128)(2,1)S(1)}, u32[]{:S(2)}, u32[]{:S(2)}) collective-permute-start(bf16[512,512]{1,0:T(8,128)(2,1)S(1)} %shard_map.163), channel_id=1, source_target_pairs={{3,2},{7,6},{11,10},{15,14},{19,18},{23,22},{27,26},{31,30}} | collective-permute-start | bytes 1572872 | tf_op jit(solution)/shard_map/ppermute | solution.py:223
  54.0 2.1 %collective-permute-start.17 = (bf16[512,512]{1,0:T(8,128)(2,1)S(1)}, bf16[512,512]{1,0:T(8,128)(2,1)S(1)}, u32[]{:S(2)}, u32[]{:S(2)}) collective-permute-start(bf16[512,512]{1,0:T(8,128)(2,1)S(1)} %shard_map.165), channel_id=1, source_target_pairs={{2,1},{6,5},{10,9},{14,13},{18,17},{22,21},{26,25},{30,29}} | collective-permute-start | bytes 1572872 | tf_op jit(solution)/shard_map/ppermute | solution.py:223
  58.0 51.8 %collective-permute-start.20 = (bf16[512,512]{1,0:T(8,128)(2,1)S(1)}, bf16[512,512]{1,0:T(8,128)(2,1)S(1)}, u32[]{:S(2)}, u32[]{:S(2)}) collective-permute-start(bf16[512,512]{1,0:T(8,128)(2,1)S(1)} %shard_map.167), channel_id=1, source_target_pairs={{1,0},{5,4},{9,8},{13,12},{17,16},{21,20},{25,24},{29,28}} | collective-permute-start | bytes 1572872 | tf_op jit(solution)/shard_map/ppermute | solution.py:223
  59.3 49.4 %collective-permute-start.21 = (bf16[128,512]{1,0:T(8,128)(2,1)S(1)}, bf16[128,512]{1,0:T(8,128)(2,1)S(1)}, u32[]{:S(2)}, u32[]{:S(2)}) collective-permute-start(bf16[128,512]{1,0:T(8,128)(2,1)S(1)} %get-tuple-element.129), channel_id=1, source_target_pairs={{1,8},{5,12},{9,16},{13,20},{17,24},{21,28},{25,0},{29,4}} | collective-permute-start | bytes 393224 | tf_op jit(solution)/shard_map/ppermute | solution.py:223
  60.6 49.2 %collective-permute-start.22 = (bf16[128,512]{1,0:T(8,128)(2,1)S(1)}, bf16[128,512]{1,0:T(8,128)(2,1)S(1)}, u32[]{:S(2)}, u32[]{:S(2)}) collective-permute-start(bf16[128,512]{1,0:T(8,128)(2,1)S(1)} %get-tuple-element.130), channel_id=1, source_target_pairs={{1,24},{5,28},{9,0},{13,4},{17,8},{21,12},{25,16},{29,20}} | collective-permute-start | bytes 393224 | tf_op jit(solution)/shard_map/ppermute | solution.py:223
  61.9 63.1 %collective-permute-start.25 = (bf16[512,512]{1,0:T(8,128)(2,1)}, bf16[512,512]{1,0:T(8,128)(2,1)}, u32[]{:S(2)}, u32[]{:S(2)}) collective-permute-start(bf16[512,512]{1,0:T(8,128)(2,1)} %get-tuple-element.137), channel_id=1, source_target_pairs={{2,3},{6,7},{10,11},{14,15},{18,19},{22,23},{26,27},{30,31}} | collective-permute-start | bytes 1572872 | tf_op jit(solution)/shard_map/ppermute | solution.py:223
  63.3 61.7 %collective-permute-start.24 = (bf16[512,512]{1,0:T(8,128)(2,1)}, bf16[512,512]{1,0:T(8,128)(2,1)}, u32[]{:S(2)}, u32[]{:S(2)}) collective-permute-start(bf16[512,512]{1,0:T(8,128)(2,1)} %get-tuple-element.136), channel_id=1, source_target_pairs={{1,2},{5,6},{9,10},{13,14},{17,18},{21,22},{25,26},{29,30}} | collective-permute-start | bytes 1572872 | tf_op jit(solution)/shard_map/ppermute | solution.py:223
  116.3 8.7 %collective-permute-start.23 = (bf16[512,512]{1,0:T(8,128)(2,1)}, bf16[512,512]{1,0:T(8,128)(2,1)}, u32[]{:S(2)}, u32[]{:S(2)}) collective-permute-start(bf16[512,512]{1,0:T(8,128)(2,1)} %get-tuple-element.135), channel_id=1, source_target_pairs={{0,1},{4,5},{8,9},{12,13},{16,17},{20,21},{24,25},{28,29}} | collective-permute-start | bytes 1572872 | tf_op jit(solution)/shard_map/ppermute | solution.py:223
  118.5 14.2 %collective-permute-start.13 = (bf16[256,512]{1,0:T(8,128)(2,1)S(1)}, bf16[256,512]{1,0:T(8,128)(2,1)S(1)}, u32[]{:S(2)}, u32[]{:S(2)}) collective-permute-start(bf16[256,512]{1,0:T(8,128)(2,1)S(1)} %get-tuple-element.143), channel_id=1, source_target_pairs={{0,4},{1,5},{2,6},{3,7},{4,0},{5,1},{6,2},{7,3},{8,12},{9,13},{10,... | collective-permute-start | bytes 786440 | tf_op jit(solution)/shard_map/ppermute | solution.py:223
  125.2 12.6 %collective-permute-start.27 = (bf16[256,512]{1,0:T(8,128)(2,1)S(1)}, bf16[256,512]{1,0:T(8,128)(2,1)S(1)}, u32[]{:S(2)}, u32[]{:S(2)}) collective-permute-start(bf16[256,512]{1,0:T(8,128)(2,1)S(1)} %constant_dynamic-slice_fusion), channel_id=1, source_target_pairs={{0,4},{1,5},{2,6},{3,7},{4,0},{5,1},{6,2},{7,3},{8,12},{9,13},{10,... | collective-permute-start | bytes 786440 | tf_op jit(solution)/shard_map/ppermute | solution.py:223
  125.7 8.7 %collective-permute-start.26 = (bf16[128,512]{1,0:T(8,128)(2,1)S(1)}, bf16[128,512]{1,0:T(8,128)(2,1)S(1)}, u32[]{:S(2)}, u32[]{:S(2)}) collective-permute-start(bf16[128,512]{1,0:T(8,128)(2,1)S(1)} %get-tuple-element.146), channel_id=1, source_target_pairs={{0,8},{4,28},{8,16},{12,4},{16,24},{20,12},{24,0},{28,20}} | collective-permute-start | bytes 393224 | tf_op jit(solution)/shard_map/ppermute | solution.py:223
  128.2 9.6 %collective-permute-start.28 = (bf16[128,512]{1,0:T(8,128)(2,1)S(1)}, bf16[128,512]{1,0:T(8,128)(2,1)S(1)}, u32[]{:S(2)}, u32[]{:S(2)}) collective-permute-start(bf16[128,512]{1,0:T(8,128)(2,1)S(1)} %get-tuple-element.147), channel_id=1, source_target_pairs={{0,28},{4,8},{8,4},{12,16},{16,12},{20,24},{24,20},{28,0}} | collective-permute-start | bytes 393224 | tf_op jit(solution)/shard_map/ppermute | solution.py:223
  (25 other events, 37.5 us)
where the time goes:
time: 140 us; the launch traced here: 139 us
  waiting for transfers between devices  54.5 us (39%)
  starting transfers between devices  42.5 us (30%)
  Pallas kernels  22.2 us (16%)
  local copies, waits for them, and re-layouts  11.5 us (8%)
  other arithmetic  5.61 us (4%)
  between operations  2.63 us (2%)
    ppermute x29, waiting for transfers between devices, send(): return lax.ppermute(value, AXES, table(rule))  54.5 us
    ppermute x29, starting transfers between devices, send(): return lax.ppermute(value, AXES, table(rule))  42.5 us
    pallas_call x20, Pallas kernels, run(): pl.pallas_call(kernel, out_shape=[jax.ShapeDtypeStruct(s, t) for s, t in...  21.8 us
    unnamed x40, local copies, waits for them, and re-layouts  9.78 us
  transfers between devices with their start and end apart: 29, of which 7 were waited for; matrix products, arithmetic and copies ran while one was open for 3% of the time, Pallas kernels for 8%

commit v1 on v0

v1 whole, which is shorter than its diff:
```python
import functools

import jax
import jax.numpy as jnp
from jax import lax
from jax.experimental import pallas as pl
from jax.experimental.pallas import tpu as pltpu
from jax.sharding import PartitionSpec as P

EPSILON = 1e-05
F32 = jnp.float32
BF16 = jnp.bfloat16
AXES = ("dom", "pipe")
INNER, OUTER = 0, 1


def mul(a, b):
    return jnp.dot(a, b, preferred_element_type=F32)


def mul_t(a, b):
    return lax.dot_general(a, b, (((1,), (1,)), ((), ())), preferred_element_type=F32)


def slope(v):
    s = jax.nn.sigmoid(v)
    return s * (1.0 + v * (1.0 - s))


def normalize(z):
    centred = z - jnp.mean(z, axis=-1, keepdims=True)
    inverse = lax.rsqrt(jnp.mean(centred * centred, axis=-1, keepdims=True) + EPSILON)
    return centred * inverse, inverse


def on_plane(plane):
    return pl.when(lax.axis_index("pipe") // 2 == plane)


def listed(lists, side, value, block):
    at = lists[side : side + 1, :1]
    picked = value[:block]
    for number in range(1, value.shape[0] // block):
        picked = jnp.where(at == number, value[number * block : (number + 1) * block], picked)
    return picked


def add_listed(lists, side, target, value, block):
    at = lists[side : side + 1, :1]
    for number in range(target.shape[0] // block):
        rows = slice(number * block, (number + 1) * block)
        target[rows, :] = target[rows, :] + jnp.where(at == number, value, 0.0)


def fold_kernel(a, b, out):
    out[...] = mul(a[...], b[...]).astype(BF16)


def forward_own_kernel(plane, h, gown, w_send, w_recv, w_node, a_out, u_out):
    @on_plane(plane)
    def _():
        edges = gown.shape[0] // 2
        own = mul(gown[...], h[...]).astype(BF16)
        a_out[...] = mul(own[:edges], w_send[...]) + mul(own[edges:], w_recv[...])
        u_out[...] = mul(h[...], w_node[...])


def forward_kernel(
    plane, lists, h, a_own, u_own, inner, outer, ghalo, gown_t, w_send, w_fold, gain, h_out, to_inner, to_outer, a_out, u_out
):
    @on_plane(plane)
    def _():
        edges = ghalo.shape[0]
        block = inner.shape[0]
        halo = (mul(ghalo[:, :block], inner[...]) + mul(ghalo[:, block:], outer[...])).astype(BF16)
        a = a_own[...] + mul(halo, w_send[...])
        a_out[...] = a
        q = (a * jax.nn.sigmoid(a)).astype(BF16)
        u = u_own[...] + mul(mul(gown_t[:, edges:], q).astype(BF16), w_fold[...])
        u_out[...] = u
        t, _ = normalize(u * jax.nn.sigmoid(u))
        out = (h[...].astype(F32) + t * gain[...]).astype(BF16)
        h_out[...] = out
        to_inner[...] = listed(lists, INNER, out, block)
        to_outer[...] = listed(lists, OUTER, out, block)


def save_kernel(plane, a, u, h, *refs):
    t_out, r_out, s_out, h_out = refs[-4:]

    @on_plane(plane)
    def _():
        s_out[...] = slope(a[...])
        u_value = u[...]
        t, inverse = normalize(u_value * jax.nn.sigmoid(u_value))
        t_out[...] = t
        r_out[...] = inverse * slope(u_value)
        h_out[...] = h[...]


def backward_kernel(
    plane,
    lists,
    upstream,
    inner,
    outer,
    t_in,
    r_in,
    s_in,
    gain,
    gown,
    ghalo_t,
    w_fold,
    w_send,
    c_out,
    cb_out,
    du_out,
    da_out,
    es_out,
    to_inner,
    to_outer,
):
    @on_plane(plane)
    def _():
        edges = gown.shape[0] // 2
        block = to_inner.shape[0]
        c_out[...] = upstream[...].astype(F32)
        if inner is not None:
            add_listed(lists, INNER, c_out, inner[...].astype(F32), block)
            add_listed(lists, OUTER, c_out, outer[...].astype(F32), block)
            cb_out[...] = c_out[...].astype(BF16)
        g = c_out[...] * gain[...]
        t = t_in[...]
        centre = jnp.mean(g, axis=-1, keepdims=True)
        along = jnp.mean(g * t, axis=-1, keepdims=True)
        du = ((g - centre - t * along) * r_in[...]).astype(BF16)
        du_out[...] = du
        spread = mul(gown[edges:, :], du).astype(BF16)
        da = (mul_t(spread, w_fold[...]) * s_in[...]).astype(BF16)
        da_out[...] = da
        es = mul_t(da, w_send[...]).astype(BF16)
        es_out[...] = es
        halo = mul(ghalo_t[...], es).astype(BF16)
        to_inner[...] = halo[:block]
        to_outer[...] = halo[block:]


def backward_own_kernel(plane, c, du, da, es, gown_t, w_node, w_recv, out, out_half):
    @on_plane(plane)
    def _():
        er = mul_t(da[...], w_recv[...]).astype(BF16)
        both = jnp.concatenate([es[...], er], axis=0)
        total = c[...] + mul_t(du[...], w_node[...]) + mul(gown_t[...], both)
        out[...] = total
        out_half[...] = total.astype(BF16)


def run(kernel, operands, outs, aliases=None, flops=0):
    return pl.pallas_call(
        kernel,
        out_shape=[jax.ShapeDtypeStruct(s, t) for s, t in outs],
        in_specs=[pl.BlockSpec(memory_space=pltpu.VMEM)] * len(operands),
        out_specs=[pl.BlockSpec(memory_space=pltpu.VMEM)] * len(outs),
        input_output_aliases=aliases or {},
        compiler_params=pltpu.CompilerParams(vmem_limit_bytes=24 * 2**20),
        cost_estimate=pl.CostEstimate(flops=flops, bytes_accessed=2**20, transcendentals=0),
    )(*operands)


def shards(
    inputs,
    cotangent,
    w_send,
    w_recv,
    w_message,
    w_node,
    w_aggregate,
    gains,
    edge_send,
    edge_recv,
    edge_count,
    halo_send,
):
    sections = lax.axis_size("pipe")
    pairs_total = lax.axis_size("dom") // 2
    phase = lax.axis_index("pipe")
    y = lax.rem(lax.axis_index("dom"), 2)
    core = lax.rem(phase, 2)
    plane_here = phase // 2
    rows, latent = inputs.shape[1:]
    edge_blocks, block = edge_send.shape
    edges = edge_blocks * block

    def send(value, rule):
        table = []
        for z in range(pairs_total):
            for which in range(2):
                for x in range(sections // 2):
                    for c in range(2):
                        tz, ty, tx, tc = rule(z, which, x, c)
                        target = (2 * (tz % pairs_total) + ty) * sections + 2 * (tx % (sections // 2)) + tc
                        table.append(((2 * z + which) * sections + 2 * x + c, target))
        return lax.ppermute(value, AXES, table)

    def flip_y(value):
        return send(value, lambda z, y, x, c: (z, 1 - y, x, c))

    def flip_core(value):
        return send(value, lambda z, y, x, c: (z, y, x, 1 - c))

    def to_home(value):
        return send(value, lambda z, y, x, c: (z, c, x, y))

    def towards(value, side, step):
        if side == INNER:
            return send(value, lambda z, y, x, c: (z, y, x + step, 1 - c))
        return send(value, lambda z, y, x, c: (z + 2 * c - 1, y, x + step, 1 - c))

    first_list = halo_send[0, :, 0]
    out_block = jnp.where(y == 1, first_list[0], first_list[1])
    boundary = lax.dynamic_slice(inputs, (core, out_block * block, 0), (1, block, latent))[0]
    numbers = jnp.concatenate([edge_count, first_list])
    packed = jnp.concatenate(
        [edge_send, edge_recv, jnp.pad(numbers, (0, block - numbers.shape[0]))[None]], axis=0
    )
    here = lax.dynamic_index_in_dim(inputs, y, 0, keepdims=False)
    there = flip_y(lax.dynamic_index_in_dim(inputs, 1 - y, 0, keepdims=False))
    outer = send(boundary, lambda z, y, x, c: (z + 2 * y - 1, c, x, 1 - y))
    packed_there = flip_y(packed)
    grad_here = lax.dynamic_index_in_dim(cotangent, y, 0, keepdims=False)
    grad_there = flip_y(lax.dynamic_index_in_dim(cotangent, 1 - y, 0, keepdims=False))

    local = core == y
    hidden = jnp.where(local, here, there)
    mine = jnp.where(local, packed, packed_there)
    mate = jnp.where(local, packed_there, packed)
    last_row = 2 * edge_blocks
    mate_list = jnp.where(core == 0, mate[last_row, edge_blocks + 1], mate[last_row, edge_blocks])
    inner = lax.dynamic_slice(jnp.where(local, there, here), (mate_list * block, 0), (block, latent))

    live = (jnp.arange(block)[None, :] < mine[last_row, :edge_blocks][:, None]).reshape(edges)
    senders = jnp.where(live, mine[:edge_blocks].reshape(edges), -1)
    receivers = jnp.where(live, mine[edge_blocks:last_row].reshape(edges), -1)
    list_next, list_prev = mine[last_row, edge_blocks], mine[last_row, edge_blocks + 1]
    sides = jnp.where(core == 0, jnp.stack([list_next, list_prev]), jnp.stack([list_prev, list_next]))
    lists = jnp.broadcast_to(sides[:, None], (2, block))

    halo_at = senders - rows
    halo_at = jnp.where(halo_at >= 0, jnp.where(core == 0, (halo_at + block) % (2 * block), halo_at), -1)
    own_at = jnp.concatenate([senders, receivers])

    def one_hot(index, width):
        return (index[:, None] == jnp.arange(width, dtype=jnp.int32)[None, :]).astype(BF16)

    def one_hot_t(index, width):
        return (index[None, :] == jnp.arange(width, dtype=jnp.int32)[:, None]).astype(BF16)

    gown = one_hot(own_at, rows)
    gown_t = one_hot_t(own_at, rows)
    ghalo = one_hot(halo_at, 2 * block)
    ghalo_t = one_hot_t(halo_at, 2 * block)

    [w_fold] = run(fold_kernel, (w_message[0], w_aggregate[0]), [(w_message.shape[1:], BF16)])
    weights = (w_send[0], w_recv[0], w_node[0], w_fold, gains)
    swapped = [flip_core(value) for value in weights]
    even = [jnp.where(core == 0, a, b) for a, b in zip(weights, swapped)]
    odd = [jnp.where(core == 0, b, a) for a, b in zip(weights, swapped)]

    wide = (rows, latent)
    edge_wide = (edges, latent)
    narrow = (block, latent)
    unit = 2 * rows * latent * latent

    saved = [(), ()]
    for tick in range(sections):
        plane, parity = tick // 2, tick % 2
        send_w, recv_w, node_w, fold_w, gain = (even, odd)[parity]
        a_own, u_own = run(
            functools.partial(forward_own_kernel, plane),
            (hidden, gown, send_w, recv_w, node_w),
            [(edge_wide, F32), (wide, F32)],
            flops=4 * unit,
        )
        hidden, to_inner, to_outer, a, u = run(
            functools.partial(forward_kernel, plane),
            (lists, hidden, a_own, u_own, inner, outer, ghalo, gown_t, send_w, fold_w, gain),
            [(wide, BF16), (narrow, BF16), (narrow, BF16), (edge_wide, F32), (wide, F32)],
            flops=4 * unit,
        )
        produced = hidden
        if tick < sections - 1:
            step = (tick + 1) // 2 - plane
            outer = towards(to_outer, OUTER, step)
            inner = towards(to_inner, INNER, step)
            if step:
                hidden = send(hidden, lambda z, y, x, c: (z, y, x + 1, c))
        saved[parity] = run(
            functools.partial(save_kernel, plane),
            (a, u, produced) + tuple(saved[parity]),
            [(wide, F32), (wide, F32), (edge_wide, F32), (wide, BF16)],
            aliases={3 + k: k for k in range(4)} if saved[parity] else None,
            flops=unit,
        )

    upstream = jnp.where(local, grad_here, grad_there)
    inner = outer = None
    finished = [None] * sections
    for tick in range(sections - 1, -1, -1):
        plane, parity = tick // 2, tick % 2
        send_w, recv_w, node_w, fold_w, gain = (even, odd)[parity]
        operands = tuple(saved[parity][:3]) + (gain, gown, ghalo_t, fold_w, send_w)
        outs = [
            (wide, F32),
            (wide, BF16),
            (wide, BF16),
            (edge_wide, BF16),
            (edge_wide, BF16),
            (narrow, BF16),
            (narrow, BF16),
        ]
        if inner is None:

            def body(lists, upstream, *refs, plane=plane):
                backward_kernel(plane, lists, upstream, None, None, *refs)

            c, cb, du, da, es, to_inner, to_outer = run(body, (lists, upstream) + operands, outs, flops=4 * unit)
        else:
            c, cb, du, da, es, to_inner, to_outer = run(
                functools.partial(backward_kernel, plane),
                (lists, upstream, inner, outer) + operands,
                outs,
                flops=4 * unit,
            )
            finished[tick + 1] = cb
        if tick > 0:
            step = (tick - 1) // 2 - plane
            outer = towards(to_outer, OUTER, step)
            inner = towards(to_inner, INNER, step)
        upstream, own_half = run(
            functools.partial(backward_own_kernel, plane),
            (c, du, da, es, gown_t, node_w, recv_w),
            [(wide, F32), (wide, BF16)],
            flops=4 * unit,
        )
        if tick > 0 and step:
            upstream = send(own_half, lambda z, y, x, c: (z, y, x + 1, c))

    def both_micro(evens, odds):
        swap = flip_core(jnp.where(core == 1, evens, odds))
        return jnp.where(core == 0, jnp.stack([evens, swap]), jnp.stack([swap, odds]))[None]

    section_out = both_micro(to_home(saved[0][3]), to_home(saved[1][3]))

    odds = to_home(jnp.where(plane_here == 0, finished[1], finished[3]))
    second = send(finished[2], lambda z, y, x, c: (z, y, x + 1, c))
    final_outer = send(to_outer, lambda z, y, x, c: (z + 2 * c - 1, 1 - c, x, y))
    final_inner = send(to_inner, lambda z, y, x, c: (z, 1 - c, x, y))
    evens = to_home(jnp.where(plane_here == 0, own_half, second))

    def added(value, side, halo):
        at = jnp.where((y == 0) == (side == INNER), first_list[0], first_list[1])
        covered = ((jnp.arange(rows) // block == at) & (plane_here == 0))[:, None]
        return value + jnp.where(covered, jnp.concatenate([halo] * (rows // block), axis=0).astype(F32), 0.0)

    evens = added(added(evens.astype(F32), INNER, final_inner), OUTER, final_outer).astype(BF16)
    return section_out, both_micro(evens, odds)


def solution(mesh):
    in_specs = (
        P(None, "dom", None),
        P(None, "dom", None),
        P("pipe", None, None),
        P("pipe", None, None),
        P("pipe", None, None),
        P("pipe", None, None),
        P("pipe", None, None),
        P("pipe", None),
        P("dom", None),
        P("dom", None),
        P("dom"),
        P("dom", None, None),
    )
    out_specs = (P("pipe", None, "dom", None), P("pipe", None, "dom", None))
    return jax.shard_map(shards, mesh=mesh, in_specs=in_specs, out_specs=out_specs, check_vma=False)
```

time: 140 us -> 121 us (0.86)
  waiting for transfers between devices: 54.5 us -> 33.2 us
  Pallas kernels: 22.2 us -> 15.4 us
  other arithmetic: 5.61 us -> 10.5 us
  between operations: 2.63 us -> 6.34 us
  local copies, waits for them, and re-layouts: 11.5 us -> 13.4 us
    ppermute x29 -> x32, waiting for transfers between devices: 54.5 us -> 33.2 us  [send(): return lax.ppermute(value, AXES, table)]
    pallas_call x20 -> x21, Pallas kernels: 21.8 us -> 15.4 us  [run(): pl.pallas_call(kernel, out_shape=[jax.ShapeDtypeStruct(s, t) for s, t in...]
    select_n x6 -> x18, other arithmetic: 4.25 us -> 9.37 us  [the longest x5 3.7 us: shards(): odd = [jnp.where(core == 0, b, a) for a, b in zip(weights, swapped)]]
    squeeze x2 -> x3, local copies, waits for them, and re-layouts: 0.96 us -> 2.56 us  [the longest x1 1.57 us: shards(): lax.dynamic_slice(inputs, (core, out_block * block, 0), (1, block, latent))]
    ppermute x29 -> x32, starting transfers between devices: 42.5 us -> 41.4 us  [send(): return lax.ppermute(value, AXES, table)]
    unnamed x40 -> x64, local copies, waits for them, and re-layouts: 9.78 us -> 9.47 us
  transfers between devices with their start and end apart: 29 -> 32, of which waited for: 7 -> 8; matrix products, arithmetic and copies ran while one was open for 3% -> 11% of each run, Pallas kernels for 8% -> 7%
where the time goes in v1:
time: 121 us; the launch traced here: 120 us
  starting transfers between devices  41.4 us (34%)
  waiting for transfers between devices  33.2 us (27%)
  Pallas kernels  15.4 us (13%)
  local copies, waits for them, and re-layouts  13.4 us (11%)
  other arithmetic  10.5 us (9%)
  between operations  6.34 us (5%)
    ppermute x32, starting transfers between devices, send(): return lax.ppermute(value, AXES, table)  41.4 us
    ppermute x32, waiting for transfers between devices, send(): return lax.ppermute(value, AXES, table)  33.2 us
    pallas_call x21, Pallas kernels, run(): pl.pallas_call(kernel, out_shape=[jax.ShapeDtypeStruct(s, t) for s, t in...  15.4 us
    unnamed x64, local copies, waits for them, and re-layouts  9.47 us
    select_n x5, other arithmetic, shards(): odd = [jnp.where(core == 0, b, a) for a, b in zip(weights, swapped)]  3.7 us
    select_n x2, other arithmetic, both_micro(): jnp.where(core == 0, jnp.stack([evens, swap]), jnp.stack([swap, odds]))  2.8 us
  transfers between devices with their start and end apart: 32, of which 8 were waited for; matrix products, arithmetic and copies ran while one was open for 11% of the time, Pallas kernels for 7%

profile of v1, /device:TPU:0, one launch (start us, length us, event | category | flops | bytes accessed | tf_op | source)
XLA Modules:
  0.0 120.2 jit_solution(4478609290761136803)
XLA Ops:
  2.1 3.0 %collective-permute-start = (s32[5,128]{1,0:T(8,128)S(1)}, s32[5,128]{1,0:T(8,128)S(1)}, u32[]{:S(2)}, u32[]{:S(2)}) collective-permute-start(s32[5,128]{1,0:T(8,128)S(1)} %pad_add_fusion), channel_id=1, source_target_pairs={{0,4},{1,5},{2,6},{3,7},{4,0},{5,1},{6,2},{7,3},{8,12},{9,13},{10,... | collective-permute-start | bytes 7688 | tf_op jit(solution)/shard_map/ppermute | solution.py:203
  8.7 1.6 %dynamic-slice_bitcast_fusion.3 = bf16[128,512]{1,0:T(8,128)(2,1)} fusion(bf16[2,256,512]{2,1,0:T(8,128)(2,1)} %param.12, s32[]{:T(128)S(6)} %select_n.274, s32[]{:T(128)S(6)} %select_n.276), kind=kLoop, calls=%fused_computation.29 | loop fusion | bytes 262152 | tf_op jit(solution)/shard_map/squeeze | solution.py:221
  12.3 3.7 %collective-permute-start.5 = (bf16[128,512]{1,0:T(8,128)(2,1)}, bf16[128,512]{1,0:T(8,128)(2,1)S(1)}, u32[]{:S(2)}, u32[]{:S(2)}) collective-permute-start(bf16[128,512]{1,0:T(8,128)(2,1)} %dynamic-slice_bitcast_fusion.3), channel_id=1, source_target_pairs={{0,25},{1,29},{2,27},{3,31},{4,8},{5,12},{6,10},{7,14},{8,1},{9,5}... | collective-permute-start | bytes 393224 | tf_op jit(solution)/shard_map/ppermute | solution.py:203
  18.5 1.3 %broadcast_select_fusion.17 = s32[2]{0:T(128)S(1)} fusion(pred[]{:T(512)S(6)} %eq.56, s32[1]{0:T(128)} %bitcast.3, s32[1]{0:T(128)} %bitcast.2), kind=kLoop, calls=%fused_computation.51 | loop fusion | flops 6 | bytes 17 | tf_op jit(solution)/shard_map/jit(_where)/select_n | solution.py:245
  23.3 1.3 %broadcast_select_fusion.1 = (bf16[512,512]{1,0:T(8,128)(2,1)S(1)}, bf16[512,512]{1,0:T(8,128)(2,1)S(1)}) fusion(bf16[512,512]{1,0:T(8,128)(2,1)} %collective-permute-done.4, pred[]{:T(512)S(6)} %eq.56, bf16[1,512,512]{2,1,0:T(8,128)(2,1)} %param.17), kind=kLoop, calls=%fused_computation.8 | loop fusion | flops 524288 | bytes 2097153 | tf_op jit(solution)/shard_map/jit(_where)/select_n | solution.py:267
  28.7 5.2 %collective-permute-done.9.outer = bf16[128,512]{1,0:T(8,128)(2,1)S(1)} collective-permute-done((bf16[128,512]{1,0:T(8,128)(2,1)S(1)}, bf16[128,512]{1,0:T(8,128)(2,1)S(1)}, u32[]{:S(2)}, u32[]{:S(2)}) %collective-permute-start.9) | collective-permute-done | bytes 131104 | tf_op jit(solution)/shard_map/ppermute | solution.py:203
  35.3 2.2 %collective-permute-start.12 = (bf16[128,512]{1,0:T(8,128)(2,1)S(1)}, bf16[128,512]{1,0:T(8,128)(2,1)S(1)}, u32[]{:S(2)}, u32[]{:S(2)}) collective-permute-start(bf16[128,512]{1,0:T(8,128)(2,1)S(1)} %get-tuple-element.86), channel_id=1, source_target_pairs={{0,27},{1,10},{2,25},{3,8},{4,31},{5,14},{6,29},{7,12},{8,3},{9,18... | collective-permute-start | bytes 393224 | tf_op jit(solution)/shard_map/ppermute | solution.py:203
  37.5 8.3 %collective-permute-done.10.h = bf16[256,512]{1,0:T(8,128)(2,1)S(1)} collective-permute-done((bf16[256,512]{1,0:T(8,128)(2,1)S(1)}, bf16[256,512]{1,0:T(8,128)(2,1)S(1)}, u32[]{:S(2)}, u32[]{:S(2)}) %collective-permute-start.10) | collective-permute-done | bytes 262176 | tf_op jit(solution)/shard_map/ppermute | solution.py:203
  47.1 1.6 %collective-permute-start.15 = (bf16[128,512]{1,0:T(8,128)(2,1)S(1)}, bf16[128,512]{1,0:T(8,128)(2,1)S(1)}, u32[]{:S(2)}, u32[]{:S(2)}) collective-permute-start(bf16[128,512]{1,0:T(8,128)(2,1)S(1)} %get-tuple-element.100), channel_id=1, source_target_pairs={{0,25},{1,8},{2,27},{3,10},{4,29},{5,12},{6,31},{7,14},{8,1},{9,16... | collective-permute-start | bytes 393224 | tf_op jit(solution)/shard_map/ppermute | solution.py:203
  49.3 4.0 %collective-permute-done.15.outer = bf16[128,512]{1,0:T(8,128)(2,1)S(1)} collective-permute-done((bf16[128,512]{1,0:T(8,128)(2,1)S(1)}, bf16[128,512]{1,0:T(8,128)(2,1)S(1)}, u32[]{:S(2)}, u32[]{:S(2)}) %collective-permute-start.15) | collective-permute-done | bytes 131104 | tf_op jit(solution)/shard_map/ppermute | solution.py:203
  54.7 1.6 %collective-permute-start.20 = (bf16[128,512]{1,0:T(8,128)(2,1)S(1)}, bf16[128,512]{1,0:T(8,128)(2,1)S(1)}, u32[]{:S(2)}, u32[]{:S(2)}) collective-permute-start(bf16[128,512]{1,0:T(8,128)(2,1)S(1)} %get-tuple-element.120), channel_id=1, source_target_pairs={{0,25},{1,8},{2,27},{3,10},{4,29},{5,12},{6,31},{7,14},{8,1},{9,16... | collective-permute-start | bytes 393224 | tf_op jit(solution)/shard_map/ppermute | solution.py:203
  58.4 2.8 %collective-permute-done.20.outer = bf16[128,512]{1,0:T(8,128)(2,1)S(1)} collective-permute-done((bf16[128,512]{1,0:T(8,128)(2,1)S(1)}, bf16[128,512]{1,0:T(8,128)(2,1)S(1)}, u32[]{:S(2)}, u32[]{:S(2)}) %collective-permute-start.20) | collective-permute-done | bytes 131104 | tf_op jit(solution)/shard_map/ppermute | solution.py:203
  62.3 5.7 %collective-permute-start.21 = (bf16[256,512]{1,0:T(8,128)(2,1)S(1)}, bf16[256,512]{1,0:T(8,128)(2,1)S(1)}, u32[]{:S(2)}, u32[]{:S(2)}) collective-permute-start(bf16[256,512]{1,0:T(8,128)(2,1)S(1)} %get-tuple-element.128), channel_id=1, source_target_pairs={{0,2},{1,3},{2,0},{3,1},{4,6},{5,7},{6,4},{7,5},{8,10},{9,11},{10,... | collective-permute-start | bytes 786440 | tf_op jit(solution)/shard_map/ppermute | solution.py:203
  69.0 10.4 %collective-permute-done.22.inner = bf16[128,512]{1,0:T(8,128)(2,1)S(1)} collective-permute-done((bf16[128,512]{1,0:T(8,128)(2,1)S(1)}, bf16[128,512]{1,0:T(8,128)(2,1)S(1)}, u32[]{:S(2)}, u32[]{:S(2)}) %collective-permute-start.22) | collective-permute-done | bytes 131104 | tf_op jit(solution)/shard_map/ppermute | solution.py:203
  79.4 1.9 %shard_map.148 = (f32[256,512]{1,0:T(8,128)S(1)}, bf16[256,512]{1,0:T(8,128)(2,1)S(1)}, bf16[256,512]{1,0:T(8,128)(2,1)S(1)}, bf16[256,512]{1,0:T(8,128)(2,1)S(1...) custom-call(s32[2,128]{1,0:T(2,128)S(1)} %broadcast_in_dim.49.lists, ...), custom_call_target="tpu_custom_call" | custom-call | flops 536870912 | bytes 1048576 | tf_op jit(solution)/shard_map/pallas_call | solution.py:159
  88.1 3.6 %collective-permute-start.13 = (bf16[256,512]{1,0:T(8,128)(2,1)}, bf16[256,512]{1,0:T(8,128)(2,1)}, u32[]{:S(2)}, u32[]{:S(2)}) collective-permute-start(bf16[256,512]{1,0:T(8,128)(2,1)} %copy-done.19), channel_id=1, source_target_pairs={{0,0},{1,4},{2,2},{3,6},{4,1},{5,5},{6,3},{7,7},{8,8},{9,12},{10,1... | collective-permute-start | bytes 786440 | tf_op jit(solution)/shard_map/ppermute | solution.py:203
  91.7 3.6 %collective-permute-start.16 = (bf16[256,512]{1,0:T(8,128)(2,1)}, bf16[256,512]{1,0:T(8,128)(2,1)}, u32[]{:S(2)}, u32[]{:S(2)}) collective-permute-start(bf16[256,512]{1,0:T(8,128)(2,1)} %copy-done.18), channel_id=1, source_target_pairs={{0,0},{1,4},{2,2},{3,6},{4,1},{5,5},{6,3},{7,7},{8,8},{9,12},{10,1... | collective-permute-start | bytes 786440 | tf_op jit(solution)/shard_map/ppermute | solution.py:203
  100.2 1.3 %shard_map.149 = (f32[256,512]{1,0:T(8,128)S(1)}, bf16[256,512]{1,0:T(8,128)(2,1)}) custom-call(f32[256,512]{1,0:T(8,128)S(1)} %copy-done.13, bf16[256,512]{1,0:T(8,128)(2,1)S(1)} %get-tuple-element.132.du, bf16[256,512]{1,0:T(8,128)(2,1)S(1)} %copy-done.15, bf16[256,512]{1,0:T(8,128)(2,1)S(1)} %copy-done.17, bf16[256,512]{1,0:T(8,128)(2,1)S(1)} %fusion.1.gown_t, ...), custom_call_target="tpu_custom_call" | custom-call | flops 536870912 | bytes 1048576 | tf_op jit(solution)/shard_map/pallas_call | solution.py:159
  101.5 2.2 %shard_map.150 = (f32[256,512]{1,0:T(8,128)S(1)}, bf16[256,512]{1,0:T(8,128)(2,1)S(1)}, bf16[256,512]{1,0:T(8,128)(2,1)S(1)}, bf16[256,512]{1,0:T(8,128)(2,1)S(1...) custom-call(s32[2,128]{1,0:T(2,128)S(1)} %broadcast_in_dim.49.lists, ...), custom_call_target="tpu_custom_call" | custom-call | flops 536870912 | bytes 1048576 | tf_op jit(solution)/shard_map/pallas_call | solution.py:159
  104.4 1.4 %shard_map.151 = (f32[256,512]{1,0:T(8,128)}, bf16[256,512]{1,0:T(8,128)(2,1)S(1)}) custom-call(f32[256,512]{1,0:T(8,128)S(1)} %get-tuple-element.138.c, bf16[256,512]{1,0:T(8,128)(2,1)S(1)} %get-tuple-element.139.du, bf16[256,512]{1,0:T(8,128)(2,1)S(1)} %get-tuple-element.140.da, bf16[256,512]{1,0:T(8,128)(2,1)S(1)} %get-tuple-element.141.es, ...), custom_call_target="tpu_custom_call" | custom-call | flops 536870912 | bytes 1048576 | tf_op jit(solution)/shard_map/pallas_call | solution.py:159
  106.6 4.9 %collective-permute-start.29 = (bf16[128,512]{1,0:T(8,128)(2,1)S(1)}, bf16[128,512]{1,0:T(8,128)(2,1)S(1)}, u32[]{:S(2)}, u32[]{:S(2)}) collective-permute-start(bf16[128,512]{1,0:T(8,128)(2,1)S(1)} %get-tuple-element.145), channel_id=1, source_target_pairs={{0,28},{1,8},{2,30},{3,10},{4,29},{5,9},{6,31},{7,11},{8,4},{9,16}... | collective-permute-start | bytes 393224 | tf_op jit(solution)/shard_map/ppermute | solution.py:203
  113.1 2.1 %collective-permute-done.29 = bf16[128,512]{1,0:T(8,128)(2,1)S(1)} collective-permute-done((bf16[128,512]{1,0:T(8,128)(2,1)S(1)}, bf16[128,512]{1,0:T(8,128)(2,1)S(1)}, u32[]{:S(2)}, u32[]{:S(2)}) %collective-permute-start.29) | collective-permute-done | bytes 131104 | tf_op jit(solution)/shard_map/ppermute | solution.py:203
  115.7 1.7 %collective-permute-start.31 = (bf16[256,512]{1,0:T(8,128)(2,1)S(1)}, bf16[256,512]{1,0:T(8,128)(2,1)S(1)}, u32[]{:S(2)}, u32[]{:S(2)}) collective-permute-start(bf16[256,512]{1,0:T(8,128)(2,1)S(1)} %get-tuple-element.148), channel_id=1, source_target_pairs={{0,1},{1,0},{2,3},{3,2},{4,5},{5,4},{6,7},{7,6},{8,9},{9,8},{10,11... | collective-permute-start | bytes 786440 | tf_op jit(solution)/shard_map/ppermute | solution.py:203
  117.4 1.9 %maximum_select_fusion = bf16[1,2,256,512]{3,2,1,0:T(8,128)(2,1)} fusion(bf16[1,1,256,512]{3,2,1,0:T(8,128)(2,1)S(1)} %bitcast.50, bf16[1,1,256,512]{3,2,1,0:T(8,128)(2,1)} %bitcast.19, bf16[1,1,256,512]{3,2,1,0:T(8,128)(2,1)} %bitcast.21, pred[]{:T(512)S(6)} %eq.56), kind=kLoop, calls=%fused_computation | loop fusion | flops 786432 | bytes 1310721 | tf_op jit(solution)/shard_map/jit(_where)/select_n | solution.py:350
  (158 shorter events, 36.6 us)
Async XLA Ops:
  2.1 10.2 %collective-permute-start = (s32[5,128]{1,0:T(8,128)S(1)}, s32[5,128]{1,0:T(8,128)S(1)}, u32[]{:S(2)}, u32[]{:S(2)}) collective-permute-start(s32[5,128]{1,0:T(8,128)S(1)} %pad_add_fusion), channel_id=1, source_target_pairs={{0,4},{1,5},{2,6},{3,7},{4,0},{5,1},{6,2},{7,3},{8,12},{9,13},{10,... | collective-permute-start | bytes 7688 | tf_op jit(solution)/shard_map/ppermute | solution.py:203
  6.0 13.7 %collective-permute-start.1 = (bf16[256,512]{1,0:T(8,128)(2,1)S(1)}, bf16[256,512]{1,0:T(8,128)(2,1)S(1)}, u32[]{:S(2)}, u32[]{:S(2)}) collective-permute-start(bf16[256,512]{1,0:T(8,128)(2,1)S(1)} %dynamic-slice_bitcast_fusion.1), channel_id=1, source_target_pairs={{0,4},{1,5},{2,6},{3,7},{4,0},{5,1},{6,2},{7,3},{8,12},{9,13},{10,... | collective-permute-start | bytes 786440 | tf_op jit(solution)/shard_map/ppermute | solution.py:203
  6.1 14.8 %collective-permute-start.2 = (bf16[512,512]{1,0:T(8,128)(2,1)}, bf16[512,512]{1,0:T(8,128)(2,1)}, u32[]{:S(2)}, u32[]{:S(2)}) collective-permute-start(bf16[512,512]{1,0:T(8,128)(2,1)} %bitcast.48), channel_id=1, source_target_pairs={{0,1},{1,0},{2,3},{3,2},{4,5},{5,4},{6,7},{7,6},{8,9},{9,8},{10,11... | collective-permute-start | bytes 1572872 | tf_op jit(solution)/shard_map/ppermute | solution.py:203
  6.2 16.0 %collective-permute-start.3 = (bf16[512,512]{1,0:T(8,128)(2,1)}, bf16[512,512]{1,0:T(8,128)(2,1)}, u32[]{:S(2)}, u32[]{:S(2)}) collective-permute-start(bf16[512,512]{1,0:T(8,128)(2,1)} %bitcast.49), channel_id=1, source_target_pairs={{0,1},{1,0},{2,3},{3,2},{4,5},{5,4},{6,7},{7,6},{8,9},{9,8},{10,11... | collective-permute-start | bytes 1572872 | tf_op jit(solution)/shard_map/ppermute | solution.py:203
  11.8 11.5 %collective-permute-start.4 = (bf16[512,512]{1,0:T(8,128)(2,1)}, bf16[512,512]{1,0:T(8,128)(2,1)}, u32[]{:S(2)}, u32[]{:S(2)}) collective-permute-start(bf16[512,512]{1,0:T(8,128)(2,1)} %bitcast.11), channel_id=1, source_target_pairs={{0,1},{1,0},{2,3},{3,2},{4,5},{5,4},{6,7},{7,6},{8,9},{9,8},{10,11... | collective-permute-start | bytes 1572872 | tf_op jit(solution)/shard_map/ppermute | solution.py:203
  12.3 13.3 %collective-permute-start.5 = (bf16[128,512]{1,0:T(8,128)(2,1)}, bf16[128,512]{1,0:T(8,128)(2,1)S(1)}, u32[]{:S(2)}, u32[]{:S(2)}) collective-permute-start(bf16[128,512]{1,0:T(8,128)(2,1)} %dynamic-slice_bitcast_fusion.3), channel_id=1, source_target_pairs={{0,25},{1,29},{2,27},{3,31},{4,8},{5,12},{6,10},{7,14},{8,1},{9,5}... | collective-permute-start | bytes 393224 | tf_op jit(solution)/shard_map/ppermute | solution.py:203
  27.7 6.2 %collective-permute-start.9 = (bf16[128,512]{1,0:T(8,128)(2,1)S(1)}, bf16[128,512]{1,0:T(8,128)(2,1)S(1)}, u32[]{:S(2)}, u32[]{:S(2)}) collective-permute-start(bf16[128,512]{1,0:T(8,128)(2,1)S(1)} %get-tuple-element.81), channel_id=1, source_target_pairs={{0,25},{1,8},{2,27},{3,10},{4,29},{5,12},{6,31},{7,14},{8,1},{9,16... | collective-permute-start | bytes 393224 | tf_op jit(solution)/shard_map/ppermute | solution.py:203
  35.1 10.8 %collective-permute-start.10 = (bf16[256,512]{1,0:T(8,128)(2,1)S(1)}, bf16[256,512]{1,0:T(8,128)(2,1)S(1)}, u32[]{:S(2)}, u32[]{:S(2)}) collective-permute-start(bf16[256,512]{1,0:T(8,128)(2,1)S(1)} %get-tuple-element.82.h), channel_id=1, source_target_pairs={{0,2},{1,3},{2,0},{3,1},{4,6},{5,7},{6,4},{7,5},{8,10},{9,11},{10,... | collective-permute-start | bytes 786440 | tf_op jit(solution)/shard_map/ppermute | solution.py:203
  35.2 13.5 %collective-permute-start.18 = (bf16[256,512]{1,0:T(8,128)(2,1)S(1)}, bf16[256,512]{1,0:T(8,128)(2,1)S(1)}, u32[]{:S(2)}, u32[]{:S(2)}) collective-permute-start(bf16[256,512]{1,0:T(8,128)(2,1)S(1)} %dynamic-slice_bitcast_fusion), channel_id=1, source_target_pairs={{0,4},{1,5},{2,6},{3,7},{4,0},{5,1},{6,2},{7,3},{8,12},{9,13},{10,... | collective-permute-start | bytes 786440 | tf_op jit(solution)/shard_map/ppermute | solution.py:203
  35.3 10.6 %collective-permute-start.11 = (bf16[128,512]{1,0:T(8,128)(2,1)S(1)}, bf16[128,512]{1,0:T(8,128)(2,1)S(1)}, u32[]{:S(2)}, u32[]{:S(2)}) collective-permute-start(bf16[128,512]{1,0:T(8,128)(2,1)S(1)} %get-tuple-element.85), channel_id=1, source_target_pairs={{0,3},{1,2},{2,1},{3,0},{4,7},{5,6},{6,5},{7,4},{8,11},{9,10},{10,... | collective-permute-start | bytes 393224 | tf_op jit(solution)/shard_map/ppermute | solution.py:203
  35.3 10.5 %collective-permute-start.12 = (bf16[128,512]{1,0:T(8,128)(2,1)S(1)}, bf16[128,512]{1,0:T(8,128)(2,1)S(1)}, u32[]{:S(2)}, u32[]{:S(2)}) collective-permute-start(bf16[128,512]{1,0:T(8,128)(2,1)S(1)} %get-tuple-element.86), channel_id=1, source_target_pairs={{0,27},{1,10},{2,25},{3,8},{4,31},{5,14},{6,29},{7,12},{8,3},{9,18... | collective-permute-start | bytes 393224 | tf_op jit(solution)/shard_map/ppermute | solution.py:203
  47.1 6.2 %collective-permute-start.15 = (bf16[128,512]{1,0:T(8,128)(2,1)S(1)}, bf16[128,512]{1,0:T(8,128)(2,1)S(1)}, u32[]{:S(2)}, u32[]{:S(2)}) collective-permute-start(bf16[128,512]{1,0:T(8,128)(2,1)S(1)} %get-tuple-element.100), channel_id=1, source_target_pairs={{0,25},{1,8},{2,27},{3,10},{4,29},{5,12},{6,31},{7,14},{8,1},{9,16... | collective-permute-start | bytes 393224 | tf_op jit(solution)/shard_map/ppermute | solution.py:203
  54.7 6.5 %collective-permute-start.20 = (bf16[128,512]{1,0:T(8,128)(2,1)S(1)}, bf16[128,512]{1,0:T(8,128)(2,1)S(1)}, u32[]{:S(2)}, u32[]{:S(2)}) collective-permute-start(bf16[128,512]{1,0:T(8,128)(2,1)S(1)} %get-tuple-element.120), channel_id=1, source_target_pairs={{0,25},{1,8},{2,27},{3,10},{4,29},{5,12},{6,31},{7,14},{8,1},{9,16... | collective-permute-start | bytes 393224 | tf_op jit(solution)/shard_map/ppermute | solution.py:203
  62.3 17.1 %collective-permute-start.21 = (bf16[256,512]{1,0:T(8,128)(2,1)S(1)}, bf16[256,512]{1,0:T(8,128)(2,1)S(1)}, u32[]{:S(2)}, u32[]{:S(2)}) collective-permute-start(bf16[256,512]{1,0:T(8,128)(2,1)S(1)} %get-tuple-element.128), channel_id=1, source_target_pairs={{0,2},{1,3},{2,0},{3,1},{4,6},{5,7},{6,4},{7,5},{8,10},{9,11},{10,... | collective-permute-start | bytes 786440 | tf_op jit(solution)/shard_map/ppermute | solution.py:203
  68.0 11.4 %collective-permute-start.22 = (bf16[128,512]{1,0:T(8,128)(2,1)S(1)}, bf16[128,512]{1,0:T(8,128)(2,1)S(1)}, u32[]{:S(2)}, u32[]{:S(2)}) collective-permute-start(bf16[128,512]{1,0:T(8,128)(2,1)S(1)} %get-tuple-element.129), channel_id=1, source_target_pairs={{0,3},{1,2},{2,1},{3,0},{4,7},{5,6},{6,5},{7,4},{8,11},{9,10},{10,... | collective-permute-start | bytes 393224 | tf_op jit(solution)/shard_map/ppermute | solution.py:203
  68.0 11.4 %collective-permute-start.23 = (bf16[128,512]{1,0:T(8,128)(2,1)S(1)}, bf16[128,512]{1,0:T(8,128)(2,1)S(1)}, u32[]{:S(2)}, u32[]{:S(2)}) collective-permute-start(bf16[128,512]{1,0:T(8,128)(2,1)S(1)} %get-tuple-element.130), channel_id=1, source_target_pairs={{0,27},{1,10},{2,25},{3,8},{4,31},{5,14},{6,29},{7,12},{8,3},{9,18... | collective-permute-start | bytes 393224 | tf_op jit(solution)/shard_map/ppermute | solution.py:203
  84.2 17.2 %collective-permute-start.24 = (bf16[128,512]{1,0:T(8,128)(2,1)}, bf16[128,512]{1,0:T(8,128)(2,1)}, u32[]{:S(2)}, u32[]{:S(2)}) collective-permute-start(bf16[128,512]{1,0:T(8,128)(2,1)} %get-tuple-element.136), channel_id=1, source_target_pairs={{0,1},{1,0},{2,3},{3,2},{4,5},{5,4},{6,7},{7,6},{8,9},{9,8},{10,11... | collective-permute-start | bytes 393224 | tf_op jit(solution)/shard_map/ppermute | solution.py:203
  84.7 16.8 %collective-permute-start.25 = (bf16[128,512]{1,0:T(8,128)(2,1)}, bf16[128,512]{1,0:T(8,128)(2,1)}, u32[]{:S(2)}, u32[]{:S(2)}) collective-permute-start(bf16[128,512]{1,0:T(8,128)(2,1)} %get-tuple-element.137), channel_id=1, source_target_pairs={{0,25},{1,8},{2,27},{3,10},{4,29},{5,12},{6,31},{7,14},{8,1},{9,16... | collective-permute-start | bytes 393224 | tf_op jit(solution)/shard_map/ppermute | solution.py:203
  88.1 23.4 %collective-permute-start.13 = (bf16[256,512]{1,0:T(8,128)(2,1)}, bf16[256,512]{1,0:T(8,128)(2,1)}, u32[]{:S(2)}, u32[]{:S(2)}) collective-permute-start(bf16[256,512]{1,0:T(8,128)(2,1)} %copy-done.19), channel_id=1, source_target_pairs={{0,0},{1,4},{2,2},{3,6},{4,1},{5,5},{6,3},{7,7},{8,8},{9,12},{10,1... | collective-permute-start | bytes 786440 | tf_op jit(solution)/shard_map/ppermute | solution.py:203
  91.7 19.8 %collective-permute-start.16 = (bf16[256,512]{1,0:T(8,128)(2,1)}, bf16[256,512]{1,0:T(8,128)(2,1)}, u32[]{:S(2)}, u32[]{:S(2)}) collective-permute-start(bf16[256,512]{1,0:T(8,128)(2,1)} %copy-done.18), channel_id=1, source_target_pairs={{0,0},{1,4},{2,2},{3,6},{4,1},{5,5},{6,3},{7,7},{8,8},{9,12},{10,1... | collective-permute-start | bytes 786440 | tf_op jit(solution)/shard_map/ppermute | solution.py:203
  95.3 10.5 %collective-permute-start.26 = (bf16[256,512]{1,0:T(8,128)(2,1)}, bf16[256,512]{1,0:T(8,128)(2,1)S(1)}, u32[]{:S(2)}, u32[]{:S(2)}) collective-permute-start(bf16[256,512]{1,0:T(8,128)(2,1)} %copy-done.22), channel_id=1, source_target_pairs={{0,2},{1,3},{2,0},{3,1},{4,6},{5,7},{6,4},{7,5},{8,10},{9,11},{10,... | collective-permute-start | bytes 786440 | tf_op jit(solution)/shard_map/ppermute | solution.py:203
  103.8 11.7 %collective-permute-start.30 = (bf16[256,512]{1,0:T(8,128)(2,1)S(1)}, bf16[256,512]{1,0:T(8,128)(2,1)S(1)}, u32[]{:S(2)}, u32[]{:S(2)}) collective-permute-start(bf16[256,512]{1,0:T(8,128)(2,1)S(1)} %broadcast_select_fusion.8), channel_id=1, source_target_pairs={{0,0},{1,4},{2,2},{3,6},{4,1},{5,5},{6,3},{7,7},{8,8},{9,12},{10,1... | collective-permute-start | bytes 786440 | tf_op jit(solution)/shard_map/ppermute | solution.py:203
  105.9 9.5 %collective-permute-start.27 = (bf16[256,512]{1,0:T(8,128)(2,1)S(1)}, bf16[256,512]{1,0:T(8,128)(2,1)S(1)}, u32[]{:S(2)}, u32[]{:S(2)}) collective-permute-start(bf16[256,512]{1,0:T(8,128)(2,1)S(1)} %broadcast_select_fusion.9), channel_id=1, source_target_pairs={{0,0},{1,4},{2,2},{3,6},{4,1},{5,5},{6,3},{7,7},{8,8},{9,12},{10,1... | collective-permute-start | bytes 786440 | tf_op jit(solution)/shard_map/ppermute | solution.py:203
  106.6 8.5 %collective-permute-start.29 = (bf16[128,512]{1,0:T(8,128)(2,1)S(1)}, bf16[128,512]{1,0:T(8,128)(2,1)S(1)}, u32[]{:S(2)}, u32[]{:S(2)}) collective-permute-start(bf16[128,512]{1,0:T(8,128)(2,1)S(1)} %get-tuple-element.145), channel_id=1, source_target_pairs={{0,28},{1,8},{2,30},{3,10},{4,29},{5,9},{6,31},{7,11},{8,4},{9,16}... | collective-permute-start | bytes 393224 | tf_op jit(solution)/shard_map/ppermute | solution.py:203
  (40 other events, 136.2 us)

commit v2 on v1

v2 whole, which is shorter than its diff:
```python
import functools

import jax
import jax.numpy as jnp
from jax import lax
from jax.experimental import pallas as pl
from jax.experimental.pallas import tpu as pltpu
from jax.sharding import PartitionSpec as P

EPSILON = 1e-05
F32 = jnp.float32
BF16 = jnp.bfloat16
AXES = ("dom", "pipe")
INNER, OUTER = 0, 1


def mul(a, b):
    return jnp.dot(a, b, preferred_element_type=F32)


def mul_t(a, b):
    return lax.dot_general(a, b, (((1,), (1,)), ((), ())), preferred_element_type=F32)


def slope(v):
    s = jax.nn.sigmoid(v)
    return s * (1.0 + v * (1.0 - s))


def normalize(z):
    centred = z - jnp.mean(z, axis=-1, keepdims=True)
    inverse = lax.rsqrt(jnp.mean(centred * centred, axis=-1, keepdims=True) + EPSILON)
    return centred * inverse, inverse


def here_is(plane=None, parity=None):
    pipe = lax.axis_index("pipe")
    wanted = jnp.bool_(True)
    if plane is not None:
        wanted = pipe // 2 == plane
    if parity is not None:
        wanted = wanted & (pipe % 2 == parity)
    return wanted


def is_local():
    return lax.axis_index("pipe") % 2 == lax.axis_index("dom") % 2


def listed(at, value, block):
    picked = value[:block]
    for number in range(1, value.shape[0] // block):
        picked = jnp.where(at == number, value[number * block : (number + 1) * block], picked)
    return picked


def add_listed(at, target, value, block):
    for number in range(target.shape[0] // block):
        rows = slice(number * block, (number + 1) * block)
        target[rows, :] = target[rows, :] + jnp.where(at == number, value, 0.0)


def rows_kernel(inputs, here, there, sems):
    micro = lax.axis_index("dom") % 2
    first = pltpu.make_async_copy(inputs.at[1 - micro], there, sems.at[0])
    second = pltpu.make_async_copy(inputs.at[micro], here, sems.at[1])
    first.start()
    second.start()
    first.wait()
    second.wait()


def boundary_kernel(lists, inputs, out, sem):
    block = out.shape[0]
    number = jnp.where(lax.axis_index("dom") % 2 == 1, lists[0], lists[1])
    start = pl.multiple_of(number * block, block)
    copy = pltpu.make_async_copy(inputs.at[lax.axis_index("pipe") % 2, pl.ds(start, block), :], out, sem)
    copy.start()
    copy.wait()


def graph_kernel(edge_blocks, packed, packed_there, gown, gown_t, ghalo, ghalo_t, lists, mate):
    block = packed.shape[1]
    rows = gown_t.shape[0]
    edges = edge_blocks * block
    first_core = lax.axis_index("pipe") % 2 == 0
    mine = jnp.where(is_local(), packed[...], packed_there[...])
    other = jnp.where(is_local(), packed_there[...], packed[...])
    tail = 2 * edge_blocks
    lane = lax.broadcasted_iota(jnp.int32, (1, block), 1)
    row = lax.broadcasted_iota(jnp.int32, (rows, block), 0)
    halo_row = lax.broadcasted_iota(jnp.int32, (2 * block, block), 0)
    for number in range(edge_blocks):
        live = lane < mine[tail : tail + 1, number : number + 1]
        sender = jnp.where(live, mine[number : number + 1], -1)
        receiver = jnp.where(live, mine[edge_blocks + number : edge_blocks + number + 1], -1)
        halo = sender - rows
        turned = jnp.where(halo < block, halo + block, halo - block)
        halo = jnp.where(halo >= 0, jnp.where(first_core, turned, halo), -1)
        here = slice(number * block, (number + 1) * block)
        received = slice(edges + number * block, edges + (number + 1) * block)
        for index, at, table, table_t in (
            (sender, here, gown, gown_t),
            (receiver, received, gown, gown_t),
            (halo, here, ghalo, ghalo_t),
        ):
            hot = (index == (halo_row if table is ghalo else row)).astype(F32)
            table_t[:, at] = hot.astype(BF16)
            table[at, :] = hot.T.astype(BF16)
    to_next, to_prev = mine[tail : tail + 1, edge_blocks : edge_blocks + 1], mine[tail : tail + 1, edge_blocks + 1 : edge_blocks + 2]
    lists[0:1, :] = jnp.broadcast_to(jnp.where(first_core, to_next, to_prev), (1, block))
    lists[1:2, :] = jnp.broadcast_to(jnp.where(first_core, to_prev, to_next), (1, block))
    to_next, to_prev = other[tail : tail + 1, edge_blocks : edge_blocks + 1], other[tail : tail + 1, edge_blocks + 1 : edge_blocks + 2]
    mate[...] = jnp.broadcast_to(jnp.where(first_core, to_prev, to_next), (1, block))


def entry_kernel(mate, here, there, hidden, inner):
    block = inner.shape[0]

    @pl.when(is_local())
    def _():
        hidden[...] = here[...]
        inner[...] = listed(mate[:, :1], there[...], block)

    @pl.when(jnp.logical_not(is_local()))
    def _():
        hidden[...] = there[...]
        inner[...] = listed(mate[:, :1], here[...], block)


def local_kernel(here, there, out):
    @pl.when(is_local())
    def _():
        out[...] = here[...]

    @pl.when(jnp.logical_not(is_local()))
    def _():
        out[...] = there[...]


def fold_kernel(a, b, out):
    out[...] = mul(a[...], b[...]).astype(BF16)


def forward_own_kernel(take, h, gown, a_out, u_out):
    w_send, w_recv, w_node, _, _ = take
    edges = gown.shape[0] // 2
    own = mul(gown[...], h[...]).astype(BF16)
    a_out[...] = mul(own[:edges], w_send[...]) + mul(own[edges:], w_recv[...])
    u_out[...] = mul(h[...], w_node[...])


def forward_kernel(take, lists, h, a_own, u_own, inner, outer, ghalo, gown_t, h_out, a_out, u_out, *to):
    w_send, _, _, w_fold, gain = take
    edges = ghalo.shape[0]
    block = inner.shape[0]
    halo = (mul(ghalo[:, :block], inner[...]) + mul(ghalo[:, block:], outer[...])).astype(BF16)
    a = a_own[...] + mul(halo, w_send[...])
    a_out[...] = a
    q = (a * jax.nn.sigmoid(a)).astype(BF16)
    u = u_own[...] + mul(mul(gown_t[:, edges:], q).astype(BF16), w_fold[...])
    u_out[...] = u
    t, _ = normalize(u * jax.nn.sigmoid(u))
    out = (h[...].astype(F32) + t * gain[...]).astype(BF16)
    h_out[...] = out
    for side, ref in enumerate(to):
        ref[...] = listed(lists[side : side + 1, :1], out, block)


def save_kernel(plane, a, u, h, *refs):
    t_out, r_out, s_out, h_out = refs[-4:]

    @pl.when(here_is(plane))
    def _():
        s_out[...] = slope(a[...])
        u_value = u[...]
        t, inverse = normalize(u_value * jax.nn.sigmoid(u_value))
        t_out[...] = t
        r_out[...] = inverse * slope(u_value)
        h_out[...] = h[...]


def backward_kernel(halo_in, finish, take, lists, upstream, *refs):
    w_send, _, _, w_fold, gain = take
    if halo_in:
        inner, outer, *refs = refs
    t_in, r_in, s_in, gown, ghalo_t, c_out, du_out, da_out, es_out, to_inner, to_outer, *rest = refs
    edges = gown.shape[0] // 2
    block = to_inner.shape[0]
    c_out[...] = upstream[...].astype(F32)
    if halo_in:
        add_listed(lists[INNER : INNER + 1, :1], c_out, inner[...].astype(F32), block)
        add_listed(lists[OUTER : OUTER + 1, :1], c_out, outer[...].astype(F32), block)
    if finish:
        rest[0][...] = c_out[...].astype(BF16)
    g = c_out[...] * gain[...]
    t = t_in[...]
    centre = jnp.mean(g, axis=-1, keepdims=True)
    along = jnp.mean(g * t, axis=-1, keepdims=True)
    du = ((g - centre - t * along) * r_in[...]).astype(BF16)
    du_out[...] = du
    spread = mul(gown[edges:, :], du).astype(BF16)
    da = (mul_t(spread, w_fold[...]) * s_in[...]).astype(BF16)
    da_out[...] = da
    es = mul_t(da, w_send[...]).astype(BF16)
    es_out[...] = es
    halo = mul(ghalo_t[...], es).astype(BF16)
    to_inner[...] = halo[:block]
    to_outer[...] = halo[block:]


def backward_own_kernel(take, c, du, da, es, gown_t, out):
    _, w_recv, w_node, _, _ = take
    er = mul_t(da[...], w_recv[...]).astype(BF16)
    both = jnp.concatenate([es[...], er], axis=0)
    total = c[...] + mul_t(du[...], w_node[...]) + mul(gown_t[...], both)
    out[...] = total.astype(out.dtype)


def add_kernel(plane, lists, value, inner, outer, *refs):
    *other, out, total = refs
    block = inner.shape[0]

    @pl.when(here_is(plane))
    def _():
        total[...] = value[...].astype(F32)
        add_listed(lists[INNER : INNER + 1, :1], total, inner[...].astype(F32), block)
        add_listed(lists[OUTER : OUTER + 1, :1], total, outer[...].astype(F32), block)
        out[...] = total[...].astype(BF16)

    if other:

        @pl.when(jnp.logical_not(here_is(plane)))
        def _():
            out[...] = other[0][...]


def turn_kernel(evens, odds, out):
    @pl.when(here_is(parity=1))
    def _():
        out[...] = evens[...]

    @pl.when(here_is(parity=0))
    def _():
        out[...] = odds[...]


def write_kernel(evens, odds, arrived, out, sems):
    core = lax.axis_index("pipe") % 2
    other = pltpu.make_async_copy(arrived, out.at[0, 1 - core], sems.at[1])
    other.start()

    @pl.when(core == 0)
    def _():
        own = pltpu.make_async_copy(evens, out.at[0, 0], sems.at[0])
        own.start()
        own.wait()

    @pl.when(core == 1)
    def _():
        own = pltpu.make_async_copy(odds, out.at[0, 1], sems.at[0])
        own.start()
        own.wait()

    other.wait()


def run(kernel, operands, outs, aliases=None, flops=0, first=pltpu.VMEM, out_space=pltpu.VMEM, scratch=()):
    spaces = [first] + [pltpu.VMEM] * (len(operands) - 1)
    return pl.pallas_call(
        kernel,
        out_shape=[jax.ShapeDtypeStruct(s, t) for s, t in outs],
        in_specs=[pl.BlockSpec(memory_space=space) for space in spaces],
        out_specs=[pl.BlockSpec(memory_space=out_space)] * len(outs),
        scratch_shapes=list(scratch),
        input_output_aliases=aliases or {},
        compiler_params=pltpu.CompilerParams(vmem_limit_bytes=16 * 2**20),
        cost_estimate=pl.CostEstimate(flops=flops, bytes_accessed=2**20, transcendentals=0),
    )(*operands)


def run_section(body, plane, parity, weights, operands, outs, flops):
    count = len(weights) // 2

    def kernel(*refs):
        mine, swapped, rest = refs[:count], refs[count : 2 * count], refs[2 * count :]

        @pl.when(here_is(plane, parity))
        def _():
            body(mine, *rest)

        @pl.when(here_is(plane, 1 - parity))
        def _():
            body(swapped, *rest)

    return run(kernel, tuple(weights) + tuple(operands), outs, flops=flops)


def shards(
    inputs,
    cotangent,
    w_send,
    w_recv,
    w_message,
    w_node,
    w_aggregate,
    gains,
    edge_send,
    edge_recv,
    edge_count,
    halo_send,
):
    sections = lax.axis_size("pipe")
    pairs_total = lax.axis_size("dom") // 2
    phase = lax.axis_index("pipe")
    y = lax.rem(lax.axis_index("dom"), 2)
    plane_here = phase // 2
    rows, latent = inputs.shape[1:]
    edge_blocks, block = edge_send.shape
    edges = edge_blocks * block

    def send(value, rule):
        table = []
        for z in range(pairs_total):
            for which in range(2):
                for x in range(sections // 2):
                    for c in range(2):
                        tz, ty, tx, tc = rule(z, which, x, c)
                        target = (2 * (tz % pairs_total) + ty) * sections + 2 * (tx % (sections // 2)) + tc
                        table.append(((2 * z + which) * sections + 2 * x + c, target))
        return lax.ppermute(value, AXES, table)

    def flip_y(value):
        return send(value, lambda z, y, x, c: (z, 1 - y, x, c))

    def flip_core(value):
        return send(value, lambda z, y, x, c: (z, y, x, 1 - c))

    def to_home(value):
        return send(value, lambda z, y, x, c: (z, c, x, y))

    def towards(value, side, step):
        if side == INNER:
            return send(value, lambda z, y, x, c: (z, y, x + step, 1 - c))
        return send(value, lambda z, y, x, c: (z + 2 * c - 1, y, x + step, 1 - c))

    wide = (rows, latent)
    edge_wide = (edges, latent)
    narrow = (block, latent)
    unit = 2 * rows * latent * latent
    dma = pltpu.SemaphoreType.DMA

    first_list = halo_send[0, :, 0]
    here, there = run(rows_kernel, (inputs,), [(wide, BF16)] * 2, first=pl.ANY, scratch=[dma((2,))])
    there = flip_y(there)
    [boundary] = pl.pallas_call(
        boundary_kernel,
        out_shape=[jax.ShapeDtypeStruct(narrow, BF16)],
        in_specs=[pl.BlockSpec(memory_space=pltpu.SMEM), pl.BlockSpec(memory_space=pl.ANY)],
        out_specs=[pl.BlockSpec(memory_space=pltpu.VMEM)],
        scratch_shapes=[dma(())],
    )(first_list, inputs)
    outer = send(boundary, lambda z, y, x, c: (z + 2 * y - 1, c, x, 1 - y))
    numbers = jnp.concatenate([edge_count, first_list])
    packed = jnp.concatenate(
        [edge_send, edge_recv, jnp.pad(numbers, (0, block - numbers.shape[0]))[None]], axis=0
    )
    packed_there = flip_y(packed)
    gown, gown_t, ghalo, ghalo_t, lists, mate = run(
        functools.partial(graph_kernel, edge_blocks),
        (packed, packed_there),
        [
            ((2 * edges, rows), BF16),
            ((rows, 2 * edges), BF16),
            ((edges, 2 * block), BF16),
            ((2 * block, edges), BF16),
            ((2, block), jnp.int32),
            ((1, block), jnp.int32),
        ],
    )
    hidden, inner = run(entry_kernel, (mate, here, there), [(wide, BF16), (narrow, BF16)])
    home_sides = jnp.where(y == 0, first_list, first_list[::-1])
    home_lists = jnp.broadcast_to(home_sides[:, None], (2, block))

    [w_fold] = run(fold_kernel, (w_message[0], w_aggregate[0]), [(w_message.shape[1:], BF16)])
    weights = (w_send[0], w_recv[0], w_node[0], w_fold, gains)
    weights = weights + tuple(flip_core(value) for value in weights)

    grad_here, grad_there = run(rows_kernel, (cotangent,), [(wide, BF16)] * 2, first=pl.ANY, scratch=[dma((2,))])
    grad_there = flip_y(grad_there)

    saved = [(), ()]
    for tick in range(sections):
        plane, parity = tick // 2, tick % 2
        a_own, u_own = run_section(
            forward_own_kernel, plane, parity, weights, (hidden, gown), [(edge_wide, F32), (wide, F32)], 4 * unit
        )
        to_send = [(narrow, BF16)] * 2 if tick < sections - 1 else []
        hidden, a, u, *to = run_section(
            forward_kernel,
            plane,
            parity,
            weights,
            (lists, hidden, a_own, u_own, inner, outer, ghalo, gown_t),
            [(wide, BF16), (edge_wide, F32), (wide, F32)] + to_send,
            4 * unit,
        )
        produced = hidden
        if to:
            step = (tick + 1) // 2 - plane
            outer = towards(to[OUTER], OUTER, step)
            if step:
                hidden = send(hidden, lambda z, y, x, c: (z, y, x + 1, c))
            inner = towards(to[INNER], INNER, step)
        saved[parity] = run(
            functools.partial(save_kernel, plane),
            (a, u, produced) + tuple(saved[parity]),
            [(wide, F32), (wide, F32), (edge_wide, F32), (wide, BF16)],
            aliases={3 + k: k for k in range(4)} if saved[parity] else None,
            flops=unit,
        )

    def both_micro(evens, odds):
        [turned] = run(turn_kernel, (evens, odds), [(wide, BF16)])
        [out] = run(
            write_kernel,
            (evens, odds, flip_core(turned)),
            [((1, 2) + wide, BF16)],
            out_space=pl.ANY,
            scratch=[dma((2,))],
        )
        return out

    [upstream] = run(local_kernel, (grad_here, grad_there), [(wide, BF16)])
    inner = outer = None
    finished = {}
    for tick in range(sections - 1, -1, -1):
        plane, parity = tick // 2, tick % 2
        step = (tick - 1) // 2 - plane if tick else 0
        crossing = tick > 0 and step != 0
        halo_in = inner is not None
        finish = halo_in and tick % 2 == 0
        outs = [
            (wide, F32),
            (wide, BF16),
            (edge_wide, BF16),
            (edge_wide, BF16),
            (narrow, BF16),
            (narrow, BF16),
        ] + ([(wide, BF16)] if finish else [])
        c, du, da, es, to_inner, to_outer, *done = run_section(
            functools.partial(backward_kernel, halo_in, finish),
            plane,
            parity,
            weights,
            (lists, upstream)
            + ((inner, outer) if halo_in else ())
            + tuple(saved[parity][:3])
            + (gown, ghalo_t),
            outs,
            4 * unit,
        )
        if done:
            finished[tick + 1] = done[0]
        if tick:
            outer = towards(to_outer, OUTER, step)
            inner = towards(to_inner, INNER, step)
        [upstream] = run_section(
            backward_own_kernel,
            plane,
            parity,
            weights,
            (c, du, da, es, gown_t),
            [(wide, F32 if tick and not crossing else BF16)],
            4 * unit,
        )
        if crossing:
            own = upstream
            upstream = send(own, lambda z, y, x, c: (z, y, x + 1, c))
            own_outer = towards(to_outer, OUTER, 0)
            own_inner = towards(to_inner, INNER, 0)
            even_h, odd_h, _ = lax.optimization_barrier((saved[0][3], saved[1][3], own))
            even_h, odd_h = to_home(even_h), to_home(odd_h)
            upstream, inner, outer, own_outer, own_inner, even_h, odd_h = lax.optimization_barrier(
                (upstream, inner, outer, own_outer, own_inner, even_h, odd_h)
            )
            [finished[tick]] = run(
                functools.partial(add_kernel, plane),
                (lists, own, own_inner, own_outer),
                [(wide, BF16)],
                scratch=[pltpu.VMEM(wide, F32)],
            )
            section_out = both_micro(even_h, odd_h)

    final_outer = send(to_outer, lambda z, y, x, c: (z + 2 * c - 1, 1 - c, x, y))
    final_inner = send(to_inner, lambda z, y, x, c: (z, 1 - c, x, y))
    last_of = [finished[1], finished[3]]
    odds = to_home(jnp.where(plane_here == 0, *last_of))
    evens = to_home(jnp.where(plane_here == 0, upstream, finished[2]))
    [evens] = run(
        functools.partial(add_kernel, 0),
        (home_lists, evens, final_inner, final_outer, evens),
        [(wide, BF16)],
        scratch=[pltpu.VMEM(wide, F32)],
    )
    return section_out, both_micro(evens, odds)


def solution(mesh):
    in_specs = (
        P(None, "dom", None),
        P(None, "dom", None),
        P("pipe", None, None),
        P("pipe", None, None),
        P("pipe", None, None),
        P("pipe", None, None),
        P("pipe", None, None),
        P("pipe", None),
        P("dom", None),
        P("dom", None),
        P("dom"),
        P("dom", None, None),
    )
    out_specs = (P("pipe", None, "dom", None), P("pipe", None, "dom", None))
    return jax.shard_map(shards, mesh=mesh, in_specs=in_specs, out_specs=out_specs, check_vma=False)
```

time: 121 us -> 133 us (1.099)
  Pallas kernels: 15.4 us -> 35.4 us
  other arithmetic: 10.5 us -> 0.15 us
  local copies, waits for them, and re-layouts: 13.4 us -> 21.8 us
  between operations: 6.34 us -> 1.31 us
  waiting for transfers between devices: 33.2 us -> 30.1 us
  starting transfers between devices: 41.4 us -> 42.9 us
    pallas_call x21 -> x32, Pallas kernels: 15.4 us -> 33.2 us  [run(): pl.pallas_call(kernel, out_shape=[jax.ShapeDtypeStruct(s, t) for s, t in...]
    unnamed x64 -> x102, local copies, waits for them, and re-layouts: 9.47 us -> 21.6 us
    select_n x18 -> x3, other arithmetic: 9.37 us -> 0.06 us  [the longest x1 0.03 us: shards(): odds = to_home(jnp.where(plane_here == 0, *last_of))]
    ppermute x32 -> x33, waiting for transfers between devices: 33.2 us -> 30.1 us  [send(): return lax.ppermute(value, AXES, table)]
    squeeze x3 -> x0, local copies, waits for them, and re-layouts: 2.56 us -> none  [the longest x1 1.57 us: shards(): lax.dynamic_slice(inputs, (core, out_block * block, 0), (1, block, latent))]
    pallas_call x0 -> x1, Pallas kernels: none -> 2.25 us  [shards(): pl.pallas_call(boundary_kernel, out_shape=[jax.ShapeDtypeStruct(narrow, B...]
    ppermute x32 -> x33, starting transfers between devices: 41.4 us -> 42.9 us  [send(): return lax.ppermute(value, AXES, table)]
  transfers between devices with their start and end apart: 32 -> 33, of which waited for: 8 -> 11; matrix products, arithmetic and copies ran while one was open for 11% -> 0% of each run, Pallas kernels for 7% -> 13%
where the time goes in v2:
time: 133 us; the launch traced here: 132 us
  starting transfers between devices  42.9 us (32%)
  Pallas kernels  35.4 us (27%)
  waiting for transfers between devices  30.1 us (23%)
  local copies, waits for them, and re-layouts  21.8 us (16%)
    ppermute x33, starting transfers between devices, send(): return lax.ppermute(value, AXES, table)  42.9 us
    pallas_call x32, Pallas kernels, run(): pl.pallas_call(kernel, out_shape=[jax.ShapeDtypeStruct(s, t) for s, t in...  33.2 us
    ppermute x33, waiting for transfers between devices, send(): return lax.ppermute(value, AXES, table)  30.1 us
    unnamed x102, local copies, waits for them, and re-layouts  21.6 us
  transfers between devices with their start and end apart: 33, of which 11 were waited for; matrix products, arithmetic and copies ran while one was open for 0% of the time, Pallas kernels for 13%

profile of v2, /device:TPU:0, one launch (start us, length us, event | category | flops | bytes accessed | tf_op | source)
XLA Modules:
  0.0 131.6 jit_solution(3607093424913880305)
XLA Ops:
  6.7 2.9 %collective-permute-start.5 = (s32[5,128]{1,0:T(8,128)S(1)}, s32[5,128]{1,0:T(8,128)S(1)}, u32[]{:S(2)}, u32[]{:S(2)}) collective-permute-start(s32[5,128]{1,0:T(8,128)S(1)} %pad_add_fusion.packed), channel_id=1, source_target_pairs={{0,4},{1,5},{2,6},{3,7},{4,0},{5,1},{6,2},{7,3},{8,12},{9,13},{10,... | collective-permute-start | bytes 7688 | tf_op jit(solution)/shard_map/ppermute | solution.py:331
  13.2 2.2 %shard_map.138 = bf16[128,512]{1,0:T(8,128)(2,1)} custom-call(s32[2]{0:T(128)} %bitcast.62, bf16[2,256,512]{2,1,0:T(8,128)(2,1)} %inputs.5), custom_call_target="tpu_custom_call" | custom-call | tf_op jit(solution)/shard_map/pallas_call | solution.py:356
  15.5 4.9 %collective-permute-done.7.there = bf16[256,512]{1,0:T(8,128)(2,1)S(1)} collective-permute-done((bf16[256,512]{1,0:T(8,128)(2,1)}, bf16[256,512]{1,0:T(8,128)(2,1)S(1)}, u32[]{:S(2)}, u32[]{:S(2)}) %collective-permute-start.7) | collective-permute-done | bytes 262176 | tf_op jit(solution)/shard_map/ppermute | solution.py:331
  21.1 2.2 %collective-permute-start.8 = (bf16[128,512]{1,0:T(8,128)(2,1)}, bf16[128,512]{1,0:T(8,128)(2,1)S(1)}, u32[]{:S(2)}, u32[]{:S(2)}) collective-permute-start(bf16[128,512]{1,0:T(8,128)(2,1)} %shard_map.138), channel_id=1, source_target_pairs={{0,25},{1,29},{2,27},{3,31},{4,8},{5,12},{6,10},{7,14},{8,1},{9,5}... | collective-permute-start | bytes 393224 | tf_op jit(solution)/shard_map/ppermute | solution.py:331
  26.4 2.0 %shard_map.137 = (f32[256,512]{1,0:T(8,128)S(1)}, f32[256,512]{1,0:T(8,128)S(1)}) custom-call(bf16[512,512]{1,0:T(8,128)(2,1)S(1)} %bitcast.10, bf16[512,512]{1,0:T(8,128)(2,1)S(1)} %bitcast.27, bf16[512,512]{1,0:T(8,128)(2,1)S(1)} %bitcast.44, bf16[512,512]{1,0:T(8,128)(2,1)S(1)} %shard_map.131.refs_3_, f32[1,512]{1,0:T(1,128)S(1)} %copy-done.18, ...), custom_call_target="tpu_custom_call" | custom-call | flops 536870912 | bytes 1048576 | tf_op jit(solution)/shard_map/pallas_call | solution.py:270
  29.0 2.4 %shard_map.139 = (bf16[256,512]{1,0:T(8,128)(2,1)S(1)}, f32[256,512]{1,0:T(8,128)S(1)}, f32[256,512]{1,0:T(8,128)S(1)}, bf16[128,512]{1,0:T(8,128)(2,1)S(1)}, bf16[128,512]{1,0:T(8,128)(2,1)S(1)}) custom-call(bf16[512,512]{1,0:T(8,128)(2,1)S(1)} %bitcast.11, bf16[512,512]{1,0:T(8,128)(2,1)S(1)} %bitcast.28, bf16[512,512]{1,0:T(8,128)(2,1)S(1)} %bitcast.45, ...), custom_call_target="tpu_custom_call" | custom-call | flops 536870912 | bytes 1048576 | tf_op jit(solution)/shard_map/pallas_call | solution.py:270
  32.3 2.0 %shard_map.140 = (f32[256,512]{1,0:T(8,128)S(1)}, f32[256,512]{1,0:T(8,128)S(1)}) custom-call(bf16[512,512]{1,0:T(8,128)(2,1)S(1)} %bitcast.12, bf16[512,512]{1,0:T(8,128)(2,1)S(1)} %bitcast.29, bf16[512,512]{1,0:T(8,128)(2,1)S(1)} %bitcast.46, bf16[512,512]{1,0:T(8,128)(2,1)S(1)} %shard_map.131.refs_3_, f32[1,512]{1,0:T(1,128)S(1)} %copy-done.18, ...), custom_call_target="tpu_custom_call" | custom-call | flops 536870912 | bytes 1048576 | tf_op jit(solution)/shard_map/pallas_call | solution.py:270
  34.3 3.3 %collective-permute-done.10.refs_15_ = bf16[128,512]{1,0:T(8,128)(2,1)S(1)} collective-permute-done((bf16[128,512]{1,0:T(8,128)(2,1)S(1)}, bf16[128,512]{1,0:T(8,128)(2,1)S(1)}, u32[]{:S(2)}, u32[]{:S(2)}) %collective-permute-start.10) | collective-permute-done | bytes 131104 | tf_op jit(solution)/shard_map/ppermute | solution.py:331
  37.6 2.4 %shard_map.141 = (bf16[256,512]{1,0:T(8,128)(2,1)S(1)}, f32[256,512]{1,0:T(8,128)S(1)}, f32[256,512]{1,0:T(8,128)S(1)}, bf16[128,512]{1,0:T(8,128)(2,1)S(1)}, bf16[128,512]{1,0:T(8,128)(2,1)S(1)}) custom-call(bf16[512,512]{1,0:T(8,128)(2,1)S(1)} %bitcast.13, bf16[512,512]{1,0:T(8,128)(2,1)S(1)} %bitcast.30, bf16[512,512]{1,0:T(8,128)(2,1)S(1)} %bitcast.47, ...), custom_call_target="tpu_custom_call" | custom-call | flops 536870912 | bytes 1048576 | tf_op jit(solution)/shard_map/pallas_call | solution.py:270
  43.4 7.3 %collective-permute-done.11.refs_10_.refs_11_ = bf16[256,512]{1,0:T(8,128)(2,1)S(1)} collective-permute-done((bf16[256,512]{1,0:T(8,128)(2,1)S(1)}, bf16[256,512]{1,0:T(8,128)(2,1)S(1)}, u32[]{:S(2)}, u32[]{:S(2)}) %collective-permute-start.11) | collective-permute-done | bytes 262176 | tf_op jit(solution)/shard_map/ppermute | solution.py:331
  53.1 3.1 %collective-permute-start.15 = (bf16[128,512]{1,0:T(8,128)(2,1)S(1)}, bf16[128,512]{1,0:T(8,128)(2,1)S(1)}, u32[]{:S(2)}, u32[]{:S(2)}) collective-permute-start(bf16[128,512]{1,0:T(8,128)(2,1)S(1)} %get-tuple-element.118), channel_id=1, source_target_pairs={{0,25},{1,8},{2,27},{3,10},{4,29},{5,12},{6,31},{7,14},{8,1},{9,16... | collective-permute-start | bytes 393224 | tf_op jit(solution)/shard_map/ppermute | solution.py:331
  58.0 2.5 %collective-permute-done.15.refs_15_ = bf16[128,512]{1,0:T(8,128)(2,1)S(1)} collective-permute-done((bf16[128,512]{1,0:T(8,128)(2,1)S(1)}, bf16[128,512]{1,0:T(8,128)(2,1)S(1)}, u32[]{:S(2)}, u32[]{:S(2)}) %collective-permute-start.15) | collective-permute-done | bytes 131104 | tf_op jit(solution)/shard_map/ppermute | solution.py:331
  62.9 2.0 %collective-permute-start.17 = (bf16[128,512]{1,0:T(8,128)(2,1)S(1)}, bf16[128,512]{1,0:T(8,128)(2,1)S(1)}, u32[]{:S(2)}, u32[]{:S(2)}) collective-permute-start(bf16[128,512]{1,0:T(8,128)(2,1)S(1)} %get-tuple-element.137), channel_id=1, source_target_pairs={{0,25},{1,8},{2,27},{3,10},{4,29},{5,12},{6,31},{7,14},{8,1},{9,16... | collective-permute-start | bytes 393224 | tf_op jit(solution)/shard_map/ppermute | solution.py:331
  67.1 2.4 %collective-permute-done.17.refs_13_ = bf16[128,512]{1,0:T(8,128)(2,1)S(1)} collective-permute-done((bf16[128,512]{1,0:T(8,128)(2,1)S(1)}, bf16[128,512]{1,0:T(8,128)(2,1)S(1)}, u32[]{:S(2)}, u32[]{:S(2)}) %collective-permute-start.17) | collective-permute-done | bytes 131104 | tf_op jit(solution)/shard_map/ppermute | solution.py:331
  72.1 4.2 %collective-permute-start.19 = (bf16[128,512]{1,0:T(8,128)(2,1)S(1)}, bf16[128,512]{1,0:T(8,128)(2,1)S(1)}, u32[]{:S(2)}, u32[]{:S(2)}) collective-permute-start(bf16[128,512]{1,0:T(8,128)(2,1)S(1)} %get-tuple-element.153), channel_id=1, source_target_pairs={{0,3},{1,2},{2,1},{3,0},{4,7},{5,6},{6,5},{7,4},{8,11},{9,10},{10,... | collective-permute-start | bytes 393224 | tf_op jit(solution)/shard_map/ppermute | solution.py:331
  76.3 2.7 %collective-permute-start.20 = (bf16[128,512]{1,0:T(8,128)(2,1)S(1)}, bf16[128,512]{1,0:T(8,128)(2,1)S(1)}, u32[]{:S(2)}, u32[]{:S(2)}) collective-permute-start(bf16[128,512]{1,0:T(8,128)(2,1)S(1)} %get-tuple-element.154), channel_id=1, source_target_pairs={{0,27},{1,10},{2,25},{3,8},{4,31},{5,14},{6,29},{7,12},{8,3},{9,18... | collective-permute-start | bytes 393224 | tf_op jit(solution)/shard_map/ppermute | solution.py:331
  81.3 6.1 %collective-permute-start.21 = (bf16[128,512]{1,0:T(8,128)(2,1)S(1)}, bf16[128,512]{1,0:T(8,128)(2,1)S(1)}, u32[]{:S(2)}, u32[]{:S(2)}) collective-permute-start(bf16[128,512]{1,0:T(8,128)(2,1)S(1)} %get-tuple-element.154), channel_id=1, source_target_pairs={{0,25},{1,8},{2,27},{3,10},{4,29},{5,12},{6,31},{7,14},{8,1},{9,16... | collective-permute-start | bytes 393224 | tf_op jit(solution)/shard_map/ppermute | solution.py:331
  87.4 2.8 %collective-permute-done.21.outer = bf16[128,512]{1,0:T(8,128)(2,1)S(1)} collective-permute-done((bf16[128,512]{1,0:T(8,128)(2,1)S(1)}, bf16[128,512]{1,0:T(8,128)(2,1)S(1)}, u32[]{:S(2)}, u32[]{:S(2)}) %collective-permute-start.21) | collective-permute-done | bytes 131104 | tf_op jit(solution)/shard_map/ppermute | solution.py:331
  92.8 3.1 %shard_map.156 = (f32[256,512]{1,0:T(8,128)S(1)}, bf16[256,512]{1,0:T(8,128)(2,1)S(1)}, bf16[256,512]{1,0:T(8,128)(2,1)S(1)}, bf16[256,512]{1,0:T(8,128)(2,1)S(1...) custom-call(bf16[512,512]{1,0:T(8,128)(2,1)S(1)} %bitcast.22, bf16[512,512]{1,0:T(8,128)(2,1)S(1)} %bitcast.39, ...), custom_call_target="tpu_custom_call" | custom-call | flops 536870912 | bytes 1048576 | tf_op jit(solution)/shard_map/pallas_call | solution.py:270
  99.6 2.6 %collective-permute-start.27 = (bf16[128,512]{1,0:T(8,128)(2,1)}, bf16[128,512]{1,0:T(8,128)(2,1)}, u32[]{:S(2)}, u32[]{:S(2)}) collective-permute-start(bf16[128,512]{1,0:T(8,128)(2,1)} %get-tuple-element.169), channel_id=1, source_target_pairs={{0,25},{1,8},{2,27},{3,10},{4,29},{5,12},{6,31},{7,14},{8,1},{9,16... | collective-permute-start | bytes 393224 | tf_op jit(solution)/shard_map/ppermute | solution.py:331
  108.0 1.9 %shard_map.157.refs_11_ = f32[256,512]{1,0:T(8,128)S(1)} custom-call(bf16[512,512]{1,0:T(8,128)(2,1)S(1)} %bitcast.23, bf16[512,512]{1,0:T(8,128)(2,1)S(1)} %bitcast.40, bf16[512,512]{1,0:T(8,128)(2,1)S(1)} %bitcast.57, bf16[512,512]{1,0:T(8,128)(2,1)S(1)} %shard_map.131.refs_3_, f32[1,512]{1,0:T(1,128)S(1)} %copy-done.18, ...), custom_call_target="tpu_custom_call" | custom-call | flops 536870912 | bytes 1048576 | tf_op jit(solution)/shard_map/pallas_call | solution.py:270
  110.0 2.7 %shard_map.158 = (f32[256,512]{1,0:T(8,128)S(1)}, bf16[256,512]{1,0:T(8,128)(2,1)S(1)}, bf16[256,512]{1,0:T(8,128)(2,1)S(1)}, bf16[256,512]{1,0:T(8,128)(2,1)S(1...) custom-call(bf16[512,512]{1,0:T(8,128)(2,1)S(1)} %bitcast.24, ...), custom_call_target="tpu_custom_call" | custom-call | flops 536870912 | bytes 1048576 | tf_op jit(solution)/shard_map/pallas_call | solution.py:270
  117.8 3.9 %collective-permute-start.29 = (bf16[128,512]{1,0:T(8,128)(2,1)S(1)}, bf16[128,512]{1,0:T(8,128)(2,1)S(1)}, u32[]{:S(2)}, u32[]{:S(2)}) collective-permute-start(bf16[128,512]{1,0:T(8,128)(2,1)S(1)} %copy-done.45), channel_id=1, source_target_pairs={{0,4},{1,0},{2,6},{3,2},{4,5},{5,1},{6,7},{7,3},{8,12},{9,8},{10,1... | collective-permute-start | bytes 393224 | tf_op jit(solution)/shard_map/ppermute | solution.py:331
  124.6 4.1 %collective-permute-done.30.outer = bf16[128,512]{1,0:T(8,128)(2,1)S(1)} collective-permute-done((bf16[128,512]{1,0:T(8,128)(2,1)S(1)}, bf16[128,512]{1,0:T(8,128)(2,1)S(1)}, u32[]{:S(2)}, u32[]{:S(2)}) %collective-permute-start.30) | collective-permute-done | bytes 131104 | tf_op jit(solution)/shard_map/ppermute | solution.py:331
  (185 shorter events, 54.7 us)
Async XLA Ops:
  3.2 23.2 %collective-permute-start.3 = (bf16[512,512]{1,0:T(8,128)(2,1)S(1)}, bf16[512,512]{1,0:T(8,128)(2,1)S(1)}, u32[]{:S(2)}, u32[]{:S(2)}) collective-permute-start(bf16[512,512]{1,0:T(8,128)(2,1)S(1)} %shard_map.131.refs_3_), channel_id=1, source_target_pairs={{0,1},{1,0},{2,3},{3,2},{4,5},{5,4},{6,7},{7,6},{8,9},{9,8},{10,11... | collective-permute-start | bytes 1572872 | tf_op jit(solution)/shard_map/ppermute | solution.py:331
  3.8 22.6 %collective-permute-start = (bf16[512,512]{1,0:T(8,128)(2,1)S(1)}, bf16[512,512]{1,0:T(8,128)(2,1)S(1)}, u32[]{:S(2)}, u32[]{:S(2)}) collective-permute-start(bf16[512,512]{1,0:T(8,128)(2,1)S(1)} %bitcast.9), channel_id=1, source_target_pairs={{0,1},{1,0},{2,3},{3,2},{4,5},{5,4},{6,7},{7,6},{8,9},{9,8},{10,11... | collective-permute-start | bytes 1572872 | tf_op jit(solution)/shard_map/ppermute | solution.py:331
  4.2 22.2 %collective-permute-start.1 = (bf16[512,512]{1,0:T(8,128)(2,1)S(1)}, bf16[512,512]{1,0:T(8,128)(2,1)}, u32[]{:S(2)}, u32[]{:S(2)}) collective-permute-start(bf16[512,512]{1,0:T(8,128)(2,1)S(1)} %bitcast.26), channel_id=1, source_target_pairs={{0,1},{1,0},{2,3},{3,2},{4,5},{5,4},{6,7},{7,6},{8,9},{9,8},{10,11... | collective-permute-start | bytes 1572872 | tf_op jit(solution)/shard_map/ppermute | solution.py:331
  4.4 22.0 %collective-permute-start.2 = (bf16[512,512]{1,0:T(8,128)(2,1)S(1)}, bf16[512,512]{1,0:T(8,128)(2,1)}, u32[]{:S(2)}, u32[]{:S(2)}) collective-permute-start(bf16[512,512]{1,0:T(8,128)(2,1)S(1)} %bitcast.43), channel_id=1, source_target_pairs={{0,1},{1,0},{2,3},{3,2},{4,5},{5,4},{6,7},{7,6},{8,9},{9,8},{10,11... | collective-permute-start | bytes 1572872 | tf_op jit(solution)/shard_map/ppermute | solution.py:331
  12.1 8.3 %collective-permute-start.7 = (bf16[256,512]{1,0:T(8,128)(2,1)}, bf16[256,512]{1,0:T(8,128)(2,1)S(1)}, u32[]{:S(2)}, u32[]{:S(2)}) collective-permute-start(bf16[256,512]{1,0:T(8,128)(2,1)} %get-tuple-element.96), channel_id=1, source_target_pairs={{0,4},{1,5},{2,6},{3,7},{4,0},{5,1},{6,2},{7,3},{8,12},{9,13},{10,... | collective-permute-start | bytes 786440 | tf_op jit(solution)/shard_map/ppermute | solution.py:331
  21.1 7.9 %collective-permute-start.8 = (bf16[128,512]{1,0:T(8,128)(2,1)}, bf16[128,512]{1,0:T(8,128)(2,1)S(1)}, u32[]{:S(2)}, u32[]{:S(2)}) collective-permute-start(bf16[128,512]{1,0:T(8,128)(2,1)} %shard_map.138), channel_id=1, source_target_pairs={{0,25},{1,29},{2,27},{3,31},{4,8},{5,12},{6,10},{7,14},{8,1},{9,5}... | collective-permute-start | bytes 393224 | tf_op jit(solution)/shard_map/ppermute | solution.py:331
  40.1 10.7 %collective-permute-start.11 = (bf16[256,512]{1,0:T(8,128)(2,1)S(1)}, bf16[256,512]{1,0:T(8,128)(2,1)S(1)}, u32[]{:S(2)}, u32[]{:S(2)}) collective-permute-start(bf16[256,512]{1,0:T(8,128)(2,1)S(1)} %get-tuple-element.109.h), channel_id=1, source_target_pairs={{0,2},{1,3},{2,0},{3,1},{4,6},{5,7},{6,4},{7,5},{8,10},{9,11},{10,... | collective-permute-start | bytes 786440 | tf_op jit(solution)/shard_map/ppermute | solution.py:331
  40.2 16.0 %collective-permute-start.6 = (bf16[256,512]{1,0:T(8,128)(2,1)S(1)}, bf16[256,512]{1,0:T(8,128)(2,1)S(1)}, u32[]{:S(2)}, u32[]{:S(2)}) collective-permute-start(bf16[256,512]{1,0:T(8,128)(2,1)S(1)} %get-tuple-element.93), channel_id=1, source_target_pairs={{0,4},{1,5},{2,6},{3,7},{4,0},{5,1},{6,2},{7,3},{8,12},{9,13},{10,... | collective-permute-start | bytes 786440 | tf_op jit(solution)/shard_map/ppermute | solution.py:331
  41.5 10.4 %collective-permute-start.12 = (bf16[128,512]{1,0:T(8,128)(2,1)S(1)}, bf16[128,512]{1,0:T(8,128)(2,1)S(1)}, u32[]{:S(2)}, u32[]{:S(2)}) collective-permute-start(bf16[128,512]{1,0:T(8,128)(2,1)S(1)} %get-tuple-element.112), channel_id=1, source_target_pairs={{0,3},{1,2},{2,1},{3,0},{4,7},{5,6},{6,5},{7,4},{8,11},{9,10},{10,... | collective-permute-start | bytes 393224 | tf_op jit(solution)/shard_map/ppermute | solution.py:331
  41.5 10.4 %collective-permute-start.13 = (bf16[128,512]{1,0:T(8,128)(2,1)S(1)}, bf16[128,512]{1,0:T(8,128)(2,1)S(1)}, u32[]{:S(2)}, u32[]{:S(2)}) collective-permute-start(bf16[128,512]{1,0:T(8,128)(2,1)S(1)} %get-tuple-element.113), channel_id=1, source_target_pairs={{0,27},{1,10},{2,25},{3,8},{4,31},{5,14},{6,29},{7,12},{8,3},{9,18... | collective-permute-start | bytes 393224 | tf_op jit(solution)/shard_map/ppermute | solution.py:331
  53.1 7.3 %collective-permute-start.15 = (bf16[128,512]{1,0:T(8,128)(2,1)S(1)}, bf16[128,512]{1,0:T(8,128)(2,1)S(1)}, u32[]{:S(2)}, u32[]{:S(2)}) collective-permute-start(bf16[128,512]{1,0:T(8,128)(2,1)S(1)} %get-tuple-element.118), channel_id=1, source_target_pairs={{0,25},{1,8},{2,27},{3,10},{4,29},{5,12},{6,31},{7,14},{8,1},{9,16... | collective-permute-start | bytes 393224 | tf_op jit(solution)/shard_map/ppermute | solution.py:331
  62.9 6.7 %collective-permute-start.17 = (bf16[128,512]{1,0:T(8,128)(2,1)S(1)}, bf16[128,512]{1,0:T(8,128)(2,1)S(1)}, u32[]{:S(2)}, u32[]{:S(2)}) collective-permute-start(bf16[128,512]{1,0:T(8,128)(2,1)S(1)} %get-tuple-element.137), channel_id=1, source_target_pairs={{0,25},{1,8},{2,27},{3,10},{4,29},{5,12},{6,31},{7,14},{8,1},{9,16... | collective-permute-start | bytes 393224 | tf_op jit(solution)/shard_map/ppermute | solution.py:331
  72.1 9.2 %collective-permute-start.19 = (bf16[128,512]{1,0:T(8,128)(2,1)S(1)}, bf16[128,512]{1,0:T(8,128)(2,1)S(1)}, u32[]{:S(2)}, u32[]{:S(2)}) collective-permute-start(bf16[128,512]{1,0:T(8,128)(2,1)S(1)} %get-tuple-element.153), channel_id=1, source_target_pairs={{0,3},{1,2},{2,1},{3,0},{4,7},{5,6},{6,5},{7,4},{8,11},{9,10},{10,... | collective-permute-start | bytes 393224 | tf_op jit(solution)/shard_map/ppermute | solution.py:331
  76.3 11.1 %collective-permute-start.20 = (bf16[128,512]{1,0:T(8,128)(2,1)S(1)}, bf16[128,512]{1,0:T(8,128)(2,1)S(1)}, u32[]{:S(2)}, u32[]{:S(2)}) collective-permute-start(bf16[128,512]{1,0:T(8,128)(2,1)S(1)} %get-tuple-element.154), channel_id=1, source_target_pairs={{0,27},{1,10},{2,25},{3,8},{4,31},{5,14},{6,29},{7,12},{8,3},{9,18... | collective-permute-start | bytes 393224 | tf_op jit(solution)/shard_map/ppermute | solution.py:331
  78.9 12.5 %collective-permute-start.23 = (bf16[256,512]{1,0:T(8,128)(2,1)S(1)}, bf16[256,512]{1,0:T(8,128)(2,1)S(1)}, u32[]{:S(2)}, u32[]{:S(2)}) collective-permute-start(bf16[256,512]{1,0:T(8,128)(2,1)S(1)} %get-tuple-element.157), channel_id=1, source_target_pairs={{0,0},{1,4},{2,2},{3,6},{4,1},{5,5},{6,3},{7,7},{8,8},{9,12},{10,1... | collective-permute-start | bytes 786440 | tf_op jit(solution)/shard_map/ppermute | solution.py:331
  79.6 12.5 %collective-permute-start.24 = (bf16[256,512]{1,0:T(8,128)(2,1)S(1)}, bf16[256,512]{1,0:T(8,128)(2,1)S(1)}, u32[]{:S(2)}, u32[]{:S(2)}) collective-permute-start(bf16[256,512]{1,0:T(8,128)(2,1)S(1)} %get-tuple-element.158), channel_id=1, source_target_pairs={{0,0},{1,4},{2,2},{3,6},{4,1},{5,5},{6,3},{7,7},{8,8},{9,12},{10,1... | collective-permute-start | bytes 786440 | tf_op jit(solution)/shard_map/ppermute | solution.py:331
  80.3 12.6 %collective-permute-start.18 = (bf16[256,512]{1,0:T(8,128)(2,1)S(1)}, bf16[256,512]{1,0:T(8,128)(2,1)S(1)}, u32[]{:S(2)}, u32[]{:S(2)}) collective-permute-start(bf16[256,512]{1,0:T(8,128)(2,1)S(1)} %shard_map.153.value), channel_id=1, source_target_pairs={{0,2},{1,3},{2,0},{3,1},{4,6},{5,7},{6,4},{7,5},{8,10},{9,11},{10,... | collective-permute-start | bytes 786440 | tf_op jit(solution)/shard_map/ppermute | solution.py:331
  81.3 8.9 %collective-permute-start.21 = (bf16[128,512]{1,0:T(8,128)(2,1)S(1)}, bf16[128,512]{1,0:T(8,128)(2,1)S(1)}, u32[]{:S(2)}, u32[]{:S(2)}) collective-permute-start(bf16[128,512]{1,0:T(8,128)(2,1)S(1)} %get-tuple-element.154), channel_id=1, source_target_pairs={{0,25},{1,8},{2,27},{3,10},{4,29},{5,12},{6,31},{7,14},{8,1},{9,16... | collective-permute-start | bytes 393224 | tf_op jit(solution)/shard_map/ppermute | solution.py:331
  98.8 11.1 %collective-permute-start.26 = (bf16[128,512]{1,0:T(8,128)(2,1)}, bf16[128,512]{1,0:T(8,128)(2,1)}, u32[]{:S(2)}, u32[]{:S(2)}) collective-permute-start(bf16[128,512]{1,0:T(8,128)(2,1)} %get-tuple-element.168), channel_id=1, source_target_pairs={{0,1},{1,0},{2,3},{3,2},{4,5},{5,4},{6,7},{7,6},{8,9},{9,8},{10,11... | collective-permute-start | bytes 393224 | tf_op jit(solution)/shard_map/ppermute | solution.py:331
  99.6 10.4 %collective-permute-start.27 = (bf16[128,512]{1,0:T(8,128)(2,1)}, bf16[128,512]{1,0:T(8,128)(2,1)}, u32[]{:S(2)}, u32[]{:S(2)}) collective-permute-start(bf16[128,512]{1,0:T(8,128)(2,1)} %get-tuple-element.169), channel_id=1, source_target_pairs={{0,25},{1,8},{2,27},{3,10},{4,29},{5,12},{6,31},{7,14},{8,1},{9,16... | collective-permute-start | bytes 393224 | tf_op jit(solution)/shard_map/ppermute | solution.py:331
  115.3 13.4 %collective-permute-start.28 = (bf16[256,512]{1,0:T(8,128)(2,1)S(1)}, bf16[256,512]{1,0:T(8,128)(2,1)S(1)}, u32[]{:S(2)}, u32[]{:S(2)}) collective-permute-start(bf16[256,512]{1,0:T(8,128)(2,1)S(1)} %broadcast_select_fusion.1), channel_id=1, source_target_pairs={{0,0},{1,4},{2,2},{3,6},{4,1},{5,5},{6,3},{7,7},{8,8},{9,12},{10,1... | collective-permute-start | bytes 786440 | tf_op jit(solution)/shard_map/ppermute | solution.py:331
  116.2 12.8 %collective-permute-start.31 = (bf16[256,512]{1,0:T(8,128)(2,1)S(1)}, bf16[256,512]{1,0:T(8,128)(2,1)S(1)}, u32[]{:S(2)}, u32[]{:S(2)}) collective-permute-start(bf16[256,512]{1,0:T(8,128)(2,1)S(1)} %broadcast_select_fusion), channel_id=1, source_target_pairs={{0,0},{1,4},{2,2},{3,6},{4,1},{5,5},{6,3},{7,7},{8,8},{9,12},{10,1... | collective-permute-start | bytes 786440 | tf_op jit(solution)/shard_map/ppermute | solution.py:331
  117.8 6.8 %collective-permute-start.29 = (bf16[128,512]{1,0:T(8,128)(2,1)S(1)}, bf16[128,512]{1,0:T(8,128)(2,1)S(1)}, u32[]{:S(2)}, u32[]{:S(2)}) collective-permute-start(bf16[128,512]{1,0:T(8,128)(2,1)S(1)} %copy-done.45), channel_id=1, source_target_pairs={{0,4},{1,0},{2,6},{3,2},{4,5},{5,1},{6,7},{7,3},{8,12},{9,8},{10,1... | collective-permute-start | bytes 393224 | tf_op jit(solution)/shard_map/ppermute | solution.py:331
  121.7 7.0 %collective-permute-start.30 = (bf16[128,512]{1,0:T(8,128)(2,1)S(1)}, bf16[128,512]{1,0:T(8,128)(2,1)S(1)}, u32[]{:S(2)}, u32[]{:S(2)}) collective-permute-start(bf16[128,512]{1,0:T(8,128)(2,1)S(1)} %copy-done.43), channel_id=1, source_target_pairs={{0,28},{1,8},{2,30},{3,10},{4,29},{5,9},{6,31},{7,11},{8,4},{9,16}... | collective-permute-start | bytes 393224 | tf_op jit(solution)/shard_map/ppermute | solution.py:331
  (60 other events, 190.5 us)

commit v3 on v2

v3 whole, which is shorter than its diff:
```python
import functools

import jax
import jax.numpy as jnp
from jax import lax
from jax.experimental import pallas as pl
from jax.experimental.pallas import tpu as pltpu
from jax.sharding import PartitionSpec as P

EPSILON = 1e-05
F32 = jnp.float32
BF16 = jnp.bfloat16
AXES = ("dom", "pipe")
INNER, OUTER = 0, 1
BESIDE = 4 * 10**9


def mul(a, b):
    return jnp.dot(a, b, preferred_element_type=F32)


def mul_t(a, b):
    return lax.dot_general(a, b, (((1,), (1,)), ((), ())), preferred_element_type=F32)


def slope(v):
    s = jax.nn.sigmoid(v)
    return s * (1.0 + v * (1.0 - s))


def normalize(z):
    centred = z - jnp.mean(z, axis=-1, keepdims=True)
    inverse = lax.rsqrt(jnp.mean(centred * centred, axis=-1, keepdims=True) + EPSILON)
    return centred * inverse, inverse


def thirds(packed):
    depth = packed.shape[0] // 3
    return [packed.at[pl.ds(number * depth, depth), :] for number in range(3)]


def here_is(plane=None, parity=None):
    pipe = lax.axis_index("pipe")
    wanted = jnp.bool_(True)
    if plane is not None:
        wanted = pipe // 2 == plane
    if parity is not None:
        wanted = wanted & (pipe % 2 == parity)
    return wanted


def is_local():
    return lax.axis_index("pipe") % 2 == lax.axis_index("dom") % 2


def listed(at, value, block):
    picked = value[:block]
    for number in range(1, value.shape[0] // block):
        picked = jnp.where(at == number, value[number * block : (number + 1) * block], picked)
    return picked


def add_listed(at, target, value, block):
    for number in range(target.shape[0] // block):
        rows = slice(number * block, (number + 1) * block)
        target[rows, :] = target[rows, :] + jnp.where(at == number, value, 0.0)


def prepare_kernel(count, halo, inputs, cotangent, send_in, recv_in, here, there, boundary, packed, sems):
    micro = lax.axis_index("dom") % 2
    block = boundary.shape[0]
    edge_blocks = send_in.shape[0]
    number = jnp.where(micro == 1, halo[0, 0, 0], halo[0, 1, 0])
    start = pl.multiple_of(number * block, block)
    edge_copies = [
        pltpu.make_async_copy(ref, packed.at[place, pl.ds(0, edge_blocks), :], sems.at[3 + place])
        for place, ref in enumerate((send_in, recv_in))
    ]
    for copy in edge_copies:
        copy.start()
    lane = lax.broadcasted_iota(jnp.int32, packed.shape[1:], 1)
    tail = jnp.where(lane == 0, halo[0, 0, 0], halo[0, 1, 0])
    for place in range(edge_blocks):
        tail = jnp.where(lane == 2 + place, count[place], tail)
    packed[2] = tail

    def fetch(source):
        copies = [
            pltpu.make_async_copy(source.at[1 - micro], there, sems.at[0]),
            pltpu.make_async_copy(
                source.at[lax.axis_index("pipe") % 2, pl.ds(start, block), :], boundary, sems.at[1]
            ),
            pltpu.make_async_copy(source.at[micro], here, sems.at[2]),
        ]
        for copy in copies:
            copy.start()
        for copy in copies:
            copy.wait()

    @pl.when(here_is(0))
    def _():
        fetch(inputs)

    @pl.when(jnp.logical_not(here_is(0)))
    def _():
        fetch(cotangent)

    for copy in edge_copies:
        copy.wait()


def fold_kernel(a, b, _, out):
    out[...] = mul(a[...], b[...]).astype(BF16)


def arrange_kernel(*refs):
    *given, even, odd = refs
    count = len(given) // 2
    mine, swapped = given[:count], given[count:]
    depth = mine[0].shape[0]

    def fill(out, sources):
        for number, source in enumerate(sources):
            out[number * depth : (number + 1) * depth, :] = source[...]

    @pl.when(here_is(parity=0))
    def _():
        fill(even, mine)
        fill(odd, swapped)

    @pl.when(here_is(parity=1))
    def _():
        fill(even, swapped)
        fill(odd, mine)


def graph_kernel(edge_blocks, packed, packed_there, gown, gown_t, ghalo, ghalo_t, lists, mate, home_lists):
    block = packed.shape[2]
    rows = gown_t.shape[0]
    edges = edge_blocks * block
    local = is_local()
    first_core = lax.axis_index("pipe") % 2 == 0
    mine = [jnp.where(local, packed[k], packed_there[k]) for k in range(3)]
    tails = mine[2], jnp.where(local, packed_there[2], packed[2])
    lane = lax.broadcasted_iota(jnp.int32, (1, block), 1)
    row = lax.broadcasted_iota(jnp.int32, (rows, block), 0)
    halo_row = lax.broadcasted_iota(jnp.int32, (2 * block, block), 0)
    for number in range(edge_blocks):
        live = lane < tails[0][:1, 2 + number : 3 + number]
        sender = jnp.where(live, mine[0][number : number + 1], -1)
        receiver = jnp.where(live, mine[1][number : number + 1], -1)
        outside = sender - rows
        turned = jnp.where(outside < block, outside + block, outside - block)
        outside = jnp.where(outside >= 0, jnp.where(first_core, turned, outside), -1)
        here = slice(number * block, (number + 1) * block)
        received = slice(edges + number * block, edges + (number + 1) * block)
        for index, at, table, table_t in (
            (sender, here, gown, gown_t),
            (receiver, received, gown, gown_t),
            (outside, here, ghalo, ghalo_t),
        ):
            hot = (index == (halo_row if table is ghalo else row)).astype(F32)
            table_t[:, at] = hot.astype(BF16)
            table[at, :] = hot.T.astype(BF16)

    def whole(tail, place):
        return jnp.broadcast_to(tail[:1, place : place + 1], (1, block))

    to_next, to_prev = whole(tails[0], 0), whole(tails[0], 1)
    lists[0:1, :] = jnp.where(first_core, to_next, to_prev)
    lists[1:2, :] = jnp.where(first_core, to_prev, to_next)
    mate[...] = jnp.where(first_core, whole(tails[1], 1), whole(tails[1], 0))
    to_next, to_prev = whole(packed[2], 0), whole(packed[2], 1)
    home_first = lax.axis_index("dom") % 2 == 0
    home_lists[0:1, :] = jnp.where(home_first, to_next, to_prev)
    home_lists[1:2, :] = jnp.where(home_first, to_prev, to_next)


def entry_kernel(mate, here, there, hidden, inner):
    block = inner.shape[0]

    @pl.when(is_local())
    def _():
        hidden[...] = here[...]
        inner[...] = listed(mate[:, :1], there[...], block)

    @pl.when(jnp.logical_not(is_local()))
    def _():
        hidden[...] = there[...]
        inner[...] = listed(mate[:, :1], here[...], block)


def forward_own_kernel(take, h, gown, a_out, u_out):
    w_send, w_recv, w_node = thirds(take[0])
    edges = gown.shape[0] // 2
    own = mul(gown[...], h[...]).astype(BF16)
    a_out[...] = mul(own[:edges], w_send[...]) + mul(own[edges:], w_recv[...])
    u_out[...] = mul(h[...], w_node[...])


def forward_kernel(take, lists, h, a_own, u_own, inner, outer, ghalo, gown_t, h_out, a_out, u_out, *to):
    packed, w_fold, gain = take
    w_send = thirds(packed)[0]
    edges = ghalo.shape[0]
    block = inner.shape[0]
    halo = (mul(ghalo[:, :block], inner[...]) + mul(ghalo[:, block:], outer[...])).astype(BF16)
    a = a_own[...] + mul(halo, w_send[...])
    a_out[...] = a
    q = (a * jax.nn.sigmoid(a)).astype(BF16)
    u = u_own[...] + mul(mul(gown_t[:, edges:], q).astype(BF16), w_fold[...])
    u_out[...] = u
    t, _ = normalize(u * jax.nn.sigmoid(u))
    out = (h[...].astype(F32) + t * gain[...]).astype(BF16)
    h_out[...] = out
    for side, ref in enumerate(to):
        ref[...] = listed(lists[side : side + 1, :1], out, block)


def save_kernel(plane, parity, a, u, h, *refs):
    t_out, r_out, s_out, h_out = refs[-4:]
    rows, edges = h.shape[0], a.shape[0]
    at = slice(parity * rows, (parity + 1) * rows)

    @pl.when(here_is(plane))
    def _():
        s_out[parity * edges : (parity + 1) * edges, :] = slope(a[...]).astype(BF16)
        u_value = u[...]
        t, inverse = normalize(u_value * jax.nn.sigmoid(u_value))
        t_out[at, :] = t.astype(BF16)
        r_out[at, :] = (inverse * slope(u_value)).astype(BF16)
        h_out[at, :] = h[...]


def pick_kernel(first, second, out):
    @pl.when(here_is(0))
    def _():
        out[...] = first[...]

    @pl.when(jnp.logical_not(here_is(0)))
    def _():
        out[...] = second[...]


def backward_kernel(halo_in, parity, take, lists, upstream, *refs):
    packed, w_fold, gain = take
    w_send = thirds(packed)[0]
    if halo_in:
        inner, outer, *refs = refs
    t_in, r_in, s_in, gown, ghalo_t, c_out, du_out, da_out, es_out, to_inner, to_outer, *rest = refs
    edges = gown.shape[0] // 2
    rows = upstream.shape[0]
    block = to_inner.shape[0]
    at = slice(parity * rows, (parity + 1) * rows)
    at_edges = slice(parity * edges, (parity + 1) * edges)
    c_out[...] = upstream[...].astype(F32)
    if halo_in:
        add_listed(lists[INNER : INNER + 1, :1], c_out, inner[...].astype(F32), block)
        add_listed(lists[OUTER : OUTER + 1, :1], c_out, outer[...].astype(F32), block)
    if rest:
        rest[0][...] = c_out[...].astype(BF16)
    g = c_out[...] * gain[...]
    t = t_in[at, :].astype(F32)
    centre = jnp.mean(g, axis=-1, keepdims=True)
    along = jnp.mean(g * t, axis=-1, keepdims=True)
    du = ((g - centre - t * along) * r_in[at, :].astype(F32)).astype(BF16)
    du_out[...] = du
    spread = mul(gown[edges:, :], du).astype(BF16)
    da = (mul_t(spread, w_fold[...]) * s_in[at_edges, :].astype(F32)).astype(BF16)
    da_out[...] = da
    es = mul_t(da, w_send[...]).astype(BF16)
    es_out[...] = es
    halo = mul(ghalo_t[...], es).astype(BF16)
    to_inner[...] = halo[:block]
    to_outer[...] = halo[block:]


def backward_own_kernel(take, c, du, da, es, gown_t, *refs):
    _, w_recv, w_node = thirds(take[0])
    out = refs[-1]
    er = mul_t(da[...], w_recv[...]).astype(BF16)
    both = jnp.concatenate([es[...], er], axis=0)
    total = c[...] + mul_t(du[...], w_node[...]) + mul(gown_t[...], both)
    out[...] = total.astype(out.dtype)


def add_kernel(plane, lists, value, inner, outer, *refs):
    *other, out, total = refs
    block = inner.shape[0]

    @pl.when(here_is(plane))
    def _():
        total[...] = value[...].astype(F32)
        add_listed(lists[INNER : INNER + 1, :1], total, inner[...].astype(F32), block)
        add_listed(lists[OUTER : OUTER + 1, :1], total, outer[...].astype(F32), block)
        out[...] = total[...].astype(BF16)

    if other:

        @pl.when(jnp.logical_not(here_is(plane)))
        def _():
            out[...] = other[0][...]


def turn_kernel(evens, odds, out):
    @pl.when(here_is(parity=1))
    def _():
        out[...] = evens[...]

    @pl.when(here_is(parity=0))
    def _():
        out[...] = odds[...]


def write_kernel(evens, odds, arrived, out, sems):
    core = lax.axis_index("pipe") % 2
    other = pltpu.make_async_copy(arrived, out.at[0, 1 - core], sems.at[1])
    other.start()

    @pl.when(core == 0)
    def _():
        own = pltpu.make_async_copy(evens, out.at[0, 0], sems.at[0])
        own.start()
        own.wait()

    @pl.when(core == 1)
    def _():
        own = pltpu.make_async_copy(odds, out.at[0, 1], sems.at[0])
        own.start()
        own.wait()

    other.wait()


def run(kernel, operands, outs, spaces=(), aliases=None, out_space=pltpu.VMEM, scratch=(), cost=1, vmem=12):
    spaces = tuple(spaces) + (pltpu.VMEM,) * (len(operands) - len(spaces))
    return pl.pallas_call(
        kernel,
        out_shape=[jax.ShapeDtypeStruct(s, t) for s, t in outs],
        in_specs=[pl.BlockSpec(memory_space=space) for space in spaces],
        out_specs=[pl.BlockSpec(memory_space=out_space)] * len(outs),
        scratch_shapes=list(scratch),
        input_output_aliases=aliases or {},
        compiler_params=pltpu.CompilerParams(vmem_limit_bytes=vmem * 2**20),
        cost_estimate=pl.CostEstimate(flops=cost, bytes_accessed=1, transcendentals=0),
    )(*operands)


def run_section(body, plane, matrices, operands, outs, elsewhere=None, cost=1):
    def kernel(*refs):
        take, rest = refs[: len(matrices)], refs[len(matrices) :]

        @pl.when(here_is(plane))
        def _():
            body(take, *rest)

        if elsewhere is not None:

            @pl.when(jnp.logical_not(here_is(plane)))
            def _():
                rest[-1][...] = rest[elsewhere][...]

    return run(kernel, tuple(matrices) + tuple(operands), outs, cost=cost)


def shards(
    inputs,
    cotangent,
    w_send,
    w_recv,
    w_message,
    w_node,
    w_aggregate,
    gains,
    edge_send,
    edge_recv,
    edge_count,
    halo_send,
):
    sections = lax.axis_size("pipe")
    pairs_total = lax.axis_size("dom") // 2
    phase = lax.axis_index("pipe")
    y = lax.rem(lax.axis_index("dom"), 2)
    plane_here = phase // 2
    rows, latent = inputs.shape[1:]
    edge_blocks, block = edge_send.shape
    edges = edge_blocks * block

    def send(value, rule):
        table = []
        for z in range(pairs_total):
            for which in range(2):
                for x in range(sections // 2):
                    for c in range(2):
                        if (target := rule(z, which, x, c)) is None:
                            continue
                        tz, ty, tx, tc = target
                        target = (2 * (tz % pairs_total) + ty) * sections + 2 * (tx % (sections // 2)) + tc
                        table.append(((2 * z + which) * sections + 2 * x + c, target))
        return lax.ppermute(value, AXES, table)

    def flip_y(value):
        return send(value, lambda z, y, x, c: (z, 1 - y, x, c))

    def flip_core(value):
        return send(value, lambda z, y, x, c: (z, y, x, 1 - c))

    def to_home(value):
        return send(value, lambda z, y, x, c: (z, c, x, y))

    def towards(value, side, step):
        if side == INNER:
            return send(value, lambda z, y, x, c: (z, y, x + step, 1 - c))
        return send(value, lambda z, y, x, c: (z + 2 * c - 1, y, x + step, 1 - c))

    wide = (rows, latent)
    edge_wide = (edges, latent)
    narrow = (block, latent)
    unit = 2 * rows * latent * latent
    dma = pltpu.SemaphoreType.DMA

    here, there, boundary, packed = run(
        prepare_kernel,
        (edge_count, halo_send, inputs, cotangent, edge_send, edge_recv),
        [(wide, BF16), (wide, BF16), (narrow, BF16), ((3, 8, block), jnp.int32)],
        spaces=(pltpu.SMEM, pltpu.SMEM) + (pltpu.HBM,) * 4,
        scratch=[dma((5,))],
    )
    packed_there = send(packed, lambda z, y, x, c: (z, 1 - y, x, 1 - c))
    there = flip_y(there)
    outer = send(boundary, lambda z, y, x, c: (z + 2 * y - 1, c, x, 1 - y))
    plain = (w_send[0], w_recv[0], w_node[0])
    swapped = tuple(flip_core(value) for value in plain)
    even, odd = run(arrange_kernel, plain + swapped, [((3 * latent, latent), BF16)] * 2, cost=BESIDE)
    [fold] = run(fold_kernel, (w_message[0], w_aggregate[0], packed_there), [((latent, latent), BF16)], cost=BESIDE)
    fold_even, fold_odd = run(arrange_kernel, (fold, flip_core(fold)), [((latent, latent), BF16)] * 2)
    gain_even, gain_odd = run(arrange_kernel, (gains, flip_core(gains)), [((1, latent), F32)] * 2)
    matrices = ((even, fold_even, gain_even), (odd, fold_odd, gain_odd))

    gown, gown_t, ghalo, ghalo_t, lists, mate, home_lists = run(
        functools.partial(graph_kernel, edge_blocks),
        (packed, packed_there),
        [
            ((2 * edges, rows), BF16),
            ((rows, 2 * edges), BF16),
            ((edges, 2 * block), BF16),
            ((2 * block, edges), BF16),
            ((2, block), jnp.int32),
            ((1, block), jnp.int32),
            ((2, block), jnp.int32),
        ],
        cost=BESIDE,
    )
    hidden, inner = run(entry_kernel, (mate, here, there), [(wide, BF16), (narrow, BF16)])
    upstream = hidden

    def both_micro(evens, odds):
        [turned] = run(turn_kernel, (evens, odds), [(wide, BF16)])
        [out] = run(
            write_kernel,
            (evens, odds, flip_core(turned)),
            [((1, 2) + wide, BF16)],
            out_space=pl.ANY,
            scratch=[dma((2,))],
        )
        return out

    def home_of_plane(value, plane):
        return send(value, lambda z, y, x, c: (z, c, x, y) if x == plane else None)

    saved = ()
    first_home = None
    for tick in range(sections):
        plane, parity = tick // 2, tick % 2
        packed, fold, gain = matrices[parity]
        a_own, u_own = run_section(
            forward_own_kernel, plane, (packed,), (hidden, gown), [(edge_wide, F32), (wide, F32)], cost=BESIDE
        )
        if tick == sections - 1:
            first_home, a_own = lax.optimization_barrier((saved[3], a_own))
            first_home = home_of_plane(first_home, 0)
        to_send = [(narrow, BF16)] * 2 if tick < sections - 1 else []
        hidden, a, u, *to = run_section(
            forward_kernel,
            plane,
            (packed, fold, gain),
            (lists, hidden, a_own, u_own, inner, outer, ghalo, gown_t),
            [(wide, BF16), (edge_wide, F32), (wide, F32)] + to_send,
        )
        produced = hidden
        if to:
            step = (tick + 1) // 2 - plane
            outer = towards(to[OUTER], OUTER, step)
            if step:
                hidden = send(hidden, lambda z, y, x, c: (z, y, x + 1, c))
            inner = towards(to[INNER], INNER, step)
        saved = run(
            functools.partial(save_kernel, plane, parity),
            (a, u, produced) + tuple(saved),
            [((2 * rows, latent), BF16), ((2 * rows, latent), BF16), ((2 * edges, latent), BF16), ((2 * rows, latent), BF16)],
            aliases={3 + k: k for k in range(4)} if saved else None,
            cost=BESIDE,
        )

    *states, both = saved
    inner = outer = crossed = None
    finished = {}
    for tick in range(sections - 1, -1, -1):
        plane, parity = tick // 2, tick % 2
        packed, fold, gain = matrices[parity]
        step = (tick - 1) // 2 - plane if tick else 0
        crossing = tick > 0 and step != 0
        halo_in = inner is not None
        finish = halo_in and tick % 2 == 0
        outs = [
            (wide, F32),
            (wide, BF16),
            (edge_wide, BF16),
            (edge_wide, BF16),
            (narrow, BF16),
            (narrow, BF16),
        ] + ([(wide, BF16)] if finish else [])
        late = (finished[3],) if tick == 0 else ()
        c, du, da, es, to_inner, to_outer, *done = run_section(
            lambda take, *refs, halo_in=halo_in, parity=parity, late=len(late): backward_kernel(
                halo_in, parity, take, *refs[late:]
            ),
            plane,
            (packed, fold, gain),
            late + (lists, upstream) + ((inner, outer) if halo_in else ()) + tuple(states) + (gown, ghalo_t),
            outs,
            elsewhere=0 if late else None,
        )
        if done:
            finished[tick + 1] = done[0]
        if tick:
            outer = towards(to_outer, OUTER, step)
            inner = towards(to_inner, INNER, step)
        late = (finished[2],) if tick == 0 else ()
        [upstream] = run_section(
            lambda take, *refs, late=len(late): backward_own_kernel(take, *refs[late:]),
            plane,
            (packed,),
            late + (c, du, da, es, gown_t),
            [(wide, F32 if tick and not crossing else BF16)],
            elsewhere=0 if late else None,
            cost=BESIDE,
        )
        if crossed is not None:
            own, late_inner, late_outer, both, upstream = lax.optimization_barrier(crossed + (both, upstream))
            late_outer = send(late_outer, lambda z, y, x, c: (z + 2 * c - 1, y, x, 1 - c) if x else None)
            late_inner = send(late_inner, lambda z, y, x, c: (z, y, x, 1 - c) if x else None)
            second_home = home_of_plane(both, 1)
            [finished[2]] = run(
                functools.partial(add_kernel, 1),
                (lists, own, late_inner, late_outer),
                [(wide, BF16)],
                scratch=[pltpu.VMEM(wide, F32)],
            )
            crossed = None
        if crossing:
            crossed = (upstream, to_inner, to_outer)
            upstream = send(upstream, lambda z, y, x, c: (z, y, x + 1, c))

    final_outer = send(to_outer, lambda z, y, x, c: (z + 2 * c - 1, 1 - c, x, y))
    final_inner = send(to_inner, lambda z, y, x, c: (z, 1 - c, x, y))
    evens = to_home(upstream)
    odds = to_home(finished[1])
    [evens] = run(
        functools.partial(add_kernel, 0),
        (home_lists, evens, final_inner, final_outer, evens),
        [(wide, BF16)],
        scratch=[pltpu.VMEM(wide, F32)],
    )
    [home] = run(pick_kernel, (first_home, second_home), [((2 * rows, latent), BF16)])
    return both_micro(home[:rows], home[rows:]), both_micro(evens, odds)


def solution(mesh):
    in_specs = (
        P(None, "dom", None),
        P(None, "dom", None),
        P("pipe", None, None),
        P("pipe", None, None),
        P("pipe", None, None),
        P("pipe", None, None),
        P("pipe", None, None),
        P("pipe", None),
        P("dom", None),
        P("dom", None),
        P("dom"),
        P("dom", None, None),
    )
    out_specs = (P("pipe", None, "dom", None), P("pipe", None, "dom", None))
    return jax.shard_map(shards, mesh=mesh, in_specs=in_specs, out_specs=out_specs, check_vma=False)
```

time: 133 us -> 110 us (0.83)
  waiting for transfers between devices: 30.1 us -> 57.7 us
  Pallas kernels: 35.4 us -> 12.5 us
  local copies, waits for them, and re-layouts: 21.8 us -> 6.37 us
  starting transfers between devices: 42.9 us -> 31 us
    ppermute x33 -> x32, waiting for transfers between devices: 30.1 us -> 57.7 us  [send(): return lax.ppermute(value, AXES, table)]
    pallas_call x32 -> x34, Pallas kernels: 33.2 us -> 12.5 us  [run(): pl.pallas_call(kernel, out_shape=[jax.ShapeDtypeStruct(s, t) for s, t in...]
    unnamed x102 -> x23, local copies, waits for them, and re-layouts: 21.6 us -> 6.33 us
    ppermute x33 -> x32, starting transfers between devices: 42.9 us -> 31 us  [send(): return lax.ppermute(value, AXES, table)]
    pallas_call x1 -> x0, Pallas kernels: 2.25 us -> none  [shards(): pl.pallas_call(boundary_kernel, out_shape=[jax.ShapeDtypeStruct(narrow, B...]
  transfers between devices with their start and end apart: 33 -> 32, of which waited for: 11 -> 14; matrix products, arithmetic and copies ran while one was open for 0% -> 0% of each run, Pallas kernels for 13% -> 6%
where the time goes in v3:
time: 110 us; the launch traced here: 109 us
  waiting for transfers between devices  57.7 us (52%)
  starting transfers between devices  31 us (28%)
  Pallas kernels  12.5 us (11%)
  local copies, waits for them, and re-layouts  6.37 us (6%)
  between operations  1.21 us (1%)
    ppermute x32, waiting for transfers between devices, send(): return lax.ppermute(value, AXES, table)  57.7 us
    ppermute x32, starting transfers between devices, send(): return lax.ppermute(value, AXES, table)  31 us
    pallas_call x34, Pallas kernels, run(): pl.pallas_call(kernel, out_shape=[jax.ShapeDtypeStruct(s, t) for s, t in...  12.5 us
    unnamed x23, local copies, waits for them, and re-layouts  6.33 us
  transfers between devices with their start and end apart: 32, of which 14 were waited for; matrix products, arithmetic and copies ran while one was open for 0% of the time, Pallas kernels for 6%

profile of v3, /device:TPU:0, one launch (start us, length us, event | category | flops | bytes accessed | tf_op | source)
XLA Modules:
  0.0 108.9 jit_solution(14119589604385315131)
XLA Ops:
  1.4 1.0 copy-done
  2.4 1.0 copy-done.1
  6.3 2.5 %collective-permute-start.3 = (s32[3,8,128]{2,1,0:T(8,128)S(1)}, s32[3,8,128]{2,1,0:T(8,128)S(1)}, u32[]{:S(2)}, u32[]{:S(2)}) collective-permute-start(s32[3,8,128]{2,1,0:T(8,128)S(1)} %get-tuple-element.97.packed), channel_id=1, source_target_pairs={{0,5},{1,4},{2,7},{3,6},{4,1},{5,0},{6,3},{7,2},{8,13},{9,12},{10,... | collective-permute-start | bytes 36872 | tf_op jit(solution)/shard_map/ppermute | solution.py:399
  10.5 3.5 %collective-permute-start.7 = (bf16[128,512]{1,0:T(8,128)(2,1)S(1)}, bf16[128,512]{1,0:T(8,128)(2,1)S(1)}, u32[]{:S(2)}, u32[]{:S(2)}) collective-permute-start(bf16[128,512]{1,0:T(8,128)(2,1)S(1)} %get-tuple-element.112), channel_id=1, source_target_pairs={{0,25},{1,29},{2,27},{3,31},{4,8},{5,12},{6,10},{7,14},{8,1},{9,5}... | collective-permute-start | bytes 393224 | tf_op jit(solution)/shard_map/ppermute | solution.py:399
  16.4 7.4 %collective-permute-done.6.there = bf16[256,512]{1,0:T(8,128)(2,1)S(1)} collective-permute-done((bf16[256,512]{1,0:T(8,128)(2,1)S(1)}, bf16[256,512]{1,0:T(8,128)(2,1)S(1)}, u32[]{:S(2)}, u32[]{:S(2)}) %collective-permute-start.6) | collective-permute-done | bytes 262176 | tf_op jit(solution)/shard_map/ppermute | solution.py:399
  25.8 1.2 %shard_map.139 = (bf16[256,512]{1,0:T(8,128)(2,1)S(1)}, f32[256,512]{1,0:T(8,128)S(1)}, f32[256,512]{1,0:T(8,128)S(1)}, bf16[128,512]{1,0:T(8,128)(2,1)S(1)}, bf16[128,512]{1,0:T(8,128)(2,1)S(1)}) custom-call(bf16[1536,512]{1,0:T(8,128)(2,1)S(1)} %get-tuple-element.96.refs_0_, bf16[512,512]{1,0:T(8,128)(2,1)S(1)} %get-tuple-element.98.refs_1_, ...), custom_call_target="tpu_custom_call" | custom-call | flops 1 | bytes 1 | tf_op jit(solution)/shard_map/pallas_call | solution.py:336
  27.2 1.1 %collective-permute-start.9 = (bf16[128,512]{1,0:T(8,128)(2,1)S(1)}, bf16[128,512]{1,0:T(8,128)(2,1)S(1)}, u32[]{:S(2)}, u32[]{:S(2)}) collective-permute-start(bf16[128,512]{1,0:T(8,128)(2,1)S(1)} %get-tuple-element.119), channel_id=1, source_target_pairs={{0,25},{1,8},{2,27},{3,10},{4,29},{5,12},{6,31},{7,14},{8,1},{9,16... | collective-permute-start | bytes 393224 | tf_op jit(solution)/shard_map/ppermute | solution.py:399
  29.6 3.8 %collective-permute-done.9.refs_8_ = bf16[128,512]{1,0:T(8,128)(2,1)S(1)} collective-permute-done((bf16[128,512]{1,0:T(8,128)(2,1)S(1)}, bf16[128,512]{1,0:T(8,128)(2,1)S(1)}, u32[]{:S(2)}, u32[]{:S(2)}) %collective-permute-start.9) | collective-permute-done | bytes 131104 | tf_op jit(solution)/shard_map/ppermute | solution.py:399
  33.5 1.2 %shard_map.141 = (bf16[256,512]{1,0:T(8,128)(2,1)S(1)}, f32[256,512]{1,0:T(8,128)S(1)}, f32[256,512]{1,0:T(8,128)S(1)}, bf16[128,512]{1,0:T(8,128)(2,1)S(1)}, bf16[128,512]{1,0:T(8,128)(2,1)S(1)}) custom-call(bf16[1536,512]{1,0:T(8,128)(2,1)S(1)} %get-tuple-element.101.refs_0_, bf16[512,512]{1,0:T(8,128)(2,1)S(1)} %get-tuple-element.102.refs_1_, ...), custom_call_target="tpu_custom_call" | custom-call | flops 1 | bytes 1 | tf_op jit(solution)/shard_map/pallas_call | solution.py:336
  35.1 2.1 %collective-permute-start.10 = (bf16[256,512]{1,0:T(8,128)(2,1)S(1)}, bf16[256,512]{1,0:T(8,128)(2,1)S(1)}, u32[]{:S(2)}, u32[]{:S(2)}) collective-permute-start(bf16[256,512]{1,0:T(8,128)(2,1)S(1)} %get-tuple-element.120.h), channel_id=1, source_target_pairs={{0,2},{1,3},{2,0},{3,1},{4,6},{5,7},{6,4},{7,5},{8,10},{9,11},{10,... | collective-permute-start | bytes 786440 | tf_op jit(solution)/shard_map/ppermute | solution.py:399
  37.7 11.2 %collective-permute-done.10.refs_1_.refs_4_ = bf16[256,512]{1,0:T(8,128)(2,1)S(1)} collective-permute-done((bf16[256,512]{1,0:T(8,128)(2,1)S(1)}, bf16[256,512]{1,0:T(8,128)(2,1)S(1)}, u32[]{:S(2)}, u32[]{:S(2)}) %collective-permute-start.10) | collective-permute-done | bytes 262176 | tf_op jit(solution)/shard_map/ppermute | solution.py:399
  49.7 1.2 %collective-permute-start.14 = (bf16[128,512]{1,0:T(8,128)(2,1)S(1)}, bf16[128,512]{1,0:T(8,128)(2,1)S(1)}, u32[]{:S(2)}, u32[]{:S(2)}) collective-permute-start(bf16[128,512]{1,0:T(8,128)(2,1)S(1)} %get-tuple-element.145), channel_id=1, source_target_pairs={{0,1},{1,0},{2,3},{3,2},{4,5},{5,4},{6,7},{7,6},{8,9},{9,8},{10,11... | collective-permute-start | bytes 393224 | tf_op jit(solution)/shard_map/ppermute | solution.py:399
  51.9 5.2 %collective-permute-done.15.refs_8_ = bf16[128,512]{1,0:T(8,128)(2,1)S(1)} collective-permute-done((bf16[128,512]{1,0:T(8,128)(2,1)S(1)}, bf16[128,512]{1,0:T(8,128)(2,1)S(1)}, u32[]{:S(2)}, u32[]{:S(2)}) %collective-permute-start.15) | collective-permute-done | bytes 131104 | tf_op jit(solution)/shard_map/ppermute | solution.py:399
  57.1 2.3 %collective-permute-start.16 = (bf16[128,512]{1,0:T(8,128)(2,1)S(1)}, bf16[128,512]{1,0:T(8,128)(2,1)S(1)}, u32[]{:S(2)}, u32[]{:S(2)}) collective-permute-start(bf16[128,512]{1,0:T(8,128)(2,1)S(1)} %get-tuple-element.161), channel_id=1, source_target_pairs={{0,1},{1,0},{2,3},{3,2},{4,5},{5,4},{6,7},{7,6},{8,9},{9,8},{10,11... | collective-permute-start | bytes 393224 | tf_op jit(solution)/shard_map/ppermute | solution.py:399
  59.4 1.0 collective-permute-done.16.refs_5_
  60.4 5.2 %collective-permute-done.17.refs_6_ = bf16[128,512]{1,0:T(8,128)(2,1)S(1)} collective-permute-done((bf16[128,512]{1,0:T(8,128)(2,1)S(1)}, bf16[128,512]{1,0:T(8,128)(2,1)S(1)}, u32[]{:S(2)}, u32[]{:S(2)}) %collective-permute-start.17) | collective-permute-done | bytes 131104 | tf_op jit(solution)/shard_map/ppermute | solution.py:399
  65.6 4.7 %collective-permute-start.18 = (bf16[256,512]{1,0:T(8,128)(2,1)S(1)}, bf16[256,512]{1,0:T(8,128)(2,1)S(1)}, u32[]{:S(2)}, u32[]{:S(2)}) collective-permute-start(bf16[256,512]{1,0:T(8,128)(2,1)S(1)} %shard_map.153.value), channel_id=1, source_target_pairs={{0,2},{1,3},{2,0},{3,1},{4,6},{5,7},{6,4},{7,5},{8,10},{9,11},{10,... | collective-permute-start | bytes 786440 | tf_op jit(solution)/shard_map/ppermute | solution.py:399
  70.9 10.8 %collective-permute-done.19.refs_5_ = bf16[128,512]{1,0:T(8,128)(2,1)S(1)} collective-permute-done((bf16[128,512]{1,0:T(8,128)(2,1)S(1)}, bf16[128,512]{1,0:T(8,128)(2,1)S(1)}, u32[]{:S(2)}, u32[]{:S(2)}) %collective-permute-start.19) | collective-permute-done | bytes 131104 | tf_op jit(solution)/shard_map/ppermute | solution.py:399
  81.8 1.2 %shard_map.154 = (f32[256,512]{1,0:T(8,128)S(1)}, bf16[256,512]{1,0:T(8,128)(2,1)S(1)}, bf16[256,512]{1,0:T(8,128)(2,1)S(1)}, bf16[256,512]{1,0:T(8,128)(2,1)S(1...) custom-call(bf16[1536,512]{1,0:T(8,128)(2,1)S(1)} %get-tuple-element.101.refs_0_, ...), custom_call_target="tpu_custom_call" | custom-call | flops 1 | bytes 1 | tf_op jit(solution)/shard_map/pallas_call | solution.py:336
  86.6 5.0 %collective-permute-done.26.refs_7_ = bf16[128,512]{1,0:T(8,128)(2,1)S(1)} collective-permute-done((bf16[128,512]{1,0:T(8,128)(2,1)S(1)}, bf16[128,512]{1,0:T(8,128)(2,1)S(1)}, u32[]{:S(2)}, u32[]{:S(2)}) %collective-permute-start.26) | collective-permute-done | bytes 131104 | tf_op jit(solution)/shard_map/ppermute | solution.py:399
  91.6 1.2 %shard_map.160 = (f32[256,512]{1,0:T(8,128)S(1)}, bf16[256,512]{1,0:T(8,128)(2,1)S(1)}, bf16[256,512]{1,0:T(8,128)(2,1)S(1)}, bf16[256,512]{1,0:T(8,128)(2,1)S(1...) custom-call(bf16[1536,512]{1,0:T(8,128)(2,1)S(1)} %get-tuple-element.96.refs_0_, ...), custom_call_target="tpu_custom_call" | custom-call | flops 1 | bytes 1 | tf_op jit(solution)/shard_map/pallas_call | solution.py:336
  94.8 4.1 %collective-permute-start.28 = (bf16[128,512]{1,0:T(8,128)(2,1)S(1)}, bf16[128,512]{1,0:T(8,128)(2,1)S(1)}, u32[]{:S(2)}, u32[]{:S(2)}) collective-permute-start(bf16[128,512]{1,0:T(8,128)(2,1)S(1)} %get-tuple-element.187), channel_id=1, source_target_pairs={{0,4},{1,0},{2,6},{3,2},{4,5},{5,1},{6,7},{7,3},{8,12},{9,8},{10,1... | collective-permute-start | bytes 393224 | tf_op jit(solution)/shard_map/ppermute | solution.py:399
  99.7 4.5 %collective-permute-done.28.inner = bf16[128,512]{1,0:T(8,128)(2,1)S(1)} collective-permute-done((bf16[128,512]{1,0:T(8,128)(2,1)S(1)}, bf16[128,512]{1,0:T(8,128)(2,1)S(1)}, u32[]{:S(2)}, u32[]{:S(2)}) %collective-permute-start.28) | collective-permute-done | bytes 131104 | tf_op jit(solution)/shard_map/ppermute | solution.py:399
  104.2 1.0 collective-permute-done.29.outer
  (98 shorter events, 24.1 us)
Async XLA Ops:
  6.3 8.4 %collective-permute-start.3 = (s32[3,8,128]{2,1,0:T(8,128)S(1)}, s32[3,8,128]{2,1,0:T(8,128)S(1)}, u32[]{:S(2)}, u32[]{:S(2)}) collective-permute-start(s32[3,8,128]{2,1,0:T(8,128)S(1)} %get-tuple-element.97.packed), channel_id=1, source_target_pairs={{0,5},{1,4},{2,7},{3,6},{4,1},{5,0},{6,3},{7,2},{8,13},{9,12},{10,... | collective-permute-start | bytes 36872 | tf_op jit(solution)/shard_map/ppermute | solution.py:399
  9.5 14.4 %collective-permute-start = (bf16[512,512]{1,0:T(8,128)(2,1)}, bf16[512,512]{1,0:T(8,128)(2,1)S(1)}, u32[]{:S(2)}, u32[]{:S(2)}) collective-permute-start(bf16[512,512]{1,0:T(8,128)(2,1)} %bitcast.7), channel_id=1, source_target_pairs={{0,1},{1,0},{2,3},{3,2},{4,5},{5,4},{6,7},{7,6},{8,9},{9,8},{10,11... | collective-permute-start | bytes 1572872 | tf_op jit(solution)/shard_map/ppermute | solution.py:399
  9.5 14.4 %collective-permute-start.1 = (bf16[512,512]{1,0:T(8,128)(2,1)}, bf16[512,512]{1,0:T(8,128)(2,1)S(1)}, u32[]{:S(2)}, u32[]{:S(2)}) collective-permute-start(bf16[512,512]{1,0:T(8,128)(2,1)} %bitcast.9), channel_id=1, source_target_pairs={{0,1},{1,0},{2,3},{3,2},{4,5},{5,4},{6,7},{7,6},{8,9},{9,8},{10,11... | collective-permute-start | bytes 1572872 | tf_op jit(solution)/shard_map/ppermute | solution.py:399
  10.0 13.9 %collective-permute-start.2 = (bf16[512,512]{1,0:T(8,128)(2,1)}, bf16[512,512]{1,0:T(8,128)(2,1)S(1)}, u32[]{:S(2)}, u32[]{:S(2)}) collective-permute-start(bf16[512,512]{1,0:T(8,128)(2,1)} %bitcast.11), channel_id=1, source_target_pairs={{0,1},{1,0},{2,3},{3,2},{4,5},{5,4},{6,7},{7,6},{8,9},{9,8},{10,11... | collective-permute-start | bytes 1572872 | tf_op jit(solution)/shard_map/ppermute | solution.py:399
  10.5 15.3 %collective-permute-start.7 = (bf16[128,512]{1,0:T(8,128)(2,1)S(1)}, bf16[128,512]{1,0:T(8,128)(2,1)S(1)}, u32[]{:S(2)}, u32[]{:S(2)}) collective-permute-start(bf16[128,512]{1,0:T(8,128)(2,1)S(1)} %get-tuple-element.112), channel_id=1, source_target_pairs={{0,25},{1,29},{2,27},{3,31},{4,8},{5,12},{6,10},{7,14},{8,1},{9,5}... | collective-permute-start | bytes 393224 | tf_op jit(solution)/shard_map/ppermute | solution.py:399
  14.7 9.0 %collective-permute-start.6 = (bf16[256,512]{1,0:T(8,128)(2,1)S(1)}, bf16[256,512]{1,0:T(8,128)(2,1)S(1)}, u32[]{:S(2)}, u32[]{:S(2)}) collective-permute-start(bf16[256,512]{1,0:T(8,128)(2,1)S(1)} %get-tuple-element.106), channel_id=1, source_target_pairs={{0,4},{1,5},{2,6},{3,7},{4,0},{5,1},{6,2},{7,3},{8,12},{9,13},{10,... | collective-permute-start | bytes 786440 | tf_op jit(solution)/shard_map/ppermute | solution.py:399
  27.2 6.3 %collective-permute-start.9 = (bf16[128,512]{1,0:T(8,128)(2,1)S(1)}, bf16[128,512]{1,0:T(8,128)(2,1)S(1)}, u32[]{:S(2)}, u32[]{:S(2)}) collective-permute-start(bf16[128,512]{1,0:T(8,128)(2,1)S(1)} %get-tuple-element.119), channel_id=1, source_target_pairs={{0,25},{1,8},{2,27},{3,10},{4,29},{5,12},{6,31},{7,14},{8,1},{9,16... | collective-permute-start | bytes 393224 | tf_op jit(solution)/shard_map/ppermute | solution.py:399
  34.6 14.3 %collective-permute-start.11 = (bf16[128,512]{1,0:T(8,128)(2,1)S(1)}, bf16[128,512]{1,0:T(8,128)(2,1)S(1)}, u32[]{:S(2)}, u32[]{:S(2)}) collective-permute-start(bf16[128,512]{1,0:T(8,128)(2,1)S(1)} %get-tuple-element.123), channel_id=1, source_target_pairs={{0,3},{1,2},{2,1},{3,0},{4,7},{5,6},{6,5},{7,4},{8,11},{9,10},{10,... | collective-permute-start | bytes 393224 | tf_op jit(solution)/shard_map/ppermute | solution.py:399
  34.7 14.2 %collective-permute-start.12 = (bf16[128,512]{1,0:T(8,128)(2,1)S(1)}, bf16[128,512]{1,0:T(8,128)(2,1)S(1)}, u32[]{:S(2)}, u32[]{:S(2)}) collective-permute-start(bf16[128,512]{1,0:T(8,128)(2,1)S(1)} %get-tuple-element.124), channel_id=1, source_target_pairs={{0,27},{1,10},{2,25},{3,8},{4,31},{5,14},{6,29},{7,12},{8,3},{9,18... | collective-permute-start | bytes 393224 | tf_op jit(solution)/shard_map/ppermute | solution.py:399
  35.1 13.8 %collective-permute-start.10 = (bf16[256,512]{1,0:T(8,128)(2,1)S(1)}, bf16[256,512]{1,0:T(8,128)(2,1)S(1)}, u32[]{:S(2)}, u32[]{:S(2)}) collective-permute-start(bf16[256,512]{1,0:T(8,128)(2,1)S(1)} %get-tuple-element.120.h), channel_id=1, source_target_pairs={{0,2},{1,3},{2,0},{3,1},{4,6},{5,7},{6,4},{7,5},{8,10},{9,11},{10,... | collective-permute-start | bytes 786440 | tf_op jit(solution)/shard_map/ppermute | solution.py:399
  49.0 8.1 %collective-permute-start.13 = (bf16[512,512]{1,0:T(8,128)(2,1)S(1)}, bf16[512,512]{1,0:T(8,128)(2,1)S(1)}, u32[]{:S(2)}, u32[]{:S(2)}) collective-permute-start(bf16[512,512]{1,0:T(8,128)(2,1)S(1)} %get-tuple-element.142.refs_3_), channel_id=1, source_target_pairs={{0,0},{1,4},{4,1},{5,5},{8,8},{9,12},{12,9},{13,13},{16,16},{17,20... | collective-permute-start | bytes 1572872 | tf_op jit(solution)/shard_map/ppermute | solution.py:399
  50.9 6.2 %collective-permute-start.15 = (bf16[128,512]{1,0:T(8,128)(2,1)S(1)}, bf16[128,512]{1,0:T(8,128)(2,1)S(1)}, u32[]{:S(2)}, u32[]{:S(2)}) collective-permute-start(bf16[128,512]{1,0:T(8,128)(2,1)S(1)} %get-tuple-element.146), channel_id=1, source_target_pairs={{0,25},{1,8},{2,27},{3,10},{4,29},{5,12},{6,31},{7,14},{8,1},{9,16... | collective-permute-start | bytes 393224 | tf_op jit(solution)/shard_map/ppermute | solution.py:399
  57.1 3.3 %collective-permute-start.16 = (bf16[128,512]{1,0:T(8,128)(2,1)S(1)}, bf16[128,512]{1,0:T(8,128)(2,1)S(1)}, u32[]{:S(2)}, u32[]{:S(2)}) collective-permute-start(bf16[128,512]{1,0:T(8,128)(2,1)S(1)} %get-tuple-element.161), channel_id=1, source_target_pairs={{0,1},{1,0},{2,3},{3,2},{4,5},{5,4},{6,7},{7,6},{8,9},{9,8},{10,11... | collective-permute-start | bytes 393224 | tf_op jit(solution)/shard_map/ppermute | solution.py:399
  59.4 6.2 %collective-permute-start.17 = (bf16[128,512]{1,0:T(8,128)(2,1)S(1)}, bf16[128,512]{1,0:T(8,128)(2,1)S(1)}, u32[]{:S(2)}, u32[]{:S(2)}) collective-permute-start(bf16[128,512]{1,0:T(8,128)(2,1)S(1)} %get-tuple-element.162), channel_id=1, source_target_pairs={{0,25},{1,8},{2,27},{3,10},{4,29},{5,12},{6,31},{7,14},{8,1},{9,16... | collective-permute-start | bytes 393224 | tf_op jit(solution)/shard_map/ppermute | solution.py:399
  65.6 16.2 %collective-permute-start.18 = (bf16[256,512]{1,0:T(8,128)(2,1)S(1)}, bf16[256,512]{1,0:T(8,128)(2,1)S(1)}, u32[]{:S(2)}, u32[]{:S(2)}) collective-permute-start(bf16[256,512]{1,0:T(8,128)(2,1)S(1)} %shard_map.153.value), channel_id=1, source_target_pairs={{0,2},{1,3},{2,0},{3,1},{4,6},{5,7},{6,4},{7,5},{8,10},{9,11},{10,... | collective-permute-start | bytes 786440 | tf_op jit(solution)/shard_map/ppermute | solution.py:399
  70.3 11.5 %collective-permute-start.19 = (bf16[128,512]{1,0:T(8,128)(2,1)S(1)}, bf16[128,512]{1,0:T(8,128)(2,1)S(1)}, u32[]{:S(2)}, u32[]{:S(2)}) collective-permute-start(bf16[128,512]{1,0:T(8,128)(2,1)S(1)} %get-tuple-element.177), channel_id=1, source_target_pairs={{0,3},{1,2},{2,1},{3,0},{4,7},{5,6},{6,5},{7,4},{8,11},{9,10},{10,... | collective-permute-start | bytes 393224 | tf_op jit(solution)/shard_map/ppermute | solution.py:399
  70.3 11.5 %collective-permute-start.20 = (bf16[128,512]{1,0:T(8,128)(2,1)S(1)}, bf16[128,512]{1,0:T(8,128)(2,1)S(1)}, u32[]{:S(2)}, u32[]{:S(2)}) collective-permute-start(bf16[128,512]{1,0:T(8,128)(2,1)S(1)} %get-tuple-element.178), channel_id=1, source_target_pairs={{0,27},{1,10},{2,25},{3,8},{4,31},{5,14},{6,29},{7,12},{8,3},{9,18... | collective-permute-start | bytes 393224 | tf_op jit(solution)/shard_map/ppermute | solution.py:399
  83.6 3.0 %collective-permute-start.23 = (bf16[128,512]{1,0:T(8,128)(2,1)S(1)}, bf16[128,512]{1,0:T(8,128)(2,1)S(1)}, u32[]{:S(2)}, u32[]{:S(2)}) collective-permute-start(bf16[128,512]{1,0:T(8,128)(2,1)S(1)} %get-tuple-element.177), channel_id=1, source_target_pairs={{2,3},{3,2},{6,7},{7,6},{10,11},{11,10},{14,15},{15,14},{18,19},{1... | collective-permute-start | bytes 393224 | tf_op jit(solution)/shard_map/ppermute | solution.py:399
  85.5 6.2 %collective-permute-start.26 = (bf16[128,512]{1,0:T(8,128)(2,1)S(1)}, bf16[128,512]{1,0:T(8,128)(2,1)S(1)}, u32[]{:S(2)}, u32[]{:S(2)}) collective-permute-start(bf16[128,512]{1,0:T(8,128)(2,1)S(1)} %get-tuple-element.182), channel_id=1, source_target_pairs={{0,25},{1,8},{2,27},{3,10},{4,29},{5,12},{6,31},{7,14},{8,1},{9,16... | collective-permute-start | bytes 393224 | tf_op jit(solution)/shard_map/ppermute | solution.py:399
  85.9 19.7 %collective-permute-start.21 = (bf16[512,512]{1,0:T(8,128)(2,1)S(1)}, bf16[512,512]{1,0:T(8,128)(2,1)S(1)}, u32[]{:S(2)}, u32[]{:S(2)}) collective-permute-start(bf16[512,512]{1,0:T(8,128)(2,1)S(1)} %get-tuple-element.174), channel_id=1, source_target_pairs={{2,2},{3,6},{6,3},{7,7},{10,10},{11,14},{14,11},{15,15},{18,18},{1... | collective-permute-start | bytes 1572872 | tf_op jit(solution)/shard_map/ppermute | solution.py:399
  93.5 11.7 %collective-permute-start.27 = (bf16[256,512]{1,0:T(8,128)(2,1)S(1)}, bf16[256,512]{1,0:T(8,128)(2,1)S(1)}, u32[]{:S(2)}, u32[]{:S(2)}) collective-permute-start(bf16[256,512]{1,0:T(8,128)(2,1)S(1)} %shard_map.161), channel_id=1, source_target_pairs={{0,0},{1,4},{2,2},{3,6},{4,1},{5,5},{6,3},{7,7},{8,8},{9,12},{10,1... | collective-permute-start | bytes 786440 | tf_op jit(solution)/shard_map/ppermute | solution.py:399
  94.2 11.3 %collective-permute-start.30 = (bf16[256,512]{1,0:T(8,128)(2,1)S(1)}, bf16[256,512]{1,0:T(8,128)(2,1)S(1)}, u32[]{:S(2)}, u32[]{:S(2)}) collective-permute-start(bf16[256,512]{1,0:T(8,128)(2,1)S(1)} %get-tuple-element.189), channel_id=1, source_target_pairs={{0,0},{1,4},{2,2},{3,6},{4,1},{5,5},{6,3},{7,7},{8,8},{9,12},{10,1... | collective-permute-start | bytes 786440 | tf_op jit(solution)/shard_map/ppermute | solution.py:399
  94.8 9.4 %collective-permute-start.28 = (bf16[128,512]{1,0:T(8,128)(2,1)S(1)}, bf16[128,512]{1,0:T(8,128)(2,1)S(1)}, u32[]{:S(2)}, u32[]{:S(2)}) collective-permute-start(bf16[128,512]{1,0:T(8,128)(2,1)S(1)} %get-tuple-element.187), channel_id=1, source_target_pairs={{0,4},{1,0},{2,6},{3,2},{4,5},{5,1},{6,7},{7,3},{8,12},{9,8},{10,1... | collective-permute-start | bytes 393224 | tf_op jit(solution)/shard_map/ppermute | solution.py:399
  99.0 6.2 %collective-permute-start.29 = (bf16[128,512]{1,0:T(8,128)(2,1)S(1)}, bf16[128,512]{1,0:T(8,128)(2,1)S(1)}, u32[]{:S(2)}, u32[]{:S(2)}) collective-permute-start(bf16[128,512]{1,0:T(8,128)(2,1)S(1)} %get-tuple-element.188), channel_id=1, source_target_pairs={{0,28},{1,8},{2,30},{3,10},{4,29},{5,9},{6,31},{7,11},{8,4},{9,16}... | collective-permute-start | bytes 393224 | tf_op jit(solution)/shard_map/ppermute | solution.py:399
  (19 other events, 47.2 us)

commit v4 on v3

v4 whole, which is shorter than its diff:
```python
import functools

import jax
import jax.numpy as jnp
from jax import lax
from jax.experimental import pallas as pl
from jax.experimental.pallas import tpu as pltpu
from jax.sharding import PartitionSpec as P

EPSILON = 1e-05
F32 = jnp.float32
BF16 = jnp.bfloat16
AXES = ("dom", "pipe")
INNER, OUTER = 0, 1
BESIDE = 4 * 10**9
LONG = 2 * 10**10


def mul(a, b):
    return jnp.dot(a, b, preferred_element_type=F32)


def mul_t(a, b):
    return lax.dot_general(a, b, (((1,), (1,)), ((), ())), preferred_element_type=F32)


def slope(v):
    s = jax.nn.sigmoid(v)
    return s * (1.0 + v * (1.0 - s))


def normalize(z):
    centred = z - jnp.mean(z, axis=-1, keepdims=True)
    inverse = lax.rsqrt(jnp.mean(centred * centred, axis=-1, keepdims=True) + EPSILON)
    return centred * inverse, inverse


def quarters(packed):
    depth = packed.shape[0] // 4
    return [packed.at[pl.ds(number * depth, depth), :] for number in range(4)]


def here_is(plane=None, parity=None):
    pipe = lax.axis_index("pipe")
    wanted = jnp.bool_(True)
    if plane is not None:
        wanted = pipe // 2 == plane
    if parity is not None:
        wanted = wanted & (pipe % 2 == parity)
    return wanted


def is_local():
    return lax.axis_index("pipe") % 2 == lax.axis_index("dom") % 2


def listed(at, value, block):
    picked = value[:block]
    for number in range(1, value.shape[0] // block):
        picked = jnp.where(at == number, value[number * block : (number + 1) * block], picked)
    return picked


def add_listed(at, target, value, block):
    for number in range(target.shape[0] // block):
        rows = slice(number * block, (number + 1) * block)
        target[rows, :] = target[rows, :] + jnp.where(at == number, value, 0.0)


def prepare_kernel(
    count,
    halo,
    inputs,
    cotangent,
    send_in,
    recv_in,
    w_send,
    w_recv,
    w_node,
    w_message,
    w_aggregate,
    here,
    there,
    boundary,
    weights,
    packed,
    factors,
    product,
    sems,
    weight_sems,
):
    micro = lax.axis_index("dom") % 2
    block = boundary.shape[0]
    depth = w_send.shape[0]
    edge_blocks = send_in.shape[0]
    number = jnp.where(micro == 1, halo[0, 0, 0], halo[0, 0, 1])
    start = pl.multiple_of(number * block, block)

    def fetch(source):
        return [
            pltpu.make_async_copy(source.at[1 - micro], there, sems.at[0]),
            pltpu.make_async_copy(
                source.at[lax.axis_index("pipe") % 2, pl.ds(start, block), :], boundary, sems.at[1]
            ),
            pltpu.make_async_copy(source.at[micro], here, sems.at[2]),
        ]

    @pl.when(here_is(0))
    def _():
        for copy in fetch(inputs):
            copy.start()

    @pl.when(jnp.logical_not(here_is(0)))
    def _():
        for copy in fetch(cotangent):
            copy.start()

    copies = [
        pltpu.make_async_copy(ref, factors.at[k], weight_sems.at[k]) for k, ref in enumerate((w_message, w_aggregate))
    ]
    copies += [
        pltpu.make_async_copy(ref, packed.at[k, pl.ds(0, edge_blocks), :], sems.at[3 + k])
        for k, ref in enumerate((send_in, recv_in))
    ]
    copies += [
        pltpu.make_async_copy(ref, weights.at[pl.ds(k * depth, depth), :], weight_sems.at[2 + k])
        for k, ref in enumerate((w_send, w_recv, w_node))
    ]
    for copy in copies:
        copy.start()
    lane = lax.broadcasted_iota(jnp.int32, packed.shape[1:], 1)
    tail = jnp.where(lane == 0, halo[0, 0, 0], halo[0, 0, 1])
    for place in range(edge_blocks):
        tail = jnp.where(lane == 2 + place, count[place], tail)
    packed[2] = tail
    for copy in copies[:2]:
        copy.wait()
    product[...] = mul(factors[0], factors[1]).astype(BF16)
    last = pltpu.make_async_copy(product, weights.at[pl.ds(3 * depth, depth), :], weight_sems.at[5])
    last.start()
    for copy in copies[2:] + fetch(inputs):
        copy.wait()
    last.wait()


def arrange_kernel(mine, swapped, even, odd):
    @pl.when(here_is(parity=0))
    def _():
        even[...] = mine[...]
        odd[...] = swapped[...]

    @pl.when(here_is(parity=1))
    def _():
        even[...] = swapped[...]
        odd[...] = mine[...]


def graph_kernel(edge_blocks, _, packed, packed_there, gown, gown_t, ghalo, ghalo_t, lists, mate, home_lists):
    block = packed.shape[2]
    rows = gown_t.shape[0]
    edges = edge_blocks * block
    local = is_local()
    first_core = lax.axis_index("pipe") % 2 == 0
    mine = [jnp.where(local, packed[k], packed_there[k]) for k in range(3)]
    tails = mine[2], jnp.where(local, packed_there[2], packed[2])
    lane = lax.broadcasted_iota(jnp.int32, (1, block), 1)
    row = lax.broadcasted_iota(jnp.int32, (rows, block), 0)
    halo_row = lax.broadcasted_iota(jnp.int32, (2 * block, block), 0)
    for number in range(edge_blocks):
        live = lane < tails[0][:1, 2 + number : 3 + number]
        sender = jnp.where(live, mine[0][number : number + 1], -1)
        receiver = jnp.where(live, mine[1][number : number + 1], -1)
        outside = sender - rows
        turned = jnp.where(outside < block, outside + block, outside - block)
        outside = jnp.where(outside >= 0, jnp.where(first_core, turned, outside), -1)
        here = slice(number * block, (number + 1) * block)
        received = slice(edges + number * block, edges + (number + 1) * block)
        for index, at, table, table_t in (
            (sender, here, gown, gown_t),
            (receiver, received, gown, gown_t),
            (outside, here, ghalo, ghalo_t),
        ):
            hot = (index == (halo_row if table is ghalo else row)).astype(F32)
            table_t[:, at] = hot.astype(BF16)
            table[at, :] = hot.T.astype(BF16)

    def whole(tail, place):
        return jnp.broadcast_to(tail[:1, place : place + 1], (1, block))

    to_next, to_prev = whole(tails[0], 0), whole(tails[0], 1)
    lists[0:1, :] = jnp.where(first_core, to_next, to_prev)
    lists[1:2, :] = jnp.where(first_core, to_prev, to_next)
    mate[...] = jnp.where(first_core, whole(tails[1], 1), whole(tails[1], 0))
    to_next, to_prev = whole(packed[2], 0), whole(packed[2], 1)
    home_first = lax.axis_index("dom") % 2 == 0
    home_lists[0:1, :] = jnp.where(home_first, to_next, to_prev)
    home_lists[1:2, :] = jnp.where(home_first, to_prev, to_next)


def entry_kernel(mate, here, there, hidden, inner):
    block = inner.shape[0]

    @pl.when(is_local())
    def _():
        hidden[...] = here[...]
        inner[...] = listed(mate[:, :1], there[...], block)

    @pl.when(jnp.logical_not(is_local()))
    def _():
        hidden[...] = there[...]
        inner[...] = listed(mate[:, :1], here[...], block)


def forward_own_kernel(take, h, gown, *refs):
    w_send, w_recv, w_node, _ = quarters(take[0])
    a_out, u_out = refs[-2:]
    edges = gown.shape[0] // 2
    own = mul(gown[...], h[...]).astype(BF16)
    a_out[...] = mul(own[:edges], w_send[...]) + mul(own[edges:], w_recv[...])
    u_out[...] = mul(h[...], w_node[...])


def forward_kernel(take, lists, h, a_own, u_own, inner, outer, ghalo, gown_t, h_out, a_out, u_out, *to):
    packed, gain = take
    w_send, _, _, w_fold = quarters(packed)
    edges = ghalo.shape[0]
    block = inner.shape[0]
    halo = (mul(ghalo[:, :block], inner[...]) + mul(ghalo[:, block:], outer[...])).astype(BF16)
    a = a_own[...] + mul(halo, w_send[...])
    a_out[...] = a
    q = (a * jax.nn.sigmoid(a)).astype(BF16)
    u = u_own[...] + mul(mul(gown_t[:, edges:], q).astype(BF16), w_fold[...])
    u_out[...] = u
    t, _ = normalize(u * jax.nn.sigmoid(u))
    out = (h[...].astype(F32) + t * gain[...]).astype(BF16)
    h_out[...] = out
    for side, ref in enumerate(to):
        ref[...] = listed(lists[side : side + 1, :1], out, block)


def save_kernel(plane, parity, a, u, h, *refs):
    t_out, r_out, s_out, h_out = refs[-4:]
    rows, edges = h.shape[0], a.shape[0]
    at = slice(parity * rows, (parity + 1) * rows)

    @pl.when(here_is(plane))
    def _():
        s_out[parity * edges : (parity + 1) * edges, :] = slope(a[...]).astype(BF16)
        u_value = u[...]
        t, inverse = normalize(u_value * jax.nn.sigmoid(u_value))
        t_out[at, :] = t.astype(BF16)
        r_out[at, :] = (inverse * slope(u_value)).astype(BF16)
        h_out[at, :] = h[...]


def backward_kernel(halo_in, finish, parity, kept, take, *refs):
    packed, gain = take
    w_send, _, _, w_fold = quarters(packed)
    lists, upstream, *refs = refs[kept:]
    if halo_in:
        inner, outer, *refs = refs
    t_in, r_in, s_in, gown, ghalo_t, c_out, du_out, da_out, es_out, *done, to_inner, to_outer = refs
    edges = gown.shape[0] // 2
    rows = upstream.shape[0]
    block = to_inner.shape[0]
    at = slice(parity * rows, (parity + 1) * rows)
    at_edges = slice(parity * edges, (parity + 1) * edges)
    c_out[...] = upstream[...].astype(F32)
    if halo_in:
        add_listed(lists[INNER : INNER + 1, :1], c_out, inner[...].astype(F32), block)
        add_listed(lists[OUTER : OUTER + 1, :1], c_out, outer[...].astype(F32), block)
    if finish:
        done[0][...] = c_out[...].astype(BF16)
    g = c_out[...] * gain[...]
    t = t_in[at, :].astype(F32)
    centre = jnp.mean(g, axis=-1, keepdims=True)
    along = jnp.mean(g * t, axis=-1, keepdims=True)
    du = ((g - centre - t * along) * r_in[at, :].astype(F32)).astype(BF16)
    du_out[...] = du
    spread = mul(gown[edges:, :], du).astype(BF16)
    da = (mul_t(spread, w_fold[...]) * s_in[at_edges, :].astype(F32)).astype(BF16)
    da_out[...] = da
    es = mul_t(da, w_send[...]).astype(BF16)
    es_out[...] = es
    halo = mul(ghalo_t[...], es).astype(BF16)
    to_inner[...] = halo[:block]
    to_outer[...] = halo[block:]


def backward_own_kernel(kept, take, *refs):
    _, w_recv, w_node, _ = quarters(take[0])
    first, refs = refs[:kept], refs[kept:]
    *beside, c, du, da, es, gown_t, out = refs
    er = mul_t(da[...], w_recv[...]).astype(BF16)
    both = jnp.concatenate([es[...], er], axis=0)
    total = c[...] + mul_t(du[...], w_node[...]) + mul(gown_t[...], both)
    if first:
        _, other, lists = first
        [inner] = beside
        block = inner.shape[0]
        at = lists[INNER : INNER + 1, :1]
        value = inner[...].astype(F32)
        total = total + jnp.concatenate(
            [jnp.where(at == number, value, 0.0) for number in range(total.shape[0] // block)], axis=0
        )
        out[total.shape[0] :, :] = other[...]
    out[: total.shape[0], :] = total.astype(out.dtype)


def add_kernel(lists, value, inner, outer, other, out, total):
    @pl.when(here_is(1))
    def _():
        rows = value.shape[0]
        total[...] = value[...].astype(F32)
        add_listed(lists[INNER : INNER + 1, :1], total, inner[...].astype(F32), inner.shape[0])
        add_listed(lists[OUTER : OUTER + 1, :1], total, outer[...].astype(F32), outer.shape[0])
        out[:rows, :] = total[...].astype(BF16)
        out[rows:, :] = other[...]


def place_kernel(lists, outer, out):
    block = outer.shape[0]
    at = lists[OUTER : OUTER + 1, :1]
    value = jnp.where(here_is(0), outer[...].astype(F32), 0.0)
    for number in range(out.shape[0] // block):
        out[number * block : (number + 1) * block, :] = jnp.where(at == number, value, 0.0)


def last_kernel(ends, placed, first_home, second_home, grads, home, turned):
    rows = placed.shape[0]
    grads[:rows, :] = (ends[:rows, :].astype(F32) + placed[...]).astype(BF16)
    grads[rows:, :] = ends[rows:, :]

    @pl.when(here_is(0))
    def _():
        home[...] = first_home[...]

    @pl.when(jnp.logical_not(here_is(0)))
    def _():
        home[...] = second_home[...]

    for place, value in enumerate((home, grads)):
        for parity in range(2):

            @pl.when(here_is(parity=1 - parity))
            def _(value=value, place=place, parity=parity):
                turned[place * rows : (place + 1) * rows, :] = value[parity * rows : (parity + 1) * rows, :]


def write_kernel(home, grads, arrived, out_home, out_grads, sems):
    core = lax.axis_index("pipe") % 2
    rows = home.shape[0] // 2
    copies = []
    for place, (value, out) in enumerate(((home, out_home), (grads, out_grads))):
        own = value.at[pl.ds(pl.multiple_of(core * rows, rows), rows), :]
        other = arrived.at[pl.ds(place * rows, rows), :]
        copies.append(pltpu.make_async_copy(own, out.at[0, core], sems.at[2 * place]))
        copies.append(pltpu.make_async_copy(other, out.at[0, 1 - core], sems.at[2 * place + 1]))
    for copy in copies:
        copy.start()
    for copy in copies:
        copy.wait()


def run(kernel, operands, outs, spaces=(), aliases=None, out_spaces=(), scratch=(), cost=1, vmem=12):
    spaces = tuple(spaces) + (pltpu.VMEM,) * (len(operands) - len(spaces))
    out_spaces = tuple(out_spaces) + (pltpu.VMEM,) * (len(outs) - len(out_spaces))
    return pl.pallas_call(
        kernel,
        out_shape=[jax.ShapeDtypeStruct(s, t) for s, t in outs],
        in_specs=[pl.BlockSpec(memory_space=space) for space in spaces],
        out_specs=[pl.BlockSpec(memory_space=space) for space in out_spaces],
        scratch_shapes=list(scratch),
        input_output_aliases=aliases or {},
        compiler_params=pltpu.CompilerParams(vmem_limit_bytes=vmem * 2**20),
        cost_estimate=pl.CostEstimate(flops=cost, bytes_accessed=1, transcendentals=0),
    )(*operands)


def run_section(body, plane, matrices, operands, outs, elsewhere=None, cost=1):
    elsewhere = elsewhere or {}

    def kernel(*refs):
        take, rest = refs[: len(matrices)], refs[len(matrices) :]

        @pl.when(here_is(plane))
        def _():
            body(take, *rest)

        if elsewhere:

            @pl.when(jnp.logical_not(here_is(plane)))
            def _():
                for source, target in elsewhere.items():
                    rest[target][...] = rest[source][...]

    return run(kernel, tuple(matrices) + tuple(operands), outs, cost=cost)


def shards(
    inputs,
    cotangent,
    w_send,
    w_recv,
    w_message,
    w_node,
    w_aggregate,
    gains,
    edge_send,
    edge_recv,
    edge_count,
    halo_send,
):
    sections = lax.axis_size("pipe")
    pairs_total = lax.axis_size("dom") // 2
    phase = lax.axis_index("pipe")
    y = lax.rem(lax.axis_index("dom"), 2)
    plane_here = phase // 2
    rows, latent = inputs.shape[1:]
    edge_blocks, block = edge_send.shape
    edges = edge_blocks * block

    def send(value, rule):
        table = []
        for z in range(pairs_total):
            for which in range(2):
                for x in range(sections // 2):
                    for c in range(2):
                        if (target := rule(z, which, x, c)) is None:
                            continue
                        tz, ty, tx, tc = target
                        target = (2 * (tz % pairs_total) + ty) * sections + 2 * (tx % (sections // 2)) + tc
                        table.append(((2 * z + which) * sections + 2 * x + c, target))
        return lax.ppermute(value, AXES, table)

    def flip_y(value):
        return send(value, lambda z, y, x, c: (z, 1 - y, x, c))

    def flip_core(value):
        return send(value, lambda z, y, x, c: (z, y, x, 1 - c))

    def to_home(value):
        return send(value, lambda z, y, x, c: (z, c, x, y))

    def towards(value, side, step):
        if side == INNER:
            return send(value, lambda z, y, x, c: (z, y, x + step, 1 - c))
        return send(value, lambda z, y, x, c: (z + 2 * c - 1, y, x + step, 1 - c))

    wide = (rows, latent)
    edge_wide = (edges, latent)
    narrow = (block, latent)
    unit = 2 * rows * latent * latent
    dma = pltpu.SemaphoreType.DMA

    here, there, boundary, weights, packed = run(
        prepare_kernel,
        (edge_count, jnp.swapaxes(halo_send, 1, 2), inputs, cotangent, edge_send, edge_recv)
        + (w_send[0], w_recv[0], w_node[0], w_message[0], w_aggregate[0]),
        [
            (wide, BF16),
            (wide, BF16),
            (narrow, BF16),
            ((4 * latent, latent), BF16),
            ((3, 8, block), jnp.int32),
        ],
        spaces=(pltpu.SMEM, pltpu.SMEM) + (pltpu.HBM,) * 9,
        scratch=[pltpu.VMEM((2, latent, latent), BF16), pltpu.VMEM((latent, latent), BF16), dma((5,)), dma((6,))],
        vmem=56,
    )
    packed_there = send(packed, lambda z, y, x, c: (z, 1 - y, x, 1 - c))
    there = flip_y(there)
    outer = send(boundary, lambda z, y, x, c: (z + 2 * y - 1, c, x, 1 - y))
    even, odd = run(arrange_kernel, (weights, flip_core(weights)), [((4 * latent, latent), BF16)] * 2)
    gain_even, gain_odd = run(arrange_kernel, (gains, flip_core(gains)), [((1, latent), F32)] * 2)
    matrices = ((even, gain_even), (odd, gain_odd))

    gown, gown_t, ghalo, ghalo_t, lists, mate, home_lists = run(
        functools.partial(graph_kernel, edge_blocks),
        (even, packed, packed_there),
        [
            ((2 * edges, rows), BF16),
            ((rows, 2 * edges), BF16),
            ((edges, 2 * block), BF16),
            ((2 * block, edges), BF16),
            ((2, block), jnp.int32),
            ((1, block), jnp.int32),
            ((2, block), jnp.int32),
        ],
    )
    hidden, inner = run(entry_kernel, (mate, here, there), [(wide, BF16), (narrow, BF16)])
    upstream = hidden

    def home_of_plane(value, plane):
        return send(value, lambda z, y, x, c: (z, c, x, y) if x == plane else None)

    saved = ()
    arrived = ()
    for tick in range(sections):
        plane, parity = tick // 2, tick % 2
        packed, gain = matrices[parity]
        a_own, u_own = run_section(
            forward_own_kernel, plane, (packed,), (hidden, gown) + arrived, [(edge_wide, F32), (wide, F32)], cost=BESIDE
        )
        to_send = [(narrow, BF16)] * 2 if tick < sections - 1 else []
        hidden, a, u, *to = run_section(
            forward_kernel,
            plane,
            (packed, gain),
            (lists, hidden, a_own, u_own, inner, outer, ghalo, gown_t),
            [(wide, BF16), (edge_wide, F32), (wide, F32)] + to_send,
        )
        produced = hidden
        if to:
            step = (tick + 1) // 2 - plane
            outer = towards(to[OUTER], OUTER, step)
            if step:
                hidden = send(hidden, lambda z, y, x, c: (z, y, x + 1, c))
            inner = towards(to[INNER], INNER, step)
            arrived = () if step else (inner,)
        saved = run(
            functools.partial(save_kernel, plane, parity),
            (a, u, produced) + tuple(saved),
            [((2 * rows, latent), BF16), ((2 * rows, latent), BF16), ((2 * edges, latent), BF16), ((2 * rows, latent), BF16)],
            aliases={3 + k: k for k in range(4)} if saved else None,
            cost=BESIDE,
        )

    *states, both = saved
    inner = outer = None
    handed = ()
    finished = {}
    for tick in range(sections - 1, -1, -1):
        plane, parity = tick // 2, tick % 2
        packed, gain = matrices[parity]
        step = (tick - 1) // 2 - plane if tick else 0
        halo_in = inner is not None
        finish = halo_in and tick % 2 == 0
        outs = [(wide, F32), (wide, BF16), (edge_wide, BF16), (edge_wide, BF16)]
        outs += [(wide, BF16)] if finish else []
        outs += [(narrow, BF16)] * 2
        kept = handed if tick == 1 else ()
        c, du, da, es, *done, to_inner, to_outer = run_section(
            functools.partial(backward_kernel, halo_in, finish, parity, len(kept)),
            plane,
            (packed, gain),
            kept + (lists, upstream) + ((inner, outer) if halo_in else ()) + tuple(states) + (gown, ghalo_t),
            outs,
            elsewhere={0: -2, 1: -1} if tick == 1 else {},
        )
        if done:
            finished[tick + 1] = done[0]
        if step == 0:
            inner = towards(to_inner, INNER, 0)
            if tick:
                outer = towards(to_outer, OUTER, 0)
        else:
            handed = (to_inner, to_outer)
            outer = towards(to_outer, OUTER, step)
            inner = towards(to_inner, INNER, step)
        beside = (inner,) if step == 0 else (first_home,)
        kept = (finished[2], finished[1], lists) if tick == 0 else ()
        [upstream] = run_section(
            functools.partial(backward_own_kernel, len(kept)),
            plane,
            (packed,),
            kept + beside + (c, du, da, es, gown_t),
            [((2 * rows, latent), BF16) if tick == 0 else (wide, BF16 if step else F32)],
            elsewhere={0: -1} if tick == 0 else {},
            cost=BESIDE if tick else 1,
        )
        if tick == sections - 1:
            first_home, upstream = lax.optimization_barrier((both, upstream))
            first_home = home_of_plane(first_home, 0)
        if step:
            own = upstream
            upstream = send(upstream, lambda z, y, x, c: (z, y, x + 1, c))
        elif tick == 1:
            second_home, upstream = lax.optimization_barrier((both, upstream))
            second_home = home_of_plane(second_home, 1)
            [finished[2]] = run(
                add_kernel,
                (lists, own, inner, outer, finished[3]),
                [((2 * rows, latent), BF16)],
                scratch=[pltpu.VMEM(wide, F32)],
            )

    final_outer = send(to_outer, lambda z, y, x, c: (z + 2 * c - 1, 1 - c, x, y))
    ends = to_home(upstream)
    [placed] = run(place_kernel, (home_lists, final_outer), [(wide, F32)], cost=LONG)
    grads, home, turned = run(last_kernel, (ends, placed, first_home, second_home), [((2 * rows, latent), BF16)] * 3)
    return tuple(
        run(
            write_kernel,
            (home, grads, flip_core(turned)),
            [((1, 2) + wide, BF16)] * 2,
            out_spaces=(pltpu.HBM,) * 2,
            scratch=[dma((4,))],
        )
    )


def solution(mesh):
    in_specs = (
        P(None, "dom", None),
        P(None, "dom", None),
        P("pipe", None, None),
        P("pipe", None, None),
        P("pipe", None, None),
        P("pipe", None, None),
        P("pipe", None, None),
        P("pipe", None),
        P("dom", None),
        P("dom", None),
        P("dom"),
        P("dom", None, None),
    )
    out_specs = (P("pipe", None, "dom", None), P("pipe", None, "dom", None))
    return jax.shard_map(shards, mesh=mesh, in_specs=in_specs, out_specs=out_specs, check_vma=False)
```

time: 110 us -> 102 us (0.927)
  waiting for transfers between devices: 57.7 us -> 33.1 us
  starting transfers between devices: 31 us -> 49.6 us
  local copies, waits for them, and re-layouts: 6.37 us -> 1.6 us
  Pallas kernels: 12.5 us -> 14.7 us
    ppermute x32 -> x25, waiting for transfers between devices: 57.7 us -> 33.1 us  [send(): return lax.ppermute(value, AXES, table)]
    ppermute x32 -> x25, starting transfers between devices: 31 us -> 49.6 us  [send(): return lax.ppermute(value, AXES, table)]
    unnamed x23 -> x8, local copies, waits for them, and re-layouts: 6.33 us -> 1.6 us
    pallas_call x34 -> x29, Pallas kernels: 12.5 us -> 14.7 us  [run(): pl.pallas_call(kernel, out_shape=[jax.ShapeDtypeStruct(s, t) for s, t in...]
  transfers between devices with their start and end apart: 32 -> 25, of which waited for: 14 -> 11; matrix products, arithmetic and copies ran while one was open for 0% -> 0% of each run, Pallas kernels for 6% -> 5%
where the time goes in v4:
time: 102 us; the launch traced here: 100 us
  starting transfers between devices  49.6 us (49%)
  waiting for transfers between devices  33.1 us (32%)
  Pallas kernels  14.7 us (14%)
  local copies, waits for them, and re-layouts  1.6 us (2%)
  between operations  1.06 us (1%)
    ppermute x25, starting transfers between devices, send(): return lax.ppermute(value, AXES, table)  49.6 us
    ppermute x25, waiting for transfers between devices, send(): return lax.ppermute(value, AXES, table)  33.1 us
    pallas_call x29, Pallas kernels, run(): pl.pallas_call(kernel, out_shape=[jax.ShapeDtypeStruct(s, t) for s, t in...  14.7 us
  transfers between devices with their start and end apart: 25, of which 11 were waited for; matrix products, arithmetic and copies ran while one was open for 0% of the time, Pallas kernels for 5%

profile of v4, /device:TPU:0, one launch (start us, length us, event | category | flops | bytes accessed | tf_op | source)
XLA Modules:
  0.0 100.1 jit_solution(12348287761598765201)
XLA Ops:
  0.6 4.2 %shard_map.131 = (bf16[256,512]{1,0:T(8,128)(2,1)}, bf16[256,512]{1,0:T(8,128)(2,1)}, bf16[128,512]{1,0:T(8,128)(2,1)}, bf16[2048,512]{1,0:T(8,128)(2,1)}, s32[3,8,128]{2,1,0:T(8,128)}) custom-call(s32[2]{0:T(128)} %count.1, s32[1,1,2]{2,1,0:T(1,128)} %bitcast.11, bf16[2,256,512]{2,1,0:T(8,128)(2,1)} %inputs.1, bf16[2,256,512]{2,1,0:T(8,128)(2,1)} %cotangent.1, ...), custom_call_target="tpu_custom_call" | custom-call | flops 1 | bytes 1 | tf_op jit(solution)/shard_map/pallas_call | solution.py:368
  5.4 2.6 %collective-permute-start.3 = (bf16[256,512]{1,0:T(8,128)(2,1)}, bf16[256,512]{1,0:T(8,128)(2,1)S(1)}, u32[]{:S(2)}, u32[]{:S(2)}) collective-permute-start(bf16[256,512]{1,0:T(8,128)(2,1)} %get-tuple-element.104), channel_id=1, source_target_pairs={{0,4},{1,5},{2,6},{3,7},{4,0},{5,1},{6,2},{7,3},{8,12},{9,13},{10,... | collective-permute-start | bytes 786440 | tf_op jit(solution)/shard_map/ppermute | solution.py:434
  8.2 3.8 %collective-permute-start.4 = (bf16[128,512]{1,0:T(8,128)(2,1)}, bf16[128,512]{1,0:T(8,128)(2,1)S(1)}, u32[]{:S(2)}, u32[]{:S(2)}) collective-permute-start(bf16[128,512]{1,0:T(8,128)(2,1)} %get-tuple-element.110), channel_id=1, source_target_pairs={{0,25},{1,29},{2,27},{3,31},{4,8},{5,12},{6,10},{7,14},{8,1},{9,5}... | collective-permute-start | bytes 393224 | tf_op jit(solution)/shard_map/ppermute | solution.py:434
  12.0 1.6 %copy-done = bf16[2048,512]{1,0:T(8,128)(2,1)S(1)} copy-done((bf16[2048,512]{1,0:T(8,128)(2,1)S(1)}, bf16[2048,512]{1,0:T(8,128)(2,1)}, u32[]{:S(2)}) %copy-start) | copy-done | bytes 2097176
  13.9 2.2 %collective-permute-done.1.packed_there = s32[3,8,128]{2,1,0:T(8,128)S(1)} collective-permute-done((s32[3,8,128]{2,1,0:T(8,128)}, s32[3,8,128]{2,1,0:T(8,128)S(1)}, u32[]{:S(2)}, u32[]{:S(2)}) %collective-permute-start.1) | collective-permute-done | bytes 12320 | tf_op jit(solution)/shard_map/ppermute | solution.py:434
  18.6 4.2 %collective-permute-start.6 = (bf16[128,512]{1,0:T(8,128)(2,1)S(1)}, bf16[128,512]{1,0:T(8,128)(2,1)S(1)}, u32[]{:S(2)}, u32[]{:S(2)}) collective-permute-start(bf16[128,512]{1,0:T(8,128)(2,1)S(1)} %get-tuple-element.117), channel_id=1, source_target_pairs={{0,25},{1,8},{2,27},{3,10},{4,29},{5,12},{6,31},{7,14},{8,1},{9,16... | collective-permute-start | bytes 393224 | tf_op jit(solution)/shard_map/ppermute | solution.py:434
  24.1 2.1 %collective-permute-done.6.refs_7_ = bf16[128,512]{1,0:T(8,128)(2,1)S(1)} collective-permute-done((bf16[128,512]{1,0:T(8,128)(2,1)S(1)}, bf16[128,512]{1,0:T(8,128)(2,1)S(1)}, u32[]{:S(2)}, u32[]{:S(2)}) %collective-permute-start.6) | collective-permute-done | bytes 131104 | tf_op jit(solution)/shard_map/ppermute | solution.py:434
  27.4 3.9 %collective-permute-start.9 = (bf16[128,512]{1,0:T(8,128)(2,1)S(1)}, bf16[128,512]{1,0:T(8,128)(2,1)S(1)}, u32[]{:S(2)}, u32[]{:S(2)}) collective-permute-start(bf16[128,512]{1,0:T(8,128)(2,1)S(1)} %get-tuple-element.122), channel_id=1, source_target_pairs={{0,27},{1,10},{2,25},{3,8},{4,31},{5,14},{6,29},{7,12},{8,3},{9,18... | collective-permute-start | bytes 393224 | tf_op jit(solution)/shard_map/ppermute | solution.py:434
  31.9 5.6 %collective-permute-done.7.refs_1_.refs_3_ = bf16[256,512]{1,0:T(8,128)(2,1)S(1)} collective-permute-done((bf16[256,512]{1,0:T(8,128)(2,1)S(1)}, bf16[256,512]{1,0:T(8,128)(2,1)S(1)}, u32[]{:S(2)}, u32[]{:S(2)}) %collective-permute-start.7) | collective-permute-done | bytes 262176 | tf_op jit(solution)/shard_map/ppermute | solution.py:434
  37.5 1.2 %collective-permute-start.10 = (bf16[128,512]{1,0:T(8,128)(2,1)S(1)}, bf16[128,512]{1,0:T(8,128)(2,1)S(1)}, u32[]{:S(2)}, u32[]{:S(2)}) collective-permute-start(bf16[128,512]{1,0:T(8,128)(2,1)S(1)} %get-tuple-element.124), channel_id=1, source_target_pairs={{0,1},{1,0},{2,3},{3,2},{4,5},{5,4},{6,7},{7,6},{8,9},{9,8},{10,11... | collective-permute-start | bytes 393224 | tf_op jit(solution)/shard_map/ppermute | solution.py:434
  38.7 4.9 %collective-permute-start.11 = (bf16[128,512]{1,0:T(8,128)(2,1)S(1)}, bf16[128,512]{1,0:T(8,128)(2,1)S(1)}, u32[]{:S(2)}, u32[]{:S(2)}) collective-permute-start(bf16[128,512]{1,0:T(8,128)(2,1)S(1)} %get-tuple-element.127), channel_id=1, source_target_pairs={{0,25},{1,8},{2,27},{3,10},{4,29},{5,12},{6,31},{7,14},{8,1},{9,16... | collective-permute-start | bytes 393224 | tf_op jit(solution)/shard_map/ppermute | solution.py:434
  43.6 3.8 %collective-permute-done.11.refs_7_ = bf16[128,512]{1,0:T(8,128)(2,1)S(1)} collective-permute-done((bf16[128,512]{1,0:T(8,128)(2,1)S(1)}, bf16[128,512]{1,0:T(8,128)(2,1)S(1)}, u32[]{:S(2)}, u32[]{:S(2)}) %collective-permute-start.11) | collective-permute-done | bytes 131104 | tf_op jit(solution)/shard_map/ppermute | solution.py:434
  47.4 1.3 %collective-permute-done.12.refs_1_.refs_4_ = bf16[128,512]{1,0:T(8,128)(2,1)S(1)} collective-permute-done((bf16[128,512]{1,0:T(8,128)(2,1)S(1)}, bf16[128,512]{1,0:T(8,128)(2,1)S(1)}, u32[]{:S(2)}, u32[]{:S(2)}) %collective-permute-start.12) | collective-permute-done | bytes 131104 | tf_op jit(solution)/shard_map/ppermute | solution.py:434
  49.4 5.0 %collective-permute-start.14 = (bf16[128,512]{1,0:T(8,128)(2,1)S(1)}, bf16[128,512]{1,0:T(8,128)(2,1)S(1)}, u32[]{:S(2)}, u32[]{:S(2)}) collective-permute-start(bf16[128,512]{1,0:T(8,128)(2,1)S(1)} %get-tuple-element.161), channel_id=1, source_target_pairs={{0,25},{1,8},{2,27},{3,10},{4,29},{5,12},{6,31},{7,14},{8,1},{9,16... | collective-permute-start | bytes 393224 | tf_op jit(solution)/shard_map/ppermute | solution.py:434
  54.4 3.7 %collective-permute-done.14.refs_5_ = bf16[128,512]{1,0:T(8,128)(2,1)S(1)} collective-permute-done((bf16[128,512]{1,0:T(8,128)(2,1)S(1)}, bf16[128,512]{1,0:T(8,128)(2,1)S(1)}, u32[]{:S(2)}, u32[]{:S(2)}) %collective-permute-start.14) | collective-permute-done | bytes 131104 | tf_op jit(solution)/shard_map/ppermute | solution.py:434
  58.1 4.9 %collective-permute-start.15 = (bf16[256,512]{1,0:T(8,128)(2,1)S(1)}, bf16[256,512]{1,0:T(8,128)(2,1)S(1)}, u32[]{:S(2)}, u32[]{:S(2)}) collective-permute-start(bf16[256,512]{1,0:T(8,128)(2,1)S(1)} %shard_map.151.value), channel_id=1, source_target_pairs={{0,2},{1,3},{2,0},{3,1},{4,6},{5,7},{6,4},{7,5},{8,10},{9,11},{10,... | collective-permute-start | bytes 786440 | tf_op jit(solution)/shard_map/ppermute | solution.py:434
  63.0 1.4 %collective-permute-start.17 = (bf16[128,512]{1,0:T(8,128)(2,1)S(1)}, bf16[128,512]{1,0:T(8,128)(2,1)S(1)}, u32[]{:S(2)}, u32[]{:S(2)}) collective-permute-start(bf16[128,512]{1,0:T(8,128)(2,1)S(1)} %get-tuple-element.167.refs_3_), channel_id=1, source_target_pairs={{0,27},{1,10},{2,25},{3,8},{4,31},{5,14},{6,29},{7,12},{8,3},{9,18... | collective-permute-start | bytes 393224 | tf_op jit(solution)/shard_map/ppermute | solution.py:434
  64.4 7.6 %collective-permute-done.16.refs_6_ = bf16[128,512]{1,0:T(8,128)(2,1)S(1)} collective-permute-done((bf16[128,512]{1,0:T(8,128)(2,1)S(1)}, bf16[128,512]{1,0:T(8,128)(2,1)S(1)}, u32[]{:S(2)}, u32[]{:S(2)}) %collective-permute-start.16) | collective-permute-done | bytes 131104 | tf_op jit(solution)/shard_map/ppermute | solution.py:434
  74.3 2.9 %collective-permute-start.19 = (bf16[128,512]{1,0:T(8,128)(2,1)S(1)}, bf16[128,512]{1,0:T(8,128)(2,1)S(1)}, u32[]{:S(2)}, u32[]{:S(2)}) collective-permute-start(bf16[128,512]{1,0:T(8,128)(2,1)S(1)} %get-tuple-element.169), channel_id=1, source_target_pairs={{0,25},{1,8},{2,27},{3,10},{4,29},{5,12},{6,31},{7,14},{8,1},{9,16... | collective-permute-start | bytes 393224 | tf_op jit(solution)/shard_map/ppermute | solution.py:434
  77.8 3.7 %collective-permute-done.19.outer.refs_5_ = bf16[128,512]{1,0:T(8,128)(2,1)S(1)} collective-permute-done((bf16[128,512]{1,0:T(8,128)(2,1)S(1)}, bf16[128,512]{1,0:T(8,128)(2,1)S(1)}, u32[]{:S(2)}, u32[]{:S(2)}) %collective-permute-start.19) | collective-permute-done | bytes 131104 | tf_op jit(solution)/shard_map/ppermute | solution.py:434
  82.8 3.9 %collective-permute-start.22 = (bf16[128,512]{1,0:T(8,128)(2,1)S(1)}, bf16[128,512]{1,0:T(8,128)(2,1)S(1)}, u32[]{:S(2)}, u32[]{:S(2)}) collective-permute-start(bf16[128,512]{1,0:T(8,128)(2,1)S(1)} %get-tuple-element.183), channel_id=1, source_target_pairs={{0,28},{1,8},{2,30},{3,10},{4,29},{5,9},{6,31},{7,11},{8,4},{9,16}... | collective-permute-start | bytes 393224 | tf_op jit(solution)/shard_map/ppermute | solution.py:434
  88.7 1.6 %collective-permute-done.22.outer = bf16[128,512]{1,0:T(8,128)(2,1)S(1)} collective-permute-done((bf16[128,512]{1,0:T(8,128)(2,1)S(1)}, bf16[128,512]{1,0:T(8,128)(2,1)S(1)}, u32[]{:S(2)}, u32[]{:S(2)}) %collective-permute-start.22) | collective-permute-done | bytes 131104 | tf_op jit(solution)/shard_map/ppermute | solution.py:434
  90.6 6.8 %collective-permute-start.24 = (bf16[512,512]{1,0:T(8,128)(2,1)S(1)}, bf16[512,512]{1,0:T(8,128)(2,1)S(1)}, u32[]{:S(2)}, u32[]{:S(2)}) collective-permute-start(bf16[512,512]{1,0:T(8,128)(2,1)S(1)} %get-tuple-element.187), channel_id=1, source_target_pairs={{0,1},{1,0},{2,3},{3,2},{4,5},{5,4},{6,7},{7,6},{8,9},{9,8},{10,11... | collective-permute-start | bytes 1572872 | tf_op jit(solution)/shard_map/ppermute | solution.py:434
  97.4 1.5 %collective-permute-done.24.arrived = bf16[512,512]{1,0:T(8,128)(2,1)S(1)} collective-permute-done((bf16[512,512]{1,0:T(8,128)(2,1)S(1)}, bf16[512,512]{1,0:T(8,128)(2,1)S(1)}, u32[]{:S(2)}, u32[]{:S(2)}) %collective-permute-start.24) | collective-permute-done | bytes 524320 | tf_op jit(solution)/shard_map/ppermute | solution.py:434
  (63 shorter events, 14.7 us)
Async XLA Ops:
  4.9 7.1 %collective-permute-start = (bf16[2048,512]{1,0:T(8,128)(2,1)}, bf16[2048,512]{1,0:T(8,128)(2,1)S(1)}, u32[]{:S(2)}, u32[]{:S(2)}) collective-permute-start(bf16[2048,512]{1,0:T(8,128)(2,1)} %get-tuple-element.95.mine), channel_id=1, source_target_pairs={{0,1},{1,0},{2,3},{3,2},{4,5},{5,4},{6,7},{7,6},{8,9},{9,8},{10,11... | collective-permute-start | bytes 6291464 | tf_op jit(solution)/shard_map/ppermute | solution.py:434
  5.4 11.0 %collective-permute-start.3 = (bf16[256,512]{1,0:T(8,128)(2,1)}, bf16[256,512]{1,0:T(8,128)(2,1)S(1)}, u32[]{:S(2)}, u32[]{:S(2)}) collective-permute-start(bf16[256,512]{1,0:T(8,128)(2,1)} %get-tuple-element.104), channel_id=1, source_target_pairs={{0,4},{1,5},{2,6},{3,7},{4,0},{5,1},{6,2},{7,3},{8,12},{9,13},{10,... | collective-permute-start | bytes 786440 | tf_op jit(solution)/shard_map/ppermute | solution.py:434
  8.0 8.1 %collective-permute-start.1 = (s32[3,8,128]{2,1,0:T(8,128)}, s32[3,8,128]{2,1,0:T(8,128)S(1)}, u32[]{:S(2)}, u32[]{:S(2)}) collective-permute-start(s32[3,8,128]{2,1,0:T(8,128)} %get-tuple-element.97.packed), channel_id=1, source_target_pairs={{0,5},{1,4},{2,7},{3,6},{4,1},{5,0},{6,3},{7,2},{8,13},{9,12},{10,... | collective-permute-start | bytes 36872 | tf_op jit(solution)/shard_map/ppermute | solution.py:434
  8.1 3.9 %collective-permute-start.2 = (f32[1,512]{1,0:T(1,128)S(1)}, f32[1,512]{1,0:T(1,128)S(1)}, u32[]{:S(2)}, u32[]{:S(2)}) collective-permute-start(f32[1,512]{1,0:T(1,128)S(1)} %copy-done.3), channel_id=1, source_target_pairs={{0,1},{1,0},{2,3},{3,2},{4,5},{5,4},{6,7},{7,6},{8,9},{9,8},{10,11... | collective-permute-start | bytes 6152 | tf_op jit(solution)/shard_map/ppermute | solution.py:434
  8.2 9.2 %collective-permute-start.4 = (bf16[128,512]{1,0:T(8,128)(2,1)}, bf16[128,512]{1,0:T(8,128)(2,1)S(1)}, u32[]{:S(2)}, u32[]{:S(2)}) collective-permute-start(bf16[128,512]{1,0:T(8,128)(2,1)} %get-tuple-element.110), channel_id=1, source_target_pairs={{0,25},{1,29},{2,27},{3,31},{4,8},{5,12},{6,10},{7,14},{8,1},{9,5}... | collective-permute-start | bytes 393224 | tf_op jit(solution)/shard_map/ppermute | solution.py:434
  18.5 4.7 %collective-permute-start.5 = (bf16[128,512]{1,0:T(8,128)(2,1)S(1)}, bf16[128,512]{1,0:T(8,128)(2,1)S(1)}, u32[]{:S(2)}, u32[]{:S(2)}) collective-permute-start(bf16[128,512]{1,0:T(8,128)(2,1)S(1)} %get-tuple-element.114), channel_id=1, source_target_pairs={{0,1},{1,0},{2,3},{3,2},{4,5},{5,4},{6,7},{7,6},{8,9},{9,8},{10,11... | collective-permute-start | bytes 393224 | tf_op jit(solution)/shard_map/ppermute | solution.py:434
  18.6 7.5 %collective-permute-start.6 = (bf16[128,512]{1,0:T(8,128)(2,1)S(1)}, bf16[128,512]{1,0:T(8,128)(2,1)S(1)}, u32[]{:S(2)}, u32[]{:S(2)}) collective-permute-start(bf16[128,512]{1,0:T(8,128)(2,1)S(1)} %get-tuple-element.117), channel_id=1, source_target_pairs={{0,25},{1,8},{2,27},{3,10},{4,29},{5,12},{6,31},{7,14},{8,1},{9,16... | collective-permute-start | bytes 393224 | tf_op jit(solution)/shard_map/ppermute | solution.py:434
  27.3 10.2 %collective-permute-start.7 = (bf16[256,512]{1,0:T(8,128)(2,1)S(1)}, bf16[256,512]{1,0:T(8,128)(2,1)S(1)}, u32[]{:S(2)}, u32[]{:S(2)}) collective-permute-start(bf16[256,512]{1,0:T(8,128)(2,1)S(1)} %get-tuple-element.118.h), channel_id=1, source_target_pairs={{0,2},{1,3},{2,0},{3,1},{4,6},{5,7},{6,4},{7,5},{8,10},{9,11},{10,... | collective-permute-start | bytes 786440 | tf_op jit(solution)/shard_map/ppermute | solution.py:434
  27.4 10.1 %collective-permute-start.8 = (bf16[128,512]{1,0:T(8,128)(2,1)S(1)}, bf16[128,512]{1,0:T(8,128)(2,1)S(1)}, u32[]{:S(2)}, u32[]{:S(2)}) collective-permute-start(bf16[128,512]{1,0:T(8,128)(2,1)S(1)} %get-tuple-element.121), channel_id=1, source_target_pairs={{0,3},{1,2},{2,1},{3,0},{4,7},{5,6},{6,5},{7,4},{8,11},{9,10},{10,... | collective-permute-start | bytes 393224 | tf_op jit(solution)/shard_map/ppermute | solution.py:434
  27.4 10.0 %collective-permute-start.9 = (bf16[128,512]{1,0:T(8,128)(2,1)S(1)}, bf16[128,512]{1,0:T(8,128)(2,1)S(1)}, u32[]{:S(2)}, u32[]{:S(2)}) collective-permute-start(bf16[128,512]{1,0:T(8,128)(2,1)S(1)} %get-tuple-element.122), channel_id=1, source_target_pairs={{0,27},{1,10},{2,25},{3,8},{4,31},{5,14},{6,29},{7,12},{8,3},{9,18... | collective-permute-start | bytes 393224 | tf_op jit(solution)/shard_map/ppermute | solution.py:434
  37.5 6.1 %collective-permute-start.10 = (bf16[128,512]{1,0:T(8,128)(2,1)S(1)}, bf16[128,512]{1,0:T(8,128)(2,1)S(1)}, u32[]{:S(2)}, u32[]{:S(2)}) collective-permute-start(bf16[128,512]{1,0:T(8,128)(2,1)S(1)} %get-tuple-element.124), channel_id=1, source_target_pairs={{0,1},{1,0},{2,3},{3,2},{4,5},{5,4},{6,7},{7,6},{8,9},{9,8},{10,11... | collective-permute-start | bytes 393224 | tf_op jit(solution)/shard_map/ppermute | solution.py:434
  38.7 8.7 %collective-permute-start.11 = (bf16[128,512]{1,0:T(8,128)(2,1)S(1)}, bf16[128,512]{1,0:T(8,128)(2,1)S(1)}, u32[]{:S(2)}, u32[]{:S(2)}) collective-permute-start(bf16[128,512]{1,0:T(8,128)(2,1)S(1)} %get-tuple-element.127), channel_id=1, source_target_pairs={{0,25},{1,8},{2,27},{3,10},{4,29},{5,12},{6,31},{7,14},{8,1},{9,16... | collective-permute-start | bytes 393224 | tf_op jit(solution)/shard_map/ppermute | solution.py:434
  48.7 9.3 %collective-permute-start.13 = (bf16[512,512]{1,0:T(8,128)(2,1)S(1)}, bf16[512,512]{1,0:T(8,128)(2,1)S(1)}, u32[]{:S(2)}, u32[]{:S(2)}) collective-permute-start(bf16[512,512]{1,0:T(8,128)(2,1)S(1)} %get-tuple-element.184), channel_id=1, source_target_pairs={{0,0},{1,4},{4,1},{5,5},{8,8},{9,12},{12,9},{13,13},{16,16},{17,20... | collective-permute-start | bytes 1572872 | tf_op jit(solution)/shard_map/ppermute | solution.py:434
  49.4 8.6 %collective-permute-start.14 = (bf16[128,512]{1,0:T(8,128)(2,1)S(1)}, bf16[128,512]{1,0:T(8,128)(2,1)S(1)}, u32[]{:S(2)}, u32[]{:S(2)}) collective-permute-start(bf16[128,512]{1,0:T(8,128)(2,1)S(1)} %get-tuple-element.161), channel_id=1, source_target_pairs={{0,25},{1,8},{2,27},{3,10},{4,29},{5,12},{6,31},{7,14},{8,1},{9,16... | collective-permute-start | bytes 393224 | tf_op jit(solution)/shard_map/ppermute | solution.py:434
  58.1 13.9 %collective-permute-start.15 = (bf16[256,512]{1,0:T(8,128)(2,1)S(1)}, bf16[256,512]{1,0:T(8,128)(2,1)S(1)}, u32[]{:S(2)}, u32[]{:S(2)}) collective-permute-start(bf16[256,512]{1,0:T(8,128)(2,1)S(1)} %shard_map.151.value), channel_id=1, source_target_pairs={{0,2},{1,3},{2,0},{3,1},{4,6},{5,7},{6,4},{7,5},{8,10},{9,11},{10,... | collective-permute-start | bytes 786440 | tf_op jit(solution)/shard_map/ppermute | solution.py:434
  63.0 9.0 %collective-permute-start.16 = (bf16[128,512]{1,0:T(8,128)(2,1)S(1)}, bf16[128,512]{1,0:T(8,128)(2,1)S(1)}, u32[]{:S(2)}, u32[]{:S(2)}) collective-permute-start(bf16[128,512]{1,0:T(8,128)(2,1)S(1)} %get-tuple-element.166.refs_2_), channel_id=1, source_target_pairs={{0,3},{1,2},{2,1},{3,0},{4,7},{5,6},{6,5},{7,4},{8,11},{9,10},{10,... | collective-permute-start | bytes 393224 | tf_op jit(solution)/shard_map/ppermute | solution.py:434
  63.0 9.0 %collective-permute-start.17 = (bf16[128,512]{1,0:T(8,128)(2,1)S(1)}, bf16[128,512]{1,0:T(8,128)(2,1)S(1)}, u32[]{:S(2)}, u32[]{:S(2)}) collective-permute-start(bf16[128,512]{1,0:T(8,128)(2,1)S(1)} %get-tuple-element.167.refs_3_), channel_id=1, source_target_pairs={{0,27},{1,10},{2,25},{3,8},{4,31},{5,14},{6,29},{7,12},{8,3},{9,18... | collective-permute-start | bytes 393224 | tf_op jit(solution)/shard_map/ppermute | solution.py:434
  73.2 4.0 %collective-permute-start.18 = (bf16[128,512]{1,0:T(8,128)(2,1)S(1)}, bf16[128,512]{1,0:T(8,128)(2,1)S(1)}, u32[]{:S(2)}, u32[]{:S(2)}) collective-permute-start(bf16[128,512]{1,0:T(8,128)(2,1)S(1)} %get-tuple-element.168), channel_id=1, source_target_pairs={{0,1},{1,0},{2,3},{3,2},{4,5},{5,4},{6,7},{7,6},{8,9},{9,8},{10,11... | collective-permute-start | bytes 393224 | tf_op jit(solution)/shard_map/ppermute | solution.py:434
  74.3 7.2 %collective-permute-start.19 = (bf16[128,512]{1,0:T(8,128)(2,1)S(1)}, bf16[128,512]{1,0:T(8,128)(2,1)S(1)}, u32[]{:S(2)}, u32[]{:S(2)}) collective-permute-start(bf16[128,512]{1,0:T(8,128)(2,1)S(1)} %get-tuple-element.169), channel_id=1, source_target_pairs={{0,25},{1,8},{2,27},{3,10},{4,29},{5,12},{6,31},{7,14},{8,1},{9,16... | collective-permute-start | bytes 393224 | tf_op jit(solution)/shard_map/ppermute | solution.py:434
  82.7 4.7 %collective-permute-start.20 = (bf16[128,512]{1,0:T(8,128)(2,1)S(1)}, bf16[128,512]{1,0:T(8,128)(2,1)S(1)}, u32[]{:S(2)}, u32[]{:S(2)}) collective-permute-start(bf16[128,512]{1,0:T(8,128)(2,1)S(1)} %get-tuple-element.177), channel_id=1, source_target_pairs={{0,1},{1,0},{2,3},{3,2},{4,5},{5,4},{6,7},{7,6},{8,9},{9,8},{10,11... | collective-permute-start | bytes 393224 | tf_op jit(solution)/shard_map/ppermute | solution.py:434
  82.8 7.5 %collective-permute-start.22 = (bf16[128,512]{1,0:T(8,128)(2,1)S(1)}, bf16[128,512]{1,0:T(8,128)(2,1)S(1)}, u32[]{:S(2)}, u32[]{:S(2)}) collective-permute-start(bf16[128,512]{1,0:T(8,128)(2,1)S(1)} %get-tuple-element.183), channel_id=1, source_target_pairs={{0,28},{1,8},{2,30},{3,10},{4,29},{5,9},{6,31},{7,11},{8,4},{9,16}... | collective-permute-start | bytes 393224 | tf_op jit(solution)/shard_map/ppermute | solution.py:434
  86.7 3.7 %collective-permute-start.23 = (bf16[512,512]{1,0:T(8,128)(2,1)S(1)}, bf16[512,512]{1,0:T(8,128)(2,1)S(1)}, u32[]{:S(2)}, u32[]{:S(2)}) collective-permute-start(bf16[512,512]{1,0:T(8,128)(2,1)S(1)} %get-tuple-element.184), channel_id=1, source_target_pairs={{2,2},{3,6},{6,3},{7,7},{10,10},{11,14},{14,11},{15,15},{18,18},{1... | collective-permute-start | bytes 1572872 | tf_op jit(solution)/shard_map/ppermute | solution.py:434
  88.0 2.4 %collective-permute-start.21 = (bf16[512,512]{1,0:T(8,128)(2,1)S(1)}, bf16[512,512]{1,0:T(8,128)(2,1)S(1)}, u32[]{:S(2)}, u32[]{:S(2)}) collective-permute-start(bf16[512,512]{1,0:T(8,128)(2,1)S(1)} %shard_map.156), channel_id=1, source_target_pairs={{0,0},{1,4},{2,2},{3,6},{4,1},{5,5},{6,3},{7,7},{8,8},{9,12},{10,1... | collective-permute-start | bytes 1572872 | tf_op jit(solution)/shard_map/ppermute | solution.py:434
  90.6 8.4 %collective-permute-start.24 = (bf16[512,512]{1,0:T(8,128)(2,1)S(1)}, bf16[512,512]{1,0:T(8,128)(2,1)S(1)}, u32[]{:S(2)}, u32[]{:S(2)}) collective-permute-start(bf16[512,512]{1,0:T(8,128)(2,1)S(1)} %get-tuple-element.187), channel_id=1, source_target_pairs={{0,1},{1,0},{2,3},{3,2},{4,5},{5,4},{6,7},{7,6},{8,9},{9,8},{10,11... | collective-permute-start | bytes 1572872 | tf_op jit(solution)/shard_map/ppermute | solution.py:434
  (5 other events, 15.3 us)

commit v5 on v4

--- a/solution.py
+++ b/solution.py
@@ -290,75 +290,92 @@
 def backward_own_kernel(kept, take, *refs):
     _, w_recv, w_node, _ = quarters(take[0])
     first, refs = refs[:kept], refs[kept:]
-    *beside, c, du, da, es, gown_t, out = refs
+    refs, out = (refs[:-2], refs[-2:]) if first else (refs[:-1], refs[-1:])
+    *beside, c, du, da, es, gown_t = refs
     er = mul_t(da[...], w_recv[...]).astype(BF16)
     both = jnp.concatenate([es[...], er], axis=0)
     total = c[...] + mul_t(du[...], w_node[...]) + mul(gown_t[...], both)
-    if first:
-        _, other, lists = first
-        [inner] = beside
-        block = inner.shape[0]
-        at = lists[INNER : INNER + 1, :1]
-        value = inner[...].astype(F32)
-        total = total + jnp.concatenate(
-            [jnp.where(at == number, value, 0.0) for number in range(total.shape[0] // block)], axis=0
-        )
-        out[total.shape[0] :, :] = other[...]
-    out[: total.shape[0], :] = total.astype(out.dtype)
-
-
-def add_kernel(lists, value, inner, outer, other, out, total):
+    if not first:
+        out[0][...] = total.astype(out[0].dtype)
+        return
+    *_, other, lists = first
+    [inner] = beside
+    block = inner.shape[0]
+    at = lists[INNER : INNER + 1, :1]
+    value = inner[...].astype(F32)
+    total = total + jnp.concatenate(
+        [jnp.where(at == number, value, 0.0) for number in range(total.shape[0] // block)], axis=0
+    )
+    order(total.astype(BF16), other[...], *out)
+
+
+def order(even, odd, first, second):
+    zero = lax.axis_index("dom") % 2 == 0
+
+    @pl.when(zero)
+    def _():
+        first[...] = even
+        second[...] = odd
+
+    @pl.when(jnp.logical_not(zero))
+    def _():
+        first[...] = odd
+        second[...] = even
+
+
+def order_kernel(both, first, second):
+    rows = first.shape[0]
+    order(both[:rows, :], both[rows:, :], first, second)
+
+
+def add_kernel(lists, value, inner, outer, other, first, second, total):
     @pl.when(here_is(1))
     def _():
-        rows = value.shape[0]
         total[...] = value[...].astype(F32)
         add_listed(lists[INNER : INNER + 1, :1], total, inner[...].astype(F32), inner.shape[0])
         add_listed(lists[OUTER : OUTER + 1, :1], total, outer[...].astype(F32), outer.shape[0])
-        out[:rows, :] = total[...].astype(BF16)
-        out[rows:, :] = other[...]
-
-
-def place_kernel(lists, outer, out):
+        order(total[...].astype(BF16), other[...], first, second)
+
+
+def place_kernel(lists, outer, flipped, first, second):
     block = outer.shape[0]
     at = lists[OUTER : OUTER + 1, :1]
-    value = jnp.where(here_is(0), outer[...].astype(F32), 0.0)
-    for number in range(out.shape[0] // block):
-        out[number * block : (number + 1) * block, :] = jnp.where(at == number, value, 0.0)
-
-
-def last_kernel(ends, placed, first_home, second_home, grads, home, turned):
-    rows = placed.shape[0]
-    grads[:rows, :] = (ends[:rows, :].astype(F32) + placed[...]).astype(BF16)
-    grads[rows:, :] = ends[rows:, :]
-
-    @pl.when(here_is(0))
-    def _():
-        home[...] = first_home[...]
-
-    @pl.when(jnp.logical_not(here_is(0)))
-    def _():
-        home[...] = second_home[...]
-
-    for place, value in enumerate((home, grads)):
-        for parity in range(2):
-
-            @pl.when(here_is(parity=1 - parity))
-            def _(value=value, place=place, parity=parity):
-                turned[place * rows : (place + 1) * rows, :] = value[parity * rows : (parity + 1) * rows, :]
-
-
-def write_kernel(home, grads, arrived, out_home, out_grads, sems):
+    for value, out in ((outer, first), (flipped, second)):
+        for number in range(out.shape[0] // block):
+            covered = jnp.broadcast_to(at == number, value.shape) & here_is(0, 0)
+            out[number * block : (number + 1) * block, :] = jnp.where(covered, value[...].astype(F32), 0.0).astype(BF16)
+
+
+def sum_kernel(*refs):
+    ends, placed, totals = (refs[2 * k : 2 * k + 2] for k in range(3))
+    for k in range(2):
+        totals[k][...] = (ends[k][...].astype(F32) + placed[k][...].astype(F32)).astype(BF16)
+
+
+def write_kernel(*refs):
+    first_home, second_home, totals = (refs[2 * k : 2 * k + 2] for k in range(3))
+    out_home, out_grads, sems = refs[6:]
     core = lax.axis_index("pipe") % 2
-    rows = home.shape[0] // 2
-    copies = []
-    for place, (value, out) in enumerate(((home, out_home), (grads, out_grads))):
-        own = value.at[pl.ds(pl.multiple_of(core * rows, rows), rows), :]
-        other = arrived.at[pl.ds(place * rows, rows), :]
-        copies.append(pltpu.make_async_copy(own, out.at[0, core], sems.at[2 * place]))
-        copies.append(pltpu.make_async_copy(other, out.at[0, 1 - core], sems.at[2 * place + 1]))
+    slots = core, 1 - core
+
+    def outputs(source):
+        return [pltpu.make_async_copy(source[k], out_home.at[0, slots[k]], sems.at[k]) for k in range(2)]
+
+    copies = [pltpu.make_async_copy(totals[k], out_grads.at[0, slots[k]], sems.at[2 + k]) for k in range(2)]
     for copy in copies:
         copy.start()
-    for copy in copies:
+
+    @pl.when(here_is(0))
+    def _():
+        for copy in outputs(first_home):
+            copy.start()
+
+    @pl.when(jnp.logical_not(here_is(0)))
+    def _():
+        for copy in outputs(second_home):
+            copy.start()
+
+    for copy in copies + outputs(first_home):
         copy.wait()
 
 
@@ -439,8 +456,11 @@
     def flip_core(value):
         return send(value, lambda z, y, x, c: (z, y, x, 1 - c))
 
-    def to_home(value):
-        return send(value, lambda z, y, x, c: (z, c, x, y))
+    def go_home(first, second, plane=None):
+        return (
+            send(first, lambda z, y, x, c: (z, c, x, y) if plane in (None, x) else None),
+            send(second, lambda z, y, x, c: (z, c, x, 1 - y) if plane in (None, x) else None),
+        )
 
     def towards(value, side, step):
         if side == INNER:
@@ -490,9 +510,6 @@
     )
     hidden, inner = run(entry_kernel, (mate, here, there), [(wide, BF16), (narrow, BF16)])
     upstream = hidden
-
-    def home_of_plane(value, plane):
-        return send(value, lambda z, y, x, c: (z, c, x, y) if x == plane else None)
 
     saved = ()
     arrived = ()
@@ -547,6 +564,7 @@
             kept + (lists, upstream) + ((inner, outer) if halo_in else ()) + tuple(states) + (gown, ghalo_t),
             outs,
             elsewhere={0: -2, 1: -1} if tick == 1 else {},
+            cost=BESIDE // 2 if tick == sections - 2 else 1,
         )
         if done:
             finished[tick + 1] = done[0]
@@ -558,41 +576,43 @@
             handed = (to_inner, to_outer)
             outer = towards(to_outer, OUTER, step)
             inner = towards(to_inner, INNER, step)
-        beside = (inner,) if step == 0 else (first_home,)
-        kept = (finished[2], finished[1], lists) if tick == 0 else ()
-        [upstream] = run_section(
+        beside = (inner,) if step == 0 else tuple(first_home)
+        kept = tuple(ends) + (finished[1], lists) if tick == 0 else ()
+        upstream, *rest = run_section(
             functools.partial(backward_own_kernel, len(kept)),
             plane,
             (packed,),
             kept + beside + (c, du, da, es, gown_t),
-            [((2 * rows, latent), BF16) if tick == 0 else (wide, BF16 if step else F32)],
-            elsewhere={0: -1} if tick == 0 else {},
+            [(wide, BF16)] * 2 if tick == 0 else [(wide, BF16 if step else F32)],
+            elsewhere={0: -2, 1: -1} if tick == 0 else {},
             cost=BESIDE if tick else 1,
         )
         if tick == sections - 1:
-            first_home, upstream = lax.optimization_barrier((both, upstream))
-            first_home = home_of_plane(first_home, 0)
+            outputs, upstream = lax.optimization_barrier((both, upstream))
+            first_home = go_home(*run(order_kernel, (outputs,), [(wide, BF16)] * 2), plane=0)
         if step:
             own = upstream
             upstream = send(upstream, lambda z, y, x, c: (z, y, x + 1, c))
         elif tick == 1:
-            second_home, upstream = lax.optimization_barrier((both, upstream))
-            second_home = home_of_plane(second_home, 1)
-            [finished[2]] = run(
+            outputs, upstream = lax.optimization_barrier((both, upstream))
+            second_home = go_home(*run(order_kernel, (outputs,), [(wide, BF16)] * 2), plane=1)
+            ends = run(
                 add_kernel,
                 (lists, own, inner, outer, finished[3]),
-                [((2 * rows, latent), BF16)],
+                [(wide, BF16)] * 2,
                 scratch=[pltpu.VMEM(wide, F32)],
             )
 
     final_outer = send(to_outer, lambda z, y, x, c: (z + 2 * c - 1, 1 - c, x, y))
-    ends = to_home(upstream)
-    [placed] = run(place_kernel, (home_lists, final_outer), [(wide, F32)], cost=LONG)
-    grads, home, turned = run(last_kernel, (ends, placed, first_home, second_home), [((2 * rows, latent), BF16)] * 3)
+    ends = go_home(upstream, *rest)
+    placed = run(
+        place_kernel, (home_lists, final_outer, flip_core(final_outer)), [(wide, BF16)] * 2
+    )
+    totals = run(sum_kernel, tuple(ends) + tuple(placed), [(wide, BF16)] * 2, cost=LONG)
     return tuple(
         run(
             write_kernel,
-            (home, grads, flip_core(turned)),
+            tuple(first_home) + tuple(second_home) + tuple(totals),
             [((1, 2) + wide, BF16)] * 2,
             out_spaces=(pltpu.HBM,) * 2,
             scratch=[dma((4,))],

time: 102 us -> 97.7 us (0.958)
  starting transfers between devices: 49.6 us -> 43.1 us
  waiting for transfers between devices: 33.1 us -> 35.9 us
    ppermute x25 -> x28, starting transfers between devices: 49.6 us -> 43.1 us  [send(): return lax.ppermute(value, AXES, table)]
    ppermute x25 -> x28, waiting for transfers between devices: 33.1 us -> 35.9 us  [send(): return lax.ppermute(value, AXES, table)]
    pallas_call x29 -> x31, Pallas kernels: 14.7 us -> 14.9 us  [run(): pl.pallas_call(kernel, out_shape=[jax.ShapeDtypeStruct(s, t) for s, t in...]
  transfers between devices with their start and end apart: 25 -> 28, of which waited for: 11 -> 10; matrix products, arithmetic and copies ran while one was open for 0% -> 0% of each run, Pallas kernels for 5% -> 5%
where the time goes in v5:
time: 97.7 us; the launch traced here: 96.7 us
  starting transfers between devices  43.1 us (44%)
  waiting for transfers between devices  35.9 us (37%)
  Pallas kernels  14.9 us (15%)
  local copies, waits for them, and re-layouts  1.6 us (2%)
  between operations  1.11 us (1%)
    ppermute x28, starting transfers between devices, send(): return lax.ppermute(value, AXES, table)  43.1 us
    ppermute x28, waiting for transfers between devices, send(): return lax.ppermute(value, AXES, table)  35.9 us
    pallas_call x31, Pallas kernels, run(): pl.pallas_call(kernel, out_shape=[jax.ShapeDtypeStruct(s, t) for s, t in...  14.9 us
  transfers between devices with their start and end apart: 28, of which 10 were waited for; matrix products, arithmetic and copies ran while one was open for 0% of the time, Pallas kernels for 5%

profile of v5, /device:TPU:0, one launch (start us, length us, event | category | flops | bytes accessed | tf_op | source)
XLA Modules:
  0.0 96.7 jit_solution(18420477331241914939)
XLA Ops:
  0.6 4.2 %shard_map.131 = (bf16[256,512]{1,0:T(8,128)(2,1)}, bf16[256,512]{1,0:T(8,128)(2,1)}, bf16[128,512]{1,0:T(8,128)(2,1)}, bf16[2048,512]{1,0:T(8,128)(2,1)}, s32[3,8,128]{2,1,0:T(8,128)}) custom-call(s32[2]{0:T(128)} %count.1, s32[1,1,2]{2,1,0:T(1,128)} %bitcast.11, bf16[2,256,512]{2,1,0:T(8,128)(2,1)} %inputs.1, bf16[2,256,512]{2,1,0:T(8,128)(2,1)} %cotangent.1, ...), custom_call_target="tpu_custom_call" | custom-call | flops 1 | bytes 1 | tf_op jit(solution)/shard_map/pallas_call | solution.py:385
  5.4 2.6 %collective-permute-start.3 = (bf16[256,512]{1,0:T(8,128)(2,1)}, bf16[256,512]{1,0:T(8,128)(2,1)S(1)}, u32[]{:S(2)}, u32[]{:S(2)}) collective-permute-start(bf16[256,512]{1,0:T(8,128)(2,1)} %get-tuple-element.113), channel_id=1, source_target_pairs={{0,4},{1,5},{2,6},{3,7},{4,0},{5,1},{6,2},{7,3},{8,12},{9,13},{10,... | collective-permute-start | bytes 786440 | tf_op jit(solution)/shard_map/ppermute | solution.py:451
  8.2 3.8 %collective-permute-start.4 = (bf16[128,512]{1,0:T(8,128)(2,1)}, bf16[128,512]{1,0:T(8,128)(2,1)S(1)}, u32[]{:S(2)}, u32[]{:S(2)}) collective-permute-start(bf16[128,512]{1,0:T(8,128)(2,1)} %get-tuple-element.119), channel_id=1, source_target_pairs={{0,25},{1,29},{2,27},{3,31},{4,8},{5,12},{6,10},{7,14},{8,1},{9,5}... | collective-permute-start | bytes 393224 | tf_op jit(solution)/shard_map/ppermute | solution.py:451
  12.0 1.6 %copy-done = bf16[2048,512]{1,0:T(8,128)(2,1)S(1)} copy-done((bf16[2048,512]{1,0:T(8,128)(2,1)S(1)}, bf16[2048,512]{1,0:T(8,128)(2,1)}, u32[]{:S(2)}) %copy-start) | copy-done | bytes 2097176
  13.9 2.2 %collective-permute-done.2.packed_there = s32[3,8,128]{2,1,0:T(8,128)S(1)} collective-permute-done((s32[3,8,128]{2,1,0:T(8,128)}, s32[3,8,128]{2,1,0:T(8,128)S(1)}, u32[]{:S(2)}, u32[]{:S(2)}) %collective-permute-start.2) | collective-permute-done | bytes 12320 | tf_op jit(solution)/shard_map/ppermute | solution.py:451
  18.6 4.1 %collective-permute-start.6 = (bf16[128,512]{1,0:T(8,128)(2,1)S(1)}, bf16[128,512]{1,0:T(8,128)(2,1)S(1)}, u32[]{:S(2)}, u32[]{:S(2)}) collective-permute-start(bf16[128,512]{1,0:T(8,128)(2,1)S(1)} %get-tuple-element.126), channel_id=1, source_target_pairs={{0,25},{1,8},{2,27},{3,10},{4,29},{5,12},{6,31},{7,14},{8,1},{9,16... | collective-permute-start | bytes 393224 | tf_op jit(solution)/shard_map/ppermute | solution.py:451
  24.1 2.1 %collective-permute-done.6.refs_7_ = bf16[128,512]{1,0:T(8,128)(2,1)S(1)} collective-permute-done((bf16[128,512]{1,0:T(8,128)(2,1)S(1)}, bf16[128,512]{1,0:T(8,128)(2,1)S(1)}, u32[]{:S(2)}, u32[]{:S(2)}) %collective-permute-start.6) | collective-permute-done | bytes 131104 | tf_op jit(solution)/shard_map/ppermute | solution.py:451
  27.5 3.9 %collective-permute-start.9 = (bf16[128,512]{1,0:T(8,128)(2,1)S(1)}, bf16[128,512]{1,0:T(8,128)(2,1)S(1)}, u32[]{:S(2)}, u32[]{:S(2)}) collective-permute-start(bf16[128,512]{1,0:T(8,128)(2,1)S(1)} %get-tuple-element.131), channel_id=1, source_target_pairs={{0,27},{1,10},{2,25},{3,8},{4,31},{5,14},{6,29},{7,12},{8,3},{9,18... | collective-permute-start | bytes 393224 | tf_op jit(solution)/shard_map/ppermute | solution.py:451
  31.9 5.6 %collective-permute-done.7.refs_1_.refs_3_ = bf16[256,512]{1,0:T(8,128)(2,1)S(1)} collective-permute-done((bf16[256,512]{1,0:T(8,128)(2,1)S(1)}, bf16[256,512]{1,0:T(8,128)(2,1)S(1)}, u32[]{:S(2)}, u32[]{:S(2)}) %collective-permute-start.7) | collective-permute-done | bytes 262176 | tf_op jit(solution)/shard_map/ppermute | solution.py:451
  37.5 1.2 %collective-permute-start.10 = (bf16[128,512]{1,0:T(8,128)(2,1)S(1)}, bf16[128,512]{1,0:T(8,128)(2,1)S(1)}, u32[]{:S(2)}, u32[]{:S(2)}) collective-permute-start(bf16[128,512]{1,0:T(8,128)(2,1)S(1)} %get-tuple-element.133), channel_id=1, source_target_pairs={{0,1},{1,0},{2,3},{3,2},{4,5},{5,4},{6,7},{7,6},{8,9},{9,8},{10,11... | collective-permute-start | bytes 393224 | tf_op jit(solution)/shard_map/ppermute | solution.py:451
  38.7 4.9 %collective-permute-start.11 = (bf16[128,512]{1,0:T(8,128)(2,1)S(1)}, bf16[128,512]{1,0:T(8,128)(2,1)S(1)}, u32[]{:S(2)}, u32[]{:S(2)}) collective-permute-start(bf16[128,512]{1,0:T(8,128)(2,1)S(1)} %get-tuple-element.136), channel_id=1, source_target_pairs={{0,25},{1,8},{2,27},{3,10},{4,29},{5,12},{6,31},{7,14},{8,1},{9,16... | collective-permute-start | bytes 393224 | tf_op jit(solution)/shard_map/ppermute | solution.py:451
  43.6 3.8 %collective-permute-done.11.refs_7_ = bf16[128,512]{1,0:T(8,128)(2,1)S(1)} collective-permute-done((bf16[128,512]{1,0:T(8,128)(2,1)S(1)}, bf16[128,512]{1,0:T(8,128)(2,1)S(1)}, u32[]{:S(2)}, u32[]{:S(2)}) %collective-permute-start.11) | collective-permute-done | bytes 131104 | tf_op jit(solution)/shard_map/ppermute | solution.py:451
  47.4 2.4 %collective-permute-start.15 = (bf16[128,512]{1,0:T(8,128)(2,1)S(1)}, bf16[128,512]{1,0:T(8,128)(2,1)S(1)}, u32[]{:S(2)}, u32[]{:S(2)}) collective-permute-start(bf16[128,512]{1,0:T(8,128)(2,1)S(1)} %get-tuple-element.172), channel_id=1, source_target_pairs={{0,25},{1,8},{2,27},{3,10},{4,29},{5,12},{6,31},{7,14},{8,1},{9,16... | collective-permute-start | bytes 393224 | tf_op jit(solution)/shard_map/ppermute | solution.py:451
  50.6 4.8 %collective-permute-start.14 = (bf16[256,512]{1,0:T(8,128)(2,1)S(1)}, bf16[256,512]{1,0:T(8,128)(2,1)S(1)}, u32[]{:S(2)}, u32[]{:S(2)}) collective-permute-start(bf16[256,512]{1,0:T(8,128)(2,1)S(1)} %get-tuple-element.170), channel_id=1, source_target_pairs={{0,1},{1,5},{4,0},{5,4},{8,9},{9,13},{12,8},{13,12},{16,17},{17,21... | collective-permute-start | bytes 786440 | tf_op jit(solution)/shard_map/ppermute | solution.py:451
  55.4 5.1 %collective-permute-done.14.refs_2_.refs_1_ = bf16[256,512]{1,0:T(8,128)(2,1)S(1)} collective-permute-done((bf16[256,512]{1,0:T(8,128)(2,1)S(1)}, bf16[256,512]{1,0:T(8,128)(2,1)S(1)}, u32[]{:S(2)}, u32[]{:S(2)}) %collective-permute-start.14) | collective-permute-done | bytes 262176 | tf_op jit(solution)/shard_map/ppermute | solution.py:451
  60.9 2.6 %collective-permute-start.18 = (bf16[128,512]{1,0:T(8,128)(2,1)S(1)}, bf16[128,512]{1,0:T(8,128)(2,1)S(1)}, u32[]{:S(2)}, u32[]{:S(2)}) collective-permute-start(bf16[128,512]{1,0:T(8,128)(2,1)S(1)} %get-tuple-element.174.refs_3_), channel_id=1, source_target_pairs={{0,27},{1,10},{2,25},{3,8},{4,31},{5,14},{6,29},{7,12},{8,3},{9,18... | collective-permute-start | bytes 393224 | tf_op jit(solution)/shard_map/ppermute | solution.py:451
  63.5 7.9 %collective-permute-done.17.refs_6_ = bf16[128,512]{1,0:T(8,128)(2,1)S(1)} collective-permute-done((bf16[128,512]{1,0:T(8,128)(2,1)S(1)}, bf16[128,512]{1,0:T(8,128)(2,1)S(1)}, u32[]{:S(2)}, u32[]{:S(2)}) %collective-permute-start.17) | collective-permute-done | bytes 131104 | tf_op jit(solution)/shard_map/ppermute | solution.py:451
  72.0 1.2 %shard_map.153 = (f32[256,512]{1,0:T(8,128)S(1)}, bf16[256,512]{1,0:T(8,128)(2,1)S(1)}, bf16[256,512]{1,0:T(8,128)(2,1)S(1)}, bf16[256,512]{1,0:T(8,128)(2,1)S(1...) custom-call(bf16[2048,512]{1,0:T(8,128)(2,1)S(1)} %get-tuple-element.105.refs_0_, ...), custom_call_target="tpu_custom_call" | custom-call | flops 1 | bytes 1 | tf_op jit(solution)/shard_map/pallas_call | solution.py:385
  73.2 1.3 %collective-permute-start.19 = (bf16[128,512]{1,0:T(8,128)(2,1)S(1)}, bf16[128,512]{1,0:T(8,128)(2,1)S(1)}, u32[]{:S(2)}, u32[]{:S(2)}) collective-permute-start(bf16[128,512]{1,0:T(8,128)(2,1)S(1)} %get-tuple-element.179), channel_id=1, source_target_pairs={{0,1},{1,0},{2,3},{3,2},{4,5},{5,4},{6,7},{7,6},{8,9},{9,8},{10,11... | collective-permute-start | bytes 393224 | tf_op jit(solution)/shard_map/ppermute | solution.py:451
  76.2 4.5 %collective-permute-done.22.outer.refs_5_ = bf16[128,512]{1,0:T(8,128)(2,1)S(1)} collective-permute-done((bf16[128,512]{1,0:T(8,128)(2,1)S(1)}, bf16[128,512]{1,0:T(8,128)(2,1)S(1)}, u32[]{:S(2)}, u32[]{:S(2)}) %collective-permute-start.22) | collective-permute-done | bytes 131104 | tf_op jit(solution)/shard_map/ppermute | solution.py:451
  81.9 3.4 %collective-permute-start.26 = (bf16[128,512]{1,0:T(8,128)(2,1)S(1)}, bf16[128,512]{1,0:T(8,128)(2,1)S(1)}, u32[]{:S(2)}, u32[]{:S(2)}) collective-permute-start(bf16[128,512]{1,0:T(8,128)(2,1)S(1)} %get-tuple-element.201), channel_id=1, source_target_pairs={{0,28},{1,8},{2,30},{3,10},{4,29},{5,9},{6,31},{7,11},{8,4},{9,16}... | collective-permute-start | bytes 393224 | tf_op jit(solution)/shard_map/ppermute | solution.py:451
  86.7 1.6 %collective-permute-start.25 = (bf16[256,512]{1,0:T(8,128)(2,1)S(1)}, bf16[256,512]{1,0:T(8,128)(2,1)S(1)}, u32[]{:S(2)}, u32[]{:S(2)}) collective-permute-start(bf16[256,512]{1,0:T(8,128)(2,1)S(1)} %get-tuple-element.199), channel_id=1, source_target_pairs={{0,1},{1,5},{2,3},{3,7},{4,0},{5,4},{6,2},{7,6},{8,9},{9,13},{10,1... | collective-permute-start | bytes 786440 | tf_op jit(solution)/shard_map/ppermute | solution.py:451
  88.3 1.3 %collective-permute-start.27 = (bf16[128,512]{1,0:T(8,128)(2,1)S(1)}, bf16[128,512]{1,0:T(8,128)(2,1)S(1)}, u32[]{:S(2)}, u32[]{:S(2)}) collective-permute-start(bf16[128,512]{1,0:T(8,128)(2,1)S(1)} %collective-permute-done.26.outer), channel_id=1, source_target_pairs={{0,1},{1,0},{2,3},{3,2},{4,5},{5,4},{6,7},{7,6},{8,9},{9,8},{10,11... | collective-permute-start | bytes 393224 | tf_op jit(solution)/shard_map/ppermute | solution.py:451
  91.2 4.2 %collective-permute-done.25.refs_1_ = bf16[256,512]{1,0:T(8,128)(2,1)S(1)} collective-permute-done((bf16[256,512]{1,0:T(8,128)(2,1)S(1)}, bf16[256,512]{1,0:T(8,128)(2,1)S(1)}, u32[]{:S(2)}, u32[]{:S(2)}) %collective-permute-start.25) | collective-permute-done | bytes 262176 | tf_op jit(solution)/shard_map/ppermute | solution.py:451
  (71 shorter events, 15.4 us)
Async XLA Ops:
  4.9 7.1 %collective-permute-start = (bf16[2048,512]{1,0:T(8,128)(2,1)}, bf16[2048,512]{1,0:T(8,128)(2,1)S(1)}, u32[]{:S(2)}, u32[]{:S(2)}) collective-permute-start(bf16[2048,512]{1,0:T(8,128)(2,1)} %get-tuple-element.104.mine), channel_id=1, source_target_pairs={{0,1},{1,0},{2,3},{3,2},{4,5},{5,4},{6,7},{7,6},{8,9},{9,8},{10,11... | collective-permute-start | bytes 6291464 | tf_op jit(solution)/shard_map/ppermute | solution.py:451
  5.4 11.0 %collective-permute-start.3 = (bf16[256,512]{1,0:T(8,128)(2,1)}, bf16[256,512]{1,0:T(8,128)(2,1)S(1)}, u32[]{:S(2)}, u32[]{:S(2)}) collective-permute-start(bf16[256,512]{1,0:T(8,128)(2,1)} %get-tuple-element.113), channel_id=1, source_target_pairs={{0,4},{1,5},{2,6},{3,7},{4,0},{5,1},{6,2},{7,3},{8,12},{9,13},{10,... | collective-permute-start | bytes 786440 | tf_op jit(solution)/shard_map/ppermute | solution.py:451
  8.0 8.1 %collective-permute-start.2 = (s32[3,8,128]{2,1,0:T(8,128)}, s32[3,8,128]{2,1,0:T(8,128)S(1)}, u32[]{:S(2)}, u32[]{:S(2)}) collective-permute-start(s32[3,8,128]{2,1,0:T(8,128)} %get-tuple-element.108.packed), channel_id=1, source_target_pairs={{0,5},{1,4},{2,7},{3,6},{4,1},{5,0},{6,3},{7,2},{8,13},{9,12},{10,... | collective-permute-start | bytes 36872 | tf_op jit(solution)/shard_map/ppermute | solution.py:451
  8.1 3.9 %collective-permute-start.1 = (f32[1,512]{1,0:T(1,128)S(1)}, f32[1,512]{1,0:T(1,128)S(1)}, u32[]{:S(2)}, u32[]{:S(2)}) collective-permute-start(f32[1,512]{1,0:T(1,128)S(1)} %copy-done.3), channel_id=1, source_target_pairs={{0,1},{1,0},{2,3},{3,2},{4,5},{5,4},{6,7},{7,6},{8,9},{9,8},{10,11... | collective-permute-start | bytes 6152 | tf_op jit(solution)/shard_map/ppermute | solution.py:451
  8.2 9.2 %collective-permute-start.4 = (bf16[128,512]{1,0:T(8,128)(2,1)}, bf16[128,512]{1,0:T(8,128)(2,1)S(1)}, u32[]{:S(2)}, u32[]{:S(2)}) collective-permute-start(bf16[128,512]{1,0:T(8,128)(2,1)} %get-tuple-element.119), channel_id=1, source_target_pairs={{0,25},{1,29},{2,27},{3,31},{4,8},{5,12},{6,10},{7,14},{8,1},{9,5}... | collective-permute-start | bytes 393224 | tf_op jit(solution)/shard_map/ppermute | solution.py:451
  18.6 4.7 %collective-permute-start.5 = (bf16[128,512]{1,0:T(8,128)(2,1)S(1)}, bf16[128,512]{1,0:T(8,128)(2,1)S(1)}, u32[]{:S(2)}, u32[]{:S(2)}) collective-permute-start(bf16[128,512]{1,0:T(8,128)(2,1)S(1)} %get-tuple-element.123), channel_id=1, source_target_pairs={{0,1},{1,0},{2,3},{3,2},{4,5},{5,4},{6,7},{7,6},{8,9},{9,8},{10,11... | collective-permute-start | bytes 393224 | tf_op jit(solution)/shard_map/ppermute | solution.py:451
  18.6 7.5 %collective-permute-start.6 = (bf16[128,512]{1,0:T(8,128)(2,1)S(1)}, bf16[128,512]{1,0:T(8,128)(2,1)S(1)}, u32[]{:S(2)}, u32[]{:S(2)}) collective-permute-start(bf16[128,512]{1,0:T(8,128)(2,1)S(1)} %get-tuple-element.126), channel_id=1, source_target_pairs={{0,25},{1,8},{2,27},{3,10},{4,29},{5,12},{6,31},{7,14},{8,1},{9,16... | collective-permute-start | bytes 393224 | tf_op jit(solution)/shard_map/ppermute | solution.py:451
  27.3 10.2 %collective-permute-start.7 = (bf16[256,512]{1,0:T(8,128)(2,1)S(1)}, bf16[256,512]{1,0:T(8,128)(2,1)S(1)}, u32[]{:S(2)}, u32[]{:S(2)}) collective-permute-start(bf16[256,512]{1,0:T(8,128)(2,1)S(1)} %get-tuple-element.127.h), channel_id=1, source_target_pairs={{0,2},{1,3},{2,0},{3,1},{4,6},{5,7},{6,4},{7,5},{8,10},{9,11},{10,... | collective-permute-start | bytes 786440 | tf_op jit(solution)/shard_map/ppermute | solution.py:451
  27.4 10.1 %collective-permute-start.8 = (bf16[128,512]{1,0:T(8,128)(2,1)S(1)}, bf16[128,512]{1,0:T(8,128)(2,1)S(1)}, u32[]{:S(2)}, u32[]{:S(2)}) collective-permute-start(bf16[128,512]{1,0:T(8,128)(2,1)S(1)} %get-tuple-element.130), channel_id=1, source_target_pairs={{0,3},{1,2},{2,1},{3,0},{4,7},{5,6},{6,5},{7,4},{8,11},{9,10},{10,... | collective-permute-start | bytes 393224 | tf_op jit(solution)/shard_map/ppermute | solution.py:451
  27.5 10.0 %collective-permute-start.9 = (bf16[128,512]{1,0:T(8,128)(2,1)S(1)}, bf16[128,512]{1,0:T(8,128)(2,1)S(1)}, u32[]{:S(2)}, u32[]{:S(2)}) collective-permute-start(bf16[128,512]{1,0:T(8,128)(2,1)S(1)} %get-tuple-element.131), channel_id=1, source_target_pairs={{0,27},{1,10},{2,25},{3,8},{4,31},{5,14},{6,29},{7,12},{8,3},{9,18... | collective-permute-start | bytes 393224 | tf_op jit(solution)/shard_map/ppermute | solution.py:451
  37.5 6.1 %collective-permute-start.10 = (bf16[128,512]{1,0:T(8,128)(2,1)S(1)}, bf16[128,512]{1,0:T(8,128)(2,1)S(1)}, u32[]{:S(2)}, u32[]{:S(2)}) collective-permute-start(bf16[128,512]{1,0:T(8,128)(2,1)S(1)} %get-tuple-element.133), channel_id=1, source_target_pairs={{0,1},{1,0},{2,3},{3,2},{4,5},{5,4},{6,7},{7,6},{8,9},{9,8},{10,11... | collective-permute-start | bytes 393224 | tf_op jit(solution)/shard_map/ppermute | solution.py:451
  38.7 8.7 %collective-permute-start.11 = (bf16[128,512]{1,0:T(8,128)(2,1)S(1)}, bf16[128,512]{1,0:T(8,128)(2,1)S(1)}, u32[]{:S(2)}, u32[]{:S(2)}) collective-permute-start(bf16[128,512]{1,0:T(8,128)(2,1)S(1)} %get-tuple-element.136), channel_id=1, source_target_pairs={{0,25},{1,8},{2,27},{3,10},{4,29},{5,12},{6,31},{7,14},{8,1},{9,16... | collective-permute-start | bytes 393224 | tf_op jit(solution)/shard_map/ppermute | solution.py:451
  47.4 8.0 %collective-permute-start.15 = (bf16[128,512]{1,0:T(8,128)(2,1)S(1)}, bf16[128,512]{1,0:T(8,128)(2,1)S(1)}, u32[]{:S(2)}, u32[]{:S(2)}) collective-permute-start(bf16[128,512]{1,0:T(8,128)(2,1)S(1)} %get-tuple-element.172), channel_id=1, source_target_pairs={{0,25},{1,8},{2,27},{3,10},{4,29},{5,12},{6,31},{7,14},{8,1},{9,16... | collective-permute-start | bytes 393224 | tf_op jit(solution)/shard_map/ppermute | solution.py:451
  49.9 5.5 %collective-permute-start.13 = (bf16[256,512]{1,0:T(8,128)(2,1)S(1)}, bf16[256,512]{1,0:T(8,128)(2,1)S(1)}, u32[]{:S(2)}, u32[]{:S(2)}) collective-permute-start(bf16[256,512]{1,0:T(8,128)(2,1)S(1)} %get-tuple-element.169), channel_id=1, source_target_pairs={{0,0},{1,4},{4,1},{5,5},{8,8},{9,12},{12,9},{13,13},{16,16},{17,20... | collective-permute-start | bytes 786440 | tf_op jit(solution)/shard_map/ppermute | solution.py:451
  50.6 9.9 %collective-permute-start.14 = (bf16[256,512]{1,0:T(8,128)(2,1)S(1)}, bf16[256,512]{1,0:T(8,128)(2,1)S(1)}, u32[]{:S(2)}, u32[]{:S(2)}) collective-permute-start(bf16[256,512]{1,0:T(8,128)(2,1)S(1)} %get-tuple-element.170), channel_id=1, source_target_pairs={{0,1},{1,5},{4,0},{5,4},{8,9},{9,13},{12,8},{13,12},{16,17},{17,21... | collective-permute-start | bytes 786440 | tf_op jit(solution)/shard_map/ppermute | solution.py:451
  60.5 11.5 %collective-permute-start.16 = (bf16[256,512]{1,0:T(8,128)(2,1)S(1)}, bf16[256,512]{1,0:T(8,128)(2,1)S(1)}, u32[]{:S(2)}, u32[]{:S(2)}) collective-permute-start(bf16[256,512]{1,0:T(8,128)(2,1)S(1)} %shard_map.152.value), channel_id=1, source_target_pairs={{0,2},{1,3},{2,0},{3,1},{4,6},{5,7},{6,4},{7,5},{8,10},{9,11},{10,... | collective-permute-start | bytes 786440 | tf_op jit(solution)/shard_map/ppermute | solution.py:451
  60.6 10.8 %collective-permute-start.17 = (bf16[128,512]{1,0:T(8,128)(2,1)S(1)}, bf16[128,512]{1,0:T(8,128)(2,1)S(1)}, u32[]{:S(2)}, u32[]{:S(2)}) collective-permute-start(bf16[128,512]{1,0:T(8,128)(2,1)S(1)} %get-tuple-element.173.refs_2_), channel_id=1, source_target_pairs={{0,3},{1,2},{2,1},{3,0},{4,7},{5,6},{6,5},{7,4},{8,11},{9,10},{10,... | collective-permute-start | bytes 393224 | tf_op jit(solution)/shard_map/ppermute | solution.py:451
  60.9 10.5 %collective-permute-start.18 = (bf16[128,512]{1,0:T(8,128)(2,1)S(1)}, bf16[128,512]{1,0:T(8,128)(2,1)S(1)}, u32[]{:S(2)}, u32[]{:S(2)}) collective-permute-start(bf16[128,512]{1,0:T(8,128)(2,1)S(1)} %get-tuple-element.174.refs_3_), channel_id=1, source_target_pairs={{0,27},{1,10},{2,25},{3,8},{4,31},{5,14},{6,29},{7,12},{8,3},{9,18... | collective-permute-start | bytes 393224 | tf_op jit(solution)/shard_map/ppermute | solution.py:451
  74.5 6.2 %collective-permute-start.22 = (bf16[128,512]{1,0:T(8,128)(2,1)S(1)}, bf16[128,512]{1,0:T(8,128)(2,1)S(1)}, u32[]{:S(2)}, u32[]{:S(2)}) collective-permute-start(bf16[128,512]{1,0:T(8,128)(2,1)S(1)} %get-tuple-element.187), channel_id=1, source_target_pairs={{0,25},{1,8},{2,27},{3,10},{4,29},{5,12},{6,31},{7,14},{8,1},{9,16... | collective-permute-start | bytes 393224 | tf_op jit(solution)/shard_map/ppermute | solution.py:451
  81.9 6.4 %collective-permute-start.26 = (bf16[128,512]{1,0:T(8,128)(2,1)S(1)}, bf16[128,512]{1,0:T(8,128)(2,1)S(1)}, u32[]{:S(2)}, u32[]{:S(2)}) collective-permute-start(bf16[128,512]{1,0:T(8,128)(2,1)S(1)} %get-tuple-element.201), channel_id=1, source_target_pairs={{0,28},{1,8},{2,30},{3,10},{4,29},{5,9},{6,31},{7,11},{8,4},{9,16}... | collective-permute-start | bytes 393224 | tf_op jit(solution)/shard_map/ppermute | solution.py:451
  86.0 5.2 %collective-permute-start.24 = (bf16[256,512]{1,0:T(8,128)(2,1)S(1)}, bf16[256,512]{1,0:T(8,128)(2,1)S(1)}, u32[]{:S(2)}, u32[]{:S(2)}) collective-permute-start(bf16[256,512]{1,0:T(8,128)(2,1)S(1)} %get-tuple-element.198), channel_id=1, source_target_pairs={{0,0},{1,4},{2,2},{3,6},{4,1},{5,5},{6,3},{7,7},{8,8},{9,12},{10,1... | collective-permute-start | bytes 786440 | tf_op jit(solution)/shard_map/ppermute | solution.py:451
  86.7 8.7 %collective-permute-start.25 = (bf16[256,512]{1,0:T(8,128)(2,1)S(1)}, bf16[256,512]{1,0:T(8,128)(2,1)S(1)}, u32[]{:S(2)}, u32[]{:S(2)}) collective-permute-start(bf16[256,512]{1,0:T(8,128)(2,1)S(1)} %get-tuple-element.199), channel_id=1, source_target_pairs={{0,1},{1,5},{2,3},{3,7},{4,0},{5,4},{6,2},{7,6},{8,9},{9,13},{10,1... | collective-permute-start | bytes 786440 | tf_op jit(solution)/shard_map/ppermute | solution.py:451
  89.6 5.9 %collective-permute-start.20 = (bf16[256,512]{1,0:T(8,128)(2,1)S(1)}, bf16[256,512]{1,0:T(8,128)(2,1)S(1)}, u32[]{:S(2)}, u32[]{:S(2)}) collective-permute-start(bf16[256,512]{1,0:T(8,128)(2,1)S(1)} %get-tuple-element.185), channel_id=1, source_target_pairs={{2,2},{3,6},{6,3},{7,7},{10,10},{11,14},{14,11},{15,15},{18,18},{1... | collective-permute-start | bytes 786440 | tf_op jit(solution)/shard_map/ppermute | solution.py:451
  90.3 5.2 %collective-permute-start.21 = (bf16[256,512]{1,0:T(8,128)(2,1)S(1)}, bf16[256,512]{1,0:T(8,128)(2,1)S(1)}, u32[]{:S(2)}, u32[]{:S(2)}) collective-permute-start(bf16[256,512]{1,0:T(8,128)(2,1)S(1)} %get-tuple-element.186), channel_id=1, source_target_pairs={{2,3},{3,7},{6,2},{7,6},{10,11},{11,15},{14,10},{15,14},{18,19},{1... | collective-permute-start | bytes 786440 | tf_op jit(solution)/shard_map/ppermute | solution.py:451
  (8 other events, 24.9 us)

commit v6 on v5

--- a/solution.py
+++ b/solution.py
@@ -67,43 +67,63 @@
         target[rows, :] = target[rows, :] + jnp.where(at == number, value, 0.0)
 
 
+def encode(values):
+    high = lax.shift_right_logical(values, 4)
+    low = values - high * 16
+    return jnp.concatenate([high.astype(F32), low.astype(F32)], axis=0).astype(BF16)
+
+
+def decode(tile):
+    half = tile.shape[0] // 2
+    tile = tile.astype(F32)
+    return (tile[:half] * 16.0 + tile[half:]).astype(jnp.int32)
+
+
 def prepare_kernel(
-    count,
-    halo,
+    count_in,
+    halo_in,
     inputs,
     cotangent,
     send_in,
     recv_in,
-    w_send,
-    w_recv,
-    w_node,
-    w_message,
-    w_aggregate,
     here,
     there,
     boundary,
-    weights,
     packed,
-    factors,
-    product,
+    count,
+    halo,
+    here_rows,
+    there_rows,
+    boundary_rows,
+    edges,
     sems,
-    weight_sems,
+    out_sems,
 ):
     micro = lax.axis_index("dom") % 2
     block = boundary.shape[0]
-    depth = w_send.shape[0]
     edge_blocks = send_in.shape[0]
-    number = jnp.where(micro == 1, halo[0, 0, 0], halo[0, 0, 1])
-    start = pl.multiple_of(number * block, block)
-
+    rows = here.shape[0]
+    lists = [
+        pltpu.make_async_copy(halo_in, halo, sems.at[0]),
+        pltpu.make_async_copy(count_in, count, sems.at[1]),
+    ]
+    ids = [
+        pltpu.make_async_copy(ref, edges.at[k, pl.ds(0, edge_blocks), :], sems.at[2 + k])
+        for k, ref in enumerate((send_in, recv_in))
+    ]
     def fetch(source):
         return [
-            pltpu.make_async_copy(source.at[1 - micro], there, sems.at[0]),
-            pltpu.make_async_copy(
-                source.at[lax.axis_index("pipe") % 2, pl.ds(start, block), :], boundary, sems.at[1]
-            ),
-            pltpu.make_async_copy(source.at[micro], here, sems.at[2]),
+            pltpu.make_async_copy(source.at[1 - micro], there_rows.at[pl.ds(0, rows), :], sems.at[4]),
+            pltpu.make_async_copy(source.at[micro], here_rows, sems.at[5]),
         ]
+
+    def fetch_boundary(source, number):
+        start = pl.multiple_of(number * block, block)
+        place = source.at[lax.axis_index("pipe") % 2, pl.ds(start, block), :]
+        return pltpu.make_async_copy(place, boundary_rows, sems.at[6])
+
+    for copy in lists + ids:
+        copy.start()
 
     @pl.when(here_is(0))
     def _():
@@ -115,35 +135,54 @@
         for copy in fetch(cotangent):
             copy.start()
 
-    copies = [
-        pltpu.make_async_copy(ref, factors.at[k], weight_sems.at[k]) for k, ref in enumerate((w_message, w_aggregate))
+    for copy in lists:
+        copy.wait()
+    number = jnp.where(micro == 1, halo[0, 0, 0], halo[0, 0, 1])
+    fetch_boundary(inputs, number).start()
+    for copy in ids:
+        copy.wait()
+    lane = lax.broadcasted_iota(jnp.int32, (1, block), 1)
+    tail = jnp.where(lane == 0, halo[0, 0, 0], jnp.where(lane == 1, halo[0, 0, 1], 0))
+    for place in range(edge_blocks):
+        tail = jnp.where(lane == 2 + place, count[place], tail)
+    spare = jnp.zeros((7 - 2 * edge_blocks, block), jnp.int32)
+    tile = encode(jnp.concatenate([edges[0, :edge_blocks, :], edges[1, :edge_blocks, :], tail, spare], axis=0))
+    packed[...] = tile
+    there_rows[rows:, :] = jnp.zeros((there_rows.shape[0] - rows, there_rows.shape[1]), BF16)
+    there_rows[rows:, :block] = tile
+    fetched = fetch(inputs)
+    leaving = [
+        pltpu.make_async_copy(there_rows, there, out_sems.at[0]),
+        pltpu.make_async_copy(here_rows, here, out_sems.at[1]),
+        pltpu.make_async_copy(boundary_rows, boundary, out_sems.at[2]),
     ]
+    fetched[0].wait()
+    leaving[0].start()
+    fetched[1].wait()
+    leaving[1].start()
+    fetch_boundary(inputs, number).wait()
+    leaving[2].start()
+    for copy in leaving:
+        copy.wait()
+
+
+def weights_kernel(w_send, w_recv, w_node, w_message, w_aggregate, out, factors, sems):
+    depth = w_send.shape[0]
+    copies = [pltpu.make_async_copy(ref, factors.at[k], sems.at[k]) for k, ref in enumerate((w_message, w_aggregate))]
     copies += [
-        pltpu.make_async_copy(ref, packed.at[k, pl.ds(0, edge_blocks), :], sems.at[3 + k])
-        for k, ref in enumerate((send_in, recv_in))
-    ]
-    copies += [
-        pltpu.make_async_copy(ref, weights.at[pl.ds(k * depth, depth), :], weight_sems.at[2 + k])
+        pltpu.make_async_copy(ref, out.at[pl.ds(k * depth, depth), :], sems.at[2 + k])
         for k, ref in enumerate((w_send, w_recv, w_node))
     ]
     for copy in copies:
         copy.start()
-    lane = lax.broadcasted_iota(jnp.int32, packed.shape[1:], 1)
-    tail = jnp.where(lane == 0, halo[0, 0, 0], halo[0, 0, 1])
-    for place in range(edge_blocks):
-        tail = jnp.where(lane == 2 + place, count[place], tail)
-    packed[2] = tail
     for copy in copies[:2]:
         copy.wait()
-    product[...] = mul(factors[0], factors[1]).astype(BF16)
-    last = pltpu.make_async_copy(product, weights.at[pl.ds(3 * depth, depth), :], weight_sems.at[5])
-    last.start()
-    for copy in copies[2:] + fetch(inputs):
+    out[3 * depth :, :] = mul(factors[0], factors[1]).astype(BF16)
+    for copy in copies[2:]:
         copy.wait()
-    last.wait()
-
-
-def arrange_kernel(mine, swapped, even, odd):
+
+
+def arrange_kernel(mine, swapped, _, even, odd):
     @pl.when(here_is(parity=0))
     def _():
         even[...] = mine[...]
@@ -155,21 +194,23 @@
         odd[...] = mine[...]
 
 
-def graph_kernel(edge_blocks, _, packed, packed_there, gown, gown_t, ghalo, ghalo_t, lists, mate, home_lists):
-    block = packed.shape[2]
+def graph_kernel(edge_blocks, packed, there, gown, gown_t, ghalo, ghalo_t, lists, mate, home_lists):
+    block = packed.shape[1]
     rows = gown_t.shape[0]
     edges = edge_blocks * block
     local = is_local()
     first_core = lax.axis_index("pipe") % 2 == 0
-    mine = [jnp.where(local, packed[k], packed_there[k]) for k in range(3)]
-    tails = mine[2], jnp.where(local, packed_there[2], packed[2])
+    last = 2 * edge_blocks
+    tiles = decode(packed[...]), decode(there[rows:, :block])
+    mine = jnp.where(local, *tiles)
+    tails = [tile[last : last + 1] for tile in (mine, jnp.where(local, tiles[1], tiles[0]), tiles[0])]
     lane = lax.broadcasted_iota(jnp.int32, (1, block), 1)
     row = lax.broadcasted_iota(jnp.int32, (rows, block), 0)
     halo_row = lax.broadcasted_iota(jnp.int32, (2 * block, block), 0)
     for number in range(edge_blocks):
-        live = lane < tails[0][:1, 2 + number : 3 + number]
-        sender = jnp.where(live, mine[0][number : number + 1], -1)
-        receiver = jnp.where(live, mine[1][number : number + 1], -1)
+        live = lane < tails[0][:, 2 + number : 3 + number]
+        sender = jnp.where(live, mine[number : number + 1], -1)
+        receiver = jnp.where(live, mine[edge_blocks + number : edge_blocks + number + 1], -1)
         outside = sender - rows
         turned = jnp.where(outside < block, outside + block, outside - block)
         outside = jnp.where(outside >= 0, jnp.where(first_core, turned, outside), -1)
@@ -191,7 +232,7 @@
     lists[0:1, :] = jnp.where(first_core, to_next, to_prev)
     lists[1:2, :] = jnp.where(first_core, to_prev, to_next)
     mate[...] = jnp.where(first_core, whole(tails[1], 1), whole(tails[1], 0))
-    to_next, to_prev = whole(packed[2], 0), whole(packed[2], 1)
+    to_next, to_prev = whole(tails[2], 0), whole(tails[2], 1)
     home_first = lax.axis_index("dom") % 2 == 0
     home_lists[0:1, :] = jnp.where(home_first, to_next, to_prev)
     home_lists[1:2, :] = jnp.where(home_first, to_prev, to_next)
@@ -203,11 +244,11 @@
     @pl.when(is_local())
     def _():
         hidden[...] = here[...]
-        inner[...] = listed(mate[:, :1], there[...], block)
+        inner[...] = listed(mate[:, :1], there[: hidden.shape[0], :], block)
 
     @pl.when(jnp.logical_not(is_local()))
     def _():
-        hidden[...] = there[...]
+        hidden[...] = there[: hidden.shape[0], :]
         inner[...] = listed(mate[:, :1], here[...], block)
 
 
@@ -234,8 +275,12 @@
     t, _ = normalize(u * jax.nn.sigmoid(u))
     out = (h[...].astype(F32) + t * gain[...]).astype(BF16)
     h_out[...] = out
-    for side, ref in enumerate(to):
+    for side, ref in zip((OUTER, INNER), reversed(to)):
         ref[...] = listed(lists[side : side + 1, :1], out, block)
+
+
+def inner_kernel(lists, h, out):
+    out[...] = listed(lists[INNER : INNER + 1, :1], h[...], out.shape[0])
 
 
 def save_kernel(plane, parity, a, u, h, *refs):
@@ -253,12 +298,11 @@
         h_out[at, :] = h[...]
 
 
-def backward_kernel(halo_in, finish, parity, kept, take, *refs):
+def backward_kernel(sides, finish, parity, kept, take, *refs):
     packed, gain = take
     w_send, _, _, w_fold = quarters(packed)
     lists, upstream, *refs = refs[kept:]
-    if halo_in:
-        inner, outer, *refs = refs
+    arrived, refs = refs[: len(sides)], refs[len(sides) :]
     t_in, r_in, s_in, gown, ghalo_t, c_out, du_out, da_out, es_out, *done, to_inner, to_outer = refs
     edges = gown.shape[0] // 2
     rows = upstream.shape[0]
@@ -266,9 +310,8 @@
     at = slice(parity * rows, (parity + 1) * rows)
     at_edges = slice(parity * edges, (parity + 1) * edges)
     c_out[...] = upstream[...].astype(F32)
-    if halo_in:
-        add_listed(lists[INNER : INNER + 1, :1], c_out, inner[...].astype(F32), block)
-        add_listed(lists[OUTER : OUTER + 1, :1], c_out, outer[...].astype(F32), block)
+    for side, ref in zip(sides, arrived):
+        add_listed(lists[side : side + 1, :1], c_out, ref[...].astype(F32), block)
     if finish:
         done[0][...] = c_out[...].astype(BF16)
     g = c_out[...] * gain[...]
@@ -287,26 +330,28 @@
     to_outer[...] = halo[block:]
 
 
-def backward_own_kernel(kept, take, *refs):
+def backward_own_kernel(add_inner, last, take, *refs):
     _, w_recv, w_node, _ = quarters(take[0])
-    first, refs = refs[:kept], refs[kept:]
-    refs, out = (refs[:-2], refs[-2:]) if first else (refs[:-1], refs[-1:])
-    *beside, c, du, da, es, gown_t = refs
+    if last:
+        _, _, other, *refs = refs
+    if add_inner:
+        lists, inner, *refs = refs
+    refs, out = (refs[:-2], refs[-2:]) if last else (refs[:-1], refs[-1:])
+    *_, c, du, da, es, gown_t = refs
     er = mul_t(da[...], w_recv[...]).astype(BF16)
     both = jnp.concatenate([es[...], er], axis=0)
     total = c[...] + mul_t(du[...], w_node[...]) + mul(gown_t[...], both)
-    if not first:
+    if add_inner:
+        block = inner.shape[0]
+        at = lists[INNER : INNER + 1, :1]
+        value = inner[...].astype(F32)
+        total = total + jnp.concatenate(
+            [jnp.where(at == number, value, 0.0) for number in range(total.shape[0] // block)], axis=0
+        )
+    if last:
+        order(total.astype(BF16), other[...], *out)
+    else:
         out[0][...] = total.astype(out[0].dtype)
-        return
-    *_, other, lists = first
-    [inner] = beside
-    block = inner.shape[0]
-    at = lists[INNER : INNER + 1, :1]
-    value = inner[...].astype(F32)
-    total = total + jnp.concatenate(
-        [jnp.where(at == number, value, 0.0) for number in range(total.shape[0] // block)], axis=0
-    )
-    order(total.astype(BF16), other[...], *out)
 
 
 def order(even, odd, first, second):
@@ -328,11 +373,10 @@
     order(both[:rows, :], both[rows:, :], first, second)
 
 
-def add_kernel(lists, value, inner, outer, other, first, second, total):
+def add_kernel(lists, value, outer, other, first, second, total):
     @pl.when(here_is(1))
     def _():
         total[...] = value[...].astype(F32)
-        add_listed(lists[INNER : INNER + 1, :1], total, inner[...].astype(F32), inner.shape[0])
         add_listed(lists[OUTER : OUTER + 1, :1], total, outer[...].astype(F32), outer.shape[0])
         order(total[...].astype(BF16), other[...], first, second)
 
@@ -473,31 +517,29 @@
     unit = 2 * rows * latent * latent
     dma = pltpu.SemaphoreType.DMA
 
-    here, there, boundary, weights, packed = run(
+    here, there, boundary, packed = run(
         prepare_kernel,
-        (edge_count, jnp.swapaxes(halo_send, 1, 2), inputs, cotangent, edge_send, edge_recv)
-        + (w_send[0], w_recv[0], w_node[0], w_message[0], w_aggregate[0]),
-        [
-            (wide, BF16),
-            (wide, BF16),
-            (narrow, BF16),
-            ((4 * latent, latent), BF16),
-            ((3, 8, block), jnp.int32),
+        (edge_count, jnp.swapaxes(halo_send, 1, 2), inputs, cotangent, edge_send, edge_recv),
+        [(wide, BF16), ((rows + 16, latent), BF16), (narrow, BF16), ((16, block), BF16)],
+        spaces=(pltpu.HBM,) * 6,
+        out_spaces=(pltpu.HBM,) * 3,
+        scratch=[
+            pltpu.SMEM((edge_blocks,), jnp.int32),
+            pltpu.SMEM((1, 1, 2), jnp.int32),
+            pltpu.VMEM(wide, BF16),
+            pltpu.VMEM((rows + 16, latent), BF16),
+            pltpu.VMEM(narrow, BF16),
+            pltpu.VMEM((2, 8, block), jnp.int32),
+            dma((7,)),
+            dma((3,)),
         ],
-        spaces=(pltpu.SMEM, pltpu.SMEM) + (pltpu.HBM,) * 9,
-        scratch=[pltpu.VMEM((2, latent, latent), BF16), pltpu.VMEM((latent, latent), BF16), dma((5,)), dma((6,))],
         vmem=56,
     )
-    packed_there = send(packed, lambda z, y, x, c: (z, 1 - y, x, 1 - c))
     there = flip_y(there)
     outer = send(boundary, lambda z, y, x, c: (z + 2 * y - 1, c, x, 1 - y))
-    even, odd = run(arrange_kernel, (weights, flip_core(weights)), [((4 * latent, latent), BF16)] * 2)
-    gain_even, gain_odd = run(arrange_kernel, (gains, flip_core(gains)), [((1, latent), F32)] * 2)
-    matrices = ((even, gain_even), (odd, gain_odd))
-
     gown, gown_t, ghalo, ghalo_t, lists, mate, home_lists = run(
         functools.partial(graph_kernel, edge_blocks),
-        (even, packed, packed_there),
+        (packed, there),
         [
             ((2 * edges, rows), BF16),
             ((rows, 2 * edges), BF16),
@@ -508,7 +550,19 @@
             ((2, block), jnp.int32),
         ],
     )
-    hidden, inner = run(entry_kernel, (mate, here, there), [(wide, BF16), (narrow, BF16)])
+    hidden, inner = run(entry_kernel, (mate, here, there), [(wide, BF16), (narrow, BF16)], cost=LONG)
+
+    [weights] = run(
+        weights_kernel,
+        (w_send[0], w_recv[0], w_node[0], w_message[0], w_aggregate[0]),
+        [((4 * latent, latent), BF16)],
+        spaces=(pltpu.HBM,) * 5,
+        scratch=[pltpu.VMEM((2, latent, latent), BF16), dma((5,))],
+        vmem=56,
+    )
+    even, odd = run(arrange_kernel, (weights, flip_core(weights), hidden), [((4 * latent, latent), BF16)] * 2)
+    gain_even, gain_odd = run(arrange_kernel, (gains, flip_core(gains), hidden), [((1, latent), F32)] * 2)
+    matrices = ((even, gain_even), (odd, gain_odd))
     upstream = hidden
 
     saved = ()
@@ -519,7 +573,8 @@
         a_own, u_own = run_section(
             forward_own_kernel, plane, (packed,), (hidden, gown) + arrived, [(edge_wide, F32), (wide, F32)], cost=BESIDE
         )
-        to_send = [(narrow, BF16)] * 2 if tick < sections - 1 else []
+        step = (tick + 1) // 2 - plane if tick < sections - 1 else None
+        to_send = [(narrow, BF16)] * {0: 2, 1: 1, None: 0}[step]
         hidden, a, u, *to = run_section(
             forward_kernel,
             plane,
@@ -529,12 +584,14 @@
         )
         produced = hidden
         if to:
-            step = (tick + 1) // 2 - plane
-            outer = towards(to[OUTER], OUTER, step)
-            if step:
-                hidden = send(hidden, lambda z, y, x, c: (z, y, x + 1, c))
-            inner = towards(to[INNER], INNER, step)
-            arrived = () if step else (inner,)
+            outer = towards(to[-1], OUTER, step)
+        if step == 0:
+            inner = towards(to[0], INNER, step)
+            arrived = (inner,)
+        elif step:
+            hidden = send(hidden, lambda z, y, x, c: (z, y, x + 1, c))
+            inner = towards(*run(inner_kernel, (lists, hidden), [(narrow, BF16)]), INNER, 0)
+            arrived = ()
         saved = run(
             functools.partial(save_kernel, plane, parity),
             (a, u, produced) + tuple(saved),
@@ -544,49 +601,44 @@
         )
 
     *states, both = saved
-    inner = outer = None
-    handed = ()
+    halos = {}
     finished = {}
     for tick in range(sections - 1, -1, -1):
         plane, parity = tick // 2, tick % 2
         packed, gain = matrices[parity]
         step = (tick - 1) // 2 - plane if tick else 0
-        halo_in = inner is not None
-        finish = halo_in and tick % 2 == 0
+        finish = bool(halos) and tick % 2 == 0
         outs = [(wide, F32), (wide, BF16), (edge_wide, BF16), (edge_wide, BF16)]
         outs += [(wide, BF16)] if finish else []
         outs += [(narrow, BF16)] * 2
-        kept = handed if tick == 1 else ()
+        kept = (to_outer,) if tick == 1 else ()
         c, du, da, es, *done, to_inner, to_outer = run_section(
-            functools.partial(backward_kernel, halo_in, finish, parity, len(kept)),
+            functools.partial(backward_kernel, tuple(halos), finish, parity, len(kept)),
             plane,
             (packed, gain),
-            kept + (lists, upstream) + ((inner, outer) if halo_in else ()) + tuple(states) + (gown, ghalo_t),
+            kept + (lists, upstream) + tuple(halos.values()) + tuple(states) + (gown, ghalo_t),
             outs,
-            elsewhere={0: -2, 1: -1} if tick == 1 else {},
+            elsewhere={0: -1} if tick == 1 else {},
             cost=BESIDE // 2 if tick == sections - 2 else 1,
         )
         if done:
             finished[tick + 1] = done[0]
-        if step == 0:
-            inner = towards(to_inner, INNER, 0)
-            if tick:
-                outer = towards(to_outer, OUTER, 0)
-        else:
-            handed = (to_inner, to_outer)
-            outer = towards(to_outer, OUTER, step)
-            inner = towards(to_inner, INNER, step)
-        beside = (inner,) if step == 0 else tuple(first_home)
-        kept = tuple(ends) + (finished[1], lists) if tick == 0 else ()
+        inner = towards(to_inner, INNER, 0)
+        halos = {OUTER: towards(to_outer, OUTER, step)} if tick else {}
+        add_inner = tick == 0 or step != 0
+        last = tuple(ends) + (finished[1],) if tick == 0 else ()
+        beside = (lists, inner) if add_inner else (inner,)
         upstream, *rest = run_section(
-            functools.partial(backward_own_kernel, len(kept)),
+            functools.partial(backward_own_kernel, add_inner, bool(last)),
             plane,
             (packed,),
-            kept + beside + (c, du, da, es, gown_t),
-            [(wide, BF16)] * 2 if tick == 0 else [(wide, BF16 if step else F32)],
-            elsewhere={0: -2, 1: -1} if tick == 0 else {},
+            last + beside + (tuple(first_home) if step else ()) + (c, du, da, es, gown_t),
+            [(wide, BF16)] * 2 if last else [(wide, BF16 if step else F32)],
+            elsewhere={0: -2, 1: -1} if last else {},
             cost=BESIDE if tick else 1,
         )
+        if not add_inner:
+            halos = {INNER: inner, **halos}
         if tick == sections - 1:
             outputs, upstream = lax.optimization_barrier((both, upstream))
             first_home = go_home(*run(order_kernel, (outputs,), [(wide, BF16)] * 2), plane=0)
@@ -598,7 +650,7 @@
             second_home = go_home(*run(order_kernel, (outputs,), [(wide, BF16)] * 2), plane=1)
             ends = run(
                 add_kernel,
-                (lists, own, inner, outer, finished[3]),
+                (lists, own, halos[OUTER], finished[3]),
                 [(wide, BF16)] * 2,
                 scratch=[pltpu.VMEM(wide, F32)],
             )

time: 97.7 us -> 94.9 us (0.971)
  starting transfers between devices: 43.1 us -> 34.3 us
  waiting for transfers between devices: 35.9 us -> 39.4 us
  Pallas kernels: 14.9 us -> 16.7 us
    ppermute x28 -> x27, starting transfers between devices: 43.1 us -> 34.3 us  [send(): return lax.ppermute(value, AXES, table)]
    ppermute x28 -> x27, waiting for transfers between devices: 35.9 us -> 39.4 us  [send(): return lax.ppermute(value, AXES, table)]
    pallas_call x31 -> x33, Pallas kernels: 14.9 us -> 16.7 us  [run(): pl.pallas_call(kernel, out_shape=[jax.ShapeDtypeStruct(s, t) for s, t in...]
  transfers between devices with their start and end apart: 28 -> 27, of which waited for: 10 -> 12; matrix products, arithmetic and copies ran while one was open for 0% -> 0% of each run, Pallas kernels for 5% -> 9%
where the time goes in v6:
time: 94.9 us; the launch traced here: 93 us
  waiting for transfers between devices  39.4 us (42%)
  starting transfers between devices  34.3 us (36%)
  Pallas kernels  16.7 us (18%)
  local copies, waits for them, and re-layouts  1.45 us (2%)
  between operations  1.15 us (1%)
    ppermute x27, waiting for transfers between devices, send(): return lax.ppermute(value, AXES, table)  39.4 us
    ppermute x27, starting transfers between devices, send(): return lax.ppermute(value, AXES, table)  34.3 us
    pallas_call x33, Pallas kernels, run(): pl.pallas_call(kernel, out_shape=[jax.ShapeDtypeStruct(s, t) for s, t in...  16.7 us
  transfers between devices with their start and end apart: 27, of which 12 were waited for; matrix products, arithmetic and copies ran while one was open for 0% of the time, Pallas kernels for 9%

profile of v6, /device:TPU:0, one launch (start us, length us, event | category | flops | bytes accessed | tf_op | source)
XLA Modules:
  0.0 93.0 jit_solution(15876264036790431362)
XLA Ops:
  0.6 3.0 %shard_map.132 = (bf16[256,512]{1,0:T(8,128)(2,1)}, bf16[272,512]{1,0:T(8,128)(2,1)}, bf16[128,512]{1,0:T(8,128)(2,1)}, bf16[16,128]{1,0:T(8,128)(2,1)}) custom-call(s32[2]{0:T(128)} %count_in.1, s32[1,1,2]{2,1,0:T(1,128)} %bitcast.11, bf16[2,256,512]{2,1,0:T(8,128)(2,1)} %inputs.1, bf16[2,256,512]{2,1,0:T(8,128)(2,1)} %cotangent.1, s32[2,128]{1,0:T(2,128)} %send_in.1, ...), custom_call_target="tpu_custom_call" | custom-call | flops 1 | bytes 1 | tf_op jit(solution)/shard_map/pallas_call | solution.py:429
  3.6 3.0 %collective-permute-start.1 = (bf16[272,512]{1,0:T(8,128)(2,1)}, bf16[272,512]{1,0:T(8,128)(2,1)S(1)}, u32[]{:S(2)}, u32[]{:S(2)}) collective-permute-start(bf16[272,512]{1,0:T(8,128)(2,1)} %get-tuple-element.103), channel_id=1, source_target_pairs={{0,4},{1,5},{2,6},{3,7},{4,0},{5,1},{6,2},{7,3},{8,12},{9,13},{10,... | collective-permute-start | bytes 835592 | tf_op jit(solution)/shard_map/ppermute | solution.py:495
  6.6 3.1 %shard_map.131.mine = bf16[2048,512]{1,0:T(8,128)(2,1)} custom-call(bf16[512,512]{1,0:T(8,128)(2,1)} %bitcast.6, bf16[512,512]{1,0:T(8,128)(2,1)} %bitcast.7, bf16[512,512]{1,0:T(8,128)(2,1)} %bitcast.8, bf16[512,512]{1,0:T(8,128)(2,1)} %bitcast.9, bf16[512,512]{1,0:T(8,128)(2,1)} %bitcast.10), custom_call_target="tpu_custom_call" | custom-call | flops 1 | bytes 1 | tf_op jit(solution)/shard_map/pallas_call | solution.py:429
  10.3 3.3 %collective-permute-start.3 = (bf16[128,512]{1,0:T(8,128)(2,1)S(1)}, bf16[128,512]{1,0:T(8,128)(2,1)S(1)}, u32[]{:S(2)}, u32[]{:S(2)}) collective-permute-start(bf16[128,512]{1,0:T(8,128)(2,1)S(1)} %copy-done.4), channel_id=1, source_target_pairs={{0,25},{1,29},{2,27},{3,31},{4,8},{5,12},{6,10},{7,14},{8,1},{9,5}... | collective-permute-start | bytes 393224 | tf_op jit(solution)/shard_map/ppermute | solution.py:495
  14.8 1.4 %copy-done = bf16[2048,512]{1,0:T(8,128)(2,1)S(1)} copy-done((bf16[2048,512]{1,0:T(8,128)(2,1)S(1)}, bf16[2048,512]{1,0:T(8,128)(2,1)}, u32[]{:S(2)}) %copy-start) | copy-done | bytes 2097176
  19.2 2.7 %collective-permute-start.5 = (bf16[128,512]{1,0:T(8,128)(2,1)S(1)}, bf16[128,512]{1,0:T(8,128)(2,1)S(1)}, u32[]{:S(2)}, u32[]{:S(2)}) collective-permute-start(bf16[128,512]{1,0:T(8,128)(2,1)S(1)} %get-tuple-element.123), channel_id=1, source_target_pairs={{0,25},{1,8},{2,27},{3,10},{4,29},{5,12},{6,31},{7,14},{8,1},{9,16... | collective-permute-start | bytes 393224 | tf_op jit(solution)/shard_map/ppermute | solution.py:495
  23.2 3.7 %collective-permute-done.5.refs_7_ = bf16[128,512]{1,0:T(8,128)(2,1)S(1)} collective-permute-done((bf16[128,512]{1,0:T(8,128)(2,1)S(1)}, bf16[128,512]{1,0:T(8,128)(2,1)S(1)}, u32[]{:S(2)}, u32[]{:S(2)}) %collective-permute-start.5) | collective-permute-done | bytes 131104 | tf_op jit(solution)/shard_map/ppermute | solution.py:495
  28.1 2.4 %collective-permute-start.8 = (bf16[128,512]{1,0:T(8,128)(2,1)S(1)}, bf16[128,512]{1,0:T(8,128)(2,1)S(1)}, u32[]{:S(2)}, u32[]{:S(2)}) collective-permute-start(bf16[128,512]{1,0:T(8,128)(2,1)S(1)} %get-tuple-element.127), channel_id=1, source_target_pairs={{0,27},{1,10},{2,25},{3,8},{4,31},{5,14},{6,29},{7,12},{8,3},{9,18... | collective-permute-start | bytes 393224 | tf_op jit(solution)/shard_map/ppermute | solution.py:495
  31.0 5.9 %collective-permute-done.6.refs_1_.h.refs_3_ = bf16[256,512]{1,0:T(8,128)(2,1)S(1)} collective-permute-done((bf16[256,512]{1,0:T(8,128)(2,1)S(1)}, bf16[256,512]{1,0:T(8,128)(2,1)S(1)}, u32[]{:S(2)}, u32[]{:S(2)}) %collective-permute-start.6) | collective-permute-done | bytes 262176 | tf_op jit(solution)/shard_map/ppermute | solution.py:495
  37.0 1.3 %collective-permute-done.7.refs_6_ = bf16[128,512]{1,0:T(8,128)(2,1)S(1)} collective-permute-done((bf16[128,512]{1,0:T(8,128)(2,1)S(1)}, bf16[128,512]{1,0:T(8,128)(2,1)S(1)}, u32[]{:S(2)}, u32[]{:S(2)}) %collective-permute-start.7) | collective-permute-done | bytes 131104 | tf_op jit(solution)/shard_map/ppermute | solution.py:495
  38.5 2.4 %collective-permute-start.10 = (bf16[128,512]{1,0:T(8,128)(2,1)S(1)}, bf16[128,512]{1,0:T(8,128)(2,1)S(1)}, u32[]{:S(2)}, u32[]{:S(2)}) collective-permute-start(bf16[128,512]{1,0:T(8,128)(2,1)S(1)} %get-tuple-element.132), channel_id=1, source_target_pairs={{0,25},{1,8},{2,27},{3,10},{4,29},{5,12},{6,31},{7,14},{8,1},{9,16... | collective-permute-start | bytes 393224 | tf_op jit(solution)/shard_map/ppermute | solution.py:495
  40.9 4.7 %collective-permute-done.10.refs_7_ = bf16[128,512]{1,0:T(8,128)(2,1)S(1)} collective-permute-done((bf16[128,512]{1,0:T(8,128)(2,1)S(1)}, bf16[128,512]{1,0:T(8,128)(2,1)S(1)}, u32[]{:S(2)}, u32[]{:S(2)}) %collective-permute-start.10) | collective-permute-done | bytes 131104 | tf_op jit(solution)/shard_map/ppermute | solution.py:495
  45.5 1.5 %collective-permute-start.14 = (bf16[128,512]{1,0:T(8,128)(2,1)S(1)}, bf16[128,512]{1,0:T(8,128)(2,1)S(1)}, u32[]{:S(2)}, u32[]{:S(2)}) collective-permute-start(bf16[128,512]{1,0:T(8,128)(2,1)S(1)} %get-tuple-element.168), channel_id=1, source_target_pairs={{0,25},{1,8},{2,27},{3,10},{4,29},{5,12},{6,31},{7,14},{8,1},{9,16... | collective-permute-start | bytes 393224 | tf_op jit(solution)/shard_map/ppermute | solution.py:495
  47.8 5.8 %collective-permute-start.13 = (bf16[256,512]{1,0:T(8,128)(2,1)S(1)}, bf16[256,512]{1,0:T(8,128)(2,1)S(1)}, u32[]{:S(2)}, u32[]{:S(2)}) collective-permute-start(bf16[256,512]{1,0:T(8,128)(2,1)S(1)} %get-tuple-element.166), channel_id=1, source_target_pairs={{0,1},{1,5},{4,0},{5,4},{8,9},{9,13},{12,8},{13,12},{16,17},{17,21... | collective-permute-start | bytes 786440 | tf_op jit(solution)/shard_map/ppermute | solution.py:495
  53.7 1.3 %collective-permute-done.15.refs_2_ = bf16[128,512]{1,0:T(8,128)(2,1)S(1)} collective-permute-done((bf16[128,512]{1,0:T(8,128)(2,1)S(1)}, bf16[128,512]{1,0:T(8,128)(2,1)S(1)}, u32[]{:S(2)}, u32[]{:S(2)}) %collective-permute-start.15) | collective-permute-done | bytes 131104 | tf_op jit(solution)/shard_map/ppermute | solution.py:495
  55.0 3.7 %collective-permute-done.13.refs_4_.refs_1_ = bf16[256,512]{1,0:T(8,128)(2,1)S(1)} collective-permute-done((bf16[256,512]{1,0:T(8,128)(2,1)S(1)}, bf16[256,512]{1,0:T(8,128)(2,1)S(1)}, u32[]{:S(2)}, u32[]{:S(2)}) %collective-permute-start.13) | collective-permute-done | bytes 262176 | tf_op jit(solution)/shard_map/ppermute | solution.py:495
  60.1 6.4 %collective-permute-done.17.refs_5_ = bf16[128,512]{1,0:T(8,128)(2,1)S(1)} collective-permute-done((bf16[128,512]{1,0:T(8,128)(2,1)S(1)}, bf16[128,512]{1,0:T(8,128)(2,1)S(1)}, u32[]{:S(2)}, u32[]{:S(2)}) %collective-permute-start.17) | collective-permute-done | bytes 131104 | tf_op jit(solution)/shard_map/ppermute | solution.py:495
  66.5 2.3 %collective-permute-done.16.refs_4_ = bf16[256,512]{1,0:T(8,128)(2,1)S(1)} collective-permute-done((bf16[256,512]{1,0:T(8,128)(2,1)S(1)}, bf16[256,512]{1,0:T(8,128)(2,1)S(1)}, u32[]{:S(2)}, u32[]{:S(2)}) %collective-permute-start.16) | collective-permute-done | bytes 262176 | tf_op jit(solution)/shard_map/ppermute | solution.py:495
  70.0 1.6 %collective-permute-start.21 = (bf16[128,512]{1,0:T(8,128)(2,1)S(1)}, bf16[128,512]{1,0:T(8,128)(2,1)S(1)}, u32[]{:S(2)}, u32[]{:S(2)}) collective-permute-start(bf16[128,512]{1,0:T(8,128)(2,1)S(1)} %get-tuple-element.183), channel_id=1, source_target_pairs={{0,25},{1,8},{2,27},{3,10},{4,29},{5,12},{6,31},{7,14},{8,1},{9,16... | collective-permute-start | bytes 393224 | tf_op jit(solution)/shard_map/ppermute | solution.py:495
  72.2 4.5 %collective-permute-done.21.outer.refs_5_ = bf16[128,512]{1,0:T(8,128)(2,1)S(1)} collective-permute-done((bf16[128,512]{1,0:T(8,128)(2,1)S(1)}, bf16[128,512]{1,0:T(8,128)(2,1)S(1)}, u32[]{:S(2)}, u32[]{:S(2)}) %collective-permute-start.21) | collective-permute-done | bytes 131104 | tf_op jit(solution)/shard_map/ppermute | solution.py:495
  76.7 1.2 %shard_map.159 = (f32[256,512]{1,0:T(8,128)S(1)}, bf16[256,512]{1,0:T(8,128)(2,1)S(1)}, bf16[256,512]{1,0:T(8,128)(2,1)S(1)}, bf16[256,512]{1,0:T(8,128)(2,1)S(1...) custom-call(bf16[2048,512]{1,0:T(8,128)(2,1)S(1)} %get-tuple-element.110.refs_0_, ...), custom_call_target="tpu_custom_call" | custom-call | flops 1 | bytes 1 | tf_op jit(solution)/shard_map/pallas_call | solution.py:429
  78.0 3.6 %collective-permute-start.25 = (bf16[128,512]{1,0:T(8,128)(2,1)S(1)}, bf16[128,512]{1,0:T(8,128)(2,1)S(1)}, u32[]{:S(2)}, u32[]{:S(2)}) collective-permute-start(bf16[128,512]{1,0:T(8,128)(2,1)S(1)} %get-tuple-element.197), channel_id=1, source_target_pairs={{0,28},{1,8},{2,30},{3,10},{4,29},{5,9},{6,31},{7,11},{8,4},{9,16}... | collective-permute-start | bytes 393224 | tf_op jit(solution)/shard_map/ppermute | solution.py:495
  82.9 1.8 %collective-permute-start.24 = (bf16[256,512]{1,0:T(8,128)(2,1)S(1)}, bf16[256,512]{1,0:T(8,128)(2,1)S(1)}, u32[]{:S(2)}, u32[]{:S(2)}) collective-permute-start(bf16[256,512]{1,0:T(8,128)(2,1)S(1)} %get-tuple-element.195), channel_id=1, source_target_pairs={{0,1},{1,5},{2,3},{3,7},{4,0},{5,4},{6,2},{7,6},{8,9},{9,13},{10,1... | collective-permute-start | bytes 786440 | tf_op jit(solution)/shard_map/ppermute | solution.py:495
  87.4 4.4 %collective-permute-done.24.refs_1_ = bf16[256,512]{1,0:T(8,128)(2,1)S(1)} collective-permute-done((bf16[256,512]{1,0:T(8,128)(2,1)S(1)}, bf16[256,512]{1,0:T(8,128)(2,1)S(1)}, u32[]{:S(2)}, u32[]{:S(2)}) %collective-permute-start.24) | collective-permute-done | bytes 262176 | tf_op jit(solution)/shard_map/ppermute | solution.py:495
  (73 shorter events, 17.2 us)
Async XLA Ops:
  3.6 10.7 %collective-permute-start.1 = (bf16[272,512]{1,0:T(8,128)(2,1)}, bf16[272,512]{1,0:T(8,128)(2,1)S(1)}, u32[]{:S(2)}, u32[]{:S(2)}) collective-permute-start(bf16[272,512]{1,0:T(8,128)(2,1)} %get-tuple-element.103), channel_id=1, source_target_pairs={{0,4},{1,5},{2,6},{3,7},{4,0},{5,1},{6,2},{7,3},{8,12},{9,13},{10,... | collective-permute-start | bytes 835592 | tf_op jit(solution)/shard_map/ppermute | solution.py:495
  9.8 5.0 %collective-permute-start = (bf16[2048,512]{1,0:T(8,128)(2,1)}, bf16[2048,512]{1,0:T(8,128)(2,1)S(1)}, u32[]{:S(2)}, u32[]{:S(2)}) collective-permute-start(bf16[2048,512]{1,0:T(8,128)(2,1)} %shard_map.131.mine), channel_id=1, source_target_pairs={{0,1},{1,0},{2,3},{3,2},{4,5},{5,4},{6,7},{7,6},{8,9},{9,8},{10,11... | collective-permute-start | bytes 6291464 | tf_op jit(solution)/shard_map/ppermute | solution.py:495
  9.8 4.9 %collective-permute-start.2 = (f32[1,512]{1,0:T(1,128)S(1)}, f32[1,512]{1,0:T(1,128)S(1)}, u32[]{:S(2)}, u32[]{:S(2)}) collective-permute-start(f32[1,512]{1,0:T(1,128)S(1)} %copy-done.2), channel_id=1, source_target_pairs={{0,1},{1,0},{2,3},{3,2},{4,5},{5,4},{6,7},{7,6},{8,9},{9,8},{10,11... | collective-permute-start | bytes 6152 | tf_op jit(solution)/shard_map/ppermute | solution.py:495
  10.3 7.7 %collective-permute-start.3 = (bf16[128,512]{1,0:T(8,128)(2,1)S(1)}, bf16[128,512]{1,0:T(8,128)(2,1)S(1)}, u32[]{:S(2)}, u32[]{:S(2)}) collective-permute-start(bf16[128,512]{1,0:T(8,128)(2,1)S(1)} %copy-done.4), channel_id=1, source_target_pairs={{0,25},{1,29},{2,27},{3,31},{4,8},{5,12},{6,10},{7,14},{8,1},{9,5}... | collective-permute-start | bytes 393224 | tf_op jit(solution)/shard_map/ppermute | solution.py:495
  19.2 3.2 %collective-permute-start.4 = (bf16[128,512]{1,0:T(8,128)(2,1)S(1)}, bf16[128,512]{1,0:T(8,128)(2,1)S(1)}, u32[]{:S(2)}, u32[]{:S(2)}) collective-permute-start(bf16[128,512]{1,0:T(8,128)(2,1)S(1)} %get-tuple-element.120), channel_id=1, source_target_pairs={{0,1},{1,0},{2,3},{3,2},{4,5},{5,4},{6,7},{7,6},{8,9},{9,8},{10,11... | collective-permute-start | bytes 393224 | tf_op jit(solution)/shard_map/ppermute | solution.py:495
  19.2 7.6 %collective-permute-start.5 = (bf16[128,512]{1,0:T(8,128)(2,1)S(1)}, bf16[128,512]{1,0:T(8,128)(2,1)S(1)}, u32[]{:S(2)}, u32[]{:S(2)}) collective-permute-start(bf16[128,512]{1,0:T(8,128)(2,1)S(1)} %get-tuple-element.123), channel_id=1, source_target_pairs={{0,25},{1,8},{2,27},{3,10},{4,29},{5,12},{6,31},{7,14},{8,1},{9,16... | collective-permute-start | bytes 393224 | tf_op jit(solution)/shard_map/ppermute | solution.py:495
  28.0 8.9 %collective-permute-start.6 = (bf16[256,512]{1,0:T(8,128)(2,1)S(1)}, bf16[256,512]{1,0:T(8,128)(2,1)S(1)}, u32[]{:S(2)}, u32[]{:S(2)}) collective-permute-start(bf16[256,512]{1,0:T(8,128)(2,1)S(1)} %get-tuple-element.124.h), channel_id=1, source_target_pairs={{0,2},{1,3},{2,0},{3,1},{4,6},{5,7},{6,4},{7,5},{8,10},{9,11},{10,... | collective-permute-start | bytes 786440 | tf_op jit(solution)/shard_map/ppermute | solution.py:495
  28.1 8.9 %collective-permute-start.8 = (bf16[128,512]{1,0:T(8,128)(2,1)S(1)}, bf16[128,512]{1,0:T(8,128)(2,1)S(1)}, u32[]{:S(2)}, u32[]{:S(2)}) collective-permute-start(bf16[128,512]{1,0:T(8,128)(2,1)S(1)} %get-tuple-element.127), channel_id=1, source_target_pairs={{0,27},{1,10},{2,25},{3,8},{4,31},{5,14},{6,29},{7,12},{8,3},{9,18... | collective-permute-start | bytes 393224 | tf_op jit(solution)/shard_map/ppermute | solution.py:495
  38.3 2.5 %collective-permute-start.9 = (bf16[128,512]{1,0:T(8,128)(2,1)S(1)}, bf16[128,512]{1,0:T(8,128)(2,1)S(1)}, u32[]{:S(2)}, u32[]{:S(2)}) collective-permute-start(bf16[128,512]{1,0:T(8,128)(2,1)S(1)} %get-tuple-element.129), channel_id=1, source_target_pairs={{0,1},{1,0},{2,3},{3,2},{4,5},{5,4},{6,7},{7,6},{8,9},{9,8},{10,11... | collective-permute-start | bytes 393224 | tf_op jit(solution)/shard_map/ppermute | solution.py:495
  38.5 7.0 %collective-permute-start.10 = (bf16[128,512]{1,0:T(8,128)(2,1)S(1)}, bf16[128,512]{1,0:T(8,128)(2,1)S(1)}, u32[]{:S(2)}, u32[]{:S(2)}) collective-permute-start(bf16[128,512]{1,0:T(8,128)(2,1)S(1)} %get-tuple-element.132), channel_id=1, source_target_pairs={{0,25},{1,8},{2,27},{3,10},{4,29},{5,12},{6,31},{7,14},{8,1},{9,16... | collective-permute-start | bytes 393224 | tf_op jit(solution)/shard_map/ppermute | solution.py:495
  45.5 8.0 %collective-permute-start.14 = (bf16[128,512]{1,0:T(8,128)(2,1)S(1)}, bf16[128,512]{1,0:T(8,128)(2,1)S(1)}, u32[]{:S(2)}, u32[]{:S(2)}) collective-permute-start(bf16[128,512]{1,0:T(8,128)(2,1)S(1)} %get-tuple-element.168), channel_id=1, source_target_pairs={{0,25},{1,8},{2,27},{3,10},{4,29},{5,12},{6,31},{7,14},{8,1},{9,16... | collective-permute-start | bytes 393224 | tf_op jit(solution)/shard_map/ppermute | solution.py:495
  47.1 7.9 %collective-permute-start.12 = (bf16[256,512]{1,0:T(8,128)(2,1)S(1)}, bf16[256,512]{1,0:T(8,128)(2,1)S(1)}, u32[]{:S(2)}, u32[]{:S(2)}) collective-permute-start(bf16[256,512]{1,0:T(8,128)(2,1)S(1)} %get-tuple-element.165), channel_id=1, source_target_pairs={{0,0},{1,4},{4,1},{5,5},{8,8},{9,12},{12,9},{13,13},{16,16},{17,20... | collective-permute-start | bytes 786440 | tf_op jit(solution)/shard_map/ppermute | solution.py:495
  47.8 10.9 %collective-permute-start.13 = (bf16[256,512]{1,0:T(8,128)(2,1)S(1)}, bf16[256,512]{1,0:T(8,128)(2,1)S(1)}, u32[]{:S(2)}, u32[]{:S(2)}) collective-permute-start(bf16[256,512]{1,0:T(8,128)(2,1)S(1)} %get-tuple-element.166), channel_id=1, source_target_pairs={{0,1},{1,5},{4,0},{5,4},{8,9},{9,13},{12,8},{13,12},{16,17},{17,21... | collective-permute-start | bytes 786440 | tf_op jit(solution)/shard_map/ppermute | solution.py:495
  58.7 10.1 %collective-permute-start.16 = (bf16[256,512]{1,0:T(8,128)(2,1)S(1)}, bf16[256,512]{1,0:T(8,128)(2,1)S(1)}, u32[]{:S(2)}, u32[]{:S(2)}) collective-permute-start(bf16[256,512]{1,0:T(8,128)(2,1)S(1)} %shard_map.154.value), channel_id=1, source_target_pairs={{0,2},{1,3},{2,0},{3,1},{4,6},{5,7},{6,4},{7,5},{8,10},{9,11},{10,... | collective-permute-start | bytes 786440 | tf_op jit(solution)/shard_map/ppermute | solution.py:495
  59.2 7.3 %collective-permute-start.17 = (bf16[128,512]{1,0:T(8,128)(2,1)S(1)}, bf16[128,512]{1,0:T(8,128)(2,1)S(1)}, u32[]{:S(2)}, u32[]{:S(2)}) collective-permute-start(bf16[128,512]{1,0:T(8,128)(2,1)S(1)} %get-tuple-element.169.refs_2_), channel_id=1, source_target_pairs={{0,27},{1,10},{2,25},{3,8},{4,31},{5,14},{6,29},{7,12},{8,3},{9,18... | collective-permute-start | bytes 393224 | tf_op jit(solution)/shard_map/ppermute | solution.py:495
  69.9 1.7 %collective-permute-start.18 = (bf16[128,512]{1,0:T(8,128)(2,1)S(1)}, bf16[128,512]{1,0:T(8,128)(2,1)S(1)}, u32[]{:S(2)}, u32[]{:S(2)}) collective-permute-start(bf16[128,512]{1,0:T(8,128)(2,1)S(1)} %get-tuple-element.175), channel_id=1, source_target_pairs={{0,1},{1,0},{2,3},{3,2},{4,5},{5,4},{6,7},{7,6},{8,9},{9,8},{10,11... | collective-permute-start | bytes 393224 | tf_op jit(solution)/shard_map/ppermute | solution.py:495
  70.0 6.7 %collective-permute-start.21 = (bf16[128,512]{1,0:T(8,128)(2,1)S(1)}, bf16[128,512]{1,0:T(8,128)(2,1)S(1)}, u32[]{:S(2)}, u32[]{:S(2)}) collective-permute-start(bf16[128,512]{1,0:T(8,128)(2,1)S(1)} %get-tuple-element.183), channel_id=1, source_target_pairs={{0,25},{1,8},{2,27},{3,10},{4,29},{5,12},{6,31},{7,14},{8,1},{9,16... | collective-permute-start | bytes 393224 | tf_op jit(solution)/shard_map/ppermute | solution.py:495
  77.9 3.6 %collective-permute-start.22 = (bf16[128,512]{1,0:T(8,128)(2,1)S(1)}, bf16[128,512]{1,0:T(8,128)(2,1)S(1)}, u32[]{:S(2)}, u32[]{:S(2)}) collective-permute-start(bf16[128,512]{1,0:T(8,128)(2,1)S(1)} %get-tuple-element.189), channel_id=1, source_target_pairs={{0,1},{1,0},{2,3},{3,2},{4,5},{5,4},{6,7},{7,6},{8,9},{9,8},{10,11... | collective-permute-start | bytes 393224 | tf_op jit(solution)/shard_map/ppermute | solution.py:495
  78.0 6.8 %collective-permute-start.25 = (bf16[128,512]{1,0:T(8,128)(2,1)S(1)}, bf16[128,512]{1,0:T(8,128)(2,1)S(1)}, u32[]{:S(2)}, u32[]{:S(2)}) collective-permute-start(bf16[128,512]{1,0:T(8,128)(2,1)S(1)} %get-tuple-element.197), channel_id=1, source_target_pairs={{0,28},{1,8},{2,30},{3,10},{4,29},{5,9},{6,31},{7,11},{8,4},{9,16}... | collective-permute-start | bytes 393224 | tf_op jit(solution)/shard_map/ppermute | solution.py:495
  82.2 5.2 %collective-permute-start.23 = (bf16[256,512]{1,0:T(8,128)(2,1)S(1)}, bf16[256,512]{1,0:T(8,128)(2,1)S(1)}, u32[]{:S(2)}, u32[]{:S(2)}) collective-permute-start(bf16[256,512]{1,0:T(8,128)(2,1)S(1)} %get-tuple-element.194), channel_id=1, source_target_pairs={{0,0},{1,4},{2,2},{3,6},{4,1},{5,5},{6,3},{7,7},{8,8},{9,12},{10,1... | collective-permute-start | bytes 786440 | tf_op jit(solution)/shard_map/ppermute | solution.py:495
  82.9 8.8 %collective-permute-start.24 = (bf16[256,512]{1,0:T(8,128)(2,1)S(1)}, bf16[256,512]{1,0:T(8,128)(2,1)S(1)}, u32[]{:S(2)}, u32[]{:S(2)}) collective-permute-start(bf16[256,512]{1,0:T(8,128)(2,1)S(1)} %get-tuple-element.195), channel_id=1, source_target_pairs={{0,1},{1,5},{2,3},{3,7},{4,0},{5,4},{6,2},{7,6},{8,9},{9,13},{10,1... | collective-permute-start | bytes 786440 | tf_op jit(solution)/shard_map/ppermute | solution.py:495
  84.7 2.5 %collective-permute-start.26 = (bf16[128,512]{1,0:T(8,128)(2,1)S(1)}, bf16[128,512]{1,0:T(8,128)(2,1)S(1)}, u32[]{:S(2)}, u32[]{:S(2)}) collective-permute-start(bf16[128,512]{1,0:T(8,128)(2,1)S(1)} %collective-permute-done.25.outer), channel_id=1, source_target_pairs={{0,1},{1,0},{2,3},{3,2},{4,5},{5,4},{6,7},{7,6},{8,9},{9,8},{10,11... | collective-permute-start | bytes 393224 | tf_op jit(solution)/shard_map/ppermute | solution.py:495
  85.8 6.0 %collective-permute-start.19 = (bf16[256,512]{1,0:T(8,128)(2,1)S(1)}, bf16[256,512]{1,0:T(8,128)(2,1)S(1)}, u32[]{:S(2)}, u32[]{:S(2)}) collective-permute-start(bf16[256,512]{1,0:T(8,128)(2,1)S(1)} %get-tuple-element.181), channel_id=1, source_target_pairs={{2,2},{3,6},{6,3},{7,7},{10,10},{11,14},{14,11},{15,15},{18,18},{1... | collective-permute-start | bytes 786440 | tf_op jit(solution)/shard_map/ppermute | solution.py:495
  86.5 5.4 %collective-permute-start.20 = (bf16[256,512]{1,0:T(8,128)(2,1)S(1)}, bf16[256,512]{1,0:T(8,128)(2,1)S(1)}, u32[]{:S(2)}, u32[]{:S(2)}) collective-permute-start(bf16[256,512]{1,0:T(8,128)(2,1)S(1)} %get-tuple-element.182), channel_id=1, source_target_pairs={{2,3},{3,7},{6,2},{7,6},{10,11},{11,15},{14,10},{15,14},{18,19},{1... | collective-permute-start | bytes 786440 | tf_op jit(solution)/shard_map/ppermute | solution.py:495
  (8 other events, 28.5 us)

commit v7 on v6

--- a/solution.py
+++ b/solution.py
@@ -117,10 +117,7 @@
             pltpu.make_async_copy(source.at[micro], here_rows, sems.at[5]),
         ]
 
-    def fetch_boundary(source, number):
-        start = pl.multiple_of(number * block, block)
-        place = source.at[lax.axis_index("pipe") % 2, pl.ds(start, block), :]
-        return pltpu.make_async_copy(place, boundary_rows, sems.at[6])
+    blocks = pltpu.make_async_copy(inputs.at[lax.axis_index("pipe") % 2], boundary_rows, sems.at[6])
 
     for copy in lists + ids:
         copy.start()
@@ -135,10 +132,10 @@
         for copy in fetch(cotangent):
             copy.start()
 
+    blocks.start()
     for copy in lists:
         copy.wait()
     number = jnp.where(micro == 1, halo[0, 0, 0], halo[0, 0, 1])
-    fetch_boundary(inputs, number).start()
     for copy in ids:
         copy.wait()
     lane = lax.broadcasted_iota(jnp.int32, (1, block), 1)
@@ -154,13 +151,15 @@
     leaving = [
         pltpu.make_async_copy(there_rows, there, out_sems.at[0]),
         pltpu.make_async_copy(here_rows, here, out_sems.at[1]),
-        pltpu.make_async_copy(boundary_rows, boundary, out_sems.at[2]),
+        pltpu.make_async_copy(
+            boundary_rows.at[pl.ds(pl.multiple_of(number * block, block), block), :], boundary, out_sems.at[2]
+        ),
     ]
     fetched[0].wait()
     leaving[0].start()
     fetched[1].wait()
     leaving[1].start()
-    fetch_boundary(inputs, number).wait()
+    blocks.wait()
     leaving[2].start()
     for copy in leaving:
         copy.wait()
@@ -182,16 +181,26 @@
         copy.wait()
 
 
-def arrange_kernel(mine, swapped, _, even, odd):
+def place_mine_kernel(mine, even, odd):
     @pl.when(here_is(parity=0))
     def _():
         even[...] = mine[...]
+
+    @pl.when(here_is(parity=1))
+    def _():
+        odd[...] = mine[...]
+
+
+def place_swapped_kernel(swapped, _, even_in, odd_in, even, odd):
+    del even_in, odd_in
+
+    @pl.when(here_is(parity=0))
+    def _():
         odd[...] = swapped[...]
 
     @pl.when(here_is(parity=1))
     def _():
         even[...] = swapped[...]
-        odd[...] = mine[...]
 
 
 def graph_kernel(edge_blocks, packed, there, gown, gown_t, ghalo, ghalo_t, lists, mate, home_lists):
@@ -238,7 +247,7 @@
     home_lists[1:2, :] = jnp.where(home_first, to_prev, to_next)
 
 
-def entry_kernel(mate, here, there, hidden, inner):
+def entry_kernel(mate, here, there, _, hidden, inner):
     block = inner.shape[0]
 
     @pl.when(is_local())
@@ -261,9 +270,10 @@
     u_out[...] = mul(h[...], w_node[...])
 
 
-def forward_kernel(take, lists, h, a_own, u_own, inner, outer, ghalo, gown_t, h_out, a_out, u_out, *to):
-    packed, gain = take
+def forward_kernel(parity, take, lists, h, a_own, u_own, inner, outer, ghalo, gown_t, h_out, a_out, u_out, *to):
+    packed, *gains = take
     w_send, _, _, w_fold = quarters(packed)
+    gain = jnp.where(here_is(parity=parity), gains[0][...], gains[1][...])
     edges = ghalo.shape[0]
     block = inner.shape[0]
     halo = (mul(ghalo[:, :block], inner[...]) + mul(ghalo[:, block:], outer[...])).astype(BF16)
@@ -273,7 +283,7 @@
     u = u_own[...] + mul(mul(gown_t[:, edges:], q).astype(BF16), w_fold[...])
     u_out[...] = u
     t, _ = normalize(u * jax.nn.sigmoid(u))
-    out = (h[...].astype(F32) + t * gain[...]).astype(BF16)
+    out = (h[...].astype(F32) + t * gain).astype(BF16)
     h_out[...] = out
     for side, ref in zip((OUTER, INNER), reversed(to)):
         ref[...] = listed(lists[side : side + 1, :1], out, block)
@@ -299,8 +309,9 @@
 
 
 def backward_kernel(sides, finish, parity, kept, take, *refs):
-    packed, gain = take
+    packed, *gains = take
     w_send, _, _, w_fold = quarters(packed)
+    gain = jnp.where(here_is(parity=parity), gains[0][...], gains[1][...])
     lists, upstream, *refs = refs[kept:]
     arrived, refs = refs[: len(sides)], refs[len(sides) :]
     t_in, r_in, s_in, gown, ghalo_t, c_out, du_out, da_out, es_out, *done, to_inner, to_outer = refs
@@ -311,10 +322,13 @@
     at_edges = slice(parity * edges, (parity + 1) * edges)
     c_out[...] = upstream[...].astype(F32)
     for side, ref in zip(sides, arrived):
-        add_listed(lists[side : side + 1, :1], c_out, ref[...].astype(F32), block)
+        if ref.shape == c_out.shape:
+            c_out[...] = c_out[...] + ref[...]
+        else:
+            add_listed(lists[side : side + 1, :1], c_out, ref[...].astype(F32), block)
     if finish:
         done[0][...] = c_out[...].astype(BF16)
-    g = c_out[...] * gain[...]
+    g = c_out[...] * gain
     t = t_in[at, :].astype(F32)
     centre = jnp.mean(g, axis=-1, keepdims=True)
     along = jnp.mean(g * t, axis=-1, keepdims=True)
@@ -381,6 +395,14 @@
         order(total[...].astype(BF16), other[...], first, second)
 
 
+def spread_kernel(lists, outer, out):
+    block = outer.shape[0]
+    at = lists[OUTER : OUTER + 1, :1]
+    value = outer[...].astype(F32)
+    for number in range(out.shape[0] // block):
+        out[number * block : (number + 1) * block, :] = jnp.where(at == number, value, 0.0)
+
+
 def place_kernel(lists, outer, flipped, first, second):
     block = outer.shape[0]
     at = lists[OUTER : OUTER + 1, :1]
@@ -508,8 +530,14 @@
 
     def towards(value, side, step):
         if side == INNER:
-            return send(value, lambda z, y, x, c: (z, y, x + step, 1 - c))
-        return send(value, lambda z, y, x, c: (z + 2 * c - 1, y, x + step, 1 - c))
+            return send(value, lambda z, y, x, c: (z, y, x, 1 - c))
+        return send(value, lambda z, y, x, c: (z + 2 * c - 1, y, x + step, 1 - c) if crosses(x, step) else None)
+
+    def crosses(x, step):
+        return step == 0 or 0 <= x + step < sections // 2
+
+    def across(value, step):
+        return send(value, lambda z, y, x, c: (z, y, x + step, c) if crosses(x, step) else None)
 
     wide = (rows, latent)
     edge_wide = (edges, latent)
@@ -528,7 +556,7 @@
             pltpu.SMEM((1, 1, 2), jnp.int32),
             pltpu.VMEM(wide, BF16),
             pltpu.VMEM((rows + 16, latent), BF16),
-            pltpu.VMEM(narrow, BF16),
+            pltpu.VMEM(wide, BF16),
             pltpu.VMEM((2, 8, block), jnp.int32),
             dma((7,)),
             dma((3,)),
@@ -550,7 +578,7 @@
             ((2, block), jnp.int32),
         ],
     )
-    hidden, inner = run(entry_kernel, (mate, here, there), [(wide, BF16), (narrow, BF16)], cost=LONG)
+    hidden, inner = run(entry_kernel, (mate, here, there, outer), [(wide, BF16), (narrow, BF16)], cost=LONG)
 
     [weights] = run(
         weights_kernel,
@@ -560,27 +588,33 @@
         scratch=[pltpu.VMEM((2, latent, latent), BF16), dma((5,))],
         vmem=56,
     )
-    even, odd = run(arrange_kernel, (weights, flip_core(weights), hidden), [((4 * latent, latent), BF16)] * 2)
-    gain_even, gain_odd = run(arrange_kernel, (gains, flip_core(gains), hidden), [((1, latent), F32)] * 2)
-    matrices = ((even, gain_even), (odd, gain_odd))
+    pair = run(place_mine_kernel, (weights,), [((4 * latent, latent), BF16)] * 2)
+    matrices = run(
+        place_swapped_kernel, (flip_core(weights), hidden, *pair), [((4 * latent, latent), BF16)] * 2, aliases={2: 0, 3: 1}
+    )
+    both_gains = (gains, flip_core(gains))
     upstream = hidden
 
     saved = ()
     arrived = ()
     for tick in range(sections):
         plane, parity = tick // 2, tick % 2
-        packed, gain = matrices[parity]
+        packed = matrices[parity]
         a_own, u_own = run_section(
             forward_own_kernel, plane, (packed,), (hidden, gown) + arrived, [(edge_wide, F32), (wide, F32)], cost=BESIDE
         )
+        if tick == sections - 1:
+            outputs, a_own = lax.optimization_barrier((saved[3], a_own))
+            first_home = go_home(*run(order_kernel, (outputs,), [(wide, BF16)] * 2), plane=0)
         step = (tick + 1) // 2 - plane if tick < sections - 1 else None
         to_send = [(narrow, BF16)] * {0: 2, 1: 1, None: 0}[step]
         hidden, a, u, *to = run_section(
-            forward_kernel,
+            functools.partial(forward_kernel, parity),
             plane,
-            (packed, gain),
+            (packed, *both_gains),
             (lists, hidden, a_own, u_own, inner, outer, ghalo, gown_t),
             [(wide, BF16), (edge_wide, F32), (wide, F32)] + to_send,
+            cost=1 if to_send else BESIDE // 2,
         )
         produced = hidden
         if to:
@@ -589,7 +623,7 @@
             inner = towards(to[0], INNER, step)
             arrived = (inner,)
         elif step:
-            hidden = send(hidden, lambda z, y, x, c: (z, y, x + 1, c))
+            hidden = across(hidden, step)
             inner = towards(*run(inner_kernel, (lists, hidden), [(narrow, BF16)]), INNER, 0)
             arrived = ()
         saved = run(
@@ -605,7 +639,7 @@
     finished = {}
     for tick in range(sections - 1, -1, -1):
         plane, parity = tick // 2, tick % 2
-        packed, gain = matrices[parity]
+        packed = matrices[parity]
         step = (tick - 1) // 2 - plane if tick else 0
         finish = bool(halos) and tick % 2 == 0
         outs = [(wide, F32), (wide, BF16), (edge_wide, BF16), (edge_wide, BF16)]
@@ -615,11 +649,10 @@
         c, du, da, es, *done, to_inner, to_outer = run_section(
             functools.partial(backward_kernel, tuple(halos), finish, parity, len(kept)),
             plane,
-            (packed, gain),
+            (packed, *both_gains),
             kept + (lists, upstream) + tuple(halos.values()) + tuple(states) + (gown, ghalo_t),
             outs,
             elsewhere={0: -1} if tick == 1 else {},
-            cost=BESIDE // 2 if tick == sections - 2 else 1,
         )
         if done:
             finished[tick + 1] = done[0]
@@ -632,19 +665,17 @@
             functools.partial(backward_own_kernel, add_inner, bool(last)),
             plane,
             (packed,),
-            last + beside + (tuple(first_home) if step else ()) + (c, du, da, es, gown_t),
+            last + beside + (tuple(first_home) if tick == sections - 1 else ()) + (c, du, da, es, gown_t),
             [(wide, BF16)] * 2 if last else [(wide, BF16 if step else F32)],
             elsewhere={0: -2, 1: -1} if last else {},
             cost=BESIDE if tick else 1,
         )
         if not add_inner:
             halos = {INNER: inner, **halos}
-        if tick == sections - 1:
-            outputs, upstream = lax.optimization_barrier((both, upstream))
-            first_home = go_home(*run(order_kernel, (outputs,), [(wide, BF16)] * 2), plane=0)
         if step:
             own = upstream
-            upstream = send(upstream, lambda z, y, x, c: (z, y, x + 1, c))
+            upstream = across(upstream, step)
+            halos = {OUTER: run(spread_kernel, (lists, halos[OUTER]), [(wide, F32)], cost=LONG)[0]}
         elif tick == 1:
             outputs, upstream = lax.optimization_barrier((both, upstream))
             second_home = go_home(*run(order_kernel, (outputs,), [(wide, BF16)] * 2), plane=1)

time: 94.9 us -> 93.9 us (0.989); the launches traced: 93 us -> 93.6 us
  waiting for transfers between devices: 39.4 us -> 41.4 us
  starting transfers between devices: 34.3 us -> 32.9 us
    ppermute x27, waiting for transfers between devices: 39.4 us -> 41.4 us  [send(): return lax.ppermute(value, AXES, table)]
    ppermute x27, starting transfers between devices: 34.3 us -> 32.9 us  [send(): return lax.ppermute(value, AXES, table)]
    pallas_call x33 -> x34, Pallas kernels: 16.7 us -> 16.5 us  [run(): pl.pallas_call(kernel, out_shape=[jax.ShapeDtypeStruct(s, t) for s, t in...]
  transfers between devices with their start and end apart: 27 -> 27, of which waited for: 12 -> 13; matrix products, arithmetic and copies ran while one was open for 0% -> 0% of each run, Pallas kernels for 9% -> 9%
where the time goes in v7:
time: 93.9 us; the launch traced here: 93.6 us
  waiting for transfers between devices  41.4 us (44%)
  starting transfers between devices  32.9 us (35%)
  Pallas kernels  16.5 us (18%)
  local copies, waits for them, and re-layouts  1.61 us (2%)
  between operations  1.17 us (1%)
    ppermute x27, waiting for transfers between devices, send(): return lax.ppermute(value, AXES, table)  41.4 us
    ppermute x27, starting transfers between devices, send(): return lax.ppermute(value, AXES, table)  32.9 us
    pallas_call x34, Pallas kernels, run(): pl.pallas_call(kernel, out_shape=[jax.ShapeDtypeStruct(s, t) for s, t in...  16.5 us
  transfers between devices with their start and end apart: 27, of which 13 were waited for; matrix products, arithmetic and copies ran while one was open for 0% of the time, Pallas kernels for 9%

profile of v7, /device:TPU:0, one launch (start us, length us, event | category | flops | bytes accessed | tf_op | source)
XLA Modules:
  0.0 93.6 jit_solution(14853010627677090092)
XLA Ops:
  0.6 2.5 %shard_map.132 = (bf16[256,512]{1,0:T(8,128)(2,1)}, bf16[272,512]{1,0:T(8,128)(2,1)}, bf16[128,512]{1,0:T(8,128)(2,1)}, bf16[16,128]{1,0:T(8,128)(2,1)}) custom-call(s32[2]{0:T(128)} %count_in.1, s32[1,1,2]{2,1,0:T(1,128)} %bitcast.11, bf16[2,256,512]{2,1,0:T(8,128)(2,1)} %inputs.1, bf16[2,256,512]{2,1,0:T(8,128)(2,1)} %cotangent.1, s32[2,128]{1,0:T(2,128)} %send_in.1, ...), custom_call_target="tpu_custom_call" | custom-call | flops 1 | bytes 1 | tf_op jit(solution)/shard_map/pallas_call | solution.py:451
  3.1 3.0 %collective-permute-start.1 = (bf16[272,512]{1,0:T(8,128)(2,1)}, bf16[272,512]{1,0:T(8,128)(2,1)S(1)}, u32[]{:S(2)}, u32[]{:S(2)}) collective-permute-start(bf16[272,512]{1,0:T(8,128)(2,1)} %get-tuple-element.103), channel_id=1, source_target_pairs={{0,4},{1,5},{2,6},{3,7},{4,0},{5,1},{6,2},{7,3},{8,12},{9,13},{10,... | collective-permute-start | bytes 835592 | tf_op jit(solution)/shard_map/ppermute | solution.py:517
  6.2 3.1 %shard_map.131.mine = bf16[2048,512]{1,0:T(8,128)(2,1)} custom-call(bf16[512,512]{1,0:T(8,128)(2,1)} %bitcast.6, bf16[512,512]{1,0:T(8,128)(2,1)} %bitcast.7, bf16[512,512]{1,0:T(8,128)(2,1)} %bitcast.8, bf16[512,512]{1,0:T(8,128)(2,1)} %bitcast.9, bf16[512,512]{1,0:T(8,128)(2,1)} %bitcast.10), custom_call_target="tpu_custom_call" | custom-call | flops 1 | bytes 1 | tf_op jit(solution)/shard_map/pallas_call | solution.py:451
  9.4 3.7 %collective-permute-start.2 = (bf16[128,512]{1,0:T(8,128)(2,1)S(1)}, bf16[128,512]{1,0:T(8,128)(2,1)S(1)}, u32[]{:S(2)}, u32[]{:S(2)}) collective-permute-start(bf16[128,512]{1,0:T(8,128)(2,1)S(1)} %copy-done.4), channel_id=1, source_target_pairs={{0,25},{1,29},{2,27},{3,31},{4,8},{5,12},{6,10},{7,14},{8,1},{9,5}... | collective-permute-start | bytes 393224 | tf_op jit(solution)/shard_map/ppermute | solution.py:517
  13.1 1.6 %copy-done = bf16[2048,512]{1,0:T(8,128)(2,1)S(1)} copy-done((bf16[2048,512]{1,0:T(8,128)(2,1)S(1)}, bf16[2048,512]{1,0:T(8,128)(2,1)}, u32[]{:S(2)}) %copy-start) | copy-done | bytes 2097176
  15.2 1.9 %collective-permute-done.2._.refs_8_ = bf16[128,512]{1,0:T(8,128)(2,1)S(1)} collective-permute-done((bf16[128,512]{1,0:T(8,128)(2,1)S(1)}, bf16[128,512]{1,0:T(8,128)(2,1)S(1)}, u32[]{:S(2)}, u32[]{:S(2)}) %collective-permute-start.2) | collective-permute-done | bytes 131104 | tf_op jit(solution)/shard_map/ppermute | solution.py:517
  19.5 3.0 %collective-permute-start.5 = (bf16[128,512]{1,0:T(8,128)(2,1)S(1)}, bf16[128,512]{1,0:T(8,128)(2,1)S(1)}, u32[]{:S(2)}, u32[]{:S(2)}) collective-permute-start(bf16[128,512]{1,0:T(8,128)(2,1)S(1)} %get-tuple-element.123), channel_id=1, source_target_pairs={{0,25},{1,8},{2,27},{3,10},{4,29},{5,12},{6,31},{7,14},{8,1},{9,16... | collective-permute-start | bytes 393224 | tf_op jit(solution)/shard_map/ppermute | solution.py:517
  23.8 3.4 %collective-permute-done.5.refs_8_ = bf16[128,512]{1,0:T(8,128)(2,1)S(1)} collective-permute-done((bf16[128,512]{1,0:T(8,128)(2,1)S(1)}, bf16[128,512]{1,0:T(8,128)(2,1)S(1)}, u32[]{:S(2)}, u32[]{:S(2)}) %collective-permute-start.5) | collective-permute-done | bytes 131104 | tf_op jit(solution)/shard_map/ppermute | solution.py:517
  28.3 1.3 %collective-permute-start.8 = (bf16[128,512]{1,0:T(8,128)(2,1)S(1)}, bf16[128,512]{1,0:T(8,128)(2,1)S(1)}, u32[]{:S(2)}, u32[]{:S(2)}) collective-permute-start(bf16[128,512]{1,0:T(8,128)(2,1)S(1)} %get-tuple-element.127), channel_id=1, source_target_pairs={{0,27},{1,10},{4,31},{5,14},{8,3},{9,18},{12,7},{13,22},{16,11},{1... | collective-permute-start | bytes 393224 | tf_op jit(solution)/shard_map/ppermute | solution.py:517
  29.6 1.3 %collective-permute-start.6 = (bf16[256,512]{1,0:T(8,128)(2,1)S(1)}, bf16[256,512]{1,0:T(8,128)(2,1)S(1)}, u32[]{:S(2)}, u32[]{:S(2)}) collective-permute-start(bf16[256,512]{1,0:T(8,128)(2,1)S(1)} %get-tuple-element.124.h), channel_id=1, source_target_pairs={{0,2},{1,3},{4,6},{5,7},{8,10},{9,11},{12,14},{13,15},{16,18},{17,... | collective-permute-start | bytes 786440 | tf_op jit(solution)/shard_map/ppermute | solution.py:517
  31.4 4.9 %collective-permute-done.6.refs_1_.h.refs_4_ = bf16[256,512]{1,0:T(8,128)(2,1)S(1)} collective-permute-done((bf16[256,512]{1,0:T(8,128)(2,1)S(1)}, bf16[256,512]{1,0:T(8,128)(2,1)S(1)}, u32[]{:S(2)}, u32[]{:S(2)}) %collective-permute-start.6) | collective-permute-done | bytes 262176 | tf_op jit(solution)/shard_map/ppermute | solution.py:517
  37.9 3.1 %collective-permute-start.12 = (bf16[128,512]{1,0:T(8,128)(2,1)S(1)}, bf16[128,512]{1,0:T(8,128)(2,1)S(1)}, u32[]{:S(2)}, u32[]{:S(2)}) collective-permute-start(bf16[128,512]{1,0:T(8,128)(2,1)S(1)} %get-tuple-element.151), channel_id=1, source_target_pairs={{0,25},{1,8},{2,27},{3,10},{4,29},{5,12},{6,31},{7,14},{8,1},{9,16... | collective-permute-start | bytes 393224 | tf_op jit(solution)/shard_map/ppermute | solution.py:517
  41.8 3.5 %collective-permute-start.11 = (bf16[256,512]{1,0:T(8,128)(2,1)S(1)}, bf16[256,512]{1,0:T(8,128)(2,1)S(1)}, u32[]{:S(2)}, u32[]{:S(2)}) collective-permute-start(bf16[256,512]{1,0:T(8,128)(2,1)S(1)} %get-tuple-element.148), channel_id=1, source_target_pairs={{0,1},{1,5},{4,0},{5,4},{8,9},{9,13},{12,8},{13,12},{16,17},{17,21... | collective-permute-start | bytes 786440 | tf_op jit(solution)/shard_map/ppermute | solution.py:517
  45.5 1.7 %collective-permute-start.14 = (bf16[128,512]{1,0:T(8,128)(2,1)S(1)}, bf16[128,512]{1,0:T(8,128)(2,1)S(1)}, u32[]{:S(2)}, u32[]{:S(2)}) collective-permute-start(bf16[128,512]{1,0:T(8,128)(2,1)S(1)} %get-tuple-element.168), channel_id=1, source_target_pairs={{0,25},{1,8},{2,27},{3,10},{4,29},{5,12},{6,31},{7,14},{8,1},{9,16... | collective-permute-start | bytes 393224 | tf_op jit(solution)/shard_map/ppermute | solution.py:517
  47.2 3.2 %collective-permute-done.11.refs_3_.refs_1_ = bf16[256,512]{1,0:T(8,128)(2,1)S(1)} collective-permute-done((bf16[256,512]{1,0:T(8,128)(2,1)S(1)}, bf16[256,512]{1,0:T(8,128)(2,1)S(1)}, u32[]{:S(2)}, u32[]{:S(2)}) %collective-permute-start.11) | collective-permute-done | bytes 262176 | tf_op jit(solution)/shard_map/ppermute | solution.py:517
  50.4 1.5 %collective-permute-done.14.refs_6_ = bf16[128,512]{1,0:T(8,128)(2,1)S(1)} collective-permute-done((bf16[128,512]{1,0:T(8,128)(2,1)S(1)}, bf16[128,512]{1,0:T(8,128)(2,1)S(1)}, u32[]{:S(2)}, u32[]{:S(2)}) %collective-permute-start.14) | collective-permute-done | bytes 131104 | tf_op jit(solution)/shard_map/ppermute | solution.py:517
  54.8 10.3 %collective-permute-done.17.outer = bf16[128,512]{1,0:T(8,128)(2,1)S(1)} collective-permute-done((bf16[128,512]{1,0:T(8,128)(2,1)S(1)}, bf16[128,512]{1,0:T(8,128)(2,1)S(1)}, u32[]{:S(2)}, u32[]{:S(2)}) %collective-permute-start.17) | collective-permute-done | bytes 131104 | tf_op jit(solution)/shard_map/ppermute | solution.py:517
  65.1 5.1 %collective-permute-done.16.refs_5_ = bf16[256,512]{1,0:T(8,128)(2,1)S(1)} collective-permute-done((bf16[256,512]{1,0:T(8,128)(2,1)S(1)}, bf16[256,512]{1,0:T(8,128)(2,1)S(1)}, u32[]{:S(2)}, u32[]{:S(2)}) %collective-permute-start.16) | collective-permute-done | bytes 262176 | tf_op jit(solution)/shard_map/ppermute | solution.py:517
  71.4 2.4 %collective-permute-start.21 = (bf16[128,512]{1,0:T(8,128)(2,1)S(1)}, bf16[128,512]{1,0:T(8,128)(2,1)S(1)}, u32[]{:S(2)}, u32[]{:S(2)}) collective-permute-start(bf16[128,512]{1,0:T(8,128)(2,1)S(1)} %get-tuple-element.183), channel_id=1, source_target_pairs={{0,25},{1,8},{2,27},{3,10},{4,29},{5,12},{6,31},{7,14},{8,1},{9,16... | collective-permute-start | bytes 393224 | tf_op jit(solution)/shard_map/ppermute | solution.py:517
  74.5 3.7 %collective-permute-done.21.outer.refs_6_ = bf16[128,512]{1,0:T(8,128)(2,1)S(1)} collective-permute-done((bf16[128,512]{1,0:T(8,128)(2,1)S(1)}, bf16[128,512]{1,0:T(8,128)(2,1)S(1)}, u32[]{:S(2)}, u32[]{:S(2)}) %collective-permute-start.21) | collective-permute-done | bytes 131104 | tf_op jit(solution)/shard_map/ppermute | solution.py:517
  79.4 2.0 %collective-permute-start.25 = (bf16[128,512]{1,0:T(8,128)(2,1)S(1)}, bf16[128,512]{1,0:T(8,128)(2,1)S(1)}, u32[]{:S(2)}, u32[]{:S(2)}) collective-permute-start(bf16[128,512]{1,0:T(8,128)(2,1)S(1)} %get-tuple-element.197), channel_id=1, source_target_pairs={{0,28},{1,8},{2,30},{3,10},{4,29},{5,9},{6,31},{7,11},{8,4},{9,16}... | collective-permute-start | bytes 393224 | tf_op jit(solution)/shard_map/ppermute | solution.py:517
  82.8 1.6 %collective-permute-start.24 = (bf16[256,512]{1,0:T(8,128)(2,1)S(1)}, bf16[256,512]{1,0:T(8,128)(2,1)S(1)}, u32[]{:S(2)}, u32[]{:S(2)}) collective-permute-start(bf16[256,512]{1,0:T(8,128)(2,1)S(1)} %get-tuple-element.195), channel_id=1, source_target_pairs={{0,1},{1,5},{2,3},{3,7},{4,0},{5,4},{6,2},{7,6},{8,9},{9,13},{10,1... | collective-permute-start | bytes 786440 | tf_op jit(solution)/shard_map/ppermute | solution.py:517
  84.4 1.6 %collective-permute-done.25.outer = bf16[128,512]{1,0:T(8,128)(2,1)S(1)} collective-permute-done((bf16[128,512]{1,0:T(8,128)(2,1)S(1)}, bf16[128,512]{1,0:T(8,128)(2,1)S(1)}, u32[]{:S(2)}, u32[]{:S(2)}) %collective-permute-start.25) | collective-permute-done | bytes 131104 | tf_op jit(solution)/shard_map/ppermute | solution.py:517
  88.1 4.2 %collective-permute-done.24.refs_1_ = bf16[256,512]{1,0:T(8,128)(2,1)S(1)} collective-permute-done((bf16[256,512]{1,0:T(8,128)(2,1)S(1)}, bf16[256,512]{1,0:T(8,128)(2,1)S(1)}, u32[]{:S(2)}, u32[]{:S(2)}) %collective-permute-start.24) | collective-permute-done | bytes 262176 | tf_op jit(solution)/shard_map/ppermute | solution.py:517
  (74 shorter events, 18.7 us)
Async XLA Ops:
  3.1 11.7 %collective-permute-start.1 = (bf16[272,512]{1,0:T(8,128)(2,1)}, bf16[272,512]{1,0:T(8,128)(2,1)S(1)}, u32[]{:S(2)}, u32[]{:S(2)}) collective-permute-start(bf16[272,512]{1,0:T(8,128)(2,1)} %get-tuple-element.103), channel_id=1, source_target_pairs={{0,4},{1,5},{2,6},{3,7},{4,0},{5,1},{6,2},{7,3},{8,12},{9,13},{10,... | collective-permute-start | bytes 835592 | tf_op jit(solution)/shard_map/ppermute | solution.py:517
  9.3 7.9 %collective-permute-start = (bf16[2048,512]{1,0:T(8,128)(2,1)}, bf16[2048,512]{1,0:T(8,128)(2,1)S(1)}, u32[]{:S(2)}, u32[]{:S(2)}) collective-permute-start(bf16[2048,512]{1,0:T(8,128)(2,1)} %shard_map.131.mine), channel_id=1, source_target_pairs={{0,1},{1,0},{2,3},{3,2},{4,5},{5,4},{6,7},{7,6},{8,9},{9,8},{10,11... | collective-permute-start | bytes 6291464 | tf_op jit(solution)/shard_map/ppermute | solution.py:517
  9.4 7.7 %collective-permute-start.2 = (bf16[128,512]{1,0:T(8,128)(2,1)S(1)}, bf16[128,512]{1,0:T(8,128)(2,1)S(1)}, u32[]{:S(2)}, u32[]{:S(2)}) collective-permute-start(bf16[128,512]{1,0:T(8,128)(2,1)S(1)} %copy-done.4), channel_id=1, source_target_pairs={{0,25},{1,29},{2,27},{3,31},{4,8},{5,12},{6,10},{7,14},{8,1},{9,5}... | collective-permute-start | bytes 393224 | tf_op jit(solution)/shard_map/ppermute | solution.py:517
  13.1 5.1 %collective-permute-start.3 = (f32[1,512]{1,0:T(1,128)S(1)}, f32[1,512]{1,0:T(1,128)S(1)}, u32[]{:S(2)}, u32[]{:S(2)}) collective-permute-start(f32[1,512]{1,0:T(1,128)S(1)} %copy-done.1), channel_id=1, source_target_pairs={{0,1},{1,0},{2,3},{3,2},{4,5},{5,4},{6,7},{7,6},{8,9},{9,8},{10,11... | collective-permute-start | bytes 6152 | tf_op jit(solution)/shard_map/ppermute | solution.py:517
  19.4 3.6 %collective-permute-start.4 = (bf16[128,512]{1,0:T(8,128)(2,1)S(1)}, bf16[128,512]{1,0:T(8,128)(2,1)S(1)}, u32[]{:S(2)}, u32[]{:S(2)}) collective-permute-start(bf16[128,512]{1,0:T(8,128)(2,1)S(1)} %get-tuple-element.120), channel_id=1, source_target_pairs={{0,1},{1,0},{2,3},{3,2},{4,5},{5,4},{6,7},{7,6},{8,9},{9,8},{10,11... | collective-permute-start | bytes 393224 | tf_op jit(solution)/shard_map/ppermute | solution.py:517
  19.5 7.7 %collective-permute-start.5 = (bf16[128,512]{1,0:T(8,128)(2,1)S(1)}, bf16[128,512]{1,0:T(8,128)(2,1)S(1)}, u32[]{:S(2)}, u32[]{:S(2)}) collective-permute-start(bf16[128,512]{1,0:T(8,128)(2,1)S(1)} %get-tuple-element.123), channel_id=1, source_target_pairs={{0,25},{1,8},{2,27},{3,10},{4,29},{5,12},{6,31},{7,14},{8,1},{9,16... | collective-permute-start | bytes 393224 | tf_op jit(solution)/shard_map/ppermute | solution.py:517
  28.3 8.2 %collective-permute-start.8 = (bf16[128,512]{1,0:T(8,128)(2,1)S(1)}, bf16[128,512]{1,0:T(8,128)(2,1)S(1)}, u32[]{:S(2)}, u32[]{:S(2)}) collective-permute-start(bf16[128,512]{1,0:T(8,128)(2,1)S(1)} %get-tuple-element.127), channel_id=1, source_target_pairs={{0,27},{1,10},{4,31},{5,14},{8,3},{9,18},{12,7},{13,22},{16,11},{1... | collective-permute-start | bytes 393224 | tf_op jit(solution)/shard_map/ppermute | solution.py:517
  29.6 6.7 %collective-permute-start.6 = (bf16[256,512]{1,0:T(8,128)(2,1)S(1)}, bf16[256,512]{1,0:T(8,128)(2,1)S(1)}, u32[]{:S(2)}, u32[]{:S(2)}) collective-permute-start(bf16[256,512]{1,0:T(8,128)(2,1)S(1)} %get-tuple-element.124.h), channel_id=1, source_target_pairs={{0,2},{1,3},{4,6},{5,7},{8,10},{9,11},{12,14},{13,15},{16,18},{17,... | collective-permute-start | bytes 786440 | tf_op jit(solution)/shard_map/ppermute | solution.py:517
  37.8 3.2 %collective-permute-start.9 = (bf16[128,512]{1,0:T(8,128)(2,1)S(1)}, bf16[128,512]{1,0:T(8,128)(2,1)S(1)}, u32[]{:S(2)}, u32[]{:S(2)}) collective-permute-start(bf16[128,512]{1,0:T(8,128)(2,1)S(1)} %get-tuple-element.144), channel_id=1, source_target_pairs={{0,1},{1,0},{2,3},{3,2},{4,5},{5,4},{6,7},{7,6},{8,9},{9,8},{10,11... | collective-permute-start | bytes 393224 | tf_op jit(solution)/shard_map/ppermute | solution.py:517
  37.9 7.5 %collective-permute-start.12 = (bf16[128,512]{1,0:T(8,128)(2,1)S(1)}, bf16[128,512]{1,0:T(8,128)(2,1)S(1)}, u32[]{:S(2)}, u32[]{:S(2)}) collective-permute-start(bf16[128,512]{1,0:T(8,128)(2,1)S(1)} %get-tuple-element.151), channel_id=1, source_target_pairs={{0,25},{1,8},{2,27},{3,10},{4,29},{5,12},{6,31},{7,14},{8,1},{9,16... | collective-permute-start | bytes 393224 | tf_op jit(solution)/shard_map/ppermute | solution.py:517
  41.1 6.1 %collective-permute-start.10 = (bf16[256,512]{1,0:T(8,128)(2,1)S(1)}, bf16[256,512]{1,0:T(8,128)(2,1)S(1)}, u32[]{:S(2)}, u32[]{:S(2)}) collective-permute-start(bf16[256,512]{1,0:T(8,128)(2,1)S(1)} %get-tuple-element.147), channel_id=1, source_target_pairs={{0,0},{1,4},{4,1},{5,5},{8,8},{9,12},{12,9},{13,13},{16,16},{17,20... | collective-permute-start | bytes 786440 | tf_op jit(solution)/shard_map/ppermute | solution.py:517
  41.8 8.7 %collective-permute-start.11 = (bf16[256,512]{1,0:T(8,128)(2,1)S(1)}, bf16[256,512]{1,0:T(8,128)(2,1)S(1)}, u32[]{:S(2)}, u32[]{:S(2)}) collective-permute-start(bf16[256,512]{1,0:T(8,128)(2,1)S(1)} %get-tuple-element.148), channel_id=1, source_target_pairs={{0,1},{1,5},{4,0},{5,4},{8,9},{9,13},{12,8},{13,12},{16,17},{17,21... | collective-permute-start | bytes 786440 | tf_op jit(solution)/shard_map/ppermute | solution.py:517
  45.5 6.5 %collective-permute-start.14 = (bf16[128,512]{1,0:T(8,128)(2,1)S(1)}, bf16[128,512]{1,0:T(8,128)(2,1)S(1)}, u32[]{:S(2)}, u32[]{:S(2)}) collective-permute-start(bf16[128,512]{1,0:T(8,128)(2,1)S(1)} %get-tuple-element.168), channel_id=1, source_target_pairs={{0,25},{1,8},{2,27},{3,10},{4,29},{5,12},{6,31},{7,14},{8,1},{9,16... | collective-permute-start | bytes 393224 | tf_op jit(solution)/shard_map/ppermute | solution.py:517
  52.0 13.1 %collective-permute-start.17 = (bf16[128,512]{1,0:T(8,128)(2,1)S(1)}, bf16[128,512]{1,0:T(8,128)(2,1)S(1)}, u32[]{:S(2)}, u32[]{:S(2)}) collective-permute-start(bf16[128,512]{1,0:T(8,128)(2,1)S(1)} %get-tuple-element.169.refs_3_), channel_id=1, source_target_pairs={{2,25},{3,8},{6,29},{7,12},{10,1},{11,16},{14,5},{15,20},{18,9},{1... | collective-permute-start | bytes 393224 | tf_op jit(solution)/shard_map/ppermute | solution.py:517
  53.5 16.8 %collective-permute-start.16 = (bf16[256,512]{1,0:T(8,128)(2,1)S(1)}, bf16[256,512]{1,0:T(8,128)(2,1)S(1)}, u32[]{:S(2)}, u32[]{:S(2)}) collective-permute-start(bf16[256,512]{1,0:T(8,128)(2,1)S(1)} %shard_map.154.value), channel_id=1, source_target_pairs={{2,0},{3,1},{6,4},{7,5},{10,8},{11,9},{14,12},{15,13},{18,16},{19,... | collective-permute-start | bytes 786440 | tf_op jit(solution)/shard_map/ppermute | solution.py:517
  71.3 2.5 %collective-permute-start.18 = (bf16[128,512]{1,0:T(8,128)(2,1)S(1)}, bf16[128,512]{1,0:T(8,128)(2,1)S(1)}, u32[]{:S(2)}, u32[]{:S(2)}) collective-permute-start(bf16[128,512]{1,0:T(8,128)(2,1)S(1)} %get-tuple-element.175), channel_id=1, source_target_pairs={{0,1},{1,0},{2,3},{3,2},{4,5},{5,4},{6,7},{7,6},{8,9},{9,8},{10,11... | collective-permute-start | bytes 393224 | tf_op jit(solution)/shard_map/ppermute | solution.py:517
  71.4 6.7 %collective-permute-start.21 = (bf16[128,512]{1,0:T(8,128)(2,1)S(1)}, bf16[128,512]{1,0:T(8,128)(2,1)S(1)}, u32[]{:S(2)}, u32[]{:S(2)}) collective-permute-start(bf16[128,512]{1,0:T(8,128)(2,1)S(1)} %get-tuple-element.183), channel_id=1, source_target_pairs={{0,25},{1,8},{2,27},{3,10},{4,29},{5,12},{6,31},{7,14},{8,1},{9,16... | collective-permute-start | bytes 393224 | tf_op jit(solution)/shard_map/ppermute | solution.py:517
  79.3 2.1 %collective-permute-start.22 = (bf16[128,512]{1,0:T(8,128)(2,1)S(1)}, bf16[128,512]{1,0:T(8,128)(2,1)S(1)}, u32[]{:S(2)}, u32[]{:S(2)}) collective-permute-start(bf16[128,512]{1,0:T(8,128)(2,1)S(1)} %get-tuple-element.189), channel_id=1, source_target_pairs={{0,1},{1,0},{2,3},{3,2},{4,5},{5,4},{6,7},{7,6},{8,9},{9,8},{10,11... | collective-permute-start | bytes 393224 | tf_op jit(solution)/shard_map/ppermute | solution.py:517
  79.4 6.6 %collective-permute-start.25 = (bf16[128,512]{1,0:T(8,128)(2,1)S(1)}, bf16[128,512]{1,0:T(8,128)(2,1)S(1)}, u32[]{:S(2)}, u32[]{:S(2)}) collective-permute-start(bf16[128,512]{1,0:T(8,128)(2,1)S(1)} %get-tuple-element.197), channel_id=1, source_target_pairs={{0,28},{1,8},{2,30},{3,10},{4,29},{5,9},{6,31},{7,11},{8,4},{9,16}... | collective-permute-start | bytes 393224 | tf_op jit(solution)/shard_map/ppermute | solution.py:517
  82.1 5.9 %collective-permute-start.23 = (bf16[256,512]{1,0:T(8,128)(2,1)S(1)}, bf16[256,512]{1,0:T(8,128)(2,1)S(1)}, u32[]{:S(2)}, u32[]{:S(2)}) collective-permute-start(bf16[256,512]{1,0:T(8,128)(2,1)S(1)} %get-tuple-element.194), channel_id=1, source_target_pairs={{0,0},{1,4},{2,2},{3,6},{4,1},{5,5},{6,3},{7,7},{8,8},{9,12},{10,1... | collective-permute-start | bytes 786440 | tf_op jit(solution)/shard_map/ppermute | solution.py:517
  82.8 9.5 %collective-permute-start.24 = (bf16[256,512]{1,0:T(8,128)(2,1)S(1)}, bf16[256,512]{1,0:T(8,128)(2,1)S(1)}, u32[]{:S(2)}, u32[]{:S(2)}) collective-permute-start(bf16[256,512]{1,0:T(8,128)(2,1)S(1)} %get-tuple-element.195), channel_id=1, source_target_pairs={{0,1},{1,5},{2,3},{3,7},{4,0},{5,4},{6,2},{7,6},{8,9},{9,13},{10,1... | collective-permute-start | bytes 786440 | tf_op jit(solution)/shard_map/ppermute | solution.py:517
  86.0 1.9 %collective-permute-start.26 = (bf16[128,512]{1,0:T(8,128)(2,1)S(1)}, bf16[128,512]{1,0:T(8,128)(2,1)S(1)}, u32[]{:S(2)}, u32[]{:S(2)}) collective-permute-start(bf16[128,512]{1,0:T(8,128)(2,1)S(1)} %collective-permute-done.25.outer), channel_id=1, source_target_pairs={{0,1},{1,0},{2,3},{3,2},{4,5},{5,4},{6,7},{7,6},{8,9},{9,8},{10,11... | collective-permute-start | bytes 393224 | tf_op jit(solution)/shard_map/ppermute | solution.py:517
  86.5 5.9 %collective-permute-start.19 = (bf16[256,512]{1,0:T(8,128)(2,1)S(1)}, bf16[256,512]{1,0:T(8,128)(2,1)S(1)}, u32[]{:S(2)}, u32[]{:S(2)}) collective-permute-start(bf16[256,512]{1,0:T(8,128)(2,1)S(1)} %get-tuple-element.181), channel_id=1, source_target_pairs={{2,2},{3,6},{6,3},{7,7},{10,10},{11,14},{14,11},{15,15},{18,18},{1... | collective-permute-start | bytes 786440 | tf_op jit(solution)/shard_map/ppermute | solution.py:517
  87.2 5.2 %collective-permute-start.20 = (bf16[256,512]{1,0:T(8,128)(2,1)S(1)}, bf16[256,512]{1,0:T(8,128)(2,1)S(1)}, u32[]{:S(2)}, u32[]{:S(2)}) collective-permute-start(bf16[256,512]{1,0:T(8,128)(2,1)S(1)} %get-tuple-element.182), channel_id=1, source_target_pairs={{2,3},{3,7},{6,2},{7,6},{10,11},{11,15},{14,10},{15,14},{18,19},{1... | collective-permute-start | bytes 786440 | tf_op jit(solution)/shard_map/ppermute | solution.py:517
  (8 other events, 35.9 us)

commit v8 on v7

--- a/solution.py
+++ b/solution.py
@@ -92,12 +92,9 @@
     packed,
     count,
     halo,
-    here_rows,
-    there_rows,
-    boundary_rows,
+    blocks,
     edges,
     sems,
-    out_sems,
 ):
     micro = lax.axis_index("dom") % 2
     block = boundary.shape[0]
@@ -113,11 +110,11 @@
     ]
     def fetch(source):
         return [
-            pltpu.make_async_copy(source.at[1 - micro], there_rows.at[pl.ds(0, rows), :], sems.at[4]),
-            pltpu.make_async_copy(source.at[micro], here_rows, sems.at[5]),
+            pltpu.make_async_copy(source.at[1 - micro], there.at[pl.ds(0, rows), :], sems.at[4]),
+            pltpu.make_async_copy(source.at[micro], here, sems.at[5]),
         ]
 
-    blocks = pltpu.make_async_copy(inputs.at[lax.axis_index("pipe") % 2], boundary_rows, sems.at[6])
+    whole = pltpu.make_async_copy(inputs.at[lax.axis_index("pipe") % 2], blocks, sems.at[6])
 
     for copy in lists + ids:
         copy.start()
@@ -132,7 +129,7 @@
         for copy in fetch(cotangent):
             copy.start()
 
-    blocks.start()
+    whole.start()
     for copy in lists:
         copy.wait()
     number = jnp.where(micro == 1, halo[0, 0, 0], halo[0, 0, 1])
@@ -145,24 +142,12 @@
     spare = jnp.zeros((7 - 2 * edge_blocks, block), jnp.int32)
     tile = encode(jnp.concatenate([edges[0, :edge_blocks, :], edges[1, :edge_blocks, :], tail, spare], axis=0))
     packed[...] = tile
-    there_rows[rows:, :] = jnp.zeros((there_rows.shape[0] - rows, there_rows.shape[1]), BF16)
-    there_rows[rows:, :block] = tile
-    fetched = fetch(inputs)
-    leaving = [
-        pltpu.make_async_copy(there_rows, there, out_sems.at[0]),
-        pltpu.make_async_copy(here_rows, here, out_sems.at[1]),
-        pltpu.make_async_copy(
-            boundary_rows.at[pl.ds(pl.multiple_of(number * block, block), block), :], boundary, out_sems.at[2]
-        ),
-    ]
-    fetched[0].wait()
-    leaving[0].start()
-    fetched[1].wait()
-    leaving[1].start()
-    blocks.wait()
-    leaving[2].start()
-    for copy in leaving:
+    there[rows:, :] = jnp.zeros((there.shape[0] - rows, there.shape[1]), BF16)
+    there[rows:, :block] = tile
+    for copy in fetch(inputs):
         copy.wait()
+    whole.wait()
+    boundary[...] = blocks[pl.ds(pl.multiple_of(number * block, block), block), :]
 
 
 def weights_kernel(w_send, w_recv, w_node, w_message, w_aggregate, out, factors, sems):
@@ -447,6 +432,10 @@
 
 def run(kernel, operands, outs, spaces=(), aliases=None, out_spaces=(), scratch=(), cost=1, vmem=12):
     spaces = tuple(spaces) + (pltpu.VMEM,) * (len(operands) - len(spaces))
+    operands = [
+        pltpu.with_memory_space_constraint(operand, space) if space == pltpu.HBM else operand
+        for operand, space in zip(operands, spaces)
+    ]
     out_spaces = tuple(out_spaces) + (pltpu.VMEM,) * (len(outs) - len(out_spaces))
     return pl.pallas_call(
         kernel,
@@ -550,18 +539,13 @@
         (edge_count, jnp.swapaxes(halo_send, 1, 2), inputs, cotangent, edge_send, edge_recv),
         [(wide, BF16), ((rows + 16, latent), BF16), (narrow, BF16), ((16, block), BF16)],
         spaces=(pltpu.HBM,) * 6,
-        out_spaces=(pltpu.HBM,) * 3,
         scratch=[
             pltpu.SMEM((edge_blocks,), jnp.int32),
             pltpu.SMEM((1, 1, 2), jnp.int32),
             pltpu.VMEM(wide, BF16),
-            pltpu.VMEM((rows + 16, latent), BF16),
-            pltpu.VMEM(wide, BF16),
             pltpu.VMEM((2, 8, block), jnp.int32),
             dma((7,)),
-            dma((3,)),
         ],
-        vmem=56,
     )
     there = flip_y(there)
     outer = send(boundary, lambda z, y, x, c: (z + 2 * y - 1, c, x, 1 - y))
@@ -586,7 +570,6 @@
         [((4 * latent, latent), BF16)],
         spaces=(pltpu.HBM,) * 5,
         scratch=[pltpu.VMEM((2, latent, latent), BF16), dma((5,))],
-        vmem=56,
     )
     pair = run(place_mine_kernel, (weights,), [((4 * latent, latent), BF16)] * 2)
     matrices = run(

time: 93.9 us -> 91.2 us (0.971)
  Pallas kernels: 16.5 us -> 13.8 us
  local copies, waits for them, and re-layouts: 1.61 us -> 0.01 us
    pallas_call x34, Pallas kernels: 16.5 us -> 13.8 us  [run(): pl.pallas_call(kernel, out_shape=[jax.ShapeDtypeStruct(s, t) for s, t in...]
    unnamed x10 -> x2, local copies, waits for them, and re-layouts: 1.61 us -> 0.01 us
  transfers between devices with their start and end apart: 27 -> 27, of which waited for: 13 -> 13; matrix products, arithmetic and copies ran while one was open for 0% -> 0% of each run, Pallas kernels for 9% -> 8%
where the time goes in v8:
time: 91.2 us; the launch traced here: 90.9 us
  waiting for transfers between devices  42.3 us (46%)
  starting transfers between devices  33.5 us (37%)
  Pallas kernels  13.8 us (15%)
  between operations  1.17 us (1%)
    ppermute x27, waiting for transfers between devices, send(): return lax.ppermute(value, AXES, table)  42.3 us
    ppermute x27, starting transfers between devices, send(): return lax.ppermute(value, AXES, table)  33.5 us
    pallas_call x34, Pallas kernels, run(): pl.pallas_call(kernel, out_shape=[jax.ShapeDtypeStruct(s, t) for s, t in...  13.8 us
  transfers between devices with their start and end apart: 27, of which 13 were waited for; matrix products, arithmetic and copies ran while one was open for 0% of the time, Pallas kernels for 8%

profile of v8, /device:TPU:0, one launch (start us, length us, event | category | flops | bytes accessed | tf_op | source)
XLA Modules:
  0.0 90.9 jit_solution(15546872548131170588)
XLA Ops:
  1.9 3.0 %collective-permute-start.1 = (bf16[272,512]{1,0:T(8,128)(2,1)S(1)}, bf16[272,512]{1,0:T(8,128)(2,1)S(1)}, u32[]{:S(2)}, u32[]{:S(2)}) collective-permute-start(bf16[272,512]{1,0:T(8,128)(2,1)S(1)} %get-tuple-element.103), channel_id=1, source_target_pairs={{0,4},{1,5},{2,6},{3,7},{4,0},{5,1},{6,2},{7,3},{8,12},{9,13},{10,... | collective-permute-start | bytes 835592 | tf_op jit(solution)/shard_map/ppermute | solution.py:506
  4.9 1.7 %shard_map.131.mine = bf16[2048,512]{1,0:T(8,128)(2,1)S(1)} custom-call(bf16[512,512]{1,0:T(8,128)(2,1)} %bitcast.6, bf16[512,512]{1,0:T(8,128)(2,1)} %bitcast.7, bf16[512,512]{1,0:T(8,128)(2,1)} %bitcast.8, bf16[512,512]{1,0:T(8,128)(2,1)} %bitcast.9, bf16[512,512]{1,0:T(8,128)(2,1)} %bitcast.10), custom_call_target="tpu_custom_call" | custom-call | flops 1 | bytes 1 | tf_op jit(solution)/shard_map/pallas_call | solution.py:440
  6.7 3.7 %collective-permute-start.2 = (bf16[128,512]{1,0:T(8,128)(2,1)S(1)}, bf16[128,512]{1,0:T(8,128)(2,1)S(1)}, u32[]{:S(2)}, u32[]{:S(2)}) collective-permute-start(bf16[128,512]{1,0:T(8,128)(2,1)S(1)} %get-tuple-element.106), channel_id=1, source_target_pairs={{0,25},{1,29},{2,27},{3,31},{4,8},{5,12},{6,10},{7,14},{8,1},{9,5}... | collective-permute-start | bytes 393224 | tf_op jit(solution)/shard_map/ppermute | solution.py:506
  10.6 1.6 %collective-permute-done.1.there = bf16[272,512]{1,0:T(8,128)(2,1)S(1)} collective-permute-done((bf16[272,512]{1,0:T(8,128)(2,1)S(1)}, bf16[272,512]{1,0:T(8,128)(2,1)S(1)}, u32[]{:S(2)}, u32[]{:S(2)}) %collective-permute-start.1) | collective-permute-done | bytes 278560 | tf_op jit(solution)/shard_map/ppermute | solution.py:506
  12.5 1.9 %collective-permute-done.2._.refs_8_ = bf16[128,512]{1,0:T(8,128)(2,1)S(1)} collective-permute-done((bf16[128,512]{1,0:T(8,128)(2,1)S(1)}, bf16[128,512]{1,0:T(8,128)(2,1)S(1)}, u32[]{:S(2)}, u32[]{:S(2)}) %collective-permute-start.2) | collective-permute-done | bytes 131104 | tf_op jit(solution)/shard_map/ppermute | solution.py:506
  16.8 3.0 %collective-permute-start.5 = (bf16[128,512]{1,0:T(8,128)(2,1)S(1)}, bf16[128,512]{1,0:T(8,128)(2,1)S(1)}, u32[]{:S(2)}, u32[]{:S(2)}) collective-permute-start(bf16[128,512]{1,0:T(8,128)(2,1)S(1)} %get-tuple-element.123), channel_id=1, source_target_pairs={{0,25},{1,8},{2,27},{3,10},{4,29},{5,12},{6,31},{7,14},{8,1},{9,16... | collective-permute-start | bytes 393224 | tf_op jit(solution)/shard_map/ppermute | solution.py:506
  21.1 3.3 %collective-permute-done.5.refs_8_ = bf16[128,512]{1,0:T(8,128)(2,1)S(1)} collective-permute-done((bf16[128,512]{1,0:T(8,128)(2,1)S(1)}, bf16[128,512]{1,0:T(8,128)(2,1)S(1)}, u32[]{:S(2)}, u32[]{:S(2)}) %collective-permute-start.5) | collective-permute-done | bytes 131104 | tf_op jit(solution)/shard_map/ppermute | solution.py:506
  25.6 1.3 %collective-permute-start.8 = (bf16[128,512]{1,0:T(8,128)(2,1)S(1)}, bf16[128,512]{1,0:T(8,128)(2,1)S(1)}, u32[]{:S(2)}, u32[]{:S(2)}) collective-permute-start(bf16[128,512]{1,0:T(8,128)(2,1)S(1)} %get-tuple-element.127), channel_id=1, source_target_pairs={{0,27},{1,10},{4,31},{5,14},{8,3},{9,18},{12,7},{13,22},{16,11},{1... | collective-permute-start | bytes 393224 | tf_op jit(solution)/shard_map/ppermute | solution.py:506
  26.9 1.3 %collective-permute-start.6 = (bf16[256,512]{1,0:T(8,128)(2,1)S(1)}, bf16[256,512]{1,0:T(8,128)(2,1)S(1)}, u32[]{:S(2)}, u32[]{:S(2)}) collective-permute-start(bf16[256,512]{1,0:T(8,128)(2,1)S(1)} %get-tuple-element.124.h), channel_id=1, source_target_pairs={{0,2},{1,3},{4,6},{5,7},{8,10},{9,11},{12,14},{13,15},{16,18},{17,... | collective-permute-start | bytes 786440 | tf_op jit(solution)/shard_map/ppermute | solution.py:506
  28.7 4.9 %collective-permute-done.6.refs_1_.h.refs_4_ = bf16[256,512]{1,0:T(8,128)(2,1)S(1)} collective-permute-done((bf16[256,512]{1,0:T(8,128)(2,1)S(1)}, bf16[256,512]{1,0:T(8,128)(2,1)S(1)}, u32[]{:S(2)}, u32[]{:S(2)}) %collective-permute-start.6) | collective-permute-done | bytes 262176 | tf_op jit(solution)/shard_map/ppermute | solution.py:506
  33.8 1.3 %collective-permute-done.7.refs_7_ = bf16[128,512]{1,0:T(8,128)(2,1)S(1)} collective-permute-done((bf16[128,512]{1,0:T(8,128)(2,1)S(1)}, bf16[128,512]{1,0:T(8,128)(2,1)S(1)}, u32[]{:S(2)}, u32[]{:S(2)}) %collective-permute-start.7) | collective-permute-done | bytes 131104 | tf_op jit(solution)/shard_map/ppermute | solution.py:506
  35.2 3.1 %collective-permute-start.12 = (bf16[128,512]{1,0:T(8,128)(2,1)S(1)}, bf16[128,512]{1,0:T(8,128)(2,1)S(1)}, u32[]{:S(2)}, u32[]{:S(2)}) collective-permute-start(bf16[128,512]{1,0:T(8,128)(2,1)S(1)} %get-tuple-element.151), channel_id=1, source_target_pairs={{0,25},{1,8},{2,27},{3,10},{4,29},{5,12},{6,31},{7,14},{8,1},{9,16... | collective-permute-start | bytes 393224 | tf_op jit(solution)/shard_map/ppermute | solution.py:506
  39.1 3.8 %collective-permute-start.11 = (bf16[256,512]{1,0:T(8,128)(2,1)S(1)}, bf16[256,512]{1,0:T(8,128)(2,1)S(1)}, u32[]{:S(2)}, u32[]{:S(2)}) collective-permute-start(bf16[256,512]{1,0:T(8,128)(2,1)S(1)} %get-tuple-element.148), channel_id=1, source_target_pairs={{0,1},{1,5},{4,0},{5,4},{8,9},{9,13},{12,8},{13,12},{16,17},{17,21... | collective-permute-start | bytes 786440 | tf_op jit(solution)/shard_map/ppermute | solution.py:506
  43.1 1.6 %collective-permute-start.14 = (bf16[128,512]{1,0:T(8,128)(2,1)S(1)}, bf16[128,512]{1,0:T(8,128)(2,1)S(1)}, u32[]{:S(2)}, u32[]{:S(2)}) collective-permute-start(bf16[128,512]{1,0:T(8,128)(2,1)S(1)} %get-tuple-element.168), channel_id=1, source_target_pairs={{0,25},{1,8},{2,27},{3,10},{4,29},{5,12},{6,31},{7,14},{8,1},{9,16... | collective-permute-start | bytes 393224 | tf_op jit(solution)/shard_map/ppermute | solution.py:506
  44.7 3.4 %collective-permute-done.11.refs_3_.refs_1_ = bf16[256,512]{1,0:T(8,128)(2,1)S(1)} collective-permute-done((bf16[256,512]{1,0:T(8,128)(2,1)S(1)}, bf16[256,512]{1,0:T(8,128)(2,1)S(1)}, u32[]{:S(2)}, u32[]{:S(2)}) %collective-permute-start.11) | collective-permute-done | bytes 262176 | tf_op jit(solution)/shard_map/ppermute | solution.py:506
  48.0 2.2 %collective-permute-done.14.refs_6_ = bf16[128,512]{1,0:T(8,128)(2,1)S(1)} collective-permute-done((bf16[128,512]{1,0:T(8,128)(2,1)S(1)}, bf16[128,512]{1,0:T(8,128)(2,1)S(1)}, u32[]{:S(2)}, u32[]{:S(2)}) %collective-permute-start.14) | collective-permute-done | bytes 131104 | tf_op jit(solution)/shard_map/ppermute | solution.py:506
  51.7 1.3 %collective-permute-start.16 = (bf16[256,512]{1,0:T(8,128)(2,1)S(1)}, bf16[256,512]{1,0:T(8,128)(2,1)S(1)}, u32[]{:S(2)}, u32[]{:S(2)}) collective-permute-start(bf16[256,512]{1,0:T(8,128)(2,1)S(1)} %shard_map.154.value), channel_id=1, source_target_pairs={{2,0},{3,1},{6,4},{7,5},{10,8},{11,9},{14,12},{15,13},{18,16},{19,... | collective-permute-start | bytes 786440 | tf_op jit(solution)/shard_map/ppermute | solution.py:506
  53.0 9.3 %collective-permute-done.17.outer = bf16[128,512]{1,0:T(8,128)(2,1)S(1)} collective-permute-done((bf16[128,512]{1,0:T(8,128)(2,1)S(1)}, bf16[128,512]{1,0:T(8,128)(2,1)S(1)}, u32[]{:S(2)}, u32[]{:S(2)}) %collective-permute-start.17) | collective-permute-done | bytes 131104 | tf_op jit(solution)/shard_map/ppermute | solution.py:506
  62.4 5.1 %collective-permute-done.16.refs_5_ = bf16[256,512]{1,0:T(8,128)(2,1)S(1)} collective-permute-done((bf16[256,512]{1,0:T(8,128)(2,1)S(1)}, bf16[256,512]{1,0:T(8,128)(2,1)S(1)}, u32[]{:S(2)}, u32[]{:S(2)}) %collective-permute-start.16) | collective-permute-done | bytes 262176 | tf_op jit(solution)/shard_map/ppermute | solution.py:506
  68.7 2.4 %collective-permute-start.21 = (bf16[128,512]{1,0:T(8,128)(2,1)S(1)}, bf16[128,512]{1,0:T(8,128)(2,1)S(1)}, u32[]{:S(2)}, u32[]{:S(2)}) collective-permute-start(bf16[128,512]{1,0:T(8,128)(2,1)S(1)} %get-tuple-element.183), channel_id=1, source_target_pairs={{0,25},{1,8},{2,27},{3,10},{4,29},{5,12},{6,31},{7,14},{8,1},{9,16... | collective-permute-start | bytes 393224 | tf_op jit(solution)/shard_map/ppermute | solution.py:506
  71.8 3.7 %collective-permute-done.21.outer.refs_6_ = bf16[128,512]{1,0:T(8,128)(2,1)S(1)} collective-permute-done((bf16[128,512]{1,0:T(8,128)(2,1)S(1)}, bf16[128,512]{1,0:T(8,128)(2,1)S(1)}, u32[]{:S(2)}, u32[]{:S(2)}) %collective-permute-start.21) | collective-permute-done | bytes 131104 | tf_op jit(solution)/shard_map/ppermute | solution.py:506
  76.7 2.5 %collective-permute-start.25 = (bf16[128,512]{1,0:T(8,128)(2,1)S(1)}, bf16[128,512]{1,0:T(8,128)(2,1)S(1)}, u32[]{:S(2)}, u32[]{:S(2)}) collective-permute-start(bf16[128,512]{1,0:T(8,128)(2,1)S(1)} %get-tuple-element.197), channel_id=1, source_target_pairs={{0,28},{1,8},{2,30},{3,10},{4,29},{5,9},{6,31},{7,11},{8,4},{9,16}... | collective-permute-start | bytes 393224 | tf_op jit(solution)/shard_map/ppermute | solution.py:506
  80.6 1.6 %collective-permute-start.24 = (bf16[256,512]{1,0:T(8,128)(2,1)S(1)}, bf16[256,512]{1,0:T(8,128)(2,1)S(1)}, u32[]{:S(2)}, u32[]{:S(2)}) collective-permute-start(bf16[256,512]{1,0:T(8,128)(2,1)S(1)} %get-tuple-element.195), channel_id=1, source_target_pairs={{0,1},{1,5},{2,3},{3,7},{4,0},{5,4},{6,2},{7,6},{8,9},{9,13},{10,1... | collective-permute-start | bytes 786440 | tf_op jit(solution)/shard_map/ppermute | solution.py:506
  85.3 4.2 %collective-permute-done.24.refs_1_ = bf16[256,512]{1,0:T(8,128)(2,1)S(1)} collective-permute-done((bf16[256,512]{1,0:T(8,128)(2,1)S(1)}, bf16[256,512]{1,0:T(8,128)(2,1)S(1)}, u32[]{:S(2)}, u32[]{:S(2)}) %collective-permute-start.24) | collective-permute-done | bytes 262176 | tf_op jit(solution)/shard_map/ppermute | solution.py:506
  (66 shorter events, 18.4 us)
Async XLA Ops:
  1.9 10.4 %collective-permute-start.1 = (bf16[272,512]{1,0:T(8,128)(2,1)S(1)}, bf16[272,512]{1,0:T(8,128)(2,1)S(1)}, u32[]{:S(2)}, u32[]{:S(2)}) collective-permute-start(bf16[272,512]{1,0:T(8,128)(2,1)S(1)} %get-tuple-element.103), channel_id=1, source_target_pairs={{0,4},{1,5},{2,6},{3,7},{4,0},{5,1},{6,2},{7,3},{8,12},{9,13},{10,... | collective-permute-start | bytes 835592 | tf_op jit(solution)/shard_map/ppermute | solution.py:506
  6.6 7.9 %collective-permute-start = (bf16[2048,512]{1,0:T(8,128)(2,1)S(1)}, bf16[2048,512]{1,0:T(8,128)(2,1)S(1)}, u32[]{:S(2)}, u32[]{:S(2)}) collective-permute-start(bf16[2048,512]{1,0:T(8,128)(2,1)S(1)} %shard_map.131.mine), channel_id=1, source_target_pairs={{0,1},{1,0},{2,3},{3,2},{4,5},{5,4},{6,7},{7,6},{8,9},{9,8},{10,11... | collective-permute-start | bytes 6291464 | tf_op jit(solution)/shard_map/ppermute | solution.py:506
  6.7 7.7 %collective-permute-start.2 = (bf16[128,512]{1,0:T(8,128)(2,1)S(1)}, bf16[128,512]{1,0:T(8,128)(2,1)S(1)}, u32[]{:S(2)}, u32[]{:S(2)}) collective-permute-start(bf16[128,512]{1,0:T(8,128)(2,1)S(1)} %get-tuple-element.106), channel_id=1, source_target_pairs={{0,25},{1,29},{2,27},{3,31},{4,8},{5,12},{6,10},{7,14},{8,1},{9,5}... | collective-permute-start | bytes 393224 | tf_op jit(solution)/shard_map/ppermute | solution.py:506
  10.4 5.1 %collective-permute-start.3 = (f32[1,512]{1,0:T(1,128)S(1)}, f32[1,512]{1,0:T(1,128)S(1)}, u32[]{:S(2)}, u32[]{:S(2)}) collective-permute-start(f32[1,512]{1,0:T(1,128)S(1)} %copy-done), channel_id=1, source_target_pairs={{0,1},{1,0},{2,3},{3,2},{4,5},{5,4},{6,7},{7,6},{8,9},{9,8},{10,11... | collective-permute-start | bytes 6152 | tf_op jit(solution)/shard_map/ppermute | solution.py:506
  16.7 3.6 %collective-permute-start.4 = (bf16[128,512]{1,0:T(8,128)(2,1)S(1)}, bf16[128,512]{1,0:T(8,128)(2,1)S(1)}, u32[]{:S(2)}, u32[]{:S(2)}) collective-permute-start(bf16[128,512]{1,0:T(8,128)(2,1)S(1)} %get-tuple-element.120), channel_id=1, source_target_pairs={{0,1},{1,0},{2,3},{3,2},{4,5},{5,4},{6,7},{7,6},{8,9},{9,8},{10,11... | collective-permute-start | bytes 393224 | tf_op jit(solution)/shard_map/ppermute | solution.py:506
  16.8 7.6 %collective-permute-start.5 = (bf16[128,512]{1,0:T(8,128)(2,1)S(1)}, bf16[128,512]{1,0:T(8,128)(2,1)S(1)}, u32[]{:S(2)}, u32[]{:S(2)}) collective-permute-start(bf16[128,512]{1,0:T(8,128)(2,1)S(1)} %get-tuple-element.123), channel_id=1, source_target_pairs={{0,25},{1,8},{2,27},{3,10},{4,29},{5,12},{6,31},{7,14},{8,1},{9,16... | collective-permute-start | bytes 393224 | tf_op jit(solution)/shard_map/ppermute | solution.py:506
  25.6 8.2 %collective-permute-start.8 = (bf16[128,512]{1,0:T(8,128)(2,1)S(1)}, bf16[128,512]{1,0:T(8,128)(2,1)S(1)}, u32[]{:S(2)}, u32[]{:S(2)}) collective-permute-start(bf16[128,512]{1,0:T(8,128)(2,1)S(1)} %get-tuple-element.127), channel_id=1, source_target_pairs={{0,27},{1,10},{4,31},{5,14},{8,3},{9,18},{12,7},{13,22},{16,11},{1... | collective-permute-start | bytes 393224 | tf_op jit(solution)/shard_map/ppermute | solution.py:506
  26.9 6.7 %collective-permute-start.6 = (bf16[256,512]{1,0:T(8,128)(2,1)S(1)}, bf16[256,512]{1,0:T(8,128)(2,1)S(1)}, u32[]{:S(2)}, u32[]{:S(2)}) collective-permute-start(bf16[256,512]{1,0:T(8,128)(2,1)S(1)} %get-tuple-element.124.h), channel_id=1, source_target_pairs={{0,2},{1,3},{4,6},{5,7},{8,10},{9,11},{12,14},{13,15},{16,18},{17,... | collective-permute-start | bytes 786440 | tf_op jit(solution)/shard_map/ppermute | solution.py:506
  35.1 3.2 %collective-permute-start.9 = (bf16[128,512]{1,0:T(8,128)(2,1)S(1)}, bf16[128,512]{1,0:T(8,128)(2,1)S(1)}, u32[]{:S(2)}, u32[]{:S(2)}) collective-permute-start(bf16[128,512]{1,0:T(8,128)(2,1)S(1)} %get-tuple-element.144), channel_id=1, source_target_pairs={{0,1},{1,0},{2,3},{3,2},{4,5},{5,4},{6,7},{7,6},{8,9},{9,8},{10,11... | collective-permute-start | bytes 393224 | tf_op jit(solution)/shard_map/ppermute | solution.py:506
  35.2 7.7 %collective-permute-start.12 = (bf16[128,512]{1,0:T(8,128)(2,1)S(1)}, bf16[128,512]{1,0:T(8,128)(2,1)S(1)}, u32[]{:S(2)}, u32[]{:S(2)}) collective-permute-start(bf16[128,512]{1,0:T(8,128)(2,1)S(1)} %get-tuple-element.151), channel_id=1, source_target_pairs={{0,25},{1,8},{2,27},{3,10},{4,29},{5,12},{6,31},{7,14},{8,1},{9,16... | collective-permute-start | bytes 393224 | tf_op jit(solution)/shard_map/ppermute | solution.py:506
  38.4 6.3 %collective-permute-start.10 = (bf16[256,512]{1,0:T(8,128)(2,1)S(1)}, bf16[256,512]{1,0:T(8,128)(2,1)S(1)}, u32[]{:S(2)}, u32[]{:S(2)}) collective-permute-start(bf16[256,512]{1,0:T(8,128)(2,1)S(1)} %get-tuple-element.147), channel_id=1, source_target_pairs={{0,0},{1,4},{4,1},{5,5},{8,8},{9,12},{12,9},{13,13},{16,16},{17,20... | collective-permute-start | bytes 786440 | tf_op jit(solution)/shard_map/ppermute | solution.py:506
  39.1 9.0 %collective-permute-start.11 = (bf16[256,512]{1,0:T(8,128)(2,1)S(1)}, bf16[256,512]{1,0:T(8,128)(2,1)S(1)}, u32[]{:S(2)}, u32[]{:S(2)}) collective-permute-start(bf16[256,512]{1,0:T(8,128)(2,1)S(1)} %get-tuple-element.148), channel_id=1, source_target_pairs={{0,1},{1,5},{4,0},{5,4},{8,9},{9,13},{12,8},{13,12},{16,17},{17,21... | collective-permute-start | bytes 786440 | tf_op jit(solution)/shard_map/ppermute | solution.py:506
  43.1 7.1 %collective-permute-start.14 = (bf16[128,512]{1,0:T(8,128)(2,1)S(1)}, bf16[128,512]{1,0:T(8,128)(2,1)S(1)}, u32[]{:S(2)}, u32[]{:S(2)}) collective-permute-start(bf16[128,512]{1,0:T(8,128)(2,1)S(1)} %get-tuple-element.168), channel_id=1, source_target_pairs={{0,25},{1,8},{2,27},{3,10},{4,29},{5,12},{6,31},{7,14},{8,1},{9,16... | collective-permute-start | bytes 393224 | tf_op jit(solution)/shard_map/ppermute | solution.py:506
  50.2 12.1 %collective-permute-start.17 = (bf16[128,512]{1,0:T(8,128)(2,1)S(1)}, bf16[128,512]{1,0:T(8,128)(2,1)S(1)}, u32[]{:S(2)}, u32[]{:S(2)}) collective-permute-start(bf16[128,512]{1,0:T(8,128)(2,1)S(1)} %get-tuple-element.169.refs_3_), channel_id=1, source_target_pairs={{2,25},{3,8},{6,29},{7,12},{10,1},{11,16},{14,5},{15,20},{18,9},{1... | collective-permute-start | bytes 393224 | tf_op jit(solution)/shard_map/ppermute | solution.py:506
  51.7 15.8 %collective-permute-start.16 = (bf16[256,512]{1,0:T(8,128)(2,1)S(1)}, bf16[256,512]{1,0:T(8,128)(2,1)S(1)}, u32[]{:S(2)}, u32[]{:S(2)}) collective-permute-start(bf16[256,512]{1,0:T(8,128)(2,1)S(1)} %shard_map.154.value), channel_id=1, source_target_pairs={{2,0},{3,1},{6,4},{7,5},{10,8},{11,9},{14,12},{15,13},{18,16},{19,... | collective-permute-start | bytes 786440 | tf_op jit(solution)/shard_map/ppermute | solution.py:506
  68.6 2.5 %collective-permute-start.18 = (bf16[128,512]{1,0:T(8,128)(2,1)S(1)}, bf16[128,512]{1,0:T(8,128)(2,1)S(1)}, u32[]{:S(2)}, u32[]{:S(2)}) collective-permute-start(bf16[128,512]{1,0:T(8,128)(2,1)S(1)} %get-tuple-element.175), channel_id=1, source_target_pairs={{0,1},{1,0},{2,3},{3,2},{4,5},{5,4},{6,7},{7,6},{8,9},{9,8},{10,11... | collective-permute-start | bytes 393224 | tf_op jit(solution)/shard_map/ppermute | solution.py:506
  68.7 6.7 %collective-permute-start.21 = (bf16[128,512]{1,0:T(8,128)(2,1)S(1)}, bf16[128,512]{1,0:T(8,128)(2,1)S(1)}, u32[]{:S(2)}, u32[]{:S(2)}) collective-permute-start(bf16[128,512]{1,0:T(8,128)(2,1)S(1)} %get-tuple-element.183), channel_id=1, source_target_pairs={{0,25},{1,8},{2,27},{3,10},{4,29},{5,12},{6,31},{7,14},{8,1},{9,16... | collective-permute-start | bytes 393224 | tf_op jit(solution)/shard_map/ppermute | solution.py:506
  76.6 2.6 %collective-permute-start.22 = (bf16[128,512]{1,0:T(8,128)(2,1)S(1)}, bf16[128,512]{1,0:T(8,128)(2,1)S(1)}, u32[]{:S(2)}, u32[]{:S(2)}) collective-permute-start(bf16[128,512]{1,0:T(8,128)(2,1)S(1)} %get-tuple-element.189), channel_id=1, source_target_pairs={{0,1},{1,0},{2,3},{3,2},{4,5},{5,4},{6,7},{7,6},{8,9},{9,8},{10,11... | collective-permute-start | bytes 393224 | tf_op jit(solution)/shard_map/ppermute | solution.py:506
  76.7 6.7 %collective-permute-start.25 = (bf16[128,512]{1,0:T(8,128)(2,1)S(1)}, bf16[128,512]{1,0:T(8,128)(2,1)S(1)}, u32[]{:S(2)}, u32[]{:S(2)}) collective-permute-start(bf16[128,512]{1,0:T(8,128)(2,1)S(1)} %get-tuple-element.197), channel_id=1, source_target_pairs={{0,28},{1,8},{2,30},{3,10},{4,29},{5,9},{6,31},{7,11},{8,4},{9,16}... | collective-permute-start | bytes 393224 | tf_op jit(solution)/shard_map/ppermute | solution.py:506
  79.9 5.5 %collective-permute-start.23 = (bf16[256,512]{1,0:T(8,128)(2,1)S(1)}, bf16[256,512]{1,0:T(8,128)(2,1)S(1)}, u32[]{:S(2)}, u32[]{:S(2)}) collective-permute-start(bf16[256,512]{1,0:T(8,128)(2,1)S(1)} %get-tuple-element.194), channel_id=1, source_target_pairs={{0,0},{1,4},{2,2},{3,6},{4,1},{5,5},{6,3},{7,7},{8,8},{9,12},{10,1... | collective-permute-start | bytes 786440 | tf_op jit(solution)/shard_map/ppermute | solution.py:506
  80.6 9.0 %collective-permute-start.24 = (bf16[256,512]{1,0:T(8,128)(2,1)S(1)}, bf16[256,512]{1,0:T(8,128)(2,1)S(1)}, u32[]{:S(2)}, u32[]{:S(2)}) collective-permute-start(bf16[256,512]{1,0:T(8,128)(2,1)S(1)} %get-tuple-element.195), channel_id=1, source_target_pairs={{0,1},{1,5},{2,3},{3,7},{4,0},{5,4},{6,2},{7,6},{8,9},{9,13},{10,1... | collective-permute-start | bytes 786440 | tf_op jit(solution)/shard_map/ppermute | solution.py:506
  83.4 1.7 %collective-permute-start.26 = (bf16[128,512]{1,0:T(8,128)(2,1)S(1)}, bf16[128,512]{1,0:T(8,128)(2,1)S(1)}, u32[]{:S(2)}, u32[]{:S(2)}) collective-permute-start(bf16[128,512]{1,0:T(8,128)(2,1)S(1)} %collective-permute-done.25.outer), channel_id=1, source_target_pairs={{0,1},{1,0},{2,3},{3,2},{4,5},{5,4},{6,7},{7,6},{8,9},{9,8},{10,11... | collective-permute-start | bytes 393224 | tf_op jit(solution)/shard_map/ppermute | solution.py:506
  83.8 5.9 %collective-permute-start.19 = (bf16[256,512]{1,0:T(8,128)(2,1)S(1)}, bf16[256,512]{1,0:T(8,128)(2,1)S(1)}, u32[]{:S(2)}, u32[]{:S(2)}) collective-permute-start(bf16[256,512]{1,0:T(8,128)(2,1)S(1)} %get-tuple-element.181), channel_id=1, source_target_pairs={{2,2},{3,6},{6,3},{7,7},{10,10},{11,14},{14,11},{15,15},{18,18},{1... | collective-permute-start | bytes 786440 | tf_op jit(solution)/shard_map/ppermute | solution.py:506
  84.5 5.2 %collective-permute-start.20 = (bf16[256,512]{1,0:T(8,128)(2,1)S(1)}, bf16[256,512]{1,0:T(8,128)(2,1)S(1)}, u32[]{:S(2)}, u32[]{:S(2)}) collective-permute-start(bf16[256,512]{1,0:T(8,128)(2,1)S(1)} %get-tuple-element.182), channel_id=1, source_target_pairs={{2,3},{3,7},{6,2},{7,6},{10,11},{11,15},{14,10},{15,14},{18,19},{1... | collective-permute-start | bytes 786440 | tf_op jit(solution)/shard_map/ppermute | solution.py:506
  (4 other events, 9.9 us)

commit v9 on v8

--- a/solution.py
+++ b/solution.py
@@ -188,7 +188,7 @@
         even[...] = swapped[...]
 
 
-def graph_kernel(edge_blocks, packed, there, gown, gown_t, ghalo, ghalo_t, lists, mate, home_lists):
+def graph_kernel(edge_blocks, packed, there, gown, gown_t, ghalo, ghalo_t, lists, home_lists):
     block = packed.shape[1]
     rows = gown_t.shape[0]
     edges = edge_blocks * block
@@ -197,7 +197,7 @@
     last = 2 * edge_blocks
     tiles = decode(packed[...]), decode(there[rows:, :block])
     mine = jnp.where(local, *tiles)
-    tails = [tile[last : last + 1] for tile in (mine, jnp.where(local, tiles[1], tiles[0]), tiles[0])]
+    tails = [tile[last : last + 1] for tile in (mine, tiles[0])]
     lane = lax.broadcasted_iota(jnp.int32, (1, block), 1)
     row = lax.broadcasted_iota(jnp.int32, (rows, block), 0)
     halo_row = lax.broadcasted_iota(jnp.int32, (2 * block, block), 0)
@@ -225,25 +225,22 @@
     to_next, to_prev = whole(tails[0], 0), whole(tails[0], 1)
     lists[0:1, :] = jnp.where(first_core, to_next, to_prev)
     lists[1:2, :] = jnp.where(first_core, to_prev, to_next)
-    mate[...] = jnp.where(first_core, whole(tails[1], 1), whole(tails[1], 0))
-    to_next, to_prev = whole(tails[2], 0), whole(tails[2], 1)
+    to_next, to_prev = whole(tails[1], 0), whole(tails[1], 1)
     home_first = lax.axis_index("dom") % 2 == 0
     home_lists[0:1, :] = jnp.where(home_first, to_next, to_prev)
     home_lists[1:2, :] = jnp.where(home_first, to_prev, to_next)
 
 
-def entry_kernel(mate, here, there, _, hidden, inner):
-    block = inner.shape[0]
-
+def entry_kernel(here, there, _, lists, hidden, to_inner):
     @pl.when(is_local())
     def _():
         hidden[...] = here[...]
-        inner[...] = listed(mate[:, :1], there[: hidden.shape[0], :], block)
 
     @pl.when(jnp.logical_not(is_local()))
     def _():
         hidden[...] = there[: hidden.shape[0], :]
-        inner[...] = listed(mate[:, :1], here[...], block)
+
+    to_inner[...] = listed(lists[INNER : INNER + 1, :1], hidden[...], to_inner.shape[0])
 
 
 def forward_own_kernel(take, h, gown, *refs):
@@ -547,9 +544,9 @@
             dma((7,)),
         ],
     )
-    there = flip_y(there)
+    there = send(there, lambda z, y, x, c: (z, 1 - y, x, c) if c == y else (z, y, x, 1 - c))
     outer = send(boundary, lambda z, y, x, c: (z + 2 * y - 1, c, x, 1 - y))
-    gown, gown_t, ghalo, ghalo_t, lists, mate, home_lists = run(
+    gown, gown_t, ghalo, ghalo_t, lists, home_lists = run(
         functools.partial(graph_kernel, edge_blocks),
         (packed, there),
         [
@@ -558,11 +555,11 @@
             ((edges, 2 * block), BF16),
             ((2 * block, edges), BF16),
             ((2, block), jnp.int32),
-            ((1, block), jnp.int32),
             ((2, block), jnp.int32),
         ],
     )
-    hidden, inner = run(entry_kernel, (mate, here, there, outer), [(wide, BF16), (narrow, BF16)], cost=LONG)
+    hidden, inner = run(entry_kernel, (here, there, outer, lists), [(wide, BF16), (narrow, BF16)], cost=LONG * 3 // 2)
+    inner = towards(inner, INNER, 0)
 
     [weights] = run(
         weights_kernel,
@@ -620,6 +617,7 @@
     *states, both = saved
     halos = {}
     finished = {}
+    second_home = ()
     for tick in range(sections - 1, -1, -1):
         plane, parity = tick // 2, tick % 2
         packed = matrices[parity]
@@ -636,6 +634,7 @@
             kept + (lists, upstream) + tuple(halos.values()) + tuple(states) + (gown, ghalo_t),
             outs,
             elsewhere={0: -1} if tick == 1 else {},
+            cost=1 if tick else BESIDE // 2,
         )
         if done:
             finished[tick + 1] = done[0]
@@ -648,7 +647,7 @@
             functools.partial(backward_own_kernel, add_inner, bool(last)),
             plane,
             (packed,),
-            last + beside + (tuple(first_home) if tick == sections - 1 else ()) + (c, du, da, es, gown_t),
+            last + beside + tuple({sections - 1: first_home, 0: second_home}.get(tick, ())) + (c, du, da, es, gown_t),
             [(wide, BF16)] * 2 if last else [(wide, BF16 if step else F32)],
             elsewhere={0: -2, 1: -1} if last else {},
             cost=BESIDE if tick else 1,

time: 91.2 us -> 90.4 us (level)
  starting transfers between devices: 33.5 us -> 29 us
  waiting for transfers between devices: 42.3 us -> 46.2 us
    ppermute x27 -> x28, starting transfers between devices: 33.5 us -> 29 us  [send(): return lax.ppermute(value, AXES, table)]
    ppermute x27 -> x28, waiting for transfers between devices: 42.3 us -> 46.2 us  [send(): return lax.ppermute(value, AXES, table)]
  transfers between devices with their start and end apart: 27 -> 28, of which waited for: 13 -> 17; matrix products, arithmetic and copies ran while one was open for 0% -> 0% of each run, Pallas kernels for 8% -> 9%
where the time goes in v9:
time: 90.4 us; the launch traced here: 90 us
  waiting for transfers between devices  46.2 us (51%)
  starting transfers between devices  29 us (32%)
  Pallas kernels  13.7 us (15%)
  between operations  1.14 us (1%)
    ppermute x28, waiting for transfers between devices, send(): return lax.ppermute(value, AXES, table)  46.2 us
    ppermute x28, starting transfers between devices, send(): return lax.ppermute(value, AXES, table)  29 us
    pallas_call x34, Pallas kernels, run(): pl.pallas_call(kernel, out_shape=[jax.ShapeDtypeStruct(s, t) for s, t in...  13.7 us
  transfers between devices with their start and end apart: 28, of which 17 were waited for; matrix products, arithmetic and copies ran while one was open for 0% of the time, Pallas kernels for 9%

profile of v9, /device:TPU:0, one launch (start us, length us, event | category | flops | bytes accessed | tf_op | source)
XLA Modules:
  0.0 90.0 jit_solution(11609562306268910335)
XLA Ops:
  0.6 1.2 %shard_map.132 = (bf16[256,512]{1,0:T(8,128)(2,1)S(1)}, bf16[272,512]{1,0:T(8,128)(2,1)S(1)}, bf16[128,512]{1,0:T(8,128)(2,1)S(1)}, bf16[16,128]{1,0:T(8,128)(2,1)S(1)}) custom-call(s32[2]{0:T(128)} %count_in.1, s32[1,1,2]{2,1,0:T(1,128)} %bitcast.11, bf16[2,256,512]{2,1,0:T(8,128)(2,1)} %inputs.1, bf16[2,256,512]{2,1,0:T(8,128)(2,1)} %cotangent.1, ...), custom_call_target="tpu_custom_call" | custom-call | flops 1 | bytes 1 | tf_op jit(solution)/shard_map/pallas_call | solution.py:437
  1.9 3.0 %collective-permute-start.1 = (bf16[272,512]{1,0:T(8,128)(2,1)S(1)}, bf16[272,512]{1,0:T(8,128)(2,1)S(1)}, u32[]{:S(2)}, u32[]{:S(2)}) collective-permute-start(bf16[272,512]{1,0:T(8,128)(2,1)S(1)} %get-tuple-element.102), channel_id=1, source_target_pairs={{0,4},{1,0},{2,6},{3,2},{4,5},{5,1},{6,7},{7,3},{8,12},{9,8},{10,1... | collective-permute-start | bytes 835592 | tf_op jit(solution)/shard_map/ppermute | solution.py:503
  4.8 2.2 %collective-permute-start.2 = (bf16[128,512]{1,0:T(8,128)(2,1)S(1)}, bf16[128,512]{1,0:T(8,128)(2,1)S(1)}, u32[]{:S(2)}, u32[]{:S(2)}) collective-permute-start(bf16[128,512]{1,0:T(8,128)(2,1)S(1)} %get-tuple-element.103), channel_id=1, source_target_pairs={{0,25},{1,29},{2,27},{3,31},{4,8},{5,12},{6,10},{7,14},{8,1},{9,5}... | collective-permute-start | bytes 393224 | tf_op jit(solution)/shard_map/ppermute | solution.py:503
  7.7 1.7 %shard_map.131.mine = bf16[2048,512]{1,0:T(8,128)(2,1)S(1)} custom-call(bf16[512,512]{1,0:T(8,128)(2,1)} %bitcast.6, bf16[512,512]{1,0:T(8,128)(2,1)} %bitcast.7, bf16[512,512]{1,0:T(8,128)(2,1)} %bitcast.8, bf16[512,512]{1,0:T(8,128)(2,1)} %bitcast.9, bf16[512,512]{1,0:T(8,128)(2,1)} %bitcast.10), custom_call_target="tpu_custom_call" | custom-call | flops 1 | bytes 1 | tf_op jit(solution)/shard_map/pallas_call | solution.py:437
  10.4 2.1 %collective-permute-done.2._.refs_8_ = bf16[128,512]{1,0:T(8,128)(2,1)S(1)} collective-permute-done((bf16[128,512]{1,0:T(8,128)(2,1)S(1)}, bf16[128,512]{1,0:T(8,128)(2,1)S(1)}, u32[]{:S(2)}, u32[]{:S(2)}) %collective-permute-start.2) | collective-permute-done | bytes 131104 | tf_op jit(solution)/shard_map/ppermute | solution.py:503
  16.0 1.5 %collective-permute-start.6 = (bf16[128,512]{1,0:T(8,128)(2,1)S(1)}, bf16[128,512]{1,0:T(8,128)(2,1)S(1)}, u32[]{:S(2)}, u32[]{:S(2)}) collective-permute-start(bf16[128,512]{1,0:T(8,128)(2,1)S(1)} %get-tuple-element.121), channel_id=1, source_target_pairs={{0,25},{1,8},{2,27},{3,10},{4,29},{5,12},{6,31},{7,14},{8,1},{9,16... | collective-permute-start | bytes 393224 | tf_op jit(solution)/shard_map/ppermute | solution.py:503
  18.8 3.5 %collective-permute-done.6.refs_8_ = bf16[128,512]{1,0:T(8,128)(2,1)S(1)} collective-permute-done((bf16[128,512]{1,0:T(8,128)(2,1)S(1)}, bf16[128,512]{1,0:T(8,128)(2,1)S(1)}, u32[]{:S(2)}, u32[]{:S(2)}) %collective-permute-start.6) | collective-permute-done | bytes 131104 | tf_op jit(solution)/shard_map/ppermute | solution.py:503
  23.4 1.8 %collective-permute-start.9 = (bf16[128,512]{1,0:T(8,128)(2,1)S(1)}, bf16[128,512]{1,0:T(8,128)(2,1)S(1)}, u32[]{:S(2)}, u32[]{:S(2)}) collective-permute-start(bf16[128,512]{1,0:T(8,128)(2,1)S(1)} %get-tuple-element.125), channel_id=1, source_target_pairs={{0,27},{1,10},{4,31},{5,14},{8,3},{9,18},{12,7},{13,22},{16,11},{1... | collective-permute-start | bytes 393224 | tf_op jit(solution)/shard_map/ppermute | solution.py:503
  25.2 1.3 %collective-permute-start.7 = (bf16[256,512]{1,0:T(8,128)(2,1)S(1)}, bf16[256,512]{1,0:T(8,128)(2,1)S(1)}, u32[]{:S(2)}, u32[]{:S(2)}) collective-permute-start(bf16[256,512]{1,0:T(8,128)(2,1)S(1)} %get-tuple-element.122.h), channel_id=1, source_target_pairs={{0,2},{1,3},{4,6},{5,7},{8,10},{9,11},{12,14},{13,15},{16,18},{17,... | collective-permute-start | bytes 786440 | tf_op jit(solution)/shard_map/ppermute | solution.py:503
  27.1 7.2 %collective-permute-done.7.refs_1_.h.refs_4_ = bf16[256,512]{1,0:T(8,128)(2,1)S(1)} collective-permute-done((bf16[256,512]{1,0:T(8,128)(2,1)S(1)}, bf16[256,512]{1,0:T(8,128)(2,1)S(1)}, u32[]{:S(2)}, u32[]{:S(2)}) %collective-permute-start.7) | collective-permute-done | bytes 262176 | tf_op jit(solution)/shard_map/ppermute | solution.py:503
  34.5 1.3 %collective-permute-done.8.refs_7_ = bf16[128,512]{1,0:T(8,128)(2,1)S(1)} collective-permute-done((bf16[128,512]{1,0:T(8,128)(2,1)S(1)}, bf16[128,512]{1,0:T(8,128)(2,1)S(1)}, u32[]{:S(2)}, u32[]{:S(2)}) %collective-permute-start.8) | collective-permute-done | bytes 131104 | tf_op jit(solution)/shard_map/ppermute | solution.py:503
  37.9 4.2 %collective-permute-start.12 = (bf16[256,512]{1,0:T(8,128)(2,1)S(1)}, bf16[256,512]{1,0:T(8,128)(2,1)S(1)}, u32[]{:S(2)}, u32[]{:S(2)}) collective-permute-start(bf16[256,512]{1,0:T(8,128)(2,1)S(1)} %get-tuple-element.146), channel_id=1, source_target_pairs={{0,1},{1,5},{4,0},{5,4},{8,9},{9,13},{12,8},{13,12},{16,17},{17,21... | collective-permute-start | bytes 786440 | tf_op jit(solution)/shard_map/ppermute | solution.py:503
  42.2 1.8 %collective-permute-start.15 = (bf16[128,512]{1,0:T(8,128)(2,1)S(1)}, bf16[128,512]{1,0:T(8,128)(2,1)S(1)}, u32[]{:S(2)}, u32[]{:S(2)}) collective-permute-start(bf16[128,512]{1,0:T(8,128)(2,1)S(1)} %get-tuple-element.166), channel_id=1, source_target_pairs={{0,25},{1,8},{2,27},{3,10},{4,29},{5,12},{6,31},{7,14},{8,1},{9,16... | collective-permute-start | bytes 393224 | tf_op jit(solution)/shard_map/ppermute | solution.py:503
  44.1 4.0 %collective-permute-done.12.refs_3_.refs_1_ = bf16[256,512]{1,0:T(8,128)(2,1)S(1)} collective-permute-done((bf16[256,512]{1,0:T(8,128)(2,1)S(1)}, bf16[256,512]{1,0:T(8,128)(2,1)S(1)}, u32[]{:S(2)}, u32[]{:S(2)}) %collective-permute-start.12) | collective-permute-done | bytes 262176 | tf_op jit(solution)/shard_map/ppermute | solution.py:503
  49.2 1.3 %collective-permute-start.18 = (bf16[128,512]{1,0:T(8,128)(2,1)S(1)}, bf16[128,512]{1,0:T(8,128)(2,1)S(1)}, u32[]{:S(2)}, u32[]{:S(2)}) collective-permute-start(bf16[128,512]{1,0:T(8,128)(2,1)S(1)} %get-tuple-element.167.refs_3_), channel_id=1, source_target_pairs={{2,25},{3,8},{6,29},{7,12},{10,1},{11,16},{14,5},{15,20},{18,9},{1... | collective-permute-start | bytes 393224 | tf_op jit(solution)/shard_map/ppermute | solution.py:503
  50.7 1.3 %collective-permute-start.17 = (bf16[256,512]{1,0:T(8,128)(2,1)S(1)}, bf16[256,512]{1,0:T(8,128)(2,1)S(1)}, u32[]{:S(2)}, u32[]{:S(2)}) collective-permute-start(bf16[256,512]{1,0:T(8,128)(2,1)S(1)} %shard_map.154.value), channel_id=1, source_target_pairs={{2,0},{3,1},{6,4},{7,5},{10,8},{11,9},{14,12},{15,13},{18,16},{19,... | collective-permute-start | bytes 786440 | tf_op jit(solution)/shard_map/ppermute | solution.py:503
  52.0 9.5 %collective-permute-done.18.outer = bf16[128,512]{1,0:T(8,128)(2,1)S(1)} collective-permute-done((bf16[128,512]{1,0:T(8,128)(2,1)S(1)}, bf16[128,512]{1,0:T(8,128)(2,1)S(1)}, u32[]{:S(2)}, u32[]{:S(2)}) %collective-permute-start.18) | collective-permute-done | bytes 131104 | tf_op jit(solution)/shard_map/ppermute | solution.py:503
  61.6 5.3 %collective-permute-done.17.refs_5_ = bf16[256,512]{1,0:T(8,128)(2,1)S(1)} collective-permute-done((bf16[256,512]{1,0:T(8,128)(2,1)S(1)}, bf16[256,512]{1,0:T(8,128)(2,1)S(1)}, u32[]{:S(2)}, u32[]{:S(2)}) %collective-permute-start.17) | collective-permute-done | bytes 262176 | tf_op jit(solution)/shard_map/ppermute | solution.py:503
  68.1 2.2 %collective-permute-start.22 = (bf16[128,512]{1,0:T(8,128)(2,1)S(1)}, bf16[128,512]{1,0:T(8,128)(2,1)S(1)}, u32[]{:S(2)}, u32[]{:S(2)}) collective-permute-start(bf16[128,512]{1,0:T(8,128)(2,1)S(1)} %get-tuple-element.181), channel_id=1, source_target_pairs={{0,25},{1,8},{2,27},{3,10},{4,29},{5,12},{6,31},{7,14},{8,1},{9,16... | collective-permute-start | bytes 393224 | tf_op jit(solution)/shard_map/ppermute | solution.py:503
  72.4 2.3 %collective-permute-done.22.outer.refs_6_ = bf16[128,512]{1,0:T(8,128)(2,1)S(1)} collective-permute-done((bf16[128,512]{1,0:T(8,128)(2,1)S(1)}, bf16[128,512]{1,0:T(8,128)(2,1)S(1)}, u32[]{:S(2)}, u32[]{:S(2)}) %collective-permute-start.22) | collective-permute-done | bytes 131104 | tf_op jit(solution)/shard_map/ppermute | solution.py:503
  75.9 2.3 %collective-permute-start.26 = (bf16[128,512]{1,0:T(8,128)(2,1)S(1)}, bf16[128,512]{1,0:T(8,128)(2,1)S(1)}, u32[]{:S(2)}, u32[]{:S(2)}) collective-permute-start(bf16[128,512]{1,0:T(8,128)(2,1)S(1)} %get-tuple-element.195), channel_id=1, source_target_pairs={{0,28},{1,8},{2,30},{3,10},{4,29},{5,9},{6,31},{7,11},{8,4},{9,16}... | collective-permute-start | bytes 393224 | tf_op jit(solution)/shard_map/ppermute | solution.py:503
  79.6 1.6 %collective-permute-start.25 = (bf16[256,512]{1,0:T(8,128)(2,1)S(1)}, bf16[256,512]{1,0:T(8,128)(2,1)S(1)}, u32[]{:S(2)}, u32[]{:S(2)}) collective-permute-start(bf16[256,512]{1,0:T(8,128)(2,1)S(1)} %get-tuple-element.193), channel_id=1, source_target_pairs={{0,1},{1,5},{2,3},{3,7},{4,0},{5,4},{6,2},{7,6},{8,9},{9,13},{10,1... | collective-permute-start | bytes 786440 | tf_op jit(solution)/shard_map/ppermute | solution.py:503
  81.2 1.3 %collective-permute-done.26.outer = bf16[128,512]{1,0:T(8,128)(2,1)S(1)} collective-permute-done((bf16[128,512]{1,0:T(8,128)(2,1)S(1)}, bf16[128,512]{1,0:T(8,128)(2,1)S(1)}, u32[]{:S(2)}, u32[]{:S(2)}) %collective-permute-start.26) | collective-permute-done | bytes 131104 | tf_op jit(solution)/shard_map/ppermute | solution.py:503
  84.1 4.7 %collective-permute-done.25.refs_1_ = bf16[256,512]{1,0:T(8,128)(2,1)S(1)} collective-permute-done((bf16[256,512]{1,0:T(8,128)(2,1)S(1)}, bf16[256,512]{1,0:T(8,128)(2,1)S(1)}, u32[]{:S(2)}, u32[]{:S(2)}) %collective-permute-start.25) | collective-permute-done | bytes 262176 | tf_op jit(solution)/shard_map/ppermute | solution.py:503
  (68 shorter events, 20.4 us)
Async XLA Ops:
  1.9 8.3 %collective-permute-start.1 = (bf16[272,512]{1,0:T(8,128)(2,1)S(1)}, bf16[272,512]{1,0:T(8,128)(2,1)S(1)}, u32[]{:S(2)}, u32[]{:S(2)}) collective-permute-start(bf16[272,512]{1,0:T(8,128)(2,1)S(1)} %get-tuple-element.102), channel_id=1, source_target_pairs={{0,4},{1,0},{2,6},{3,2},{4,5},{5,1},{6,7},{7,3},{8,12},{9,8},{10,1... | collective-permute-start | bytes 835592 | tf_op jit(solution)/shard_map/ppermute | solution.py:503
  4.8 7.7 %collective-permute-start.2 = (bf16[128,512]{1,0:T(8,128)(2,1)S(1)}, bf16[128,512]{1,0:T(8,128)(2,1)S(1)}, u32[]{:S(2)}, u32[]{:S(2)}) collective-permute-start(bf16[128,512]{1,0:T(8,128)(2,1)S(1)} %get-tuple-element.103), channel_id=1, source_target_pairs={{0,25},{1,29},{2,27},{3,31},{4,8},{5,12},{6,10},{7,14},{8,1},{9,5}... | collective-permute-start | bytes 393224 | tf_op jit(solution)/shard_map/ppermute | solution.py:503
  7.0 7.5 %collective-permute-start.3 = (f32[1,512]{1,0:T(1,128)}, f32[1,512]{1,0:T(1,128)S(1)}, u32[]{:S(2)}, u32[]{:S(2)}) collective-permute-start(f32[1,512]{1,0:T(1,128)} %refs_1_.15), channel_id=1, source_target_pairs={{0,1},{1,0},{2,3},{3,2},{4,5},{5,4},{6,7},{7,6},{8,9},{9,8},{10,11... | collective-permute-start | bytes 6152 | tf_op jit(solution)/shard_map/ppermute | solution.py:503
  9.4 4.2 %collective-permute-start = (bf16[2048,512]{1,0:T(8,128)(2,1)S(1)}, bf16[2048,512]{1,0:T(8,128)(2,1)S(1)}, u32[]{:S(2)}, u32[]{:S(2)}) collective-permute-start(bf16[2048,512]{1,0:T(8,128)(2,1)S(1)} %shard_map.131.mine), channel_id=1, source_target_pairs={{0,1},{1,0},{2,3},{3,2},{4,5},{5,4},{6,7},{7,6},{8,9},{9,8},{10,11... | collective-permute-start | bytes 6291464 | tf_op jit(solution)/shard_map/ppermute | solution.py:503
  12.6 2.0 %collective-permute-start.4 = (bf16[128,512]{1,0:T(8,128)(2,1)S(1)}, bf16[128,512]{1,0:T(8,128)(2,1)S(1)}, u32[]{:S(2)}, u32[]{:S(2)}) collective-permute-start(bf16[128,512]{1,0:T(8,128)(2,1)S(1)} %get-tuple-element.114), channel_id=1, source_target_pairs={{0,1},{1,0},{2,3},{3,2},{4,5},{5,4},{6,7},{7,6},{8,9},{9,8},{10,11... | collective-permute-start | bytes 393224 | tf_op jit(solution)/shard_map/ppermute | solution.py:503
  15.8 2.2 %collective-permute-start.5 = (bf16[128,512]{1,0:T(8,128)(2,1)S(1)}, bf16[128,512]{1,0:T(8,128)(2,1)S(1)}, u32[]{:S(2)}, u32[]{:S(2)}) collective-permute-start(bf16[128,512]{1,0:T(8,128)(2,1)S(1)} %get-tuple-element.118), channel_id=1, source_target_pairs={{0,1},{1,0},{2,3},{3,2},{4,5},{5,4},{6,7},{7,6},{8,9},{9,8},{10,11... | collective-permute-start | bytes 393224 | tf_op jit(solution)/shard_map/ppermute | solution.py:503
  16.0 6.3 %collective-permute-start.6 = (bf16[128,512]{1,0:T(8,128)(2,1)S(1)}, bf16[128,512]{1,0:T(8,128)(2,1)S(1)}, u32[]{:S(2)}, u32[]{:S(2)}) collective-permute-start(bf16[128,512]{1,0:T(8,128)(2,1)S(1)} %get-tuple-element.121), channel_id=1, source_target_pairs={{0,25},{1,8},{2,27},{3,10},{4,29},{5,12},{6,31},{7,14},{8,1},{9,16... | collective-permute-start | bytes 393224 | tf_op jit(solution)/shard_map/ppermute | solution.py:503
  23.4 11.0 %collective-permute-start.9 = (bf16[128,512]{1,0:T(8,128)(2,1)S(1)}, bf16[128,512]{1,0:T(8,128)(2,1)S(1)}, u32[]{:S(2)}, u32[]{:S(2)}) collective-permute-start(bf16[128,512]{1,0:T(8,128)(2,1)S(1)} %get-tuple-element.125), channel_id=1, source_target_pairs={{0,27},{1,10},{4,31},{5,14},{8,3},{9,18},{12,7},{13,22},{16,11},{1... | collective-permute-start | bytes 393224 | tf_op jit(solution)/shard_map/ppermute | solution.py:503
  25.2 9.1 %collective-permute-start.7 = (bf16[256,512]{1,0:T(8,128)(2,1)S(1)}, bf16[256,512]{1,0:T(8,128)(2,1)S(1)}, u32[]{:S(2)}, u32[]{:S(2)}) collective-permute-start(bf16[256,512]{1,0:T(8,128)(2,1)S(1)} %get-tuple-element.122.h), channel_id=1, source_target_pairs={{0,2},{1,3},{4,6},{5,7},{8,10},{9,11},{12,14},{13,15},{16,18},{17,... | collective-permute-start | bytes 786440 | tf_op jit(solution)/shard_map/ppermute | solution.py:503
  35.9 6.3 %collective-permute-start.13 = (bf16[128,512]{1,0:T(8,128)(2,1)S(1)}, bf16[128,512]{1,0:T(8,128)(2,1)S(1)}, u32[]{:S(2)}, u32[]{:S(2)}) collective-permute-start(bf16[128,512]{1,0:T(8,128)(2,1)S(1)} %get-tuple-element.149), channel_id=1, source_target_pairs={{0,25},{1,8},{2,27},{3,10},{4,29},{5,12},{6,31},{7,14},{8,1},{9,16... | collective-permute-start | bytes 393224 | tf_op jit(solution)/shard_map/ppermute | solution.py:503
  37.2 6.9 %collective-permute-start.11 = (bf16[256,512]{1,0:T(8,128)(2,1)S(1)}, bf16[256,512]{1,0:T(8,128)(2,1)S(1)}, u32[]{:S(2)}, u32[]{:S(2)}) collective-permute-start(bf16[256,512]{1,0:T(8,128)(2,1)S(1)} %get-tuple-element.145), channel_id=1, source_target_pairs={{0,0},{1,4},{4,1},{5,5},{8,8},{9,12},{12,9},{13,13},{16,16},{17,20... | collective-permute-start | bytes 786440 | tf_op jit(solution)/shard_map/ppermute | solution.py:503
  37.9 10.1 %collective-permute-start.12 = (bf16[256,512]{1,0:T(8,128)(2,1)S(1)}, bf16[256,512]{1,0:T(8,128)(2,1)S(1)}, u32[]{:S(2)}, u32[]{:S(2)}) collective-permute-start(bf16[256,512]{1,0:T(8,128)(2,1)S(1)} %get-tuple-element.146), channel_id=1, source_target_pairs={{0,1},{1,5},{4,0},{5,4},{8,9},{9,13},{12,8},{13,12},{16,17},{17,21... | collective-permute-start | bytes 786440 | tf_op jit(solution)/shard_map/ppermute | solution.py:503
  42.2 1.8 %collective-permute-start.14 = (bf16[128,512]{1,0:T(8,128)(2,1)S(1)}, bf16[128,512]{1,0:T(8,128)(2,1)S(1)}, u32[]{:S(2)}, u32[]{:S(2)}) collective-permute-start(bf16[128,512]{1,0:T(8,128)(2,1)S(1)} %get-tuple-element.161), channel_id=1, source_target_pairs={{0,1},{1,0},{2,3},{3,2},{4,5},{5,4},{6,7},{7,6},{8,9},{9,8},{10,11... | collective-permute-start | bytes 393224 | tf_op jit(solution)/shard_map/ppermute | solution.py:503
  42.2 6.9 %collective-permute-start.15 = (bf16[128,512]{1,0:T(8,128)(2,1)S(1)}, bf16[128,512]{1,0:T(8,128)(2,1)S(1)}, u32[]{:S(2)}, u32[]{:S(2)}) collective-permute-start(bf16[128,512]{1,0:T(8,128)(2,1)S(1)} %get-tuple-element.166), channel_id=1, source_target_pairs={{0,25},{1,8},{2,27},{3,10},{4,29},{5,12},{6,31},{7,14},{8,1},{9,16... | collective-permute-start | bytes 393224 | tf_op jit(solution)/shard_map/ppermute | solution.py:503
  49.2 12.3 %collective-permute-start.18 = (bf16[128,512]{1,0:T(8,128)(2,1)S(1)}, bf16[128,512]{1,0:T(8,128)(2,1)S(1)}, u32[]{:S(2)}, u32[]{:S(2)}) collective-permute-start(bf16[128,512]{1,0:T(8,128)(2,1)S(1)} %get-tuple-element.167.refs_3_), channel_id=1, source_target_pairs={{2,25},{3,8},{6,29},{7,12},{10,1},{11,16},{14,5},{15,20},{18,9},{1... | collective-permute-start | bytes 393224 | tf_op jit(solution)/shard_map/ppermute | solution.py:503
  50.7 16.2 %collective-permute-start.17 = (bf16[256,512]{1,0:T(8,128)(2,1)S(1)}, bf16[256,512]{1,0:T(8,128)(2,1)S(1)}, u32[]{:S(2)}, u32[]{:S(2)}) collective-permute-start(bf16[256,512]{1,0:T(8,128)(2,1)S(1)} %shard_map.154.value), channel_id=1, source_target_pairs={{2,0},{3,1},{6,4},{7,5},{10,8},{11,9},{14,12},{15,13},{18,16},{19,... | collective-permute-start | bytes 786440 | tf_op jit(solution)/shard_map/ppermute | solution.py:503
  68.0 2.3 %collective-permute-start.19 = (bf16[128,512]{1,0:T(8,128)(2,1)S(1)}, bf16[128,512]{1,0:T(8,128)(2,1)S(1)}, u32[]{:S(2)}, u32[]{:S(2)}) collective-permute-start(bf16[128,512]{1,0:T(8,128)(2,1)S(1)} %get-tuple-element.173), channel_id=1, source_target_pairs={{0,1},{1,0},{2,3},{3,2},{4,5},{5,4},{6,7},{7,6},{8,9},{9,8},{10,11... | collective-permute-start | bytes 393224 | tf_op jit(solution)/shard_map/ppermute | solution.py:503
  68.1 6.6 %collective-permute-start.22 = (bf16[128,512]{1,0:T(8,128)(2,1)S(1)}, bf16[128,512]{1,0:T(8,128)(2,1)S(1)}, u32[]{:S(2)}, u32[]{:S(2)}) collective-permute-start(bf16[128,512]{1,0:T(8,128)(2,1)S(1)} %get-tuple-element.181), channel_id=1, source_target_pairs={{0,25},{1,8},{2,27},{3,10},{4,29},{5,12},{6,31},{7,14},{8,1},{9,16... | collective-permute-start | bytes 393224 | tf_op jit(solution)/shard_map/ppermute | solution.py:503
  71.0 7.2 %collective-permute-start.20 = (bf16[256,512]{1,0:T(8,128)(2,1)S(1)}, bf16[256,512]{1,0:T(8,128)(2,1)S(1)}, u32[]{:S(2)}, u32[]{:S(2)}) collective-permute-start(bf16[256,512]{1,0:T(8,128)(2,1)S(1)} %get-tuple-element.179), channel_id=1, source_target_pairs={{2,2},{3,6},{6,3},{7,7},{10,10},{11,14},{14,11},{15,15},{18,18},{1... | collective-permute-start | bytes 786440 | tf_op jit(solution)/shard_map/ppermute | solution.py:503
  71.7 6.5 %collective-permute-start.21 = (bf16[256,512]{1,0:T(8,128)(2,1)S(1)}, bf16[256,512]{1,0:T(8,128)(2,1)S(1)}, u32[]{:S(2)}, u32[]{:S(2)}) collective-permute-start(bf16[256,512]{1,0:T(8,128)(2,1)S(1)} %get-tuple-element.180), channel_id=1, source_target_pairs={{2,3},{3,7},{6,2},{7,6},{10,11},{11,15},{14,10},{15,14},{18,19},{1... | collective-permute-start | bytes 786440 | tf_op jit(solution)/shard_map/ppermute | solution.py:503
  75.8 2.4 %collective-permute-start.23 = (bf16[128,512]{1,0:T(8,128)(2,1)S(1)}, bf16[128,512]{1,0:T(8,128)(2,1)S(1)}, u32[]{:S(2)}, u32[]{:S(2)}) collective-permute-start(bf16[128,512]{1,0:T(8,128)(2,1)S(1)} %get-tuple-element.187), channel_id=1, source_target_pairs={{0,1},{1,0},{2,3},{3,2},{4,5},{5,4},{6,7},{7,6},{8,9},{9,8},{10,11... | collective-permute-start | bytes 393224 | tf_op jit(solution)/shard_map/ppermute | solution.py:503
  75.9 6.6 %collective-permute-start.26 = (bf16[128,512]{1,0:T(8,128)(2,1)S(1)}, bf16[128,512]{1,0:T(8,128)(2,1)S(1)}, u32[]{:S(2)}, u32[]{:S(2)}) collective-permute-start(bf16[128,512]{1,0:T(8,128)(2,1)S(1)} %get-tuple-element.195), channel_id=1, source_target_pairs={{0,28},{1,8},{2,30},{3,10},{4,29},{5,9},{6,31},{7,11},{8,4},{9,16}... | collective-permute-start | bytes 393224 | tf_op jit(solution)/shard_map/ppermute | solution.py:503
  78.9 5.1 %collective-permute-start.24 = (bf16[256,512]{1,0:T(8,128)(2,1)S(1)}, bf16[256,512]{1,0:T(8,128)(2,1)S(1)}, u32[]{:S(2)}, u32[]{:S(2)}) collective-permute-start(bf16[256,512]{1,0:T(8,128)(2,1)S(1)} %get-tuple-element.192), channel_id=1, source_target_pairs={{0,0},{1,4},{2,2},{3,6},{4,1},{5,5},{6,3},{7,7},{8,8},{9,12},{10,1... | collective-permute-start | bytes 786440 | tf_op jit(solution)/shard_map/ppermute | solution.py:503
  79.6 9.1 %collective-permute-start.25 = (bf16[256,512]{1,0:T(8,128)(2,1)S(1)}, bf16[256,512]{1,0:T(8,128)(2,1)S(1)}, u32[]{:S(2)}, u32[]{:S(2)}) collective-permute-start(bf16[256,512]{1,0:T(8,128)(2,1)S(1)} %get-tuple-element.193), channel_id=1, source_target_pairs={{0,1},{1,5},{2,3},{3,7},{4,0},{5,4},{6,2},{7,6},{8,9},{9,13},{10,1... | collective-permute-start | bytes 786440 | tf_op jit(solution)/shard_map/ppermute | solution.py:503
  (5 other events, 6.3 us)

commit v10 on v9

--- a/solution.py
+++ b/solution.py
@@ -517,13 +517,10 @@
     def towards(value, side, step):
         if side == INNER:
             return send(value, lambda z, y, x, c: (z, y, x, 1 - c))
-        return send(value, lambda z, y, x, c: (z + 2 * c - 1, y, x + step, 1 - c) if crosses(x, step) else None)
-
-    def crosses(x, step):
-        return step == 0 or 0 <= x + step < sections // 2
-
-    def across(value, step):
-        return send(value, lambda z, y, x, c: (z, y, x + step, c) if crosses(x, step) else None)
+        return send(value, lambda z, y, x, c: (z + 2 * c - 1, y, x + step, 1 - c) if x + min(step, 0) >= 0 else None)
+
+    def across(value):
+        return send(value, lambda z, y, x, c: (z, y, x + 1, c))
 
     wide = (rows, latent)
     edge_wide = (edges, latent)
@@ -603,7 +600,7 @@
             inner = towards(to[0], INNER, step)
             arrived = (inner,)
         elif step:
-            hidden = across(hidden, step)
+            hidden = across(hidden)
             inner = towards(*run(inner_kernel, (lists, hidden), [(narrow, BF16)]), INNER, 0)
             arrived = ()
         saved = run(
@@ -656,7 +653,7 @@
             halos = {INNER: inner, **halos}
         if step:
             own = upstream
-            upstream = across(upstream, step)
+            upstream = across(upstream)
             halos = {OUTER: run(spread_kernel, (lists, halos[OUTER]), [(wide, F32)], cost=LONG)[0]}
         elif tick == 1:
             outputs, upstream = lax.optimization_barrier((both, upstream))

time: 90.4 us -> 88.4 us (0.978)
  waiting for transfers between devices: 46.2 us -> 39.2 us
  starting transfers between devices: 29 us -> 34.1 us
    ppermute x28, waiting for transfers between devices: 46.2 us -> 39.2 us  [send(): return lax.ppermute(value, AXES, table)]
    ppermute x28, starting transfers between devices: 29 us -> 34.1 us  [send(): return lax.ppermute(value, AXES, table)]
  transfers between devices with their start and end apart: 28 -> 28, of which waited for: 17 -> 16; matrix products, arithmetic and copies ran while one was open for 0% -> 0% of each run, Pallas kernels for 9% -> 9%
where the time goes in v10:
time: 88.4 us; the launch traced here: 88.2 us
  waiting for transfers between devices  39.2 us (44%)
  starting transfers between devices  34.1 us (39%)
  Pallas kernels  13.7 us (15%)
  between operations  1.12 us (1%)
    ppermute x28, waiting for transfers between devices, send(): return lax.ppermute(value, AXES, table)  39.2 us
    ppermute x28, starting transfers between devices, send(): return lax.ppermute(value, AXES, table)  34.1 us
    pallas_call x34, Pallas kernels, run(): pl.pallas_call(kernel, out_shape=[jax.ShapeDtypeStruct(s, t) for s, t in...  13.7 us
  transfers between devices with their start and end apart: 28, of which 16 were waited for; matrix products, arithmetic and copies ran while one was open for 0% of the time, Pallas kernels for 9%

profile of v10, /device:TPU:0, one launch (start us, length us, event | category | flops | bytes accessed | tf_op | source)
XLA Modules:
  0.0 88.2 jit_solution(1192382398948151747)
XLA Ops:
  0.6 1.2 %shard_map.132 = (bf16[256,512]{1,0:T(8,128)(2,1)S(1)}, bf16[272,512]{1,0:T(8,128)(2,1)S(1)}, bf16[128,512]{1,0:T(8,128)(2,1)S(1)}, bf16[16,128]{1,0:T(8,128)(2,1)S(1)}) custom-call(s32[2]{0:T(128)} %count_in.1, s32[1,1,2]{2,1,0:T(1,128)} %bitcast.11, bf16[2,256,512]{2,1,0:T(8,128)(2,1)} %inputs.1, bf16[2,256,512]{2,1,0:T(8,128)(2,1)} %cotangent.1, ...), custom_call_target="tpu_custom_call" | custom-call | flops 1 | bytes 1 | tf_op jit(solution)/shard_map/pallas_call | solution.py:437
  1.9 3.0 %collective-permute-start.1 = (bf16[272,512]{1,0:T(8,128)(2,1)S(1)}, bf16[272,512]{1,0:T(8,128)(2,1)S(1)}, u32[]{:S(2)}, u32[]{:S(2)}) collective-permute-start(bf16[272,512]{1,0:T(8,128)(2,1)S(1)} %get-tuple-element.102), channel_id=1, source_target_pairs={{0,4},{1,0},{2,6},{3,2},{4,5},{5,1},{6,7},{7,3},{8,12},{9,8},{10,1... | collective-permute-start | bytes 835592 | tf_op jit(solution)/shard_map/ppermute | solution.py:503
  4.8 2.2 %collective-permute-start.2 = (bf16[128,512]{1,0:T(8,128)(2,1)S(1)}, bf16[128,512]{1,0:T(8,128)(2,1)S(1)}, u32[]{:S(2)}, u32[]{:S(2)}) collective-permute-start(bf16[128,512]{1,0:T(8,128)(2,1)S(1)} %get-tuple-element.103), channel_id=1, source_target_pairs={{0,25},{1,29},{2,27},{3,31},{4,8},{5,12},{6,10},{7,14},{8,1},{9,5}... | collective-permute-start | bytes 393224 | tf_op jit(solution)/shard_map/ppermute | solution.py:503
  7.7 1.7 %shard_map.131.mine = bf16[2048,512]{1,0:T(8,128)(2,1)S(1)} custom-call(bf16[512,512]{1,0:T(8,128)(2,1)} %bitcast.6, bf16[512,512]{1,0:T(8,128)(2,1)} %bitcast.7, bf16[512,512]{1,0:T(8,128)(2,1)} %bitcast.8, bf16[512,512]{1,0:T(8,128)(2,1)} %bitcast.9, bf16[512,512]{1,0:T(8,128)(2,1)} %bitcast.10), custom_call_target="tpu_custom_call" | custom-call | flops 1 | bytes 1 | tf_op jit(solution)/shard_map/pallas_call | solution.py:437
  10.4 2.1 %collective-permute-done.2._.refs_8_ = bf16[128,512]{1,0:T(8,128)(2,1)S(1)} collective-permute-done((bf16[128,512]{1,0:T(8,128)(2,1)S(1)}, bf16[128,512]{1,0:T(8,128)(2,1)S(1)}, u32[]{:S(2)}, u32[]{:S(2)}) %collective-permute-start.2) | collective-permute-done | bytes 131104 | tf_op jit(solution)/shard_map/ppermute | solution.py:503
  16.0 1.5 %collective-permute-start.6 = (bf16[128,512]{1,0:T(8,128)(2,1)S(1)}, bf16[128,512]{1,0:T(8,128)(2,1)S(1)}, u32[]{:S(2)}, u32[]{:S(2)}) collective-permute-start(bf16[128,512]{1,0:T(8,128)(2,1)S(1)} %get-tuple-element.121), channel_id=1, source_target_pairs={{0,25},{1,8},{2,27},{3,10},{4,29},{5,12},{6,31},{7,14},{8,1},{9,16... | collective-permute-start | bytes 393224 | tf_op jit(solution)/shard_map/ppermute | solution.py:503
  18.8 3.5 %collective-permute-done.6.refs_8_ = bf16[128,512]{1,0:T(8,128)(2,1)S(1)} collective-permute-done((bf16[128,512]{1,0:T(8,128)(2,1)S(1)}, bf16[128,512]{1,0:T(8,128)(2,1)S(1)}, u32[]{:S(2)}, u32[]{:S(2)}) %collective-permute-start.6) | collective-permute-done | bytes 131104 | tf_op jit(solution)/shard_map/ppermute | solution.py:503
  23.5 2.8 %collective-permute-start.7 = (bf16[256,512]{1,0:T(8,128)(2,1)S(1)}, bf16[256,512]{1,0:T(8,128)(2,1)S(1)}, u32[]{:S(2)}, u32[]{:S(2)}) collective-permute-start(bf16[256,512]{1,0:T(8,128)(2,1)S(1)} %get-tuple-element.122.h), channel_id=1, source_target_pairs={{0,2},{1,3},{2,0},{3,1},{4,6},{5,7},{6,4},{7,5},{8,10},{9,11},{10,... | collective-permute-start | bytes 786440 | tf_op jit(solution)/shard_map/ppermute | solution.py:503
  26.8 7.8 %collective-permute-done.7.refs_1_.h.refs_4_ = bf16[256,512]{1,0:T(8,128)(2,1)S(1)} collective-permute-done((bf16[256,512]{1,0:T(8,128)(2,1)S(1)}, bf16[256,512]{1,0:T(8,128)(2,1)S(1)}, u32[]{:S(2)}, u32[]{:S(2)}) %collective-permute-start.7) | collective-permute-done | bytes 262176 | tf_op jit(solution)/shard_map/ppermute | solution.py:503
  34.8 1.3 %collective-permute-done.8.refs_7_ = bf16[128,512]{1,0:T(8,128)(2,1)S(1)} collective-permute-done((bf16[128,512]{1,0:T(8,128)(2,1)S(1)}, bf16[128,512]{1,0:T(8,128)(2,1)S(1)}, u32[]{:S(2)}, u32[]{:S(2)}) %collective-permute-start.8) | collective-permute-done | bytes 131104 | tf_op jit(solution)/shard_map/ppermute | solution.py:503
  38.2 4.2 %collective-permute-start.12 = (bf16[256,512]{1,0:T(8,128)(2,1)S(1)}, bf16[256,512]{1,0:T(8,128)(2,1)S(1)}, u32[]{:S(2)}, u32[]{:S(2)}) collective-permute-start(bf16[256,512]{1,0:T(8,128)(2,1)S(1)} %get-tuple-element.146), channel_id=1, source_target_pairs={{0,1},{1,5},{4,0},{5,4},{8,9},{9,13},{12,8},{13,12},{16,17},{17,21... | collective-permute-start | bytes 786440 | tf_op jit(solution)/shard_map/ppermute | solution.py:503
  42.6 1.7 %collective-permute-start.15 = (bf16[128,512]{1,0:T(8,128)(2,1)S(1)}, bf16[128,512]{1,0:T(8,128)(2,1)S(1)}, u32[]{:S(2)}, u32[]{:S(2)}) collective-permute-start(bf16[128,512]{1,0:T(8,128)(2,1)S(1)} %get-tuple-element.166), channel_id=1, source_target_pairs={{0,25},{1,8},{2,27},{3,10},{4,29},{5,12},{6,31},{7,14},{8,1},{9,16... | collective-permute-start | bytes 393224 | tf_op jit(solution)/shard_map/ppermute | solution.py:503
  44.4 4.0 %collective-permute-done.12.refs_3_.refs_1_ = bf16[256,512]{1,0:T(8,128)(2,1)S(1)} collective-permute-done((bf16[256,512]{1,0:T(8,128)(2,1)S(1)}, bf16[256,512]{1,0:T(8,128)(2,1)S(1)}, u32[]{:S(2)}, u32[]{:S(2)}) %collective-permute-start.12) | collective-permute-done | bytes 262176 | tf_op jit(solution)/shard_map/ppermute | solution.py:503
  48.3 1.5 %collective-permute-done.15.refs_6_ = bf16[128,512]{1,0:T(8,128)(2,1)S(1)} collective-permute-done((bf16[128,512]{1,0:T(8,128)(2,1)S(1)}, bf16[128,512]{1,0:T(8,128)(2,1)S(1)}, u32[]{:S(2)}, u32[]{:S(2)}) %collective-permute-start.15) | collective-permute-done | bytes 131104 | tf_op jit(solution)/shard_map/ppermute | solution.py:503
  49.8 1.3 %collective-permute-start.18 = (bf16[128,512]{1,0:T(8,128)(2,1)S(1)}, bf16[128,512]{1,0:T(8,128)(2,1)S(1)}, u32[]{:S(2)}, u32[]{:S(2)}) collective-permute-start(bf16[128,512]{1,0:T(8,128)(2,1)S(1)} %get-tuple-element.167.refs_3_), channel_id=1, source_target_pairs={{2,25},{3,8},{6,29},{7,12},{10,1},{11,16},{14,5},{15,20},{18,9},{1... | collective-permute-start | bytes 393224 | tf_op jit(solution)/shard_map/ppermute | solution.py:503
  51.3 5.4 %collective-permute-start.17 = (bf16[256,512]{1,0:T(8,128)(2,1)S(1)}, bf16[256,512]{1,0:T(8,128)(2,1)S(1)}, u32[]{:S(2)}, u32[]{:S(2)}) collective-permute-start(bf16[256,512]{1,0:T(8,128)(2,1)S(1)} %shard_map.154.value), channel_id=1, source_target_pairs={{0,2},{1,3},{2,0},{3,1},{4,6},{5,7},{6,4},{7,5},{8,10},{9,11},{10,... | collective-permute-start | bytes 786440 | tf_op jit(solution)/shard_map/ppermute | solution.py:503
  56.7 3.0 %collective-permute-done.18.outer = bf16[128,512]{1,0:T(8,128)(2,1)S(1)} collective-permute-done((bf16[128,512]{1,0:T(8,128)(2,1)S(1)}, bf16[128,512]{1,0:T(8,128)(2,1)S(1)}, u32[]{:S(2)}, u32[]{:S(2)}) %collective-permute-start.18) | collective-permute-done | bytes 131104 | tf_op jit(solution)/shard_map/ppermute | solution.py:503
  59.7 5.0 %collective-permute-done.17.refs_5_ = bf16[256,512]{1,0:T(8,128)(2,1)S(1)} collective-permute-done((bf16[256,512]{1,0:T(8,128)(2,1)S(1)}, bf16[256,512]{1,0:T(8,128)(2,1)S(1)}, u32[]{:S(2)}, u32[]{:S(2)}) %collective-permute-start.17) | collective-permute-done | bytes 262176 | tf_op jit(solution)/shard_map/ppermute | solution.py:503
  65.9 1.3 %collective-permute-start.22 = (bf16[128,512]{1,0:T(8,128)(2,1)S(1)}, bf16[128,512]{1,0:T(8,128)(2,1)S(1)}, u32[]{:S(2)}, u32[]{:S(2)}) collective-permute-start(bf16[128,512]{1,0:T(8,128)(2,1)S(1)} %get-tuple-element.181), channel_id=1, source_target_pairs={{0,25},{1,8},{2,27},{3,10},{4,29},{5,12},{6,31},{7,14},{8,1},{9,16... | collective-permute-start | bytes 393224 | tf_op jit(solution)/shard_map/ppermute | solution.py:503
  69.3 2.9 %collective-permute-done.22.outer.refs_6_ = bf16[128,512]{1,0:T(8,128)(2,1)S(1)} collective-permute-done((bf16[128,512]{1,0:T(8,128)(2,1)S(1)}, bf16[128,512]{1,0:T(8,128)(2,1)S(1)}, u32[]{:S(2)}, u32[]{:S(2)}) %collective-permute-start.22) | collective-permute-done | bytes 131104 | tf_op jit(solution)/shard_map/ppermute | solution.py:503
  73.5 3.4 %collective-permute-start.26 = (bf16[128,512]{1,0:T(8,128)(2,1)S(1)}, bf16[128,512]{1,0:T(8,128)(2,1)S(1)}, u32[]{:S(2)}, u32[]{:S(2)}) collective-permute-start(bf16[128,512]{1,0:T(8,128)(2,1)S(1)} %get-tuple-element.195), channel_id=1, source_target_pairs={{0,28},{1,8},{2,30},{3,10},{4,29},{5,9},{6,31},{7,11},{8,4},{9,16}... | collective-permute-start | bytes 393224 | tf_op jit(solution)/shard_map/ppermute | solution.py:503
  78.2 1.6 %collective-permute-start.25 = (bf16[256,512]{1,0:T(8,128)(2,1)S(1)}, bf16[256,512]{1,0:T(8,128)(2,1)S(1)}, u32[]{:S(2)}, u32[]{:S(2)}) collective-permute-start(bf16[256,512]{1,0:T(8,128)(2,1)S(1)} %get-tuple-element.193), channel_id=1, source_target_pairs={{0,1},{1,5},{2,3},{3,7},{4,0},{5,4},{6,2},{7,6},{8,9},{9,13},{10,1... | collective-permute-start | bytes 786440 | tf_op jit(solution)/shard_map/ppermute | solution.py:503
  79.8 1.2 %collective-permute-start.27 = (bf16[128,512]{1,0:T(8,128)(2,1)S(1)}, bf16[128,512]{1,0:T(8,128)(2,1)S(1)}, u32[]{:S(2)}, u32[]{:S(2)}) collective-permute-start(bf16[128,512]{1,0:T(8,128)(2,1)S(1)} %collective-permute-done.26.outer), channel_id=1, source_target_pairs={{0,1},{1,0},{2,3},{3,2},{4,5},{5,4},{6,7},{7,6},{8,9},{9,8},{10,11... | collective-permute-start | bytes 393224 | tf_op jit(solution)/shard_map/ppermute | solution.py:503
  82.2 4.6 %collective-permute-done.25.refs_1_ = bf16[256,512]{1,0:T(8,128)(2,1)S(1)} collective-permute-done((bf16[256,512]{1,0:T(8,128)(2,1)S(1)}, bf16[256,512]{1,0:T(8,128)(2,1)S(1)}, u32[]{:S(2)}, u32[]{:S(2)}) %collective-permute-start.25) | collective-permute-done | bytes 262176 | tf_op jit(solution)/shard_map/ppermute | solution.py:503
  (68 shorter events, 18.9 us)
Async XLA Ops:
  1.9 8.3 %collective-permute-start.1 = (bf16[272,512]{1,0:T(8,128)(2,1)S(1)}, bf16[272,512]{1,0:T(8,128)(2,1)S(1)}, u32[]{:S(2)}, u32[]{:S(2)}) collective-permute-start(bf16[272,512]{1,0:T(8,128)(2,1)S(1)} %get-tuple-element.102), channel_id=1, source_target_pairs={{0,4},{1,0},{2,6},{3,2},{4,5},{5,1},{6,7},{7,3},{8,12},{9,8},{10,1... | collective-permute-start | bytes 835592 | tf_op jit(solution)/shard_map/ppermute | solution.py:503
  4.8 7.7 %collective-permute-start.2 = (bf16[128,512]{1,0:T(8,128)(2,1)S(1)}, bf16[128,512]{1,0:T(8,128)(2,1)S(1)}, u32[]{:S(2)}, u32[]{:S(2)}) collective-permute-start(bf16[128,512]{1,0:T(8,128)(2,1)S(1)} %get-tuple-element.103), channel_id=1, source_target_pairs={{0,25},{1,29},{2,27},{3,31},{4,8},{5,12},{6,10},{7,14},{8,1},{9,5}... | collective-permute-start | bytes 393224 | tf_op jit(solution)/shard_map/ppermute | solution.py:503
  7.0 7.5 %collective-permute-start.3 = (f32[1,512]{1,0:T(1,128)}, f32[1,512]{1,0:T(1,128)S(1)}, u32[]{:S(2)}, u32[]{:S(2)}) collective-permute-start(f32[1,512]{1,0:T(1,128)} %refs_1_.15), channel_id=1, source_target_pairs={{0,1},{1,0},{2,3},{3,2},{4,5},{5,4},{6,7},{7,6},{8,9},{9,8},{10,11... | collective-permute-start | bytes 6152 | tf_op jit(solution)/shard_map/ppermute | solution.py:503
  9.4 4.2 %collective-permute-start = (bf16[2048,512]{1,0:T(8,128)(2,1)S(1)}, bf16[2048,512]{1,0:T(8,128)(2,1)S(1)}, u32[]{:S(2)}, u32[]{:S(2)}) collective-permute-start(bf16[2048,512]{1,0:T(8,128)(2,1)S(1)} %shard_map.131.mine), channel_id=1, source_target_pairs={{0,1},{1,0},{2,3},{3,2},{4,5},{5,4},{6,7},{7,6},{8,9},{9,8},{10,11... | collective-permute-start | bytes 6291464 | tf_op jit(solution)/shard_map/ppermute | solution.py:503
  12.6 2.0 %collective-permute-start.4 = (bf16[128,512]{1,0:T(8,128)(2,1)S(1)}, bf16[128,512]{1,0:T(8,128)(2,1)S(1)}, u32[]{:S(2)}, u32[]{:S(2)}) collective-permute-start(bf16[128,512]{1,0:T(8,128)(2,1)S(1)} %get-tuple-element.114), channel_id=1, source_target_pairs={{0,1},{1,0},{2,3},{3,2},{4,5},{5,4},{6,7},{7,6},{8,9},{9,8},{10,11... | collective-permute-start | bytes 393224 | tf_op jit(solution)/shard_map/ppermute | solution.py:503
  15.8 2.2 %collective-permute-start.5 = (bf16[128,512]{1,0:T(8,128)(2,1)S(1)}, bf16[128,512]{1,0:T(8,128)(2,1)S(1)}, u32[]{:S(2)}, u32[]{:S(2)}) collective-permute-start(bf16[128,512]{1,0:T(8,128)(2,1)S(1)} %get-tuple-element.118), channel_id=1, source_target_pairs={{0,1},{1,0},{2,3},{3,2},{4,5},{5,4},{6,7},{7,6},{8,9},{9,8},{10,11... | collective-permute-start | bytes 393224 | tf_op jit(solution)/shard_map/ppermute | solution.py:503
  16.0 6.3 %collective-permute-start.6 = (bf16[128,512]{1,0:T(8,128)(2,1)S(1)}, bf16[128,512]{1,0:T(8,128)(2,1)S(1)}, u32[]{:S(2)}, u32[]{:S(2)}) collective-permute-start(bf16[128,512]{1,0:T(8,128)(2,1)S(1)} %get-tuple-element.121), channel_id=1, source_target_pairs={{0,25},{1,8},{2,27},{3,10},{4,29},{5,12},{6,31},{7,14},{8,1},{9,16... | collective-permute-start | bytes 393224 | tf_op jit(solution)/shard_map/ppermute | solution.py:503
  23.4 11.3 %collective-permute-start.9 = (bf16[128,512]{1,0:T(8,128)(2,1)S(1)}, bf16[128,512]{1,0:T(8,128)(2,1)S(1)}, u32[]{:S(2)}, u32[]{:S(2)}) collective-permute-start(bf16[128,512]{1,0:T(8,128)(2,1)S(1)} %get-tuple-element.125), channel_id=1, source_target_pairs={{0,27},{1,10},{2,25},{3,8},{4,31},{5,14},{6,29},{7,12},{8,3},{9,18... | collective-permute-start | bytes 393224 | tf_op jit(solution)/shard_map/ppermute | solution.py:503
  23.5 11.1 %collective-permute-start.7 = (bf16[256,512]{1,0:T(8,128)(2,1)S(1)}, bf16[256,512]{1,0:T(8,128)(2,1)S(1)}, u32[]{:S(2)}, u32[]{:S(2)}) collective-permute-start(bf16[256,512]{1,0:T(8,128)(2,1)S(1)} %get-tuple-element.122.h), channel_id=1, source_target_pairs={{0,2},{1,3},{2,0},{3,1},{4,6},{5,7},{6,4},{7,5},{8,10},{9,11},{10,... | collective-permute-start | bytes 786440 | tf_op jit(solution)/shard_map/ppermute | solution.py:503
  36.2 6.3 %collective-permute-start.13 = (bf16[128,512]{1,0:T(8,128)(2,1)S(1)}, bf16[128,512]{1,0:T(8,128)(2,1)S(1)}, u32[]{:S(2)}, u32[]{:S(2)}) collective-permute-start(bf16[128,512]{1,0:T(8,128)(2,1)S(1)} %get-tuple-element.149), channel_id=1, source_target_pairs={{0,25},{1,8},{2,27},{3,10},{4,29},{5,12},{6,31},{7,14},{8,1},{9,16... | collective-permute-start | bytes 393224 | tf_op jit(solution)/shard_map/ppermute | solution.py:503
  37.5 6.9 %collective-permute-start.11 = (bf16[256,512]{1,0:T(8,128)(2,1)S(1)}, bf16[256,512]{1,0:T(8,128)(2,1)S(1)}, u32[]{:S(2)}, u32[]{:S(2)}) collective-permute-start(bf16[256,512]{1,0:T(8,128)(2,1)S(1)} %get-tuple-element.145), channel_id=1, source_target_pairs={{0,0},{1,4},{4,1},{5,5},{8,8},{9,12},{12,9},{13,13},{16,16},{17,20... | collective-permute-start | bytes 786440 | tf_op jit(solution)/shard_map/ppermute | solution.py:503
  38.2 10.1 %collective-permute-start.12 = (bf16[256,512]{1,0:T(8,128)(2,1)S(1)}, bf16[256,512]{1,0:T(8,128)(2,1)S(1)}, u32[]{:S(2)}, u32[]{:S(2)}) collective-permute-start(bf16[256,512]{1,0:T(8,128)(2,1)S(1)} %get-tuple-element.146), channel_id=1, source_target_pairs={{0,1},{1,5},{4,0},{5,4},{8,9},{9,13},{12,8},{13,12},{16,17},{17,21... | collective-permute-start | bytes 786440 | tf_op jit(solution)/shard_map/ppermute | solution.py:503
  42.5 1.8 %collective-permute-start.14 = (bf16[128,512]{1,0:T(8,128)(2,1)S(1)}, bf16[128,512]{1,0:T(8,128)(2,1)S(1)}, u32[]{:S(2)}, u32[]{:S(2)}) collective-permute-start(bf16[128,512]{1,0:T(8,128)(2,1)S(1)} %get-tuple-element.161), channel_id=1, source_target_pairs={{0,1},{1,0},{2,3},{3,2},{4,5},{5,4},{6,7},{7,6},{8,9},{9,8},{10,11... | collective-permute-start | bytes 393224 | tf_op jit(solution)/shard_map/ppermute | solution.py:503
  42.6 7.2 %collective-permute-start.15 = (bf16[128,512]{1,0:T(8,128)(2,1)S(1)}, bf16[128,512]{1,0:T(8,128)(2,1)S(1)}, u32[]{:S(2)}, u32[]{:S(2)}) collective-permute-start(bf16[128,512]{1,0:T(8,128)(2,1)S(1)} %get-tuple-element.166), channel_id=1, source_target_pairs={{0,25},{1,8},{2,27},{3,10},{4,29},{5,12},{6,31},{7,14},{8,1},{9,16... | collective-permute-start | bytes 393224 | tf_op jit(solution)/shard_map/ppermute | solution.py:503
  49.8 9.9 %collective-permute-start.18 = (bf16[128,512]{1,0:T(8,128)(2,1)S(1)}, bf16[128,512]{1,0:T(8,128)(2,1)S(1)}, u32[]{:S(2)}, u32[]{:S(2)}) collective-permute-start(bf16[128,512]{1,0:T(8,128)(2,1)S(1)} %get-tuple-element.167.refs_3_), channel_id=1, source_target_pairs={{2,25},{3,8},{6,29},{7,12},{10,1},{11,16},{14,5},{15,20},{18,9},{1... | collective-permute-start | bytes 393224 | tf_op jit(solution)/shard_map/ppermute | solution.py:503
  51.3 13.4 %collective-permute-start.17 = (bf16[256,512]{1,0:T(8,128)(2,1)S(1)}, bf16[256,512]{1,0:T(8,128)(2,1)S(1)}, u32[]{:S(2)}, u32[]{:S(2)}) collective-permute-start(bf16[256,512]{1,0:T(8,128)(2,1)S(1)} %shard_map.154.value), channel_id=1, source_target_pairs={{0,2},{1,3},{2,0},{3,1},{4,6},{5,7},{6,4},{7,5},{8,10},{9,11},{10,... | collective-permute-start | bytes 786440 | tf_op jit(solution)/shard_map/ppermute | solution.py:503
  65.9 6.3 %collective-permute-start.22 = (bf16[128,512]{1,0:T(8,128)(2,1)S(1)}, bf16[128,512]{1,0:T(8,128)(2,1)S(1)}, u32[]{:S(2)}, u32[]{:S(2)}) collective-permute-start(bf16[128,512]{1,0:T(8,128)(2,1)S(1)} %get-tuple-element.181), channel_id=1, source_target_pairs={{0,25},{1,8},{2,27},{3,10},{4,29},{5,12},{6,31},{7,14},{8,1},{9,16... | collective-permute-start | bytes 393224 | tf_op jit(solution)/shard_map/ppermute | solution.py:503
  67.9 8.9 %collective-permute-start.20 = (bf16[256,512]{1,0:T(8,128)(2,1)S(1)}, bf16[256,512]{1,0:T(8,128)(2,1)S(1)}, u32[]{:S(2)}, u32[]{:S(2)}) collective-permute-start(bf16[256,512]{1,0:T(8,128)(2,1)S(1)} %get-tuple-element.179), channel_id=1, source_target_pairs={{2,2},{3,6},{6,3},{7,7},{10,10},{11,14},{14,11},{15,15},{18,18},{1... | collective-permute-start | bytes 786440 | tf_op jit(solution)/shard_map/ppermute | solution.py:503
  68.6 8.2 %collective-permute-start.21 = (bf16[256,512]{1,0:T(8,128)(2,1)S(1)}, bf16[256,512]{1,0:T(8,128)(2,1)S(1)}, u32[]{:S(2)}, u32[]{:S(2)}) collective-permute-start(bf16[256,512]{1,0:T(8,128)(2,1)S(1)} %get-tuple-element.180), channel_id=1, source_target_pairs={{2,3},{3,7},{6,2},{7,6},{10,11},{11,15},{14,10},{15,14},{18,19},{1... | collective-permute-start | bytes 786440 | tf_op jit(solution)/shard_map/ppermute | solution.py:503
  73.4 3.4 %collective-permute-start.23 = (bf16[128,512]{1,0:T(8,128)(2,1)S(1)}, bf16[128,512]{1,0:T(8,128)(2,1)S(1)}, u32[]{:S(2)}, u32[]{:S(2)}) collective-permute-start(bf16[128,512]{1,0:T(8,128)(2,1)S(1)} %get-tuple-element.187), channel_id=1, source_target_pairs={{0,1},{1,0},{2,3},{3,2},{4,5},{5,4},{6,7},{7,6},{8,9},{9,8},{10,11... | collective-permute-start | bytes 393224 | tf_op jit(solution)/shard_map/ppermute | solution.py:503
  73.5 6.4 %collective-permute-start.26 = (bf16[128,512]{1,0:T(8,128)(2,1)S(1)}, bf16[128,512]{1,0:T(8,128)(2,1)S(1)}, u32[]{:S(2)}, u32[]{:S(2)}) collective-permute-start(bf16[128,512]{1,0:T(8,128)(2,1)S(1)} %get-tuple-element.195), channel_id=1, source_target_pairs={{0,28},{1,8},{2,30},{3,10},{4,29},{5,9},{6,31},{7,11},{8,4},{9,16}... | collective-permute-start | bytes 393224 | tf_op jit(solution)/shard_map/ppermute | solution.py:503
  77.5 4.7 %collective-permute-start.24 = (bf16[256,512]{1,0:T(8,128)(2,1)S(1)}, bf16[256,512]{1,0:T(8,128)(2,1)S(1)}, u32[]{:S(2)}, u32[]{:S(2)}) collective-permute-start(bf16[256,512]{1,0:T(8,128)(2,1)S(1)} %get-tuple-element.192), channel_id=1, source_target_pairs={{0,0},{1,4},{2,2},{3,6},{4,1},{5,5},{6,3},{7,7},{8,8},{9,12},{10,1... | collective-permute-start | bytes 786440 | tf_op jit(solution)/shard_map/ppermute | solution.py:503
  78.2 8.6 %collective-permute-start.25 = (bf16[256,512]{1,0:T(8,128)(2,1)S(1)}, bf16[256,512]{1,0:T(8,128)(2,1)S(1)}, u32[]{:S(2)}, u32[]{:S(2)}) collective-permute-start(bf16[256,512]{1,0:T(8,128)(2,1)S(1)} %get-tuple-element.193), channel_id=1, source_target_pairs={{0,1},{1,5},{2,3},{3,7},{4,0},{5,4},{6,2},{7,6},{8,9},{9,13},{10,1... | collective-permute-start | bytes 786440 | tf_op jit(solution)/shard_map/ppermute | solution.py:503
  79.8 2.2 %collective-permute-start.27 = (bf16[128,512]{1,0:T(8,128)(2,1)S(1)}, bf16[128,512]{1,0:T(8,128)(2,1)S(1)}, u32[]{:S(2)}, u32[]{:S(2)}) collective-permute-start(bf16[128,512]{1,0:T(8,128)(2,1)S(1)} %collective-permute-done.26.outer), channel_id=1, source_target_pairs={{0,1},{1,0},{2,3},{3,2},{4,5},{5,4},{6,7},{7,6},{8,9},{9,8},{10,11... | collective-permute-start | bytes 393224 | tf_op jit(solution)/shard_map/ppermute | solution.py:503
  (5 other events, 6.4 us)

commit v11 on v10

--- a/solution.py
+++ b/solution.py
@@ -252,20 +252,24 @@
     u_out[...] = mul(h[...], w_node[...])
 
 
-def forward_kernel(parity, take, lists, h, a_own, u_own, inner, outer, ghalo, gown_t, h_out, a_out, u_out, *to):
+def forward_kernel(parity, last, take, lists, h, a_own, u_own, inner, outer, ghalo, gown_t, *refs):
     packed, *gains = take
     w_send, _, _, w_fold = quarters(packed)
     gain = jnp.where(here_is(parity=parity), gains[0][...], gains[1][...])
     edges = ghalo.shape[0]
     block = inner.shape[0]
-    halo = (mul(ghalo[:, :block], inner[...]) + mul(ghalo[:, block:], outer[...])).astype(BF16)
+    halo = mul(ghalo[...], jnp.concatenate([inner[...], outer[...]], axis=0)).astype(BF16)
     a = a_own[...] + mul(halo, w_send[...])
-    a_out[...] = a
     q = (a * jax.nn.sigmoid(a)).astype(BF16)
     u = u_own[...] + mul(mul(gown_t[:, edges:], q).astype(BF16), w_fold[...])
+    t, inverse = normalize(u * jax.nn.sigmoid(u))
+    out = (h[...].astype(F32) + t * gain).astype(BF16)
+    if last:
+        keep(parity, a, u, t, inverse, out, *refs[-4:])
+        return
+    h_out, a_out, u_out, *to = refs
+    a_out[...] = a
     u_out[...] = u
-    t, _ = normalize(u * jax.nn.sigmoid(u))
-    out = (h[...].astype(F32) + t * gain).astype(BF16)
     h_out[...] = out
     for side, ref in zip((OUTER, INNER), reversed(to)):
         ref[...] = listed(lists[side : side + 1, :1], out, block)
@@ -275,19 +279,21 @@
     out[...] = listed(lists[INNER : INNER + 1, :1], h[...], out.shape[0])
 
 
-def save_kernel(plane, parity, a, u, h, *refs):
-    t_out, r_out, s_out, h_out = refs[-4:]
+def keep(parity, a, u, t, inverse, h, t_out, r_out, s_out, h_out):
     rows, edges = h.shape[0], a.shape[0]
     at = slice(parity * rows, (parity + 1) * rows)
-
+    s_out[parity * edges : (parity + 1) * edges, :] = slope(a).astype(BF16)
+    t_out[at, :] = t.astype(BF16)
+    r_out[at, :] = (inverse * slope(u)).astype(BF16)
+    h_out[at, :] = h
+
+
+def save_kernel(plane, parity, a, u, h, *refs):
     @pl.when(here_is(plane))
     def _():
-        s_out[parity * edges : (parity + 1) * edges, :] = slope(a[...]).astype(BF16)
         u_value = u[...]
         t, inverse = normalize(u_value * jax.nn.sigmoid(u_value))
-        t_out[at, :] = t.astype(BF16)
-        r_out[at, :] = (inverse * slope(u_value)).astype(BF16)
-        h_out[at, :] = h[...]
+        keep(parity, a[...], u_value, t, inverse, h[...], *refs[-4:])
 
 
 def backward_kernel(sides, finish, parity, kept, take, *refs):
@@ -446,7 +452,7 @@
     )(*operands)
 
 
-def run_section(body, plane, matrices, operands, outs, elsewhere=None, cost=1):
+def run_section(body, plane, matrices, operands, outs, elsewhere=None, aliases=None, cost=1):
     elsewhere = elsewhere or {}
 
     def kernel(*refs):
@@ -463,7 +469,8 @@
                 for source, target in elsewhere.items():
                     rest[target][...] = rest[source][...]
 
-    return run(kernel, tuple(matrices) + tuple(operands), outs, cost=cost)
+    aliases = {len(matrices) + source: target for source, target in (aliases or {}).items()}
+    return run(kernel, tuple(matrices) + tuple(operands), outs, aliases=aliases, cost=cost)
 
 
 def shards(
@@ -525,6 +532,7 @@
     wide = (rows, latent)
     edge_wide = (edges, latent)
     narrow = (block, latent)
+    both_wide = (2 * rows, latent)
     unit = 2 * rows * latent * latent
     dma = pltpu.SemaphoreType.DMA
 
@@ -585,14 +593,21 @@
             first_home = go_home(*run(order_kernel, (outputs,), [(wide, BF16)] * 2), plane=0)
         step = (tick + 1) // 2 - plane if tick < sections - 1 else None
         to_send = [(narrow, BF16)] * {0: 2, 1: 1, None: 0}[step]
-        hidden, a, u, *to = run_section(
-            functools.partial(forward_kernel, parity),
+        last = tick == sections - 1
+        state = [(both_wide, BF16), (both_wide, BF16), ((2 * edges, latent), BF16), (both_wide, BF16)]
+        made = run_section(
+            functools.partial(forward_kernel, parity, last),
             plane,
             (packed, *both_gains),
-            (lists, hidden, a_own, u_own, inner, outer, ghalo, gown_t),
-            [(wide, BF16), (edge_wide, F32), (wide, F32)] + to_send,
-            cost=1 if to_send else BESIDE // 2,
+            (lists, hidden, a_own, u_own, inner, outer, ghalo, gown_t) + (tuple(saved) if last else ()),
+            state if last else [(wide, BF16), (edge_wide, F32), (wide, F32)] + to_send,
+            aliases={8 + k: k for k in range(4)} if last else None,
+            cost=BESIDE // 2 if last else 1,
         )
+        if last:
+            saved = made
+            break
+        hidden, a, u, *to = made
         produced = hidden
         if to:
             outer = towards(to[-1], OUTER, step)
@@ -606,7 +621,7 @@
         saved = run(
             functools.partial(save_kernel, plane, parity),
             (a, u, produced) + tuple(saved),
-            [((2 * rows, latent), BF16), ((2 * rows, latent), BF16), ((2 * edges, latent), BF16), ((2 * rows, latent), BF16)],
+            state,
             aliases={3 + k: k for k in range(4)} if saved else None,
             cost=BESIDE,
         )

time: 88.4 us -> 87.8 us (level)
  starting transfers between devices: 34.1 us -> 32.6 us
  waiting for transfers between devices: 39.2 us -> 40.3 us
    ppermute x28, starting transfers between devices: 34.1 us -> 32.6 us  [send(): return lax.ppermute(value, AXES, table)]
    ppermute x28, waiting for transfers between devices: 39.2 us -> 40.3 us  [send(): return lax.ppermute(value, AXES, table)]
    pallas_call x34 -> x33, Pallas kernels: 13.7 us -> 13.6 us  [run(): pl.pallas_call(kernel, out_shape=[jax.ShapeDtypeStruct(s, t) for s, t in...]
  transfers between devices with their start and end apart: 28 -> 28, of which waited for: 16 -> 17; matrix products, arithmetic and copies ran while one was open for 0% -> 0% of each run, Pallas kernels for 9% -> 9%
where the time goes in v11:
time: 87.8 us; the launch traced here: 87.5 us
  waiting for transfers between devices  40.3 us (46%)
  starting transfers between devices  32.6 us (37%)
  Pallas kernels  13.6 us (15%)
  between operations  1.12 us (1%)
    ppermute x28, waiting for transfers between devices, send(): return lax.ppermute(value, AXES, table)  40.3 us
    ppermute x28, starting transfers between devices, send(): return lax.ppermute(value, AXES, table)  32.6 us
    pallas_call x33, Pallas kernels, run(): pl.pallas_call(kernel, out_shape=[jax.ShapeDtypeStruct(s, t) for s, t in...  13.6 us
  transfers between devices with their start and end apart: 28, of which 17 were waited for; matrix products, arithmetic and copies ran while one was open for 0% of the time, Pallas kernels for 9%

profile of v11, /device:TPU:0, one launch (start us, length us, event | category | flops | bytes accessed | tf_op | source)
XLA Modules:
  0.0 87.5 jit_solution(12372000206136703772)
XLA Ops:
  0.6 1.2 %shard_map.132 = (bf16[256,512]{1,0:T(8,128)(2,1)S(1)}, bf16[272,512]{1,0:T(8,128)(2,1)S(1)}, bf16[128,512]{1,0:T(8,128)(2,1)S(1)}, bf16[16,128]{1,0:T(8,128)(2,1)S(1)}) custom-call(s32[2]{0:T(128)} %count_in.1, s32[1,1,2]{2,1,0:T(1,128)} %bitcast.11, bf16[2,256,512]{2,1,0:T(8,128)(2,1)} %inputs.1, bf16[2,256,512]{2,1,0:T(8,128)(2,1)} %cotangent.1, ...), custom_call_target="tpu_custom_call" | custom-call | flops 1 | bytes 1 | tf_op jit(solution)/shard_map/pallas_call | solution.py:443
  1.9 3.0 %collective-permute-start.1 = (bf16[272,512]{1,0:T(8,128)(2,1)S(1)}, bf16[272,512]{1,0:T(8,128)(2,1)S(1)}, u32[]{:S(2)}, u32[]{:S(2)}) collective-permute-start(bf16[272,512]{1,0:T(8,128)(2,1)S(1)} %get-tuple-element.99), channel_id=1, source_target_pairs={{0,4},{1,0},{2,6},{3,2},{4,5},{5,1},{6,7},{7,3},{8,12},{9,8},{10,1... | collective-permute-start | bytes 835592 | tf_op jit(solution)/shard_map/ppermute | solution.py:510
  4.8 2.2 %collective-permute-start.2 = (bf16[128,512]{1,0:T(8,128)(2,1)S(1)}, bf16[128,512]{1,0:T(8,128)(2,1)S(1)}, u32[]{:S(2)}, u32[]{:S(2)}) collective-permute-start(bf16[128,512]{1,0:T(8,128)(2,1)S(1)} %get-tuple-element.100), channel_id=1, source_target_pairs={{0,25},{1,29},{2,27},{3,31},{4,8},{5,12},{6,10},{7,14},{8,1},{9,5}... | collective-permute-start | bytes 393224 | tf_op jit(solution)/shard_map/ppermute | solution.py:510
  7.7 1.7 %shard_map.131.mine = bf16[2048,512]{1,0:T(8,128)(2,1)S(1)} custom-call(bf16[512,512]{1,0:T(8,128)(2,1)} %bitcast.6, bf16[512,512]{1,0:T(8,128)(2,1)} %bitcast.7, bf16[512,512]{1,0:T(8,128)(2,1)} %bitcast.8, bf16[512,512]{1,0:T(8,128)(2,1)} %bitcast.9, bf16[512,512]{1,0:T(8,128)(2,1)} %bitcast.10), custom_call_target="tpu_custom_call" | custom-call | flops 1 | bytes 1 | tf_op jit(solution)/shard_map/pallas_call | solution.py:443
  10.4 2.1 %collective-permute-done.2._.refs_8_ = bf16[128,512]{1,0:T(8,128)(2,1)S(1)} collective-permute-done((bf16[128,512]{1,0:T(8,128)(2,1)S(1)}, bf16[128,512]{1,0:T(8,128)(2,1)S(1)}, u32[]{:S(2)}, u32[]{:S(2)}) %collective-permute-start.2) | collective-permute-done | bytes 131104 | tf_op jit(solution)/shard_map/ppermute | solution.py:510
  15.9 1.5 %collective-permute-start.6 = (bf16[128,512]{1,0:T(8,128)(2,1)S(1)}, bf16[128,512]{1,0:T(8,128)(2,1)S(1)}, u32[]{:S(2)}, u32[]{:S(2)}) collective-permute-start(bf16[128,512]{1,0:T(8,128)(2,1)S(1)} %get-tuple-element.118), channel_id=1, source_target_pairs={{0,25},{1,8},{2,27},{3,10},{4,29},{5,12},{6,31},{7,14},{8,1},{9,16... | collective-permute-start | bytes 393224 | tf_op jit(solution)/shard_map/ppermute | solution.py:510
  18.7 3.5 %collective-permute-done.6.refs_8_ = bf16[128,512]{1,0:T(8,128)(2,1)S(1)} collective-permute-done((bf16[128,512]{1,0:T(8,128)(2,1)S(1)}, bf16[128,512]{1,0:T(8,128)(2,1)S(1)}, u32[]{:S(2)}, u32[]{:S(2)}) %collective-permute-start.6) | collective-permute-done | bytes 131104 | tf_op jit(solution)/shard_map/ppermute | solution.py:510
  23.4 2.8 %collective-permute-start.7 = (bf16[256,512]{1,0:T(8,128)(2,1)S(1)}, bf16[256,512]{1,0:T(8,128)(2,1)S(1)}, u32[]{:S(2)}, u32[]{:S(2)}) collective-permute-start(bf16[256,512]{1,0:T(8,128)(2,1)S(1)} %get-tuple-element.119.h), channel_id=1, source_target_pairs={{0,2},{1,3},{2,0},{3,1},{4,6},{5,7},{6,4},{7,5},{8,10},{9,11},{10,... | collective-permute-start | bytes 786440 | tf_op jit(solution)/shard_map/ppermute | solution.py:510
  26.7 7.8 %collective-permute-done.7.refs_1_.h.refs_4_ = bf16[256,512]{1,0:T(8,128)(2,1)S(1)} collective-permute-done((bf16[256,512]{1,0:T(8,128)(2,1)S(1)}, bf16[256,512]{1,0:T(8,128)(2,1)S(1)}, u32[]{:S(2)}, u32[]{:S(2)}) %collective-permute-start.7) | collective-permute-done | bytes 262176 | tf_op jit(solution)/shard_map/ppermute | solution.py:510
  34.7 1.3 %collective-permute-done.8.refs_7_ = bf16[128,512]{1,0:T(8,128)(2,1)S(1)} collective-permute-done((bf16[128,512]{1,0:T(8,128)(2,1)S(1)}, bf16[128,512]{1,0:T(8,128)(2,1)S(1)}, u32[]{:S(2)}, u32[]{:S(2)}) %collective-permute-start.8) | collective-permute-done | bytes 131104 | tf_op jit(solution)/shard_map/ppermute | solution.py:510
  38.1 4.2 %collective-permute-start.12 = (bf16[256,512]{1,0:T(8,128)(2,1)S(1)}, bf16[256,512]{1,0:T(8,128)(2,1)S(1)}, u32[]{:S(2)}, u32[]{:S(2)}) collective-permute-start(bf16[256,512]{1,0:T(8,128)(2,1)S(1)} %get-tuple-element.143), channel_id=1, source_target_pairs={{0,1},{1,5},{4,0},{5,4},{8,9},{9,13},{12,8},{13,12},{16,17},{17,21... | collective-permute-start | bytes 786440 | tf_op jit(solution)/shard_map/ppermute | solution.py:510
  42.5 1.8 %collective-permute-start.15 = (bf16[128,512]{1,0:T(8,128)(2,1)S(1)}, bf16[128,512]{1,0:T(8,128)(2,1)S(1)}, u32[]{:S(2)}, u32[]{:S(2)}) collective-permute-start(bf16[128,512]{1,0:T(8,128)(2,1)S(1)} %get-tuple-element.160), channel_id=1, source_target_pairs={{0,25},{1,8},{2,27},{3,10},{4,29},{5,12},{6,31},{7,14},{8,1},{9,16... | collective-permute-start | bytes 393224 | tf_op jit(solution)/shard_map/ppermute | solution.py:510
  44.2 4.0 %collective-permute-done.12.refs_3_.refs_1_ = bf16[256,512]{1,0:T(8,128)(2,1)S(1)} collective-permute-done((bf16[256,512]{1,0:T(8,128)(2,1)S(1)}, bf16[256,512]{1,0:T(8,128)(2,1)S(1)}, u32[]{:S(2)}, u32[]{:S(2)}) %collective-permute-start.12) | collective-permute-done | bytes 262176 | tf_op jit(solution)/shard_map/ppermute | solution.py:510
  48.2 1.4 %collective-permute-done.15.refs_6_ = bf16[128,512]{1,0:T(8,128)(2,1)S(1)} collective-permute-done((bf16[128,512]{1,0:T(8,128)(2,1)S(1)}, bf16[128,512]{1,0:T(8,128)(2,1)S(1)}, u32[]{:S(2)}, u32[]{:S(2)}) %collective-permute-start.15) | collective-permute-done | bytes 131104 | tf_op jit(solution)/shard_map/ppermute | solution.py:510
  49.7 1.3 %collective-permute-start.18 = (bf16[128,512]{1,0:T(8,128)(2,1)S(1)}, bf16[128,512]{1,0:T(8,128)(2,1)S(1)}, u32[]{:S(2)}, u32[]{:S(2)}) collective-permute-start(bf16[128,512]{1,0:T(8,128)(2,1)S(1)} %get-tuple-element.161.refs_3_), channel_id=1, source_target_pairs={{2,25},{3,8},{6,29},{7,12},{10,1},{11,16},{14,5},{15,20},{18,9},{1... | collective-permute-start | bytes 393224 | tf_op jit(solution)/shard_map/ppermute | solution.py:510
  51.2 4.9 %collective-permute-start.17 = (bf16[256,512]{1,0:T(8,128)(2,1)S(1)}, bf16[256,512]{1,0:T(8,128)(2,1)S(1)}, u32[]{:S(2)}, u32[]{:S(2)}) collective-permute-start(bf16[256,512]{1,0:T(8,128)(2,1)S(1)} %shard_map.153.value), channel_id=1, source_target_pairs={{0,2},{1,3},{2,0},{3,1},{4,6},{5,7},{6,4},{7,5},{8,10},{9,11},{10,... | collective-permute-start | bytes 786440 | tf_op jit(solution)/shard_map/ppermute | solution.py:510
  56.1 3.6 %collective-permute-done.18.outer = bf16[128,512]{1,0:T(8,128)(2,1)S(1)} collective-permute-done((bf16[128,512]{1,0:T(8,128)(2,1)S(1)}, bf16[128,512]{1,0:T(8,128)(2,1)S(1)}, u32[]{:S(2)}, u32[]{:S(2)}) %collective-permute-start.18) | collective-permute-done | bytes 131104 | tf_op jit(solution)/shard_map/ppermute | solution.py:510
  59.8 4.8 %collective-permute-done.17.refs_5_ = bf16[256,512]{1,0:T(8,128)(2,1)S(1)} collective-permute-done((bf16[256,512]{1,0:T(8,128)(2,1)S(1)}, bf16[256,512]{1,0:T(8,128)(2,1)S(1)}, u32[]{:S(2)}, u32[]{:S(2)}) %collective-permute-start.17) | collective-permute-done | bytes 262176 | tf_op jit(solution)/shard_map/ppermute | solution.py:510
  65.8 1.2 %collective-permute-start.22 = (bf16[128,512]{1,0:T(8,128)(2,1)S(1)}, bf16[128,512]{1,0:T(8,128)(2,1)S(1)}, u32[]{:S(2)}, u32[]{:S(2)}) collective-permute-start(bf16[128,512]{1,0:T(8,128)(2,1)S(1)} %get-tuple-element.175), channel_id=1, source_target_pairs={{0,25},{1,8},{2,27},{3,10},{4,29},{5,12},{6,31},{7,14},{8,1},{9,16... | collective-permute-start | bytes 393224 | tf_op jit(solution)/shard_map/ppermute | solution.py:510
  69.1 3.0 %collective-permute-done.22.outer.refs_6_ = bf16[128,512]{1,0:T(8,128)(2,1)S(1)} collective-permute-done((bf16[128,512]{1,0:T(8,128)(2,1)S(1)}, bf16[128,512]{1,0:T(8,128)(2,1)S(1)}, u32[]{:S(2)}, u32[]{:S(2)}) %collective-permute-start.22) | collective-permute-done | bytes 131104 | tf_op jit(solution)/shard_map/ppermute | solution.py:510
  72.1 1.2 %shard_map.159 = (f32[256,512]{1,0:T(8,128)S(1)}, bf16[256,512]{1,0:T(8,128)(2,1)S(1)}, bf16[256,512]{1,0:T(8,128)(2,1)S(1)}, bf16[256,512]{1,0:T(8,128)(2,1)S(1...) custom-call(bf16[2048,512]{1,0:T(8,128)(2,1)S(1)} %get-tuple-element.106.refs_0_, ...), custom_call_target="tpu_custom_call" | custom-call | flops 2000000000 | bytes 1 | tf_op jit(solution)/shard_map/pallas_call | solution.py:443
  73.3 2.8 %collective-permute-start.26 = (bf16[128,512]{1,0:T(8,128)(2,1)S(1)}, bf16[128,512]{1,0:T(8,128)(2,1)S(1)}, u32[]{:S(2)}, u32[]{:S(2)}) collective-permute-start(bf16[128,512]{1,0:T(8,128)(2,1)S(1)} %get-tuple-element.189), channel_id=1, source_target_pairs={{0,28},{1,8},{2,30},{3,10},{4,29},{5,9},{6,31},{7,11},{8,4},{9,16}... | collective-permute-start | bytes 393224 | tf_op jit(solution)/shard_map/ppermute | solution.py:510
  77.6 1.6 %collective-permute-start.25 = (bf16[256,512]{1,0:T(8,128)(2,1)S(1)}, bf16[256,512]{1,0:T(8,128)(2,1)S(1)}, u32[]{:S(2)}, u32[]{:S(2)}) collective-permute-start(bf16[256,512]{1,0:T(8,128)(2,1)S(1)} %get-tuple-element.187), channel_id=1, source_target_pairs={{0,1},{1,5},{2,3},{3,7},{4,0},{5,4},{6,2},{7,6},{8,9},{9,13},{10,1... | collective-permute-start | bytes 786440 | tf_op jit(solution)/shard_map/ppermute | solution.py:510
  81.6 4.6 %collective-permute-done.25.refs_1_ = bf16[256,512]{1,0:T(8,128)(2,1)S(1)} collective-permute-done((bf16[256,512]{1,0:T(8,128)(2,1)S(1)}, bf16[256,512]{1,0:T(8,128)(2,1)S(1)}, u32[]{:S(2)}, u32[]{:S(2)}) %collective-permute-start.25) | collective-permute-done | bytes 262176 | tf_op jit(solution)/shard_map/ppermute | solution.py:510
  (67 shorter events, 18.9 us)
Async XLA Ops:
  1.9 8.3 %collective-permute-start.1 = (bf16[272,512]{1,0:T(8,128)(2,1)S(1)}, bf16[272,512]{1,0:T(8,128)(2,1)S(1)}, u32[]{:S(2)}, u32[]{:S(2)}) collective-permute-start(bf16[272,512]{1,0:T(8,128)(2,1)S(1)} %get-tuple-element.99), channel_id=1, source_target_pairs={{0,4},{1,0},{2,6},{3,2},{4,5},{5,1},{6,7},{7,3},{8,12},{9,8},{10,1... | collective-permute-start | bytes 835592 | tf_op jit(solution)/shard_map/ppermute | solution.py:510
  4.8 7.7 %collective-permute-start.2 = (bf16[128,512]{1,0:T(8,128)(2,1)S(1)}, bf16[128,512]{1,0:T(8,128)(2,1)S(1)}, u32[]{:S(2)}, u32[]{:S(2)}) collective-permute-start(bf16[128,512]{1,0:T(8,128)(2,1)S(1)} %get-tuple-element.100), channel_id=1, source_target_pairs={{0,25},{1,29},{2,27},{3,31},{4,8},{5,12},{6,10},{7,14},{8,1},{9,5}... | collective-permute-start | bytes 393224 | tf_op jit(solution)/shard_map/ppermute | solution.py:510
  7.0 7.5 %collective-permute-start.3 = (f32[1,512]{1,0:T(1,128)}, f32[1,512]{1,0:T(1,128)S(1)}, u32[]{:S(2)}, u32[]{:S(2)}) collective-permute-start(f32[1,512]{1,0:T(1,128)} %refs_1_.15), channel_id=1, source_target_pairs={{0,1},{1,0},{2,3},{3,2},{4,5},{5,4},{6,7},{7,6},{8,9},{9,8},{10,11... | collective-permute-start | bytes 6152 | tf_op jit(solution)/shard_map/ppermute | solution.py:510
  9.4 4.2 %collective-permute-start = (bf16[2048,512]{1,0:T(8,128)(2,1)S(1)}, bf16[2048,512]{1,0:T(8,128)(2,1)S(1)}, u32[]{:S(2)}, u32[]{:S(2)}) collective-permute-start(bf16[2048,512]{1,0:T(8,128)(2,1)S(1)} %shard_map.131.mine), channel_id=1, source_target_pairs={{0,1},{1,0},{2,3},{3,2},{4,5},{5,4},{6,7},{7,6},{8,9},{9,8},{10,11... | collective-permute-start | bytes 6291464 | tf_op jit(solution)/shard_map/ppermute | solution.py:510
  12.6 2.0 %collective-permute-start.4 = (bf16[128,512]{1,0:T(8,128)(2,1)S(1)}, bf16[128,512]{1,0:T(8,128)(2,1)S(1)}, u32[]{:S(2)}, u32[]{:S(2)}) collective-permute-start(bf16[128,512]{1,0:T(8,128)(2,1)S(1)} %get-tuple-element.111), channel_id=1, source_target_pairs={{0,1},{1,0},{2,3},{3,2},{4,5},{5,4},{6,7},{7,6},{8,9},{9,8},{10,11... | collective-permute-start | bytes 393224 | tf_op jit(solution)/shard_map/ppermute | solution.py:510
  15.7 2.2 %collective-permute-start.5 = (bf16[128,512]{1,0:T(8,128)(2,1)S(1)}, bf16[128,512]{1,0:T(8,128)(2,1)S(1)}, u32[]{:S(2)}, u32[]{:S(2)}) collective-permute-start(bf16[128,512]{1,0:T(8,128)(2,1)S(1)} %get-tuple-element.115), channel_id=1, source_target_pairs={{0,1},{1,0},{2,3},{3,2},{4,5},{5,4},{6,7},{7,6},{8,9},{9,8},{10,11... | collective-permute-start | bytes 393224 | tf_op jit(solution)/shard_map/ppermute | solution.py:510
  15.9 6.3 %collective-permute-start.6 = (bf16[128,512]{1,0:T(8,128)(2,1)S(1)}, bf16[128,512]{1,0:T(8,128)(2,1)S(1)}, u32[]{:S(2)}, u32[]{:S(2)}) collective-permute-start(bf16[128,512]{1,0:T(8,128)(2,1)S(1)} %get-tuple-element.118), channel_id=1, source_target_pairs={{0,25},{1,8},{2,27},{3,10},{4,29},{5,12},{6,31},{7,14},{8,1},{9,16... | collective-permute-start | bytes 393224 | tf_op jit(solution)/shard_map/ppermute | solution.py:510
  23.3 11.3 %collective-permute-start.9 = (bf16[128,512]{1,0:T(8,128)(2,1)S(1)}, bf16[128,512]{1,0:T(8,128)(2,1)S(1)}, u32[]{:S(2)}, u32[]{:S(2)}) collective-permute-start(bf16[128,512]{1,0:T(8,128)(2,1)S(1)} %get-tuple-element.122), channel_id=1, source_target_pairs={{0,27},{1,10},{2,25},{3,8},{4,31},{5,14},{6,29},{7,12},{8,3},{9,18... | collective-permute-start | bytes 393224 | tf_op jit(solution)/shard_map/ppermute | solution.py:510
  23.4 11.1 %collective-permute-start.7 = (bf16[256,512]{1,0:T(8,128)(2,1)S(1)}, bf16[256,512]{1,0:T(8,128)(2,1)S(1)}, u32[]{:S(2)}, u32[]{:S(2)}) collective-permute-start(bf16[256,512]{1,0:T(8,128)(2,1)S(1)} %get-tuple-element.119.h), channel_id=1, source_target_pairs={{0,2},{1,3},{2,0},{3,1},{4,6},{5,7},{6,4},{7,5},{8,10},{9,11},{10,... | collective-permute-start | bytes 786440 | tf_op jit(solution)/shard_map/ppermute | solution.py:510
  36.1 6.3 %collective-permute-start.13 = (bf16[128,512]{1,0:T(8,128)(2,1)S(1)}, bf16[128,512]{1,0:T(8,128)(2,1)S(1)}, u32[]{:S(2)}, u32[]{:S(2)}) collective-permute-start(bf16[128,512]{1,0:T(8,128)(2,1)S(1)} %get-tuple-element.146), channel_id=1, source_target_pairs={{0,25},{1,8},{2,27},{3,10},{4,29},{5,12},{6,31},{7,14},{8,1},{9,16... | collective-permute-start | bytes 393224 | tf_op jit(solution)/shard_map/ppermute | solution.py:510
  37.4 6.8 %collective-permute-start.11 = (bf16[256,512]{1,0:T(8,128)(2,1)S(1)}, bf16[256,512]{1,0:T(8,128)(2,1)S(1)}, u32[]{:S(2)}, u32[]{:S(2)}) collective-permute-start(bf16[256,512]{1,0:T(8,128)(2,1)S(1)} %get-tuple-element.142), channel_id=1, source_target_pairs={{0,0},{1,4},{4,1},{5,5},{8,8},{9,12},{12,9},{13,13},{16,16},{17,20... | collective-permute-start | bytes 786440 | tf_op jit(solution)/shard_map/ppermute | solution.py:510
  38.1 10.1 %collective-permute-start.12 = (bf16[256,512]{1,0:T(8,128)(2,1)S(1)}, bf16[256,512]{1,0:T(8,128)(2,1)S(1)}, u32[]{:S(2)}, u32[]{:S(2)}) collective-permute-start(bf16[256,512]{1,0:T(8,128)(2,1)S(1)} %get-tuple-element.143), channel_id=1, source_target_pairs={{0,1},{1,5},{4,0},{5,4},{8,9},{9,13},{12,8},{13,12},{16,17},{17,21... | collective-permute-start | bytes 786440 | tf_op jit(solution)/shard_map/ppermute | solution.py:510
  42.4 1.8 %collective-permute-start.14 = (bf16[128,512]{1,0:T(8,128)(2,1)S(1)}, bf16[128,512]{1,0:T(8,128)(2,1)S(1)}, u32[]{:S(2)}, u32[]{:S(2)}) collective-permute-start(bf16[128,512]{1,0:T(8,128)(2,1)S(1)} %get-tuple-element.155), channel_id=1, source_target_pairs={{0,1},{1,0},{2,3},{3,2},{4,5},{5,4},{6,7},{7,6},{8,9},{9,8},{10,11... | collective-permute-start | bytes 393224 | tf_op jit(solution)/shard_map/ppermute | solution.py:510
  42.5 7.2 %collective-permute-start.15 = (bf16[128,512]{1,0:T(8,128)(2,1)S(1)}, bf16[128,512]{1,0:T(8,128)(2,1)S(1)}, u32[]{:S(2)}, u32[]{:S(2)}) collective-permute-start(bf16[128,512]{1,0:T(8,128)(2,1)S(1)} %get-tuple-element.160), channel_id=1, source_target_pairs={{0,25},{1,8},{2,27},{3,10},{4,29},{5,12},{6,31},{7,14},{8,1},{9,16... | collective-permute-start | bytes 393224 | tf_op jit(solution)/shard_map/ppermute | solution.py:510
  49.7 10.0 %collective-permute-start.18 = (bf16[128,512]{1,0:T(8,128)(2,1)S(1)}, bf16[128,512]{1,0:T(8,128)(2,1)S(1)}, u32[]{:S(2)}, u32[]{:S(2)}) collective-permute-start(bf16[128,512]{1,0:T(8,128)(2,1)S(1)} %get-tuple-element.161.refs_3_), channel_id=1, source_target_pairs={{2,25},{3,8},{6,29},{7,12},{10,1},{11,16},{14,5},{15,20},{18,9},{1... | collective-permute-start | bytes 393224 | tf_op jit(solution)/shard_map/ppermute | solution.py:510
  51.2 13.4 %collective-permute-start.17 = (bf16[256,512]{1,0:T(8,128)(2,1)S(1)}, bf16[256,512]{1,0:T(8,128)(2,1)S(1)}, u32[]{:S(2)}, u32[]{:S(2)}) collective-permute-start(bf16[256,512]{1,0:T(8,128)(2,1)S(1)} %shard_map.153.value), channel_id=1, source_target_pairs={{0,2},{1,3},{2,0},{3,1},{4,6},{5,7},{6,4},{7,5},{8,10},{9,11},{10,... | collective-permute-start | bytes 786440 | tf_op jit(solution)/shard_map/ppermute | solution.py:510
  65.8 6.3 %collective-permute-start.22 = (bf16[128,512]{1,0:T(8,128)(2,1)S(1)}, bf16[128,512]{1,0:T(8,128)(2,1)S(1)}, u32[]{:S(2)}, u32[]{:S(2)}) collective-permute-start(bf16[128,512]{1,0:T(8,128)(2,1)S(1)} %get-tuple-element.175), channel_id=1, source_target_pairs={{0,25},{1,8},{2,27},{3,10},{4,29},{5,12},{6,31},{7,14},{8,1},{9,16... | collective-permute-start | bytes 393224 | tf_op jit(solution)/shard_map/ppermute | solution.py:510
  67.7 8.5 %collective-permute-start.20 = (bf16[256,512]{1,0:T(8,128)(2,1)S(1)}, bf16[256,512]{1,0:T(8,128)(2,1)S(1)}, u32[]{:S(2)}, u32[]{:S(2)}) collective-permute-start(bf16[256,512]{1,0:T(8,128)(2,1)S(1)} %get-tuple-element.173), channel_id=1, source_target_pairs={{2,2},{3,6},{6,3},{7,7},{10,10},{11,14},{14,11},{15,15},{18,18},{1... | collective-permute-start | bytes 786440 | tf_op jit(solution)/shard_map/ppermute | solution.py:510
  68.4 7.8 %collective-permute-start.21 = (bf16[256,512]{1,0:T(8,128)(2,1)S(1)}, bf16[256,512]{1,0:T(8,128)(2,1)S(1)}, u32[]{:S(2)}, u32[]{:S(2)}) collective-permute-start(bf16[256,512]{1,0:T(8,128)(2,1)S(1)} %get-tuple-element.174), channel_id=1, source_target_pairs={{2,3},{3,7},{6,2},{7,6},{10,11},{11,15},{14,10},{15,14},{18,19},{1... | collective-permute-start | bytes 786440 | tf_op jit(solution)/shard_map/ppermute | solution.py:510
  73.3 2.9 %collective-permute-start.23 = (bf16[128,512]{1,0:T(8,128)(2,1)S(1)}, bf16[128,512]{1,0:T(8,128)(2,1)S(1)}, u32[]{:S(2)}, u32[]{:S(2)}) collective-permute-start(bf16[128,512]{1,0:T(8,128)(2,1)S(1)} %get-tuple-element.181), channel_id=1, source_target_pairs={{0,1},{1,0},{2,3},{3,2},{4,5},{5,4},{6,7},{7,6},{8,9},{9,8},{10,11... | collective-permute-start | bytes 393224 | tf_op jit(solution)/shard_map/ppermute | solution.py:510
  73.3 6.4 %collective-permute-start.26 = (bf16[128,512]{1,0:T(8,128)(2,1)S(1)}, bf16[128,512]{1,0:T(8,128)(2,1)S(1)}, u32[]{:S(2)}, u32[]{:S(2)}) collective-permute-start(bf16[128,512]{1,0:T(8,128)(2,1)S(1)} %get-tuple-element.189), channel_id=1, source_target_pairs={{0,28},{1,8},{2,30},{3,10},{4,29},{5,9},{6,31},{7,11},{8,4},{9,16}... | collective-permute-start | bytes 393224 | tf_op jit(solution)/shard_map/ppermute | solution.py:510
  76.9 4.7 %collective-permute-start.24 = (bf16[256,512]{1,0:T(8,128)(2,1)S(1)}, bf16[256,512]{1,0:T(8,128)(2,1)S(1)}, u32[]{:S(2)}, u32[]{:S(2)}) collective-permute-start(bf16[256,512]{1,0:T(8,128)(2,1)S(1)} %get-tuple-element.186), channel_id=1, source_target_pairs={{0,0},{1,4},{2,2},{3,6},{4,1},{5,5},{6,3},{7,7},{8,8},{9,12},{10,1... | collective-permute-start | bytes 786440 | tf_op jit(solution)/shard_map/ppermute | solution.py:510
  77.6 8.7 %collective-permute-start.25 = (bf16[256,512]{1,0:T(8,128)(2,1)S(1)}, bf16[256,512]{1,0:T(8,128)(2,1)S(1)}, u32[]{:S(2)}, u32[]{:S(2)}) collective-permute-start(bf16[256,512]{1,0:T(8,128)(2,1)S(1)} %get-tuple-element.187), channel_id=1, source_target_pairs={{0,1},{1,5},{2,3},{3,7},{4,0},{5,4},{6,2},{7,6},{8,9},{9,13},{10,1... | collective-permute-start | bytes 786440 | tf_op jit(solution)/shard_map/ppermute | solution.py:510
  79.7 1.8 %collective-permute-start.27 = (bf16[128,512]{1,0:T(8,128)(2,1)S(1)}, bf16[128,512]{1,0:T(8,128)(2,1)S(1)}, u32[]{:S(2)}, u32[]{:S(2)}) collective-permute-start(bf16[128,512]{1,0:T(8,128)(2,1)S(1)} %collective-permute-done.26.outer), channel_id=1, source_target_pairs={{0,1},{1,0},{2,3},{3,2},{4,5},{5,4},{6,7},{7,6},{8,9},{9,8},{10,11... | collective-permute-start | bytes 393224 | tf_op jit(solution)/shard_map/ppermute | solution.py:510
  (5 other events, 6.4 us)

commit v12 on v11

--- a/solution.py
+++ b/solution.py
@@ -609,9 +609,8 @@
             break
         hidden, a, u, *to = made
         produced = hidden
-        if to:
+        if step == 0:
             outer = towards(to[-1], OUTER, step)
-        if step == 0:
             inner = towards(to[0], INNER, step)
             arrived = (inner,)
         elif step:
@@ -623,8 +622,11 @@
             (a, u, produced) + tuple(saved),
             state,
             aliases={3 + k: k for k in range(4)} if saved else None,
-            cost=BESIDE,
+            cost=1 if step else BESIDE,
         )
+        if step:
+            to_outer, *saved = lax.optimization_barrier((to[-1], *saved))
+            outer = towards(to_outer, OUTER, step)
 
     *states, both = saved
     halos = {}

time: 87.8 us -> 87.6 us (level)
  starting transfers between devices: 32.6 us -> 30.1 us
  waiting for transfers between devices: 40.3 us -> 42.5 us
    ppermute x28, starting transfers between devices: 32.6 us -> 30.1 us  [send(): return lax.ppermute(value, AXES, table)]
    ppermute x28, waiting for transfers between devices: 40.3 us -> 42.5 us  [send(): return lax.ppermute(value, AXES, table)]
where the time goes in v12:
time: 87.6 us; the launch traced here: 87.3 us
  waiting for transfers between devices  42.5 us (49%)
  starting transfers between devices  30.1 us (34%)
  Pallas kernels  13.6 us (16%)
  between operations  1.12 us (1%)
    ppermute x28, waiting for transfers between devices, send(): return lax.ppermute(value, AXES, table)  42.5 us
    ppermute x28, starting transfers between devices, send(): return lax.ppermute(value, AXES, table)  30.1 us
    pallas_call x33, Pallas kernels, run(): pl.pallas_call(kernel, out_shape=[jax.ShapeDtypeStruct(s, t) for s, t in...  13.6 us
  transfers between devices with their start and end apart: 28, of which 17 were waited for; matrix products, arithmetic and copies ran while one was open for 0% of the time, Pallas kernels for 9%

profile of v12, /device:TPU:0, one launch (start us, length us, event | category | flops | bytes accessed | tf_op | source)
XLA Modules:
  0.0 87.3 jit_solution(11778517930630566375)
XLA Ops:
  0.6 1.2 %shard_map.132 = (bf16[256,512]{1,0:T(8,128)(2,1)S(1)}, bf16[272,512]{1,0:T(8,128)(2,1)S(1)}, bf16[128,512]{1,0:T(8,128)(2,1)S(1)}, bf16[16,128]{1,0:T(8,128)(2,1)S(1)}) custom-call(s32[2]{0:T(128)} %count_in.1, s32[1,1,2]{2,1,0:T(1,128)} %bitcast.11, bf16[2,256,512]{2,1,0:T(8,128)(2,1)} %inputs.1, bf16[2,256,512]{2,1,0:T(8,128)(2,1)} %cotangent.1, ...), custom_call_target="tpu_custom_call" | custom-call | flops 1 | bytes 1 | tf_op jit(solution)/shard_map/pallas_call | solution.py:443
  1.9 3.0 %collective-permute-start.1 = (bf16[272,512]{1,0:T(8,128)(2,1)S(1)}, bf16[272,512]{1,0:T(8,128)(2,1)S(1)}, u32[]{:S(2)}, u32[]{:S(2)}) collective-permute-start(bf16[272,512]{1,0:T(8,128)(2,1)S(1)} %get-tuple-element.104), channel_id=1, source_target_pairs={{0,4},{1,0},{2,6},{3,2},{4,5},{5,1},{6,7},{7,3},{8,12},{9,8},{10,1... | collective-permute-start | bytes 835592 | tf_op jit(solution)/shard_map/ppermute | solution.py:510
  4.8 2.2 %collective-permute-start.2 = (bf16[128,512]{1,0:T(8,128)(2,1)S(1)}, bf16[128,512]{1,0:T(8,128)(2,1)S(1)}, u32[]{:S(2)}, u32[]{:S(2)}) collective-permute-start(bf16[128,512]{1,0:T(8,128)(2,1)S(1)} %get-tuple-element.105), channel_id=1, source_target_pairs={{0,25},{1,29},{2,27},{3,31},{4,8},{5,12},{6,10},{7,14},{8,1},{9,5}... | collective-permute-start | bytes 393224 | tf_op jit(solution)/shard_map/ppermute | solution.py:510
  7.7 1.7 %shard_map.131.mine = bf16[2048,512]{1,0:T(8,128)(2,1)S(1)} custom-call(bf16[512,512]{1,0:T(8,128)(2,1)} %bitcast.6, bf16[512,512]{1,0:T(8,128)(2,1)} %bitcast.7, bf16[512,512]{1,0:T(8,128)(2,1)} %bitcast.8, bf16[512,512]{1,0:T(8,128)(2,1)} %bitcast.9, bf16[512,512]{1,0:T(8,128)(2,1)} %bitcast.10), custom_call_target="tpu_custom_call" | custom-call | flops 1 | bytes 1 | tf_op jit(solution)/shard_map/pallas_call | solution.py:443
  10.4 2.1 %collective-permute-done.2._.refs_8_ = bf16[128,512]{1,0:T(8,128)(2,1)S(1)} collective-permute-done((bf16[128,512]{1,0:T(8,128)(2,1)S(1)}, bf16[128,512]{1,0:T(8,128)(2,1)S(1)}, u32[]{:S(2)}, u32[]{:S(2)}) %collective-permute-start.2) | collective-permute-done | bytes 131104 | tf_op jit(solution)/shard_map/ppermute | solution.py:510
  15.9 1.5 %collective-permute-start.6 = (bf16[128,512]{1,0:T(8,128)(2,1)S(1)}, bf16[128,512]{1,0:T(8,128)(2,1)S(1)}, u32[]{:S(2)}, u32[]{:S(2)}) collective-permute-start(bf16[128,512]{1,0:T(8,128)(2,1)S(1)} %get-tuple-element.123), channel_id=1, source_target_pairs={{0,25},{1,8},{2,27},{3,10},{4,29},{5,12},{6,31},{7,14},{8,1},{9,16... | collective-permute-start | bytes 393224 | tf_op jit(solution)/shard_map/ppermute | solution.py:510
  18.2 4.0 %collective-permute-done.6.refs_8_ = bf16[128,512]{1,0:T(8,128)(2,1)S(1)} collective-permute-done((bf16[128,512]{1,0:T(8,128)(2,1)S(1)}, bf16[128,512]{1,0:T(8,128)(2,1)S(1)}, u32[]{:S(2)}, u32[]{:S(2)}) %collective-permute-start.6) | collective-permute-done | bytes 131104 | tf_op jit(solution)/shard_map/ppermute | solution.py:510
  24.4 1.5 %collective-permute-start.9 = (bf16[128,512]{1,0:T(8,128)(2,1)S(1)}, bf16[128,512]{1,0:T(8,128)(2,1)S(1)}, u32[]{:S(2)}, u32[]{:S(2)}) collective-permute-start(bf16[128,512]{1,0:T(8,128)(2,1)S(1)} %get-tuple-element.140), channel_id=1, source_target_pairs={{0,27},{1,10},{2,25},{3,8},{4,31},{5,14},{6,29},{7,12},{8,3},{9,18... | collective-permute-start | bytes 393224 | tf_op jit(solution)/shard_map/ppermute | solution.py:510
  25.9 8.5 %collective-permute-done.7.refs_1_.h.refs_4_ = bf16[256,512]{1,0:T(8,128)(2,1)S(1)} collective-permute-done((bf16[256,512]{1,0:T(8,128)(2,1)S(1)}, bf16[256,512]{1,0:T(8,128)(2,1)S(1)}, u32[]{:S(2)}, u32[]{:S(2)}) %collective-permute-start.7) | collective-permute-done | bytes 262176 | tf_op jit(solution)/shard_map/ppermute | solution.py:510
  34.6 1.3 %collective-permute-done.8.refs_7_ = bf16[128,512]{1,0:T(8,128)(2,1)S(1)} collective-permute-done((bf16[128,512]{1,0:T(8,128)(2,1)S(1)}, bf16[128,512]{1,0:T(8,128)(2,1)S(1)}, u32[]{:S(2)}, u32[]{:S(2)}) %collective-permute-start.8) | collective-permute-done | bytes 131104 | tf_op jit(solution)/shard_map/ppermute | solution.py:510
  38.0 4.0 %collective-permute-start.12 = (bf16[256,512]{1,0:T(8,128)(2,1)S(1)}, bf16[256,512]{1,0:T(8,128)(2,1)S(1)}, u32[]{:S(2)}, u32[]{:S(2)}) collective-permute-start(bf16[256,512]{1,0:T(8,128)(2,1)S(1)} %get-tuple-element.153), channel_id=1, source_target_pairs={{0,1},{1,5},{4,0},{5,4},{8,9},{9,13},{12,8},{13,12},{16,17},{17,21... | collective-permute-start | bytes 786440 | tf_op jit(solution)/shard_map/ppermute | solution.py:510
  42.3 1.8 %collective-permute-start.15 = (bf16[128,512]{1,0:T(8,128)(2,1)S(1)}, bf16[128,512]{1,0:T(8,128)(2,1)S(1)}, u32[]{:S(2)}, u32[]{:S(2)}) collective-permute-start(bf16[128,512]{1,0:T(8,128)(2,1)S(1)} %get-tuple-element.170), channel_id=1, source_target_pairs={{0,25},{1,8},{2,27},{3,10},{4,29},{5,12},{6,31},{7,14},{8,1},{9,16... | collective-permute-start | bytes 393224 | tf_op jit(solution)/shard_map/ppermute | solution.py:510
  44.2 4.0 %collective-permute-done.12.refs_3_.refs_1_ = bf16[256,512]{1,0:T(8,128)(2,1)S(1)} collective-permute-done((bf16[256,512]{1,0:T(8,128)(2,1)S(1)}, bf16[256,512]{1,0:T(8,128)(2,1)S(1)}, u32[]{:S(2)}, u32[]{:S(2)}) %collective-permute-start.12) | collective-permute-done | bytes 262176 | tf_op jit(solution)/shard_map/ppermute | solution.py:510
  48.1 1.4 %collective-permute-done.15.refs_6_ = bf16[128,512]{1,0:T(8,128)(2,1)S(1)} collective-permute-done((bf16[128,512]{1,0:T(8,128)(2,1)S(1)}, bf16[128,512]{1,0:T(8,128)(2,1)S(1)}, u32[]{:S(2)}, u32[]{:S(2)}) %collective-permute-start.15) | collective-permute-done | bytes 131104 | tf_op jit(solution)/shard_map/ppermute | solution.py:510
  49.5 1.3 %collective-permute-start.18 = (bf16[128,512]{1,0:T(8,128)(2,1)S(1)}, bf16[128,512]{1,0:T(8,128)(2,1)S(1)}, u32[]{:S(2)}, u32[]{:S(2)}) collective-permute-start(bf16[128,512]{1,0:T(8,128)(2,1)S(1)} %get-tuple-element.171.refs_3_), channel_id=1, source_target_pairs={{2,25},{3,8},{6,29},{7,12},{10,1},{11,16},{14,5},{15,20},{18,9},{1... | collective-permute-start | bytes 393224 | tf_op jit(solution)/shard_map/ppermute | solution.py:510
  51.0 5.0 %collective-permute-start.17 = (bf16[256,512]{1,0:T(8,128)(2,1)S(1)}, bf16[256,512]{1,0:T(8,128)(2,1)S(1)}, u32[]{:S(2)}, u32[]{:S(2)}) collective-permute-start(bf16[256,512]{1,0:T(8,128)(2,1)S(1)} %shard_map.153.value), channel_id=1, source_target_pairs={{0,2},{1,3},{2,0},{3,1},{4,6},{5,7},{6,4},{7,5},{8,10},{9,11},{10,... | collective-permute-start | bytes 786440 | tf_op jit(solution)/shard_map/ppermute | solution.py:510
  56.0 3.6 %collective-permute-done.18.outer = bf16[128,512]{1,0:T(8,128)(2,1)S(1)} collective-permute-done((bf16[128,512]{1,0:T(8,128)(2,1)S(1)}, bf16[128,512]{1,0:T(8,128)(2,1)S(1)}, u32[]{:S(2)}, u32[]{:S(2)}) %collective-permute-start.18) | collective-permute-done | bytes 131104 | tf_op jit(solution)/shard_map/ppermute | solution.py:510
  59.7 4.7 %collective-permute-done.17.refs_5_ = bf16[256,512]{1,0:T(8,128)(2,1)S(1)} collective-permute-done((bf16[256,512]{1,0:T(8,128)(2,1)S(1)}, bf16[256,512]{1,0:T(8,128)(2,1)S(1)}, u32[]{:S(2)}, u32[]{:S(2)}) %collective-permute-start.17) | collective-permute-done | bytes 262176 | tf_op jit(solution)/shard_map/ppermute | solution.py:510
  65.6 1.2 %collective-permute-start.22 = (bf16[128,512]{1,0:T(8,128)(2,1)S(1)}, bf16[128,512]{1,0:T(8,128)(2,1)S(1)}, u32[]{:S(2)}, u32[]{:S(2)}) collective-permute-start(bf16[128,512]{1,0:T(8,128)(2,1)S(1)} %get-tuple-element.185), channel_id=1, source_target_pairs={{0,25},{1,8},{2,27},{3,10},{4,29},{5,12},{6,31},{7,14},{8,1},{9,16... | collective-permute-start | bytes 393224 | tf_op jit(solution)/shard_map/ppermute | solution.py:510
  69.0 3.0 %collective-permute-done.22.outer.refs_6_ = bf16[128,512]{1,0:T(8,128)(2,1)S(1)} collective-permute-done((bf16[128,512]{1,0:T(8,128)(2,1)S(1)}, bf16[128,512]{1,0:T(8,128)(2,1)S(1)}, u32[]{:S(2)}, u32[]{:S(2)}) %collective-permute-start.22) | collective-permute-done | bytes 131104 | tf_op jit(solution)/shard_map/ppermute | solution.py:510
  73.2 1.9 %collective-permute-start.26 = (bf16[128,512]{1,0:T(8,128)(2,1)S(1)}, bf16[128,512]{1,0:T(8,128)(2,1)S(1)}, u32[]{:S(2)}, u32[]{:S(2)}) collective-permute-start(bf16[128,512]{1,0:T(8,128)(2,1)S(1)} %get-tuple-element.199), channel_id=1, source_target_pairs={{0,28},{1,8},{2,30},{3,10},{4,29},{5,9},{6,31},{7,11},{8,4},{9,16}... | collective-permute-start | bytes 393224 | tf_op jit(solution)/shard_map/ppermute | solution.py:510
  76.5 1.6 %collective-permute-start.25 = (bf16[256,512]{1,0:T(8,128)(2,1)S(1)}, bf16[256,512]{1,0:T(8,128)(2,1)S(1)}, u32[]{:S(2)}, u32[]{:S(2)}) collective-permute-start(bf16[256,512]{1,0:T(8,128)(2,1)S(1)} %get-tuple-element.197), channel_id=1, source_target_pairs={{0,1},{1,5},{2,3},{3,7},{4,0},{5,4},{6,2},{7,6},{8,9},{9,13},{10,1... | collective-permute-start | bytes 786440 | tf_op jit(solution)/shard_map/ppermute | solution.py:510
  78.1 1.4 %collective-permute-done.26.outer = bf16[128,512]{1,0:T(8,128)(2,1)S(1)} collective-permute-done((bf16[128,512]{1,0:T(8,128)(2,1)S(1)}, bf16[128,512]{1,0:T(8,128)(2,1)S(1)}, u32[]{:S(2)}, u32[]{:S(2)}) %collective-permute-start.26) | collective-permute-done | bytes 131104 | tf_op jit(solution)/shard_map/ppermute | solution.py:510
  81.4 4.7 %collective-permute-done.25.refs_1_ = bf16[256,512]{1,0:T(8,128)(2,1)S(1)} collective-permute-done((bf16[256,512]{1,0:T(8,128)(2,1)S(1)}, bf16[256,512]{1,0:T(8,128)(2,1)S(1)}, u32[]{:S(2)}, u32[]{:S(2)}) %collective-permute-start.25) | collective-permute-done | bytes 262176 | tf_op jit(solution)/shard_map/ppermute | solution.py:510
  (67 shorter events, 19.7 us)
Async XLA Ops:
  1.9 8.3 %collective-permute-start.1 = (bf16[272,512]{1,0:T(8,128)(2,1)S(1)}, bf16[272,512]{1,0:T(8,128)(2,1)S(1)}, u32[]{:S(2)}, u32[]{:S(2)}) collective-permute-start(bf16[272,512]{1,0:T(8,128)(2,1)S(1)} %get-tuple-element.104), channel_id=1, source_target_pairs={{0,4},{1,0},{2,6},{3,2},{4,5},{5,1},{6,7},{7,3},{8,12},{9,8},{10,1... | collective-permute-start | bytes 835592 | tf_op jit(solution)/shard_map/ppermute | solution.py:510
  4.8 7.7 %collective-permute-start.2 = (bf16[128,512]{1,0:T(8,128)(2,1)S(1)}, bf16[128,512]{1,0:T(8,128)(2,1)S(1)}, u32[]{:S(2)}, u32[]{:S(2)}) collective-permute-start(bf16[128,512]{1,0:T(8,128)(2,1)S(1)} %get-tuple-element.105), channel_id=1, source_target_pairs={{0,25},{1,29},{2,27},{3,31},{4,8},{5,12},{6,10},{7,14},{8,1},{9,5}... | collective-permute-start | bytes 393224 | tf_op jit(solution)/shard_map/ppermute | solution.py:510
  7.0 7.5 %collective-permute-start.3 = (f32[1,512]{1,0:T(1,128)}, f32[1,512]{1,0:T(1,128)S(1)}, u32[]{:S(2)}, u32[]{:S(2)}) collective-permute-start(f32[1,512]{1,0:T(1,128)} %refs_1_.15), channel_id=1, source_target_pairs={{0,1},{1,0},{2,3},{3,2},{4,5},{5,4},{6,7},{7,6},{8,9},{9,8},{10,11... | collective-permute-start | bytes 6152 | tf_op jit(solution)/shard_map/ppermute | solution.py:510
  9.4 4.2 %collective-permute-start = (bf16[2048,512]{1,0:T(8,128)(2,1)S(1)}, bf16[2048,512]{1,0:T(8,128)(2,1)S(1)}, u32[]{:S(2)}, u32[]{:S(2)}) collective-permute-start(bf16[2048,512]{1,0:T(8,128)(2,1)S(1)} %shard_map.131.mine), channel_id=1, source_target_pairs={{0,1},{1,0},{2,3},{3,2},{4,5},{5,4},{6,7},{7,6},{8,9},{9,8},{10,11... | collective-permute-start | bytes 6291464 | tf_op jit(solution)/shard_map/ppermute | solution.py:510
  12.6 2.0 %collective-permute-start.4 = (bf16[128,512]{1,0:T(8,128)(2,1)S(1)}, bf16[128,512]{1,0:T(8,128)(2,1)S(1)}, u32[]{:S(2)}, u32[]{:S(2)}) collective-permute-start(bf16[128,512]{1,0:T(8,128)(2,1)S(1)} %get-tuple-element.116), channel_id=1, source_target_pairs={{0,1},{1,0},{2,3},{3,2},{4,5},{5,4},{6,7},{7,6},{8,9},{9,8},{10,11... | collective-permute-start | bytes 393224 | tf_op jit(solution)/shard_map/ppermute | solution.py:510
  15.7 1.7 %collective-permute-start.5 = (bf16[128,512]{1,0:T(8,128)(2,1)S(1)}, bf16[128,512]{1,0:T(8,128)(2,1)S(1)}, u32[]{:S(2)}, u32[]{:S(2)}) collective-permute-start(bf16[128,512]{1,0:T(8,128)(2,1)S(1)} %get-tuple-element.120), channel_id=1, source_target_pairs={{0,1},{1,0},{2,3},{3,2},{4,5},{5,4},{6,7},{7,6},{8,9},{9,8},{10,11... | collective-permute-start | bytes 393224 | tf_op jit(solution)/shard_map/ppermute | solution.py:510
  15.9 6.3 %collective-permute-start.6 = (bf16[128,512]{1,0:T(8,128)(2,1)S(1)}, bf16[128,512]{1,0:T(8,128)(2,1)S(1)}, u32[]{:S(2)}, u32[]{:S(2)}) collective-permute-start(bf16[128,512]{1,0:T(8,128)(2,1)S(1)} %get-tuple-element.123), channel_id=1, source_target_pairs={{0,25},{1,8},{2,27},{3,10},{4,29},{5,12},{6,31},{7,14},{8,1},{9,16... | collective-permute-start | bytes 393224 | tf_op jit(solution)/shard_map/ppermute | solution.py:510
  23.3 11.1 %collective-permute-start.7 = (bf16[256,512]{1,0:T(8,128)(2,1)S(1)}, bf16[256,512]{1,0:T(8,128)(2,1)S(1)}, u32[]{:S(2)}, u32[]{:S(2)}) collective-permute-start(bf16[256,512]{1,0:T(8,128)(2,1)S(1)} %get-tuple-element.124.h), channel_id=1, source_target_pairs={{0,2},{1,3},{2,0},{3,1},{4,6},{5,7},{6,4},{7,5},{8,10},{9,11},{10,... | collective-permute-start | bytes 786440 | tf_op jit(solution)/shard_map/ppermute | solution.py:510
  24.4 10.2 %collective-permute-start.9 = (bf16[128,512]{1,0:T(8,128)(2,1)S(1)}, bf16[128,512]{1,0:T(8,128)(2,1)S(1)}, u32[]{:S(2)}, u32[]{:S(2)}) collective-permute-start(bf16[128,512]{1,0:T(8,128)(2,1)S(1)} %get-tuple-element.140), channel_id=1, source_target_pairs={{0,27},{1,10},{2,25},{3,8},{4,31},{5,14},{6,29},{7,12},{8,3},{9,18... | collective-permute-start | bytes 393224 | tf_op jit(solution)/shard_map/ppermute | solution.py:510
  36.0 6.3 %collective-permute-start.13 = (bf16[128,512]{1,0:T(8,128)(2,1)S(1)}, bf16[128,512]{1,0:T(8,128)(2,1)S(1)}, u32[]{:S(2)}, u32[]{:S(2)}) collective-permute-start(bf16[128,512]{1,0:T(8,128)(2,1)S(1)} %get-tuple-element.156), channel_id=1, source_target_pairs={{0,25},{1,8},{2,27},{3,10},{4,29},{5,12},{6,31},{7,14},{8,1},{9,16... | collective-permute-start | bytes 393224 | tf_op jit(solution)/shard_map/ppermute | solution.py:510
  37.3 6.8 %collective-permute-start.11 = (bf16[256,512]{1,0:T(8,128)(2,1)S(1)}, bf16[256,512]{1,0:T(8,128)(2,1)S(1)}, u32[]{:S(2)}, u32[]{:S(2)}) collective-permute-start(bf16[256,512]{1,0:T(8,128)(2,1)S(1)} %get-tuple-element.152), channel_id=1, source_target_pairs={{0,0},{1,4},{4,1},{5,5},{8,8},{9,12},{12,9},{13,13},{16,16},{17,20... | collective-permute-start | bytes 786440 | tf_op jit(solution)/shard_map/ppermute | solution.py:510
  38.0 10.1 %collective-permute-start.12 = (bf16[256,512]{1,0:T(8,128)(2,1)S(1)}, bf16[256,512]{1,0:T(8,128)(2,1)S(1)}, u32[]{:S(2)}, u32[]{:S(2)}) collective-permute-start(bf16[256,512]{1,0:T(8,128)(2,1)S(1)} %get-tuple-element.153), channel_id=1, source_target_pairs={{0,1},{1,5},{4,0},{5,4},{8,9},{9,13},{12,8},{13,12},{16,17},{17,21... | collective-permute-start | bytes 786440 | tf_op jit(solution)/shard_map/ppermute | solution.py:510
  42.3 1.8 %collective-permute-start.14 = (bf16[128,512]{1,0:T(8,128)(2,1)S(1)}, bf16[128,512]{1,0:T(8,128)(2,1)S(1)}, u32[]{:S(2)}, u32[]{:S(2)}) collective-permute-start(bf16[128,512]{1,0:T(8,128)(2,1)S(1)} %get-tuple-element.165), channel_id=1, source_target_pairs={{0,1},{1,0},{2,3},{3,2},{4,5},{5,4},{6,7},{7,6},{8,9},{9,8},{10,11... | collective-permute-start | bytes 393224 | tf_op jit(solution)/shard_map/ppermute | solution.py:510
  42.3 7.2 %collective-permute-start.15 = (bf16[128,512]{1,0:T(8,128)(2,1)S(1)}, bf16[128,512]{1,0:T(8,128)(2,1)S(1)}, u32[]{:S(2)}, u32[]{:S(2)}) collective-permute-start(bf16[128,512]{1,0:T(8,128)(2,1)S(1)} %get-tuple-element.170), channel_id=1, source_target_pairs={{0,25},{1,8},{2,27},{3,10},{4,29},{5,12},{6,31},{7,14},{8,1},{9,16... | collective-permute-start | bytes 393224 | tf_op jit(solution)/shard_map/ppermute | solution.py:510
  49.5 10.1 %collective-permute-start.18 = (bf16[128,512]{1,0:T(8,128)(2,1)S(1)}, bf16[128,512]{1,0:T(8,128)(2,1)S(1)}, u32[]{:S(2)}, u32[]{:S(2)}) collective-permute-start(bf16[128,512]{1,0:T(8,128)(2,1)S(1)} %get-tuple-element.171.refs_3_), channel_id=1, source_target_pairs={{2,25},{3,8},{6,29},{7,12},{10,1},{11,16},{14,5},{15,20},{18,9},{1... | collective-permute-start | bytes 393224 | tf_op jit(solution)/shard_map/ppermute | solution.py:510
  51.0 13.4 %collective-permute-start.17 = (bf16[256,512]{1,0:T(8,128)(2,1)S(1)}, bf16[256,512]{1,0:T(8,128)(2,1)S(1)}, u32[]{:S(2)}, u32[]{:S(2)}) collective-permute-start(bf16[256,512]{1,0:T(8,128)(2,1)S(1)} %shard_map.153.value), channel_id=1, source_target_pairs={{0,2},{1,3},{2,0},{3,1},{4,6},{5,7},{6,4},{7,5},{8,10},{9,11},{10,... | collective-permute-start | bytes 786440 | tf_op jit(solution)/shard_map/ppermute | solution.py:510
  65.6 6.3 %collective-permute-start.22 = (bf16[128,512]{1,0:T(8,128)(2,1)S(1)}, bf16[128,512]{1,0:T(8,128)(2,1)S(1)}, u32[]{:S(2)}, u32[]{:S(2)}) collective-permute-start(bf16[128,512]{1,0:T(8,128)(2,1)S(1)} %get-tuple-element.185), channel_id=1, source_target_pairs={{0,25},{1,8},{2,27},{3,10},{4,29},{5,12},{6,31},{7,14},{8,1},{9,16... | collective-permute-start | bytes 393224 | tf_op jit(solution)/shard_map/ppermute | solution.py:510
  67.6 7.6 %collective-permute-start.20 = (bf16[256,512]{1,0:T(8,128)(2,1)S(1)}, bf16[256,512]{1,0:T(8,128)(2,1)S(1)}, u32[]{:S(2)}, u32[]{:S(2)}) collective-permute-start(bf16[256,512]{1,0:T(8,128)(2,1)S(1)} %get-tuple-element.183), channel_id=1, source_target_pairs={{2,2},{3,6},{6,3},{7,7},{10,10},{11,14},{14,11},{15,15},{18,18},{1... | collective-permute-start | bytes 786440 | tf_op jit(solution)/shard_map/ppermute | solution.py:510
  68.3 6.9 %collective-permute-start.21 = (bf16[256,512]{1,0:T(8,128)(2,1)S(1)}, bf16[256,512]{1,0:T(8,128)(2,1)S(1)}, u32[]{:S(2)}, u32[]{:S(2)}) collective-permute-start(bf16[256,512]{1,0:T(8,128)(2,1)S(1)} %get-tuple-element.184), channel_id=1, source_target_pairs={{2,3},{3,7},{6,2},{7,6},{10,11},{11,15},{14,10},{15,14},{18,19},{1... | collective-permute-start | bytes 786440 | tf_op jit(solution)/shard_map/ppermute | solution.py:510
  73.1 2.0 %collective-permute-start.23 = (bf16[128,512]{1,0:T(8,128)(2,1)S(1)}, bf16[128,512]{1,0:T(8,128)(2,1)S(1)}, u32[]{:S(2)}, u32[]{:S(2)}) collective-permute-start(bf16[128,512]{1,0:T(8,128)(2,1)S(1)} %get-tuple-element.191), channel_id=1, source_target_pairs={{0,1},{1,0},{2,3},{3,2},{4,5},{5,4},{6,7},{7,6},{8,9},{9,8},{10,11... | collective-permute-start | bytes 393224 | tf_op jit(solution)/shard_map/ppermute | solution.py:510
  73.2 6.4 %collective-permute-start.26 = (bf16[128,512]{1,0:T(8,128)(2,1)S(1)}, bf16[128,512]{1,0:T(8,128)(2,1)S(1)}, u32[]{:S(2)}, u32[]{:S(2)}) collective-permute-start(bf16[128,512]{1,0:T(8,128)(2,1)S(1)} %get-tuple-element.199), channel_id=1, source_target_pairs={{0,28},{1,8},{2,30},{3,10},{4,29},{5,9},{6,31},{7,11},{8,4},{9,16}... | collective-permute-start | bytes 393224 | tf_op jit(solution)/shard_map/ppermute | solution.py:510
  75.8 5.5 %collective-permute-start.24 = (bf16[256,512]{1,0:T(8,128)(2,1)S(1)}, bf16[256,512]{1,0:T(8,128)(2,1)S(1)}, u32[]{:S(2)}, u32[]{:S(2)}) collective-permute-start(bf16[256,512]{1,0:T(8,128)(2,1)S(1)} %get-tuple-element.196), channel_id=1, source_target_pairs={{0,0},{1,4},{2,2},{3,6},{4,1},{5,5},{6,3},{7,7},{8,8},{9,12},{10,1... | collective-permute-start | bytes 786440 | tf_op jit(solution)/shard_map/ppermute | solution.py:510
  76.5 9.5 %collective-permute-start.25 = (bf16[256,512]{1,0:T(8,128)(2,1)S(1)}, bf16[256,512]{1,0:T(8,128)(2,1)S(1)}, u32[]{:S(2)}, u32[]{:S(2)}) collective-permute-start(bf16[256,512]{1,0:T(8,128)(2,1)S(1)} %get-tuple-element.197), channel_id=1, source_target_pairs={{0,1},{1,5},{2,3},{3,7},{4,0},{5,4},{6,2},{7,6},{8,9},{9,13},{10,1... | collective-permute-start | bytes 786440 | tf_op jit(solution)/shard_map/ppermute | solution.py:510
  79.5 1.6 %collective-permute-start.27 = (bf16[128,512]{1,0:T(8,128)(2,1)S(1)}, bf16[128,512]{1,0:T(8,128)(2,1)S(1)}, u32[]{:S(2)}, u32[]{:S(2)}) collective-permute-start(bf16[128,512]{1,0:T(8,128)(2,1)S(1)} %collective-permute-done.26.outer), channel_id=1, source_target_pairs={{0,1},{1,0},{2,3},{3,2},{4,5},{5,4},{6,7},{7,6},{8,9},{9,8},{10,11... | collective-permute-start | bytes 393224 | tf_op jit(solution)/shard_map/ppermute | solution.py:510
  (5 other events, 6.4 us)

commit v13 on v12

--- a/solution.py
+++ b/solution.py
@@ -12,7 +12,7 @@
 BF16 = jnp.bfloat16
 AXES = ("dom", "pipe")
 INNER, OUTER = 0, 1
-BESIDE = 4 * 10**9
+BESIDE = 2 * 10**9
 LONG = 2 * 10**10
 
 

time: 87.6 us -> 87.6 us (level)
  no operation moved by 1% of the time
where the time goes in v13:
time: 87.6 us; the launch traced here: 87.3 us
  waiting for transfers between devices  42.5 us (49%)
  starting transfers between devices  30.1 us (34%)
  Pallas kernels  13.6 us (16%)
  between operations  1.11 us (1%)
    ppermute x28, waiting for transfers between devices, send(): return lax.ppermute(value, AXES, table)  42.5 us
    ppermute x28, starting transfers between devices, send(): return lax.ppermute(value, AXES, table)  30.1 us
    pallas_call x33, Pallas kernels, run(): pl.pallas_call(kernel, out_shape=[jax.ShapeDtypeStruct(s, t) for s, t in...  13.6 us
  transfers between devices with their start and end apart: 28, of which 17 were waited for; matrix products, arithmetic and copies ran while one was open for 0% of the time, Pallas kernels for 9%

profile of v13, /device:TPU:0, one launch (start us, length us, event | category | flops | bytes accessed | tf_op | source)
XLA Modules:
  0.0 87.3 jit_solution(18186241239150735877)
XLA Ops:
  0.6 1.2 %shard_map.132 = (bf16[256,512]{1,0:T(8,128)(2,1)S(1)}, bf16[272,512]{1,0:T(8,128)(2,1)S(1)}, bf16[128,512]{1,0:T(8,128)(2,1)S(1)}, bf16[16,128]{1,0:T(8,128)(2,1)S(1)}) custom-call(s32[2]{0:T(128)} %count_in.1, s32[1,1,2]{2,1,0:T(1,128)} %bitcast.11, bf16[2,256,512]{2,1,0:T(8,128)(2,1)} %inputs.1, bf16[2,256,512]{2,1,0:T(8,128)(2,1)} %cotangent.1, ...), custom_call_target="tpu_custom_call" | custom-call | flops 1 | bytes 1 | tf_op jit(solution)/shard_map/pallas_call | solution.py:443
  1.9 3.0 %collective-permute-start.1 = (bf16[272,512]{1,0:T(8,128)(2,1)S(1)}, bf16[272,512]{1,0:T(8,128)(2,1)S(1)}, u32[]{:S(2)}, u32[]{:S(2)}) collective-permute-start(bf16[272,512]{1,0:T(8,128)(2,1)S(1)} %get-tuple-element.104), channel_id=1, source_target_pairs={{0,4},{1,0},{2,6},{3,2},{4,5},{5,1},{6,7},{7,3},{8,12},{9,8},{10,1... | collective-permute-start | bytes 835592 | tf_op jit(solution)/shard_map/ppermute | solution.py:510
  4.8 2.2 %collective-permute-start.2 = (bf16[128,512]{1,0:T(8,128)(2,1)S(1)}, bf16[128,512]{1,0:T(8,128)(2,1)S(1)}, u32[]{:S(2)}, u32[]{:S(2)}) collective-permute-start(bf16[128,512]{1,0:T(8,128)(2,1)S(1)} %get-tuple-element.105), channel_id=1, source_target_pairs={{0,25},{1,29},{2,27},{3,31},{4,8},{5,12},{6,10},{7,14},{8,1},{9,5}... | collective-permute-start | bytes 393224 | tf_op jit(solution)/shard_map/ppermute | solution.py:510
  7.7 1.7 %shard_map.131.mine = bf16[2048,512]{1,0:T(8,128)(2,1)S(1)} custom-call(bf16[512,512]{1,0:T(8,128)(2,1)} %bitcast.6, bf16[512,512]{1,0:T(8,128)(2,1)} %bitcast.7, bf16[512,512]{1,0:T(8,128)(2,1)} %bitcast.8, bf16[512,512]{1,0:T(8,128)(2,1)} %bitcast.9, bf16[512,512]{1,0:T(8,128)(2,1)} %bitcast.10), custom_call_target="tpu_custom_call" | custom-call | flops 1 | bytes 1 | tf_op jit(solution)/shard_map/pallas_call | solution.py:443
  10.4 2.1 %collective-permute-done.2._.refs_8_ = bf16[128,512]{1,0:T(8,128)(2,1)S(1)} collective-permute-done((bf16[128,512]{1,0:T(8,128)(2,1)S(1)}, bf16[128,512]{1,0:T(8,128)(2,1)S(1)}, u32[]{:S(2)}, u32[]{:S(2)}) %collective-permute-start.2) | collective-permute-done | bytes 131104 | tf_op jit(solution)/shard_map/ppermute | solution.py:510
  15.9 1.5 %collective-permute-start.6 = (bf16[128,512]{1,0:T(8,128)(2,1)S(1)}, bf16[128,512]{1,0:T(8,128)(2,1)S(1)}, u32[]{:S(2)}, u32[]{:S(2)}) collective-permute-start(bf16[128,512]{1,0:T(8,128)(2,1)S(1)} %get-tuple-element.123), channel_id=1, source_target_pairs={{0,25},{1,8},{2,27},{3,10},{4,29},{5,12},{6,31},{7,14},{8,1},{9,16... | collective-permute-start | bytes 393224 | tf_op jit(solution)/shard_map/ppermute | solution.py:510
  18.2 4.0 %collective-permute-done.6.refs_8_ = bf16[128,512]{1,0:T(8,128)(2,1)S(1)} collective-permute-done((bf16[128,512]{1,0:T(8,128)(2,1)S(1)}, bf16[128,512]{1,0:T(8,128)(2,1)S(1)}, u32[]{:S(2)}, u32[]{:S(2)}) %collective-permute-start.6) | collective-permute-done | bytes 131104 | tf_op jit(solution)/shard_map/ppermute | solution.py:510
  24.4 1.5 %collective-permute-start.9 = (bf16[128,512]{1,0:T(8,128)(2,1)S(1)}, bf16[128,512]{1,0:T(8,128)(2,1)S(1)}, u32[]{:S(2)}, u32[]{:S(2)}) collective-permute-start(bf16[128,512]{1,0:T(8,128)(2,1)S(1)} %get-tuple-element.140), channel_id=1, source_target_pairs={{0,27},{1,10},{2,25},{3,8},{4,31},{5,14},{6,29},{7,12},{8,3},{9,18... | collective-permute-start | bytes 393224 | tf_op jit(solution)/shard_map/ppermute | solution.py:510
  25.9 8.5 %collective-permute-done.7.refs_1_.h.refs_4_ = bf16[256,512]{1,0:T(8,128)(2,1)S(1)} collective-permute-done((bf16[256,512]{1,0:T(8,128)(2,1)S(1)}, bf16[256,512]{1,0:T(8,128)(2,1)S(1)}, u32[]{:S(2)}, u32[]{:S(2)}) %collective-permute-start.7) | collective-permute-done | bytes 262176 | tf_op jit(solution)/shard_map/ppermute | solution.py:510
  34.6 1.3 %collective-permute-done.8.refs_7_ = bf16[128,512]{1,0:T(8,128)(2,1)S(1)} collective-permute-done((bf16[128,512]{1,0:T(8,128)(2,1)S(1)}, bf16[128,512]{1,0:T(8,128)(2,1)S(1)}, u32[]{:S(2)}, u32[]{:S(2)}) %collective-permute-start.8) | collective-permute-done | bytes 131104 | tf_op jit(solution)/shard_map/ppermute | solution.py:510
  38.0 4.0 %collective-permute-start.12 = (bf16[256,512]{1,0:T(8,128)(2,1)S(1)}, bf16[256,512]{1,0:T(8,128)(2,1)S(1)}, u32[]{:S(2)}, u32[]{:S(2)}) collective-permute-start(bf16[256,512]{1,0:T(8,128)(2,1)S(1)} %get-tuple-element.153), channel_id=1, source_target_pairs={{0,1},{1,5},{4,0},{5,4},{8,9},{9,13},{12,8},{13,12},{16,17},{17,21... | collective-permute-start | bytes 786440 | tf_op jit(solution)/shard_map/ppermute | solution.py:510
  42.3 1.8 %collective-permute-start.15 = (bf16[128,512]{1,0:T(8,128)(2,1)S(1)}, bf16[128,512]{1,0:T(8,128)(2,1)S(1)}, u32[]{:S(2)}, u32[]{:S(2)}) collective-permute-start(bf16[128,512]{1,0:T(8,128)(2,1)S(1)} %get-tuple-element.170), channel_id=1, source_target_pairs={{0,25},{1,8},{2,27},{3,10},{4,29},{5,12},{6,31},{7,14},{8,1},{9,16... | collective-permute-start | bytes 393224 | tf_op jit(solution)/shard_map/ppermute | solution.py:510
  44.2 4.0 %collective-permute-done.12.refs_3_.refs_1_ = bf16[256,512]{1,0:T(8,128)(2,1)S(1)} collective-permute-done((bf16[256,512]{1,0:T(8,128)(2,1)S(1)}, bf16[256,512]{1,0:T(8,128)(2,1)S(1)}, u32[]{:S(2)}, u32[]{:S(2)}) %collective-permute-start.12) | collective-permute-done | bytes 262176 | tf_op jit(solution)/shard_map/ppermute | solution.py:510
  48.1 1.4 %collective-permute-done.15.refs_6_ = bf16[128,512]{1,0:T(8,128)(2,1)S(1)} collective-permute-done((bf16[128,512]{1,0:T(8,128)(2,1)S(1)}, bf16[128,512]{1,0:T(8,128)(2,1)S(1)}, u32[]{:S(2)}, u32[]{:S(2)}) %collective-permute-start.15) | collective-permute-done | bytes 131104 | tf_op jit(solution)/shard_map/ppermute | solution.py:510
  49.5 1.3 %collective-permute-start.18 = (bf16[128,512]{1,0:T(8,128)(2,1)S(1)}, bf16[128,512]{1,0:T(8,128)(2,1)S(1)}, u32[]{:S(2)}, u32[]{:S(2)}) collective-permute-start(bf16[128,512]{1,0:T(8,128)(2,1)S(1)} %get-tuple-element.171.refs_3_), channel_id=1, source_target_pairs={{2,25},{3,8},{6,29},{7,12},{10,1},{11,16},{14,5},{15,20},{18,9},{1... | collective-permute-start | bytes 393224 | tf_op jit(solution)/shard_map/ppermute | solution.py:510
  51.0 5.0 %collective-permute-start.17 = (bf16[256,512]{1,0:T(8,128)(2,1)S(1)}, bf16[256,512]{1,0:T(8,128)(2,1)S(1)}, u32[]{:S(2)}, u32[]{:S(2)}) collective-permute-start(bf16[256,512]{1,0:T(8,128)(2,1)S(1)} %shard_map.153.value), channel_id=1, source_target_pairs={{0,2},{1,3},{2,0},{3,1},{4,6},{5,7},{6,4},{7,5},{8,10},{9,11},{10,... | collective-permute-start | bytes 786440 | tf_op jit(solution)/shard_map/ppermute | solution.py:510
  56.0 3.6 %collective-permute-done.18.outer = bf16[128,512]{1,0:T(8,128)(2,1)S(1)} collective-permute-done((bf16[128,512]{1,0:T(8,128)(2,1)S(1)}, bf16[128,512]{1,0:T(8,128)(2,1)S(1)}, u32[]{:S(2)}, u32[]{:S(2)}) %collective-permute-start.18) | collective-permute-done | bytes 131104 | tf_op jit(solution)/shard_map/ppermute | solution.py:510
  59.7 4.7 %collective-permute-done.17.refs_5_ = bf16[256,512]{1,0:T(8,128)(2,1)S(1)} collective-permute-done((bf16[256,512]{1,0:T(8,128)(2,1)S(1)}, bf16[256,512]{1,0:T(8,128)(2,1)S(1)}, u32[]{:S(2)}, u32[]{:S(2)}) %collective-permute-start.17) | collective-permute-done | bytes 262176 | tf_op jit(solution)/shard_map/ppermute | solution.py:510
  65.6 1.2 %collective-permute-start.22 = (bf16[128,512]{1,0:T(8,128)(2,1)S(1)}, bf16[128,512]{1,0:T(8,128)(2,1)S(1)}, u32[]{:S(2)}, u32[]{:S(2)}) collective-permute-start(bf16[128,512]{1,0:T(8,128)(2,1)S(1)} %get-tuple-element.185), channel_id=1, source_target_pairs={{0,25},{1,8},{2,27},{3,10},{4,29},{5,12},{6,31},{7,14},{8,1},{9,16... | collective-permute-start | bytes 393224 | tf_op jit(solution)/shard_map/ppermute | solution.py:510
  69.0 3.0 %collective-permute-done.22.outer.refs_6_ = bf16[128,512]{1,0:T(8,128)(2,1)S(1)} collective-permute-done((bf16[128,512]{1,0:T(8,128)(2,1)S(1)}, bf16[128,512]{1,0:T(8,128)(2,1)S(1)}, u32[]{:S(2)}, u32[]{:S(2)}) %collective-permute-start.22) | collective-permute-done | bytes 131104 | tf_op jit(solution)/shard_map/ppermute | solution.py:510
  73.2 1.9 %collective-permute-start.26 = (bf16[128,512]{1,0:T(8,128)(2,1)S(1)}, bf16[128,512]{1,0:T(8,128)(2,1)S(1)}, u32[]{:S(2)}, u32[]{:S(2)}) collective-permute-start(bf16[128,512]{1,0:T(8,128)(2,1)S(1)} %get-tuple-element.199), channel_id=1, source_target_pairs={{0,28},{1,8},{2,30},{3,10},{4,29},{5,9},{6,31},{7,11},{8,4},{9,16}... | collective-permute-start | bytes 393224 | tf_op jit(solution)/shard_map/ppermute | solution.py:510
  76.5 1.6 %collective-permute-start.25 = (bf16[256,512]{1,0:T(8,128)(2,1)S(1)}, bf16[256,512]{1,0:T(8,128)(2,1)S(1)}, u32[]{:S(2)}, u32[]{:S(2)}) collective-permute-start(bf16[256,512]{1,0:T(8,128)(2,1)S(1)} %get-tuple-element.197), channel_id=1, source_target_pairs={{0,1},{1,5},{2,3},{3,7},{4,0},{5,4},{6,2},{7,6},{8,9},{9,13},{10,1... | collective-permute-start | bytes 786440 | tf_op jit(solution)/shard_map/ppermute | solution.py:510
  78.1 1.4 %collective-permute-done.26.outer = bf16[128,512]{1,0:T(8,128)(2,1)S(1)} collective-permute-done((bf16[128,512]{1,0:T(8,128)(2,1)S(1)}, bf16[128,512]{1,0:T(8,128)(2,1)S(1)}, u32[]{:S(2)}, u32[]{:S(2)}) %collective-permute-start.26) | collective-permute-done | bytes 131104 | tf_op jit(solution)/shard_map/ppermute | solution.py:510
  81.4 4.7 %collective-permute-done.25.refs_1_ = bf16[256,512]{1,0:T(8,128)(2,1)S(1)} collective-permute-done((bf16[256,512]{1,0:T(8,128)(2,1)S(1)}, bf16[256,512]{1,0:T(8,128)(2,1)S(1)}, u32[]{:S(2)}, u32[]{:S(2)}) %collective-permute-start.25) | collective-permute-done | bytes 262176 | tf_op jit(solution)/shard_map/ppermute | solution.py:510
  (67 shorter events, 19.7 us)
Async XLA Ops:
  1.9 8.3 %collective-permute-start.1 = (bf16[272,512]{1,0:T(8,128)(2,1)S(1)}, bf16[272,512]{1,0:T(8,128)(2,1)S(1)}, u32[]{:S(2)}, u32[]{:S(2)}) collective-permute-start(bf16[272,512]{1,0:T(8,128)(2,1)S(1)} %get-tuple-element.104), channel_id=1, source_target_pairs={{0,4},{1,0},{2,6},{3,2},{4,5},{5,1},{6,7},{7,3},{8,12},{9,8},{10,1... | collective-permute-start | bytes 835592 | tf_op jit(solution)/shard_map/ppermute | solution.py:510
  4.8 7.7 %collective-permute-start.2 = (bf16[128,512]{1,0:T(8,128)(2,1)S(1)}, bf16[128,512]{1,0:T(8,128)(2,1)S(1)}, u32[]{:S(2)}, u32[]{:S(2)}) collective-permute-start(bf16[128,512]{1,0:T(8,128)(2,1)S(1)} %get-tuple-element.105), channel_id=1, source_target_pairs={{0,25},{1,29},{2,27},{3,31},{4,8},{5,12},{6,10},{7,14},{8,1},{9,5}... | collective-permute-start | bytes 393224 | tf_op jit(solution)/shard_map/ppermute | solution.py:510
  7.0 7.5 %collective-permute-start.3 = (f32[1,512]{1,0:T(1,128)}, f32[1,512]{1,0:T(1,128)S(1)}, u32[]{:S(2)}, u32[]{:S(2)}) collective-permute-start(f32[1,512]{1,0:T(1,128)} %refs_1_.15), channel_id=1, source_target_pairs={{0,1},{1,0},{2,3},{3,2},{4,5},{5,4},{6,7},{7,6},{8,9},{9,8},{10,11... | collective-permute-start | bytes 6152 | tf_op jit(solution)/shard_map/ppermute | solution.py:510
  9.4 4.2 %collective-permute-start = (bf16[2048,512]{1,0:T(8,128)(2,1)S(1)}, bf16[2048,512]{1,0:T(8,128)(2,1)S(1)}, u32[]{:S(2)}, u32[]{:S(2)}) collective-permute-start(bf16[2048,512]{1,0:T(8,128)(2,1)S(1)} %shard_map.131.mine), channel_id=1, source_target_pairs={{0,1},{1,0},{2,3},{3,2},{4,5},{5,4},{6,7},{7,6},{8,9},{9,8},{10,11... | collective-permute-start | bytes 6291464 | tf_op jit(solution)/shard_map/ppermute | solution.py:510
  12.6 2.0 %collective-permute-start.4 = (bf16[128,512]{1,0:T(8,128)(2,1)S(1)}, bf16[128,512]{1,0:T(8,128)(2,1)S(1)}, u32[]{:S(2)}, u32[]{:S(2)}) collective-permute-start(bf16[128,512]{1,0:T(8,128)(2,1)S(1)} %get-tuple-element.116), channel_id=1, source_target_pairs={{0,1},{1,0},{2,3},{3,2},{4,5},{5,4},{6,7},{7,6},{8,9},{9,8},{10,11... | collective-permute-start | bytes 393224 | tf_op jit(solution)/shard_map/ppermute | solution.py:510
  15.7 1.7 %collective-permute-start.5 = (bf16[128,512]{1,0:T(8,128)(2,1)S(1)}, bf16[128,512]{1,0:T(8,128)(2,1)S(1)}, u32[]{:S(2)}, u32[]{:S(2)}) collective-permute-start(bf16[128,512]{1,0:T(8,128)(2,1)S(1)} %get-tuple-element.120), channel_id=1, source_target_pairs={{0,1},{1,0},{2,3},{3,2},{4,5},{5,4},{6,7},{7,6},{8,9},{9,8},{10,11... | collective-permute-start | bytes 393224 | tf_op jit(solution)/shard_map/ppermute | solution.py:510
  15.9 6.3 %collective-permute-start.6 = (bf16[128,512]{1,0:T(8,128)(2,1)S(1)}, bf16[128,512]{1,0:T(8,128)(2,1)S(1)}, u32[]{:S(2)}, u32[]{:S(2)}) collective-permute-start(bf16[128,512]{1,0:T(8,128)(2,1)S(1)} %get-tuple-element.123), channel_id=1, source_target_pairs={{0,25},{1,8},{2,27},{3,10},{4,29},{5,12},{6,31},{7,14},{8,1},{9,16... | collective-permute-start | bytes 393224 | tf_op jit(solution)/shard_map/ppermute | solution.py:510
  23.3 11.1 %collective-permute-start.7 = (bf16[256,512]{1,0:T(8,128)(2,1)S(1)}, bf16[256,512]{1,0:T(8,128)(2,1)S(1)}, u32[]{:S(2)}, u32[]{:S(2)}) collective-permute-start(bf16[256,512]{1,0:T(8,128)(2,1)S(1)} %get-tuple-element.124.h), channel_id=1, source_target_pairs={{0,2},{1,3},{2,0},{3,1},{4,6},{5,7},{6,4},{7,5},{8,10},{9,11},{10,... | collective-permute-start | bytes 786440 | tf_op jit(solution)/shard_map/ppermute | solution.py:510
  24.4 10.2 %collective-permute-start.9 = (bf16[128,512]{1,0:T(8,128)(2,1)S(1)}, bf16[128,512]{1,0:T(8,128)(2,1)S(1)}, u32[]{:S(2)}, u32[]{:S(2)}) collective-permute-start(bf16[128,512]{1,0:T(8,128)(2,1)S(1)} %get-tuple-element.140), channel_id=1, source_target_pairs={{0,27},{1,10},{2,25},{3,8},{4,31},{5,14},{6,29},{7,12},{8,3},{9,18... | collective-permute-start | bytes 393224 | tf_op jit(solution)/shard_map/ppermute | solution.py:510
  36.0 6.3 %collective-permute-start.13 = (bf16[128,512]{1,0:T(8,128)(2,1)S(1)}, bf16[128,512]{1,0:T(8,128)(2,1)S(1)}, u32[]{:S(2)}, u32[]{:S(2)}) collective-permute-start(bf16[128,512]{1,0:T(8,128)(2,1)S(1)} %get-tuple-element.156), channel_id=1, source_target_pairs={{0,25},{1,8},{2,27},{3,10},{4,29},{5,12},{6,31},{7,14},{8,1},{9,16... | collective-permute-start | bytes 393224 | tf_op jit(solution)/shard_map/ppermute | solution.py:510
  37.3 6.8 %collective-permute-start.11 = (bf16[256,512]{1,0:T(8,128)(2,1)S(1)}, bf16[256,512]{1,0:T(8,128)(2,1)S(1)}, u32[]{:S(2)}, u32[]{:S(2)}) collective-permute-start(bf16[256,512]{1,0:T(8,128)(2,1)S(1)} %get-tuple-element.152), channel_id=1, source_target_pairs={{0,0},{1,4},{4,1},{5,5},{8,8},{9,12},{12,9},{13,13},{16,16},{17,20... | collective-permute-start | bytes 786440 | tf_op jit(solution)/shard_map/ppermute | solution.py:510
  38.0 10.1 %collective-permute-start.12 = (bf16[256,512]{1,0:T(8,128)(2,1)S(1)}, bf16[256,512]{1,0:T(8,128)(2,1)S(1)}, u32[]{:S(2)}, u32[]{:S(2)}) collective-permute-start(bf16[256,512]{1,0:T(8,128)(2,1)S(1)} %get-tuple-element.153), channel_id=1, source_target_pairs={{0,1},{1,5},{4,0},{5,4},{8,9},{9,13},{12,8},{13,12},{16,17},{17,21... | collective-permute-start | bytes 786440 | tf_op jit(solution)/shard_map/ppermute | solution.py:510
  42.3 1.8 %collective-permute-start.14 = (bf16[128,512]{1,0:T(8,128)(2,1)S(1)}, bf16[128,512]{1,0:T(8,128)(2,1)S(1)}, u32[]{:S(2)}, u32[]{:S(2)}) collective-permute-start(bf16[128,512]{1,0:T(8,128)(2,1)S(1)} %get-tuple-element.165), channel_id=1, source_target_pairs={{0,1},{1,0},{2,3},{3,2},{4,5},{5,4},{6,7},{7,6},{8,9},{9,8},{10,11... | collective-permute-start | bytes 393224 | tf_op jit(solution)/shard_map/ppermute | solution.py:510
  42.3 7.2 %collective-permute-start.15 = (bf16[128,512]{1,0:T(8,128)(2,1)S(1)}, bf16[128,512]{1,0:T(8,128)(2,1)S(1)}, u32[]{:S(2)}, u32[]{:S(2)}) collective-permute-start(bf16[128,512]{1,0:T(8,128)(2,1)S(1)} %get-tuple-element.170), channel_id=1, source_target_pairs={{0,25},{1,8},{2,27},{3,10},{4,29},{5,12},{6,31},{7,14},{8,1},{9,16... | collective-permute-start | bytes 393224 | tf_op jit(solution)/shard_map/ppermute | solution.py:510
  49.5 10.1 %collective-permute-start.18 = (bf16[128,512]{1,0:T(8,128)(2,1)S(1)}, bf16[128,512]{1,0:T(8,128)(2,1)S(1)}, u32[]{:S(2)}, u32[]{:S(2)}) collective-permute-start(bf16[128,512]{1,0:T(8,128)(2,1)S(1)} %get-tuple-element.171.refs_3_), channel_id=1, source_target_pairs={{2,25},{3,8},{6,29},{7,12},{10,1},{11,16},{14,5},{15,20},{18,9},{1... | collective-permute-start | bytes 393224 | tf_op jit(solution)/shard_map/ppermute | solution.py:510
  51.0 13.4 %collective-permute-start.17 = (bf16[256,512]{1,0:T(8,128)(2,1)S(1)}, bf16[256,512]{1,0:T(8,128)(2,1)S(1)}, u32[]{:S(2)}, u32[]{:S(2)}) collective-permute-start(bf16[256,512]{1,0:T(8,128)(2,1)S(1)} %shard_map.153.value), channel_id=1, source_target_pairs={{0,2},{1,3},{2,0},{3,1},{4,6},{5,7},{6,4},{7,5},{8,10},{9,11},{10,... | collective-permute-start | bytes 786440 | tf_op jit(solution)/shard_map/ppermute | solution.py:510
  65.6 6.3 %collective-permute-start.22 = (bf16[128,512]{1,0:T(8,128)(2,1)S(1)}, bf16[128,512]{1,0:T(8,128)(2,1)S(1)}, u32[]{:S(2)}, u32[]{:S(2)}) collective-permute-start(bf16[128,512]{1,0:T(8,128)(2,1)S(1)} %get-tuple-element.185), channel_id=1, source_target_pairs={{0,25},{1,8},{2,27},{3,10},{4,29},{5,12},{6,31},{7,14},{8,1},{9,16... | collective-permute-start | bytes 393224 | tf_op jit(solution)/shard_map/ppermute | solution.py:510
  67.6 7.6 %collective-permute-start.20 = (bf16[256,512]{1,0:T(8,128)(2,1)S(1)}, bf16[256,512]{1,0:T(8,128)(2,1)S(1)}, u32[]{:S(2)}, u32[]{:S(2)}) collective-permute-start(bf16[256,512]{1,0:T(8,128)(2,1)S(1)} %get-tuple-element.183), channel_id=1, source_target_pairs={{2,2},{3,6},{6,3},{7,7},{10,10},{11,14},{14,11},{15,15},{18,18},{1... | collective-permute-start | bytes 786440 | tf_op jit(solution)/shard_map/ppermute | solution.py:510
  68.3 6.9 %collective-permute-start.21 = (bf16[256,512]{1,0:T(8,128)(2,1)S(1)}, bf16[256,512]{1,0:T(8,128)(2,1)S(1)}, u32[]{:S(2)}, u32[]{:S(2)}) collective-permute-start(bf16[256,512]{1,0:T(8,128)(2,1)S(1)} %get-tuple-element.184), channel_id=1, source_target_pairs={{2,3},{3,7},{6,2},{7,6},{10,11},{11,15},{14,10},{15,14},{18,19},{1... | collective-permute-start | bytes 786440 | tf_op jit(solution)/shard_map/ppermute | solution.py:510
  73.1 2.0 %collective-permute-start.23 = (bf16[128,512]{1,0:T(8,128)(2,1)S(1)}, bf16[128,512]{1,0:T(8,128)(2,1)S(1)}, u32[]{:S(2)}, u32[]{:S(2)}) collective-permute-start(bf16[128,512]{1,0:T(8,128)(2,1)S(1)} %get-tuple-element.191), channel_id=1, source_target_pairs={{0,1},{1,0},{2,3},{3,2},{4,5},{5,4},{6,7},{7,6},{8,9},{9,8},{10,11... | collective-permute-start | bytes 393224 | tf_op jit(solution)/shard_map/ppermute | solution.py:510
  73.2 6.4 %collective-permute-start.26 = (bf16[128,512]{1,0:T(8,128)(2,1)S(1)}, bf16[128,512]{1,0:T(8,128)(2,1)S(1)}, u32[]{:S(2)}, u32[]{:S(2)}) collective-permute-start(bf16[128,512]{1,0:T(8,128)(2,1)S(1)} %get-tuple-element.199), channel_id=1, source_target_pairs={{0,28},{1,8},{2,30},{3,10},{4,29},{5,9},{6,31},{7,11},{8,4},{9,16}... | collective-permute-start | bytes 393224 | tf_op jit(solution)/shard_map/ppermute | solution.py:510
  75.8 5.5 %collective-permute-start.24 = (bf16[256,512]{1,0:T(8,128)(2,1)S(1)}, bf16[256,512]{1,0:T(8,128)(2,1)S(1)}, u32[]{:S(2)}, u32[]{:S(2)}) collective-permute-start(bf16[256,512]{1,0:T(8,128)(2,1)S(1)} %get-tuple-element.196), channel_id=1, source_target_pairs={{0,0},{1,4},{2,2},{3,6},{4,1},{5,5},{6,3},{7,7},{8,8},{9,12},{10,1... | collective-permute-start | bytes 786440 | tf_op jit(solution)/shard_map/ppermute | solution.py:510
  76.5 9.5 %collective-permute-start.25 = (bf16[256,512]{1,0:T(8,128)(2,1)S(1)}, bf16[256,512]{1,0:T(8,128)(2,1)S(1)}, u32[]{:S(2)}, u32[]{:S(2)}) collective-permute-start(bf16[256,512]{1,0:T(8,128)(2,1)S(1)} %get-tuple-element.197), channel_id=1, source_target_pairs={{0,1},{1,5},{2,3},{3,7},{4,0},{5,4},{6,2},{7,6},{8,9},{9,13},{10,1... | collective-permute-start | bytes 786440 | tf_op jit(solution)/shard_map/ppermute | solution.py:510
  79.6 1.6 %collective-permute-start.27 = (bf16[128,512]{1,0:T(8,128)(2,1)S(1)}, bf16[128,512]{1,0:T(8,128)(2,1)S(1)}, u32[]{:S(2)}, u32[]{:S(2)}) collective-permute-start(bf16[128,512]{1,0:T(8,128)(2,1)S(1)} %collective-permute-done.26.outer), channel_id=1, source_target_pairs={{0,1},{1,0},{2,3},{3,2},{4,5},{5,4},{6,7},{7,6},{8,9},{9,8},{10,11... | collective-permute-start | bytes 393224 | tf_op jit(solution)/shard_map/ppermute | solution.py:510
  (5 other events, 6.4 us)

commit v14 on v13

--- a/solution.py
+++ b/solution.py
@@ -252,7 +252,7 @@
     u_out[...] = mul(h[...], w_node[...])
 
 
-def forward_kernel(parity, last, take, lists, h, a_own, u_own, inner, outer, ghalo, gown_t, *refs):
+def forward_kernel(parity, first, last, take, lists, h, a_own, u_own, inner, outer, ghalo, gown_t, *refs):
     packed, *gains = take
     w_send, _, _, w_fold = quarters(packed)
     gain = jnp.where(here_is(parity=parity), gains[0][...], gains[1][...])
@@ -267,9 +267,13 @@
     if last:
         keep(parity, a, u, t, inverse, out, *refs[-4:])
         return
-    h_out, a_out, u_out, *to = refs
-    a_out[...] = a
-    u_out[...] = u
+    if first:
+        h_out, *to = refs[:3]
+        keep(parity, a, u, t, inverse, out, *refs[3:])
+    else:
+        h_out, a_out, u_out, *to = refs
+        a_out[...] = a
+        u_out[...] = u
     h_out[...] = out
     for side, ref in zip((OUTER, INNER), reversed(to)):
         ref[...] = listed(lists[side : side + 1, :1], out, block)
@@ -596,18 +600,25 @@
         last = tick == sections - 1
         state = [(both_wide, BF16), (both_wide, BF16), ((2 * edges, latent), BF16), (both_wide, BF16)]
         made = run_section(
-            functools.partial(forward_kernel, parity, last),
+            functools.partial(forward_kernel, parity, tick == 0, last),
             plane,
             (packed, *both_gains),
             (lists, hidden, a_own, u_own, inner, outer, ghalo, gown_t) + (tuple(saved) if last else ()),
-            state if last else [(wide, BF16), (edge_wide, F32), (wide, F32)] + to_send,
+            state
+            if last
+            else [(wide, BF16)] + to_send + state
+            if tick == 0
+            else [(wide, BF16), (edge_wide, F32), (wide, F32)] + to_send,
             aliases={8 + k: k for k in range(4)} if last else None,
             cost=BESIDE // 2 if last else 1,
         )
         if last:
             saved = made
             break
-        hidden, a, u, *to = made
+        if tick == 0:
+            hidden, to, saved = made[0], made[1:3], made[3:]
+        else:
+            hidden, a, u, *to = made
         produced = hidden
         if step == 0:
             outer = towards(to[-1], OUTER, step)
@@ -617,6 +628,8 @@
             hidden = across(hidden)
             inner = towards(*run(inner_kernel, (lists, hidden), [(narrow, BF16)]), INNER, 0)
             arrived = ()
+        if tick == 0:
+            continue
         saved = run(
             functools.partial(save_kernel, plane, parity),
             (a, u, produced) + tuple(saved),

time: 87.6 us -> 87.8 us (level)
    pallas_call x33 -> x32, Pallas kernels: 13.6 us -> 13.2 us  [run(): pl.pallas_call(kernel, out_shape=[jax.ShapeDtypeStruct(s, t) for s, t in...]
  transfers between devices with their start and end apart: 28 -> 28, of which waited for: 17 -> 18; matrix products, arithmetic and copies ran while one was open for 0% -> 0% of each run, Pallas kernels for 9% -> 8%
where the time goes in v14:
time: 87.8 us; the launch traced here: 87.5 us
  waiting for transfers between devices  42.9 us (49%)
  starting transfers between devices  30.4 us (35%)
  Pallas kernels  13.2 us (15%)
  between operations  1.1 us (1%)
    ppermute x28, waiting for transfers between devices, send(): return lax.ppermute(value, AXES, table)  42.9 us
    ppermute x28, starting transfers between devices, send(): return lax.ppermute(value, AXES, table)  30.4 us
    pallas_call x32, Pallas kernels, run(): pl.pallas_call(kernel, out_shape=[jax.ShapeDtypeStruct(s, t) for s, t in...  13.2 us
  transfers between devices with their start and end apart: 28, of which 18 were waited for; matrix products, arithmetic and copies ran while one was open for 0% of the time, Pallas kernels for 8%

profile of v14, /device:TPU:0, one launch (start us, length us, event | category | flops | bytes accessed | tf_op | source)
XLA Modules:
  0.0 87.5 jit_solution(15557859679719008793)
XLA Ops:
  0.6 1.2 %shard_map.132 = (bf16[256,512]{1,0:T(8,128)(2,1)S(1)}, bf16[272,512]{1,0:T(8,128)(2,1)S(1)}, bf16[128,512]{1,0:T(8,128)(2,1)S(1)}, bf16[16,128]{1,0:T(8,128)(2,1)S(1)}) custom-call(s32[2]{0:T(128)} %count_in.1, s32[1,1,2]{2,1,0:T(1,128)} %bitcast.11, bf16[2,256,512]{2,1,0:T(8,128)(2,1)} %inputs.1, bf16[2,256,512]{2,1,0:T(8,128)(2,1)} %cotangent.1, ...), custom_call_target="tpu_custom_call" | custom-call | flops 1 | bytes 1 | tf_op jit(solution)/shard_map/pallas_call | solution.py:447
  1.9 3.0 %collective-permute-start.1 = (bf16[272,512]{1,0:T(8,128)(2,1)S(1)}, bf16[272,512]{1,0:T(8,128)(2,1)S(1)}, u32[]{:S(2)}, u32[]{:S(2)}) collective-permute-start(bf16[272,512]{1,0:T(8,128)(2,1)S(1)} %get-tuple-element.102), channel_id=1, source_target_pairs={{0,4},{1,0},{2,6},{3,2},{4,5},{5,1},{6,7},{7,3},{8,12},{9,8},{10,1... | collective-permute-start | bytes 835592 | tf_op jit(solution)/shard_map/ppermute | solution.py:514
  4.8 2.2 %collective-permute-start.2 = (bf16[128,512]{1,0:T(8,128)(2,1)S(1)}, bf16[128,512]{1,0:T(8,128)(2,1)S(1)}, u32[]{:S(2)}, u32[]{:S(2)}) collective-permute-start(bf16[128,512]{1,0:T(8,128)(2,1)S(1)} %get-tuple-element.103), channel_id=1, source_target_pairs={{0,25},{1,29},{2,27},{3,31},{4,8},{5,12},{6,10},{7,14},{8,1},{9,5}... | collective-permute-start | bytes 393224 | tf_op jit(solution)/shard_map/ppermute | solution.py:514
  7.7 1.7 %shard_map.131.mine = bf16[2048,512]{1,0:T(8,128)(2,1)S(1)} custom-call(bf16[512,512]{1,0:T(8,128)(2,1)} %bitcast.6, bf16[512,512]{1,0:T(8,128)(2,1)} %bitcast.7, bf16[512,512]{1,0:T(8,128)(2,1)} %bitcast.8, bf16[512,512]{1,0:T(8,128)(2,1)} %bitcast.9, bf16[512,512]{1,0:T(8,128)(2,1)} %bitcast.10), custom_call_target="tpu_custom_call" | custom-call | flops 1 | bytes 1 | tf_op jit(solution)/shard_map/pallas_call | solution.py:447
  10.4 2.1 %collective-permute-done.2._.refs_8_ = bf16[128,512]{1,0:T(8,128)(2,1)S(1)} collective-permute-done((bf16[128,512]{1,0:T(8,128)(2,1)S(1)}, bf16[128,512]{1,0:T(8,128)(2,1)S(1)}, u32[]{:S(2)}, u32[]{:S(2)}) %collective-permute-start.2) | collective-permute-done | bytes 131104 | tf_op jit(solution)/shard_map/ppermute | solution.py:514
  14.6 1.3 %shard_map.138 = (bf16[256,512]{1,0:T(8,128)(2,1)S(1)}, bf16[128,512]{1,0:T(8,128)(2,1)S(1)}, bf16[128,512]{1,0:T(8,128)(2,1)S(1)}, bf16[512,512]{1,0:T(8,128)(2...) custom-call(bf16[2048,512]{1,0:T(8,128)(2,1)S(1)} %get-tuple-element.109.refs_0_, ...), custom_call_target="tpu_custom_call" | custom-call | flops 1 | bytes 1 | tf_op jit(solution)/shard_map/pallas_call | solution.py:447
  16.1 1.5 %collective-permute-start.6 = (bf16[128,512]{1,0:T(8,128)(2,1)S(1)}, bf16[128,512]{1,0:T(8,128)(2,1)S(1)}, u32[]{:S(2)}, u32[]{:S(2)}) collective-permute-start(bf16[128,512]{1,0:T(8,128)(2,1)S(1)} %get-tuple-element.121), channel_id=1, source_target_pairs={{0,25},{1,8},{2,27},{3,10},{4,29},{5,12},{6,31},{7,14},{8,1},{9,16... | collective-permute-start | bytes 393224 | tf_op jit(solution)/shard_map/ppermute | solution.py:514
  18.4 4.0 %collective-permute-done.6.refs_8_ = bf16[128,512]{1,0:T(8,128)(2,1)S(1)} collective-permute-done((bf16[128,512]{1,0:T(8,128)(2,1)S(1)}, bf16[128,512]{1,0:T(8,128)(2,1)S(1)}, u32[]{:S(2)}, u32[]{:S(2)}) %collective-permute-start.6) | collective-permute-done | bytes 131104 | tf_op jit(solution)/shard_map/ppermute | solution.py:514
  24.1 2.0 %collective-permute-start.9 = (bf16[128,512]{1,0:T(8,128)(2,1)S(1)}, bf16[128,512]{1,0:T(8,128)(2,1)S(1)}, u32[]{:S(2)}, u32[]{:S(2)}) collective-permute-start(bf16[128,512]{1,0:T(8,128)(2,1)S(1)} %get-tuple-element.136), channel_id=1, source_target_pairs={{0,27},{1,10},{2,25},{3,8},{4,31},{5,14},{6,29},{7,12},{8,3},{9,18... | collective-permute-start | bytes 393224 | tf_op jit(solution)/shard_map/ppermute | solution.py:514
  26.1 8.5 %collective-permute-done.7.refs_1_.h.refs_4_ = bf16[256,512]{1,0:T(8,128)(2,1)S(1)} collective-permute-done((bf16[256,512]{1,0:T(8,128)(2,1)S(1)}, bf16[256,512]{1,0:T(8,128)(2,1)S(1)}, u32[]{:S(2)}, u32[]{:S(2)}) %collective-permute-start.7) | collective-permute-done | bytes 262176 | tf_op jit(solution)/shard_map/ppermute | solution.py:514
  34.8 1.3 %collective-permute-done.8.refs_7_ = bf16[128,512]{1,0:T(8,128)(2,1)S(1)} collective-permute-done((bf16[128,512]{1,0:T(8,128)(2,1)S(1)}, bf16[128,512]{1,0:T(8,128)(2,1)S(1)}, u32[]{:S(2)}, u32[]{:S(2)}) %collective-permute-start.8) | collective-permute-done | bytes 131104 | tf_op jit(solution)/shard_map/ppermute | solution.py:514
  38.2 4.0 %collective-permute-start.12 = (bf16[256,512]{1,0:T(8,128)(2,1)S(1)}, bf16[256,512]{1,0:T(8,128)(2,1)S(1)}, u32[]{:S(2)}, u32[]{:S(2)}) collective-permute-start(bf16[256,512]{1,0:T(8,128)(2,1)S(1)} %get-tuple-element.149), channel_id=1, source_target_pairs={{0,1},{1,5},{4,0},{5,4},{8,9},{9,13},{12,8},{13,12},{16,17},{17,21... | collective-permute-start | bytes 786440 | tf_op jit(solution)/shard_map/ppermute | solution.py:514
  42.5 1.8 %collective-permute-start.15 = (bf16[128,512]{1,0:T(8,128)(2,1)S(1)}, bf16[128,512]{1,0:T(8,128)(2,1)S(1)}, u32[]{:S(2)}, u32[]{:S(2)}) collective-permute-start(bf16[128,512]{1,0:T(8,128)(2,1)S(1)} %get-tuple-element.166), channel_id=1, source_target_pairs={{0,25},{1,8},{2,27},{3,10},{4,29},{5,12},{6,31},{7,14},{8,1},{9,16... | collective-permute-start | bytes 393224 | tf_op jit(solution)/shard_map/ppermute | solution.py:514
  44.3 4.0 %collective-permute-done.12.refs_3_.refs_1_ = bf16[256,512]{1,0:T(8,128)(2,1)S(1)} collective-permute-done((bf16[256,512]{1,0:T(8,128)(2,1)S(1)}, bf16[256,512]{1,0:T(8,128)(2,1)S(1)}, u32[]{:S(2)}, u32[]{:S(2)}) %collective-permute-start.12) | collective-permute-done | bytes 262176 | tf_op jit(solution)/shard_map/ppermute | solution.py:514
  48.3 1.4 %collective-permute-done.15.refs_6_ = bf16[128,512]{1,0:T(8,128)(2,1)S(1)} collective-permute-done((bf16[128,512]{1,0:T(8,128)(2,1)S(1)}, bf16[128,512]{1,0:T(8,128)(2,1)S(1)}, u32[]{:S(2)}, u32[]{:S(2)}) %collective-permute-start.15) | collective-permute-done | bytes 131104 | tf_op jit(solution)/shard_map/ppermute | solution.py:514
  49.7 1.3 %collective-permute-start.18 = (bf16[128,512]{1,0:T(8,128)(2,1)S(1)}, bf16[128,512]{1,0:T(8,128)(2,1)S(1)}, u32[]{:S(2)}, u32[]{:S(2)}) collective-permute-start(bf16[128,512]{1,0:T(8,128)(2,1)S(1)} %get-tuple-element.167.refs_3_), channel_id=1, source_target_pairs={{2,25},{3,8},{6,29},{7,12},{10,1},{11,16},{14,5},{15,20},{18,9},{1... | collective-permute-start | bytes 393224 | tf_op jit(solution)/shard_map/ppermute | solution.py:514
  51.1 5.0 %collective-permute-start.17 = (bf16[256,512]{1,0:T(8,128)(2,1)S(1)}, bf16[256,512]{1,0:T(8,128)(2,1)S(1)}, u32[]{:S(2)}, u32[]{:S(2)}) collective-permute-start(bf16[256,512]{1,0:T(8,128)(2,1)S(1)} %shard_map.152.value), channel_id=1, source_target_pairs={{0,2},{1,3},{2,0},{3,1},{4,6},{5,7},{6,4},{7,5},{8,10},{9,11},{10,... | collective-permute-start | bytes 786440 | tf_op jit(solution)/shard_map/ppermute | solution.py:514
  56.0 3.8 %collective-permute-done.18.outer = bf16[128,512]{1,0:T(8,128)(2,1)S(1)} collective-permute-done((bf16[128,512]{1,0:T(8,128)(2,1)S(1)}, bf16[128,512]{1,0:T(8,128)(2,1)S(1)}, u32[]{:S(2)}, u32[]{:S(2)}) %collective-permute-start.18) | collective-permute-done | bytes 131104 | tf_op jit(solution)/shard_map/ppermute | solution.py:514
  59.9 4.7 %collective-permute-done.17.refs_5_ = bf16[256,512]{1,0:T(8,128)(2,1)S(1)} collective-permute-done((bf16[256,512]{1,0:T(8,128)(2,1)S(1)}, bf16[256,512]{1,0:T(8,128)(2,1)S(1)}, u32[]{:S(2)}, u32[]{:S(2)}) %collective-permute-start.17) | collective-permute-done | bytes 262176 | tf_op jit(solution)/shard_map/ppermute | solution.py:514
  69.1 3.0 %collective-permute-done.22.outer.refs_6_ = bf16[128,512]{1,0:T(8,128)(2,1)S(1)} collective-permute-done((bf16[128,512]{1,0:T(8,128)(2,1)S(1)}, bf16[128,512]{1,0:T(8,128)(2,1)S(1)}, u32[]{:S(2)}, u32[]{:S(2)}) %collective-permute-start.22) | collective-permute-done | bytes 131104 | tf_op jit(solution)/shard_map/ppermute | solution.py:514
  73.4 1.9 %collective-permute-start.26 = (bf16[128,512]{1,0:T(8,128)(2,1)S(1)}, bf16[128,512]{1,0:T(8,128)(2,1)S(1)}, u32[]{:S(2)}, u32[]{:S(2)}) collective-permute-start(bf16[128,512]{1,0:T(8,128)(2,1)S(1)} %get-tuple-element.195), channel_id=1, source_target_pairs={{0,28},{1,8},{2,30},{3,10},{4,29},{5,9},{6,31},{7,11},{8,4},{9,16}... | collective-permute-start | bytes 393224 | tf_op jit(solution)/shard_map/ppermute | solution.py:514
  76.7 1.6 %collective-permute-start.25 = (bf16[256,512]{1,0:T(8,128)(2,1)S(1)}, bf16[256,512]{1,0:T(8,128)(2,1)S(1)}, u32[]{:S(2)}, u32[]{:S(2)}) collective-permute-start(bf16[256,512]{1,0:T(8,128)(2,1)S(1)} %get-tuple-element.193), channel_id=1, source_target_pairs={{0,1},{1,5},{2,3},{3,7},{4,0},{5,4},{6,2},{7,6},{8,9},{9,13},{10,1... | collective-permute-start | bytes 786440 | tf_op jit(solution)/shard_map/ppermute | solution.py:514
  78.3 1.4 %collective-permute-done.26.outer = bf16[128,512]{1,0:T(8,128)(2,1)S(1)} collective-permute-done((bf16[128,512]{1,0:T(8,128)(2,1)S(1)}, bf16[128,512]{1,0:T(8,128)(2,1)S(1)}, u32[]{:S(2)}, u32[]{:S(2)}) %collective-permute-start.26) | collective-permute-done | bytes 131104 | tf_op jit(solution)/shard_map/ppermute | solution.py:514
  81.5 4.7 %collective-permute-done.25.refs_1_ = bf16[256,512]{1,0:T(8,128)(2,1)S(1)} collective-permute-done((bf16[256,512]{1,0:T(8,128)(2,1)S(1)}, bf16[256,512]{1,0:T(8,128)(2,1)S(1)}, u32[]{:S(2)}, u32[]{:S(2)}) %collective-permute-start.25) | collective-permute-done | bytes 262176 | tf_op jit(solution)/shard_map/ppermute | solution.py:514
  (66 shorter events, 19.1 us)
Async XLA Ops:
  1.9 8.3 %collective-permute-start.1 = (bf16[272,512]{1,0:T(8,128)(2,1)S(1)}, bf16[272,512]{1,0:T(8,128)(2,1)S(1)}, u32[]{:S(2)}, u32[]{:S(2)}) collective-permute-start(bf16[272,512]{1,0:T(8,128)(2,1)S(1)} %get-tuple-element.102), channel_id=1, source_target_pairs={{0,4},{1,0},{2,6},{3,2},{4,5},{5,1},{6,7},{7,3},{8,12},{9,8},{10,1... | collective-permute-start | bytes 835592 | tf_op jit(solution)/shard_map/ppermute | solution.py:514
  4.8 7.7 %collective-permute-start.2 = (bf16[128,512]{1,0:T(8,128)(2,1)S(1)}, bf16[128,512]{1,0:T(8,128)(2,1)S(1)}, u32[]{:S(2)}, u32[]{:S(2)}) collective-permute-start(bf16[128,512]{1,0:T(8,128)(2,1)S(1)} %get-tuple-element.103), channel_id=1, source_target_pairs={{0,25},{1,29},{2,27},{3,31},{4,8},{5,12},{6,10},{7,14},{8,1},{9,5}... | collective-permute-start | bytes 393224 | tf_op jit(solution)/shard_map/ppermute | solution.py:514
  7.0 7.5 %collective-permute-start.3 = (f32[1,512]{1,0:T(1,128)}, f32[1,512]{1,0:T(1,128)S(1)}, u32[]{:S(2)}, u32[]{:S(2)}) collective-permute-start(f32[1,512]{1,0:T(1,128)} %refs_1_.15), channel_id=1, source_target_pairs={{0,1},{1,0},{2,3},{3,2},{4,5},{5,4},{6,7},{7,6},{8,9},{9,8},{10,11... | collective-permute-start | bytes 6152 | tf_op jit(solution)/shard_map/ppermute | solution.py:514
  9.4 4.2 %collective-permute-start = (bf16[2048,512]{1,0:T(8,128)(2,1)S(1)}, bf16[2048,512]{1,0:T(8,128)(2,1)S(1)}, u32[]{:S(2)}, u32[]{:S(2)}) collective-permute-start(bf16[2048,512]{1,0:T(8,128)(2,1)S(1)} %shard_map.131.mine), channel_id=1, source_target_pairs={{0,1},{1,0},{2,3},{3,2},{4,5},{5,4},{6,7},{7,6},{8,9},{9,8},{10,11... | collective-permute-start | bytes 6291464 | tf_op jit(solution)/shard_map/ppermute | solution.py:514
  12.6 2.0 %collective-permute-start.4 = (bf16[128,512]{1,0:T(8,128)(2,1)S(1)}, bf16[128,512]{1,0:T(8,128)(2,1)S(1)}, u32[]{:S(2)}, u32[]{:S(2)}) collective-permute-start(bf16[128,512]{1,0:T(8,128)(2,1)S(1)} %get-tuple-element.114), channel_id=1, source_target_pairs={{0,1},{1,0},{2,3},{3,2},{4,5},{5,4},{6,7},{7,6},{8,9},{9,8},{10,11... | collective-permute-start | bytes 393224 | tf_op jit(solution)/shard_map/ppermute | solution.py:514
  15.9 1.7 %collective-permute-start.5 = (bf16[128,512]{1,0:T(8,128)(2,1)S(1)}, bf16[128,512]{1,0:T(8,128)(2,1)S(1)}, u32[]{:S(2)}, u32[]{:S(2)}) collective-permute-start(bf16[128,512]{1,0:T(8,128)(2,1)S(1)} %get-tuple-element.118), channel_id=1, source_target_pairs={{0,1},{1,0},{2,3},{3,2},{4,5},{5,4},{6,7},{7,6},{8,9},{9,8},{10,11... | collective-permute-start | bytes 393224 | tf_op jit(solution)/shard_map/ppermute | solution.py:514
  16.1 6.3 %collective-permute-start.6 = (bf16[128,512]{1,0:T(8,128)(2,1)S(1)}, bf16[128,512]{1,0:T(8,128)(2,1)S(1)}, u32[]{:S(2)}, u32[]{:S(2)}) collective-permute-start(bf16[128,512]{1,0:T(8,128)(2,1)S(1)} %get-tuple-element.121), channel_id=1, source_target_pairs={{0,25},{1,8},{2,27},{3,10},{4,29},{5,12},{6,31},{7,14},{8,1},{9,16... | collective-permute-start | bytes 393224 | tf_op jit(solution)/shard_map/ppermute | solution.py:514
  23.5 11.1 %collective-permute-start.7 = (bf16[256,512]{1,0:T(8,128)(2,1)S(1)}, bf16[256,512]{1,0:T(8,128)(2,1)S(1)}, u32[]{:S(2)}, u32[]{:S(2)}) collective-permute-start(bf16[256,512]{1,0:T(8,128)(2,1)S(1)} %get-tuple-element.122.h), channel_id=1, source_target_pairs={{0,2},{1,3},{2,0},{3,1},{4,6},{5,7},{6,4},{7,5},{8,10},{9,11},{10,... | collective-permute-start | bytes 786440 | tf_op jit(solution)/shard_map/ppermute | solution.py:514
  24.1 10.7 %collective-permute-start.9 = (bf16[128,512]{1,0:T(8,128)(2,1)S(1)}, bf16[128,512]{1,0:T(8,128)(2,1)S(1)}, u32[]{:S(2)}, u32[]{:S(2)}) collective-permute-start(bf16[128,512]{1,0:T(8,128)(2,1)S(1)} %get-tuple-element.136), channel_id=1, source_target_pairs={{0,27},{1,10},{2,25},{3,8},{4,31},{5,14},{6,29},{7,12},{8,3},{9,18... | collective-permute-start | bytes 393224 | tf_op jit(solution)/shard_map/ppermute | solution.py:514
  36.2 6.3 %collective-permute-start.13 = (bf16[128,512]{1,0:T(8,128)(2,1)S(1)}, bf16[128,512]{1,0:T(8,128)(2,1)S(1)}, u32[]{:S(2)}, u32[]{:S(2)}) collective-permute-start(bf16[128,512]{1,0:T(8,128)(2,1)S(1)} %get-tuple-element.152), channel_id=1, source_target_pairs={{0,25},{1,8},{2,27},{3,10},{4,29},{5,12},{6,31},{7,14},{8,1},{9,16... | collective-permute-start | bytes 393224 | tf_op jit(solution)/shard_map/ppermute | solution.py:514
  37.5 6.8 %collective-permute-start.11 = (bf16[256,512]{1,0:T(8,128)(2,1)S(1)}, bf16[256,512]{1,0:T(8,128)(2,1)S(1)}, u32[]{:S(2)}, u32[]{:S(2)}) collective-permute-start(bf16[256,512]{1,0:T(8,128)(2,1)S(1)} %get-tuple-element.148), channel_id=1, source_target_pairs={{0,0},{1,4},{4,1},{5,5},{8,8},{9,12},{12,9},{13,13},{16,16},{17,20... | collective-permute-start | bytes 786440 | tf_op jit(solution)/shard_map/ppermute | solution.py:514
  38.2 10.1 %collective-permute-start.12 = (bf16[256,512]{1,0:T(8,128)(2,1)S(1)}, bf16[256,512]{1,0:T(8,128)(2,1)S(1)}, u32[]{:S(2)}, u32[]{:S(2)}) collective-permute-start(bf16[256,512]{1,0:T(8,128)(2,1)S(1)} %get-tuple-element.149), channel_id=1, source_target_pairs={{0,1},{1,5},{4,0},{5,4},{8,9},{9,13},{12,8},{13,12},{16,17},{17,21... | collective-permute-start | bytes 786440 | tf_op jit(solution)/shard_map/ppermute | solution.py:514
  42.5 1.8 %collective-permute-start.14 = (bf16[128,512]{1,0:T(8,128)(2,1)S(1)}, bf16[128,512]{1,0:T(8,128)(2,1)S(1)}, u32[]{:S(2)}, u32[]{:S(2)}) collective-permute-start(bf16[128,512]{1,0:T(8,128)(2,1)S(1)} %get-tuple-element.161), channel_id=1, source_target_pairs={{0,1},{1,0},{2,3},{3,2},{4,5},{5,4},{6,7},{7,6},{8,9},{9,8},{10,11... | collective-permute-start | bytes 393224 | tf_op jit(solution)/shard_map/ppermute | solution.py:514
  42.5 7.2 %collective-permute-start.15 = (bf16[128,512]{1,0:T(8,128)(2,1)S(1)}, bf16[128,512]{1,0:T(8,128)(2,1)S(1)}, u32[]{:S(2)}, u32[]{:S(2)}) collective-permute-start(bf16[128,512]{1,0:T(8,128)(2,1)S(1)} %get-tuple-element.166), channel_id=1, source_target_pairs={{0,25},{1,8},{2,27},{3,10},{4,29},{5,12},{6,31},{7,14},{8,1},{9,16... | collective-permute-start | bytes 393224 | tf_op jit(solution)/shard_map/ppermute | solution.py:514
  49.7 10.1 %collective-permute-start.18 = (bf16[128,512]{1,0:T(8,128)(2,1)S(1)}, bf16[128,512]{1,0:T(8,128)(2,1)S(1)}, u32[]{:S(2)}, u32[]{:S(2)}) collective-permute-start(bf16[128,512]{1,0:T(8,128)(2,1)S(1)} %get-tuple-element.167.refs_3_), channel_id=1, source_target_pairs={{2,25},{3,8},{6,29},{7,12},{10,1},{11,16},{14,5},{15,20},{18,9},{1... | collective-permute-start | bytes 393224 | tf_op jit(solution)/shard_map/ppermute | solution.py:514
  51.1 13.5 %collective-permute-start.17 = (bf16[256,512]{1,0:T(8,128)(2,1)S(1)}, bf16[256,512]{1,0:T(8,128)(2,1)S(1)}, u32[]{:S(2)}, u32[]{:S(2)}) collective-permute-start(bf16[256,512]{1,0:T(8,128)(2,1)S(1)} %shard_map.152.value), channel_id=1, source_target_pairs={{0,2},{1,3},{2,0},{3,1},{4,6},{5,7},{6,4},{7,5},{8,10},{9,11},{10,... | collective-permute-start | bytes 786440 | tf_op jit(solution)/shard_map/ppermute | solution.py:514
  65.8 6.3 %collective-permute-start.22 = (bf16[128,512]{1,0:T(8,128)(2,1)S(1)}, bf16[128,512]{1,0:T(8,128)(2,1)S(1)}, u32[]{:S(2)}, u32[]{:S(2)}) collective-permute-start(bf16[128,512]{1,0:T(8,128)(2,1)S(1)} %get-tuple-element.181), channel_id=1, source_target_pairs={{0,25},{1,8},{2,27},{3,10},{4,29},{5,12},{6,31},{7,14},{8,1},{9,16... | collective-permute-start | bytes 393224 | tf_op jit(solution)/shard_map/ppermute | solution.py:514
  67.8 7.6 %collective-permute-start.20 = (bf16[256,512]{1,0:T(8,128)(2,1)S(1)}, bf16[256,512]{1,0:T(8,128)(2,1)S(1)}, u32[]{:S(2)}, u32[]{:S(2)}) collective-permute-start(bf16[256,512]{1,0:T(8,128)(2,1)S(1)} %get-tuple-element.179), channel_id=1, source_target_pairs={{2,2},{3,6},{6,3},{7,7},{10,10},{11,14},{14,11},{15,15},{18,18},{1... | collective-permute-start | bytes 786440 | tf_op jit(solution)/shard_map/ppermute | solution.py:514
  68.4 6.9 %collective-permute-start.21 = (bf16[256,512]{1,0:T(8,128)(2,1)S(1)}, bf16[256,512]{1,0:T(8,128)(2,1)S(1)}, u32[]{:S(2)}, u32[]{:S(2)}) collective-permute-start(bf16[256,512]{1,0:T(8,128)(2,1)S(1)} %get-tuple-element.180), channel_id=1, source_target_pairs={{2,3},{3,7},{6,2},{7,6},{10,11},{11,15},{14,10},{15,14},{18,19},{1... | collective-permute-start | bytes 786440 | tf_op jit(solution)/shard_map/ppermute | solution.py:514
  73.3 2.0 %collective-permute-start.23 = (bf16[128,512]{1,0:T(8,128)(2,1)S(1)}, bf16[128,512]{1,0:T(8,128)(2,1)S(1)}, u32[]{:S(2)}, u32[]{:S(2)}) collective-permute-start(bf16[128,512]{1,0:T(8,128)(2,1)S(1)} %get-tuple-element.187), channel_id=1, source_target_pairs={{0,1},{1,0},{2,3},{3,2},{4,5},{5,4},{6,7},{7,6},{8,9},{9,8},{10,11... | collective-permute-start | bytes 393224 | tf_op jit(solution)/shard_map/ppermute | solution.py:514
  73.4 6.4 %collective-permute-start.26 = (bf16[128,512]{1,0:T(8,128)(2,1)S(1)}, bf16[128,512]{1,0:T(8,128)(2,1)S(1)}, u32[]{:S(2)}, u32[]{:S(2)}) collective-permute-start(bf16[128,512]{1,0:T(8,128)(2,1)S(1)} %get-tuple-element.195), channel_id=1, source_target_pairs={{0,28},{1,8},{2,30},{3,10},{4,29},{5,9},{6,31},{7,11},{8,4},{9,16}... | collective-permute-start | bytes 393224 | tf_op jit(solution)/shard_map/ppermute | solution.py:514
  76.0 5.5 %collective-permute-start.24 = (bf16[256,512]{1,0:T(8,128)(2,1)S(1)}, bf16[256,512]{1,0:T(8,128)(2,1)S(1)}, u32[]{:S(2)}, u32[]{:S(2)}) collective-permute-start(bf16[256,512]{1,0:T(8,128)(2,1)S(1)} %get-tuple-element.192), channel_id=1, source_target_pairs={{0,0},{1,4},{2,2},{3,6},{4,1},{5,5},{6,3},{7,7},{8,8},{9,12},{10,1... | collective-permute-start | bytes 786440 | tf_op jit(solution)/shard_map/ppermute | solution.py:514
  76.7 9.5 %collective-permute-start.25 = (bf16[256,512]{1,0:T(8,128)(2,1)S(1)}, bf16[256,512]{1,0:T(8,128)(2,1)S(1)}, u32[]{:S(2)}, u32[]{:S(2)}) collective-permute-start(bf16[256,512]{1,0:T(8,128)(2,1)S(1)} %get-tuple-element.193), channel_id=1, source_target_pairs={{0,1},{1,5},{2,3},{3,7},{4,0},{5,4},{6,2},{7,6},{8,9},{9,13},{10,1... | collective-permute-start | bytes 786440 | tf_op jit(solution)/shard_map/ppermute | solution.py:514
  79.7 1.6 %collective-permute-start.27 = (bf16[128,512]{1,0:T(8,128)(2,1)S(1)}, bf16[128,512]{1,0:T(8,128)(2,1)S(1)}, u32[]{:S(2)}, u32[]{:S(2)}) collective-permute-start(bf16[128,512]{1,0:T(8,128)(2,1)S(1)} %collective-permute-done.26.outer), channel_id=1, source_target_pairs={{0,1},{1,0},{2,3},{3,2},{4,5},{5,4},{6,7},{7,6},{8,9},{9,8},{10,11... | collective-permute-start | bytes 393224 | tf_op jit(solution)/shard_map/ppermute | solution.py:514
  (5 other events, 6.4 us)
